TPU v7x, 32 devices: a whole 2x2x4 slice. The times are simulated.
32 devices in a mesh: samp: 4 (over z), feat: 8 (over y, x, core).
Axes of the slice: x: 2, y: 2, z: 4, core: 2. Of those that a mesh axis runs over, the one named last changes fastest.
Arguments:
- inputs: bfloat16 [440, 8192], P(None, ('samp', 'feat')), may hold values from -6 to 6
- probs: bfloat16 [147, 8192], P(None, ('samp', 'feat')), may hold values from 0 to 1, as said below
- labels: int32 [8192], P(('samp', 'feat')), may hold values from 0 to 146
- proj_weight: bfloat16 [440, 32768], P(None, ('feat', 'samp')), may hold values from -0.25 to 0.25
- phase: bfloat16 [1, 32768], P(None, ('feat', 'samp')), may hold values from -3.140625 to 3.140625
- direction: bfloat16 [147, 32768], P(None, ('feat', 'samp')), may hold values from -0.03125 to 0.03125
- damping: float32 [1], replicated, may hold values from 300 to 3000
Outputs:
- hess_vec: float32 [147, 32768], P(None, ('feat', 'samp'))
- gradient: float32 [147, 32768], P(None, ('feat', 'samp'))
Inputs may be any that keep to these rules, and one draw needn't show every extreme that they name: Each column of probs is positive and sums to one up to rounding.
All inputs are finite; a program needn't handle non-finite values.
Results may differ from a plain program's by a relative error of at most 0.005.
The roundings to bfloat16 on the way count: a program that leaves them out, or rounds other values in their place, can miss the bound.
Values may be sent and summed in bfloat16 or wider, within the bound.
No kernel may reach another device: no remote copies, remote signals or barrier semaphores. Data moves between devices by JAX's collectives and lax.ppermute only.
A program may use at most 64 MiB of HBM per device.

v0:
```python
import jax
import jax.numpy as jnp
from jax import lax
from jax.sharding import PartitionSpec as P


def on_device(inputs, probs, labels, proj_weight, phase, direction, damping):
    classes = probs.shape[0]
    own_prob = probs.astype(jnp.float32)
    class_ids = lax.broadcasted_iota(jnp.int32, probs.shape, 0)
    onehot = (class_ids == labels[None, :]).astype(jnp.float32)
    own_resid = (own_prob - onehot).astype(jnp.bfloat16)
    w_all, phase_all, dir_all = (
        lax.all_gather(proj_weight, "samp", axis=1, tiled=True),
        lax.all_gather(phase, "samp", axis=1, tiled=True),
        lax.all_gather(direction, "samp", axis=1, tiled=True),
    )
    phase_col = phase_all.astype(jnp.float32).T
    x_all, resid_all, probs_all = (
        lax.all_gather(inputs, "feat", axis=1, tiled=True),
        lax.all_gather(own_resid, "feat", axis=1, tiled=True),
        lax.all_gather(probs, "feat", axis=1, tiled=True),
    )
    rows = x_all.shape[1]
    width = w_all.shape[1]
    block = min(512, rows)
    count = rows // block
    dims = (((1,), (1,)), ((), ()))

    def features(start):
        x_block = lax.dynamic_slice_in_dim(x_all, start, block, 1)
        proj = lax.dot_general(
            w_all, x_block, (((0,), (0,)), ((), ())), preferred_element_type=jnp.float32
        )
        return jnp.cos(proj + phase_col).astype(jnp.bfloat16)

    empty_tangent = jnp.zeros((classes, rows), jnp.float32)
    empty_block = jnp.zeros((classes, width), jnp.float32)

    def first_early(index, carry):
        tangent, grad_acc = carry
        start = index * block
        feats = features(start)
        piece = jnp.dot(dir_all, feats, preferred_element_type=jnp.float32)
        tangent = lax.dynamic_update_slice_in_dim(tangent, piece, start, 1)
        resid_block = lax.dynamic_slice_in_dim(resid_all, start, block, 1)
        grad_acc = grad_acc + lax.dot_general(
            resid_block, feats, dims, preferred_element_type=jnp.float32
        )
        return (tangent, grad_acc)

    tangent, grad_acc = lax.fori_loop(0, count, first_early, (empty_tangent, empty_block))
    gradient = lax.psum_scatter(grad_acc, "samp", scatter_dimension=1, tiled=True)
    total = lax.psum(tangent.astype(jnp.bfloat16), "feat").astype(jnp.float32)
    prob = probs_all.astype(jnp.float32)
    mixed = jnp.sum(prob * total, axis=0, keepdims=True)
    curv_all = (prob * (total - mixed)).astype(jnp.bfloat16)

    def second_early(index, hv_acc):
        start = index * block
        feats = features(start)
        curv_block = lax.dynamic_slice_in_dim(curv_all, start, block, 1)
        return hv_acc + lax.dot_general(curv_block, feats, dims, preferred_element_type=jnp.float32)

    hv_acc = lax.fori_loop(0, count, second_early, empty_block)
    hv_share = lax.psum_scatter(
        hv_acc.astype(jnp.bfloat16), "samp", scatter_dimension=1, tiled=True
    ).astype(jnp.float32)
    hess_vec = hv_share + damping[0] * direction.astype(jnp.float32)
    return (hess_vec, gradient)


def solution(mesh):
    placed = (
        P(None, ("samp", "feat")),
        P(None, ("samp", "feat")),
        P(("samp", "feat")),
        P(None, ("feat", "samp")),
        P(None, ("feat", "samp")),
        P(None, ("feat", "samp")),
        P(),
    )
    return jax.shard_map(
        on_device,
        mesh=mesh,
        in_specs=placed,
        out_specs=(P(None, ("feat", "samp")), P(None, ("feat", "samp"))),
        check_vma=False,
    )
```

profile of v0, /device:TPU:0, one launch (start us, length us, event | category | flops | bytes accessed | tf_op | source)
XLA Modules:
  0.0 576.7 jit_solution(1397754802884494409)
XLA Ops:
  7.2 0.0 all-gather.8.cloned.1.call-start
  7.2 0.7 all-gather.8.cloned.1.call-update
  7.9 0.0 all-gather.4.cloned.1.call-start
  7.9 0.7 all-gather.4.cloned.1.call-update
  8.6 0.0 all-gather.6.cloned.1.call-start
  8.7 0.7 all-gather.6.cloned.1.call-update
  9.4 0.0 all-reduce.2.cloned.1.call-start
  9.4 15.0 %all_gather.21 = bf16[1,4096]{1,0:T(2,128)(2,1)S(1)} all-gather(bf16[1,1024]{1,0:T(2,128)(2,1)} %param.15), channel_id=1, replica_groups=mesh['samp'=4,'feat'=8] {'samp'}, dimensions={1}, use_global_device_ids=true | all-gather | bytes 10240 | tf_op jit(solution)/shard_map/all_gather | solution.py:15
  24.5 0.9 subtract_convert_fusion
  25.4 11.9 %all_gather.23 = bf16[147,2048]{1,0:T(8,128)(2,1)S(1)} all-gather(bf16[147,256]{1,0:T(8,128)(2,1)S(1)} %subtract_convert_fusion), channel_id=1, replica_groups=mesh['samp'=4,'feat'=8] {'feat'}, dimensions={1}, use_global_device_ids=true | all-gather | bytes 677376 | tf_op jit(solution)/shard_map/all_gather | solution.py:21
  37.3 6.6 %all-gather.8.cloned.1.call-done = bf16[147,4096]{1,0:T(8,128)(2,1)} async-done(((bf16[147,1024]{1,0:T(8,128)(2,1)}), bf16[147,4096]{1,0:T(8,128)(2,1)}) %all-gather.8.cloned.1.call-update) | async-done | bytes 1204240 | tf_op jit(solution)/shard_map/all_gather | solution.py:16
  44.0 27.8 %all-gather.4.cloned.1.call-done = bf16[440,2048]{1,0:T(8,128)(2,1)} async-done(((bf16[440,256]{1,0:T(8,128)(2,1)}), bf16[440,2048]{1,0:T(8,128)(2,1)}) %all-gather.4.cloned.1.call-update) | async-done | bytes 1802256 | tf_op jit(solution)/shard_map/all_gather | solution.py:20
  71.7 72.6 %all-gather.6.cloned.1.call-done = bf16[440,4096]{1,0:T(8,128)(2,1)} async-done(((bf16[440,1024]{1,0:T(8,128)(2,1)}), bf16[440,4096]{1,0:T(8,128)(2,1)}) %all-gather.6.cloned.1.call-update) | async-done | bytes 3604496 | tf_op jit(solution)/shard_map/all_gather | solution.py:14
  144.4 0.9 broadcast_in_dim.9
  145.3 150.6 %while.30 = (s32[]{:T(128)}, bf16[147,2048]{1,0:T(8,128)(2,1)}, f32[147,4096]{1,0:T(8,128)S(1)}, bf16[440,2048]{1,0:T(8,128)(2,1)}, bf16[440,4096]{1,0:T(8,128)(...) while((s32[]{:T(128)}, bf16[147,2048]{1,0:T(8,128)(2,1)}, ...), condition=%wide.region_1.0_spmd.clone, body=%wide.region_0.0_spmd.clone.sunk | while | flops 3084017664 | bytes 44818668 | solution.py:52
  145.3 31.7 %cosine_convert_fusion.3 = bf16[512,4096]{1,0:T(8,128)(2,1)} fusion(bf16[440,4096]{1,0:T(8,128)(2,1)} %get-tuple-element.444, f32[4096]{0:T(1024)S(1)} %bitcast.32, bf16[440,2048]{1,0:T(8,128)(2,1)} %get-tuple-element.443, s32[]{:T(128)S(6)} %select_n.21), kind=kOutput, calls=%fused_computation.clone.1 | convolution fusion | flops 1849688064 | bytes 8265732 | tf_op jit(solution)/shard_map/while/body/eval_jaxpr/dot_general | solution.py:32
  176.9 3.6 convolution_add_fusion.4
  180.6 0.2 copy-done.4
  180.8 2.2 fusion.33
  182.9 31.6 %cosine_convert_fusion.3 = bf16[512,4096]{1,0:T(8,128)(2,1)} fusion(bf16[440,4096]{1,0:T(8,128)(2,1)} %get-tuple-element.444, f32[4096]{0:T(1024)S(1)} %bitcast.32, bf16[440,2048]{1,0:T(8,128)(2,1)} %get-tuple-element.443, s32[]{:T(128)S(6)} %select_n.21), kind=kOutput, calls=%fused_computation.clone.1 | convolution fusion | flops 1849688064 | bytes 8265732 | tf_op jit(solution)/shard_map/while/body/eval_jaxpr/dot_general | solution.py:32
  214.6 3.6 convolution_add_fusion.4
  218.2 0.2 copy-done.4
  218.4 2.2 fusion.33
  220.6 31.6 %cosine_convert_fusion.3 = bf16[512,4096]{1,0:T(8,128)(2,1)} fusion(bf16[440,4096]{1,0:T(8,128)(2,1)} %get-tuple-element.444, f32[4096]{0:T(1024)S(1)} %bitcast.32, bf16[440,2048]{1,0:T(8,128)(2,1)} %get-tuple-element.443, s32[]{:T(128)S(6)} %select_n.21), kind=kOutput, calls=%fused_computation.clone.1 | convolution fusion | flops 1849688064 | bytes 8265732 | tf_op jit(solution)/shard_map/while/body/eval_jaxpr/dot_general | solution.py:32
  252.2 3.6 convolution_add_fusion.4
  255.8 0.2 copy-done.4
  256.0 2.2 fusion.33
  258.2 31.6 %cosine_convert_fusion.3 = bf16[512,4096]{1,0:T(8,128)(2,1)} fusion(bf16[440,4096]{1,0:T(8,128)(2,1)} %get-tuple-element.444, f32[4096]{0:T(1024)S(1)} %bitcast.32, bf16[440,2048]{1,0:T(8,128)(2,1)} %get-tuple-element.443, s32[]{:T(128)S(6)} %select_n.21), kind=kOutput, calls=%fused_computation.clone.1 | convolution fusion | flops 1849688064 | bytes 8265732 | tf_op jit(solution)/shard_map/while/body/eval_jaxpr/dot_general | solution.py:32
  289.8 3.6 convolution_add_fusion.4
  293.5 0.2 copy-done.4
  293.7 2.2 fusion.33
  295.9 0.0 reduce-scatter.3.cloned.1.call-start
  295.9 13.1 %all_gather.18 = bf16[147,2048]{1,0:T(8,128)(2,1)S(1)} all-gather(bf16[147,256]{1,0:T(8,128)(2,1)S(1)} %copy-done.3), channel_id=1, replica_groups=mesh['samp'=4,'feat'=8] {'feat'}, dimensions={1}, use_global_device_ids=true | all-gather | bytes 677376 | tf_op jit(solution)/shard_map/all_gather | solution.py:22
  309.0 40.6 %all-reduce.2.cloned.1.call-done = bf16[147,2048]{1,0:T(8,128)(2,1)} async-done(((bf16[147,2048]{1,0:T(8,128)(2,1)}), bf16[147,2048]{1,0:T(8,128)(2,1)}) %all-reduce.2.cloned.1.call-update) | async-done | bytes 602128 | tf_op jit(solution)/shard_map/psum | solution.py:54
  349.6 1.3 fusion.11
  350.9 2.1 fusion.10
  353.0 132.4 %while.31 = (s32[]{:T(128)}, f32[147,4096]{1,0:T(8,128)}, bf16[147,2048]{1,0:T(8,128)(2,1)}, bf16[440,2048]{1,0:T(8,128)(2,1)}, bf16[440,4096]{1,0:T(8,128)(2,1)...) while((s32[]{:T(128)}, f32[147,4096]{1,0:T(8,128)}, ...), condition=%wide.region_5.0_spmd.clone, body=%wide.region_4.0_spmd.clone.sunk | while | flops 2467454976 | bytes 9127580 | solution.py:65
  353.0 32.8 %convolution_add_fusion.5 = f32[147,4096]{1,0:T(8,128)} fusion(f32[147,4096]{1,0:T(8,128)} %get-tuple-element.463, pred[]{:T(512)S(6)} %compare.7, bf16[440,4096]{1,0:T(8,128)(2,1)} %get-tuple-element.476, f32[4096]{0:T(1024)S(1)} %bitcast.33, bf16[440,2048]{1,0:T(8,128)(2,1)} %get-tuple-element.475, s32[]{:T(128)S(6)} %select_n.22, ...), kind=kOutput, calls=%fused_computation.9.clone.1 | convolution fusion | flops 2467454976 | bytes 9127424 | tf_op jit(solution)/shard_map/while/body/eval_jaxpr/dot_general | solution.py:63
  385.8 33.2 %convolution_add_fusion.5 = f32[147,4096]{1,0:T(8,128)} fusion(f32[147,4096]{1,0:T(8,128)} %get-tuple-element.463, pred[]{:T(512)S(6)} %compare.7, bf16[440,4096]{1,0:T(8,128)(2,1)} %get-tuple-element.476, f32[4096]{0:T(1024)S(1)} %bitcast.33, bf16[440,2048]{1,0:T(8,128)(2,1)} %get-tuple-element.475, s32[]{:T(128)S(6)} %select_n.22, ...), kind=kOutput, calls=%fused_computation.9.clone.1 | convolution fusion | flops 2467454976 | bytes 9127424 | tf_op jit(solution)/shard_map/while/body/eval_jaxpr/dot_general | solution.py:63
  419.0 33.2 %convolution_add_fusion.5 = f32[147,4096]{1,0:T(8,128)} fusion(f32[147,4096]{1,0:T(8,128)} %get-tuple-element.463, pred[]{:T(512)S(6)} %compare.7, bf16[440,4096]{1,0:T(8,128)(2,1)} %get-tuple-element.476, f32[4096]{0:T(1024)S(1)} %bitcast.33, bf16[440,2048]{1,0:T(8,128)(2,1)} %get-tuple-element.475, s32[]{:T(128)S(6)} %select_n.22, ...), kind=kOutput, calls=%fused_computation.9.clone.1 | convolution fusion | flops 2467454976 | bytes 9127424 | tf_op jit(solution)/shard_map/while/body/eval_jaxpr/dot_general | solution.py:63
  452.2 33.2 %convolution_add_fusion.5 = f32[147,4096]{1,0:T(8,128)} fusion(f32[147,4096]{1,0:T(8,128)} %get-tuple-element.463, pred[]{:T(512)S(6)} %compare.7, bf16[440,4096]{1,0:T(8,128)(2,1)} %get-tuple-element.476, f32[4096]{0:T(1024)S(1)} %bitcast.33, bf16[440,2048]{1,0:T(8,128)(2,1)} %get-tuple-element.475, s32[]{:T(128)S(6)} %select_n.22, ...), kind=kOutput, calls=%fused_computation.9.clone.1 | convolution fusion | flops 2467454976 | bytes 9127424 | tf_op jit(solution)/shard_map/while/body/eval_jaxpr/dot_general | solution.py:63
  485.4 2.9 convert_element_type.54
  488.3 0.0 reduce-scatter.3.cloned.1.call-update
  488.3 0.0 reduce-scatter.5.cloned.1.call-start
  488.3 0.5 reduce-scatter.5.cloned.1.call-update
  489.5 28.7 %reduce-scatter.3.cloned.1.call-done = bf16[147,1024]{1,0:T(8,128)(2,1)} async-done(((bf16[147,4096]{1,0:T(8,128)(2,1)}), bf16[147,1024]{1,0:T(8,128)(2,1)}) %reduce-scatter.3.cloned.1.call-update) | async-done | bytes 301072 | tf_op jit(solution)/shard_map/reduce_scatter | solution.py:66
  518.2 1.9 multiply_add_fusion
  520.1 49.7 %reduce-scatter.5.cloned.1.call-done = f32[147,1024]{1,0:T(8,128)} async-done(((f32[147,4096]{1,0:T(8,128)}), f32[147,1024]{1,0:T(8,128)}) %reduce-scatter.5.cloned.1.call-update) | async-done | bytes 602128 | tf_op jit(solution)/shard_map/reduce_scatter | solution.py:53
  (22 shorter events, 0.1 us)
Async XLA Ops:
  7.2 36.8 %all-gather.8.cloned.1.call-start = ((), (), s32[]{:S(2)}) async-start(), calls=%async_computation.4 | async-start | bytes 1556480 | tf_op jit(solution)/shard_map/all_gather | solution.py:16
  7.9 63.8 %all-gather.4.cloned.1.call-start = ((), (), s32[]{:S(2)}) async-start(), calls=%async_computation.2 | async-start | bytes 2027520 | tf_op jit(solution)/shard_map/all_gather | solution.py:20
  8.6 135.7 %all-gather.6.cloned.1.call-start = ((), (), s32[]{:S(2)}) async-start(), calls=%async_computation.3 | async-start | bytes 4505600 | tf_op jit(solution)/shard_map/all_gather | solution.py:14
  9.4 340.2 %all-reduce.2.cloned.1.call-start = ((), (), s32[]{:S(2)}) async-start(), calls=%async_computation.5 | async-start | bytes 1245184 | tf_op jit(solution)/shard_map/psum | solution.py:54
  145.3 150.7 %copy-start.3 = (bf16[147,256]{1,0:T(8,128)(2,1)S(1)}, bf16[147,256]{1,0:T(8,128)(2,1)}, u32[]{:S(2)}) copy-start(bf16[147,256]{1,0:T(8,128)(2,1)} %param.12) | copy-start | bytes 225796
  176.9 3.6 copy-start
  176.9 3.8 copy-start.4
  214.6 3.6 copy-start
  214.6 3.8 copy-start.4
  252.2 3.6 copy-start
  252.2 3.8 copy-start.4
  289.8 3.6 copy-start
  289.8 3.8 copy-start.4
  295.8 57.1 %copy-start.1 = (f32[147,4096]{1,0:T(8,128)}, f32[147,4096]{1,0:T(8,128)S(1)}, u32[]{:S(2)}) copy-start(f32[147,4096]{1,0:T(8,128)S(1)} %get-tuple-element.253) | copy-start | bytes 7225348
  295.9 222.4 %reduce-scatter.3.cloned.1.call-start = ((), (), s32[]{:S(2)}) async-start(), calls=%async_computation.6 | async-start | bytes 1556480 | tf_op jit(solution)/shard_map/reduce_scatter | solution.py:66
  488.3 30.0 %copy-start.2 = (bf16[147,1024]{1,0:T(8,128)(2,1)S(1)}, bf16[147,1024]{1,0:T(8,128)(2,1)}, u32[]{:S(2)}) copy-start(bf16[147,1024]{1,0:T(8,128)(2,1)} %param.16) | copy-start | bytes 903172
  488.3 81.6 %reduce-scatter.5.cloned.1.call-start = ((), (), s32[]{:S(2)}) async-start(), calls=%async_computation.7 | async-start | bytes 3112960 | tf_op jit(solution)/shard_map/reduce_scatter | solution.py:53
Sparse Core Ops, SparseCore 0:
  9.6 34.3 all-gather.7
  45.8 25.8 all-gather.3
  73.3 71.0 all-gather.5
  296.0 53.5 all-reduce.1
  488.4 29.7 reduce-scatter.2
  521.0 48.8 reduce-scatter.4
where the time goes:
time: 577 us
  matrix products  282 us (49%)
  waiting for transfers between devices  229 us (40%)
  blocking collectives  40 us (7%)
  between operations  14.8 us (3%)
  other arithmetic  9.11 us (2%)
    dot_general x4, matrix products, second_early(): lax.dot_general(curv_block, feats, dims, preferred_element_type=jnp.float32)  132 us
    dot_general x4, matrix products, features(): lax.dot_general(w_all, x_block, (((0,), (0,)), ((), ())), preferred_eleme...  127 us
    all_gather x1, waiting for transfers between devices, on_device(): lax.all_gather(proj_weight, 'samp', axis=1, tiled=True)  72.6 us
    reduce_scatter x1, waiting for transfers between devices, on_device(): lax.psum_scatter(grad_acc, 'samp', scatter_dimension=1, tiled=True)  49.7 us
    psum x1, waiting for transfers between devices, on_device(): total = lax.psum(tangent.astype(jnp.bfloat16), 'feat').astype(jnp.float32)  40.6 us
    reduce_scatter x1, waiting for transfers between devices, on_device(): lax.psum_scatter(hv_acc.astype(jnp.bfloat16), 'samp', scatter_dimension=1...  28.7 us
    all_gather x1, waiting for transfers between devices, on_device(): lax.all_gather(inputs, 'feat', axis=1, tiled=True)  27.8 us
    all_gather x1, blocking collectives, on_device(): lax.all_gather(phase, 'samp', axis=1, tiled=True)  15 us
  transfers between devices with their start and end apart: 6, of which 6 were waited for; matrix products, arithmetic and copies ran while one was open for 0% of the time, Pallas kernels for 0%

commit v1 on v0

v1 whole, which is shorter than its diff:
```python
import functools
import math

import jax
import jax.numpy as jnp
from jax import lax
from jax.experimental import pallas as pl
from jax.experimental.pallas import tpu as pltpu
from jax.sharding import PartitionSpec as P

F32, BF16 = jnp.float32, jnp.bfloat16
VMEM = 48 * 2**20
COEFS = (0.99999921, -19.73898036, 64.92865742, -85.27162153, 58.79049212, -21.07110563)
ROUNDER = 12582912.0


def up(value, step):
    return -(-value // step) * step


def params():
    return pltpu.CompilerParams(vmem_limit_bytes=VMEM)


def cosine(angle):
    turns = angle * (0.5 / math.pi)
    rest = turns - ((turns + ROUNDER) - ROUNDER)
    square = rest * rest
    total = square * COEFS[-1] + COEFS[-2]
    for coef in COEFS[-3::-1]:
        total = total * square + coef
    return total


def pack_kernel(raw, classes, x_ref, p_ref, l_ref, w_ref, ph_ref, d_ref, xo_ref, wo_ref):
    depth = up(raw + 1, 16)
    rows = xo_ref.shape[0]
    n, f = xo_ref.shape[1], wo_ref.shape[1]
    xo_ref[:raw, :] = x_ref[...]
    first = lax.broadcasted_iota(jnp.int32, (depth - raw, n), 0) == 0
    xo_ref[raw:depth, :] = jnp.where(first, 1.0, 0.0).astype(BF16)
    ids = lax.broadcasted_iota(jnp.int32, (classes, n), 0)
    onehot = (ids == l_ref[...]).astype(F32)
    xo_ref[depth : depth + classes, :] = (p_ref[...].astype(F32) - onehot).astype(BF16)
    xo_ref[depth + classes :, :] = jnp.zeros((rows - depth - classes, n), BF16)
    wo_ref[:raw, :] = w_ref[...]
    head = lax.broadcasted_iota(jnp.int32, (depth - raw, f), 0) == 0
    wo_ref[raw:depth, :] = jnp.where(head, ph_ref[...].astype(F32), 0.0).astype(BF16)
    wo_ref[depth : depth + classes, :] = d_ref[...]
    wo_ref[depth + classes :, :] = jnp.zeros((rows - depth - classes, f), BF16)


def turn_kernel(depth, *refs):
    count = len(refs) - 2
    xt_ref, r_ref = refs[count:]
    n = refs[0].shape[1]
    for j in range(count):
        xt_ref[j * n : (j + 1) * n, :] = refs[j][:depth, :].T
        r_ref[:, j * n : (j + 1) * n] = refs[j][depth:, :]


def feature_kernel(depth, cuts, has_total, last, half, xt_ref, *refs):
    refs = list(refs)
    w_refs = [refs.pop(0) for _ in cuts]
    t_ref = refs.pop(0) if has_total else None
    f_ref = refs.pop(0)
    proj, spot = None, 0
    for w_ref in w_refs:
        end = min(spot + w_ref.shape[0], depth)
        part = jnp.dot(xt_ref[:, spot:end], w_ref[: end - spot, :], preferred_element_type=F32)
        proj = part if proj is None else proj + part
        spot += w_ref.shape[0]
    direction = w_refs[-1][w_refs[-1].shape[0] - (spot - depth) :, :]
    feats = cosine(proj).astype(BF16)
    f_ref[...] = feats
    tangent = lax.dot_general(feats, direction, (((1,), (1,)), ((), ())), preferred_element_type=F32)
    if has_total:
        tangent = tangent + t_ref[...]
    if not last:
        refs[0][...] = tangent
    else:
        other_ref, own_ref = refs
        step = pl.program_id(0)

        @pl.when(step < half)
        def _():
            other_ref[...] = tangent.T.astype(BF16)

        @pl.when(step >= half)
        def _():
            own_ref[...] = tangent.T


def make_features(xt, ws, depth, total, last, block):
    n, f = xt.shape[0], ws[0].shape[1]
    wide = sum(w.shape[0] for w in ws) - depth
    steps = n // block
    half = steps // 2
    ins = [pl.BlockSpec((block, depth), lambda i: (i, 0))]
    ins += [pl.BlockSpec(w.shape, lambda i: (0, 0)) for w in ws]
    args = [xt, *ws]
    if total is not None:
        ins.append(pl.BlockSpec((block, wide), lambda i: (i, 0)))
        args.append(total)
    outs = [pl.BlockSpec((block, f), lambda i: (i, 0))]
    shapes = [jax.ShapeDtypeStruct((n, f), BF16)]
    if last:
        outs.append(pl.BlockSpec((wide, block), lambda i: (0, jnp.minimum(i, half - 1))))
        outs.append(pl.BlockSpec((wide, block), lambda i: (0, jnp.maximum(i - half, 0))))
        shapes.append(jax.ShapeDtypeStruct((wide, n // 2), BF16))
        shapes.append(jax.ShapeDtypeStruct((wide, n // 2), F32))
    else:
        outs.append(pl.BlockSpec((block, wide), lambda i: (i, 0)))
        shapes.append(jax.ShapeDtypeStruct((n, wide), F32))
    cost = pl.CostEstimate(flops=2 * n * f * (depth + wide), bytes_accessed=2 * n * f, transcendentals=0)
    return pl.pallas_call(
        functools.partial(feature_kernel, depth, [w.shape for w in ws], total is not None, last, half),
        grid=(steps,),
        in_specs=ins,
        out_specs=outs,
        out_shape=shapes,
        compiler_params=params(),
        cost_estimate=cost,
    )(*args)


def spread_kernel(own_ref, got_ref, keep_ref, *send_refs):
    n = keep_ref.shape[1]
    total = own_ref[...] + got_ref[...].astype(F32)
    keep_ref[...] = total[:, :n]
    for j, ref in enumerate(send_refs):
        ref[...] = total[:, (j + 1) * n : (j + 2) * n].astype(BF16)


def curve_kernel(classes, keep_ref, *refs):
    got_refs, p_ref, c_ref = refs[:-2], refs[-2], refs[-1]
    total = keep_ref[...]
    for ref in got_refs:
        total = total + ref[...].astype(F32)
    total = total[:classes, :]
    prob = p_ref[...].astype(F32)
    mixed = jnp.sum(prob * total, axis=0, keepdims=True)
    c_ref[:classes, :] = (prob * (total - mixed)).astype(BF16)
    c_ref[classes:, :] = jnp.zeros((c_ref.shape[0] - classes, c_ref.shape[1]), BF16)


def share_kernel(*refs):
    left_refs, f_ref, o_ref = refs[:-2], refs[-2], refs[-1]
    total, spot = None, 0
    for ref in left_refs:
        n = ref.shape[1]
        part = jnp.dot(ref[...], f_ref[spot : spot + n, :], preferred_element_type=F32)
        total = part if total is None else total + part
        spot += n
    o_ref[...] = total.astype(o_ref.dtype)


def make_share(lefts, feats, dtype, tile):
    n, f = feats.shape
    wide = lefts[0].shape[0]
    return pl.pallas_call(
        share_kernel,
        grid=(f // tile,),
        in_specs=[pl.BlockSpec(a.shape, lambda i: (0, 0)) for a in lefts]
        + [pl.BlockSpec((n, tile), lambda i: (0, i))],
        out_specs=pl.BlockSpec((wide, tile), lambda i: (0, i)),
        out_shape=jax.ShapeDtypeStruct((wide, f), dtype),
        compiler_params=params(),
        cost_estimate=pl.CostEstimate(flops=2 * n * f * wide, bytes_accessed=2 * n * f, transcendentals=0),
    )(*lefts, feats)


def whole(kernel, shapes, *args):
    return pl.pallas_call(kernel, out_shape=shapes, compiler_params=params())(*args)


def on_device(line, ys, xs, inputs, probs, labels, proj_weight, phase, direction, damping):
    raw, own = inputs.shape
    classes = probs.shape[0]
    width = proj_weight.shape[1]
    depth = up(raw + 1, 16)
    wide = up(classes, 8)

    def swap_core(a):
        return lax.ppermute(a, "feat", [(i, i ^ 1) for i in range(2 * xs * ys)])

    def along(a, k):
        return lax.ppermute(a, "samp", [(i, (i + k) % line) for i in range(line)])

    def across(a, dy, dx):
        def to(i):
            y, x, c = i // (2 * xs), i // 2 % xs, i % 2
            return ((y + dy) % ys * xs + (x + dx) % xs) * 2 + c

        return lax.ppermute(a, "feat", [(i, to(i)) for i in range(2 * xs * ys)])

    offsets = [(dy, dx) for dy in range(ys) for dx in range(xs)]
    x_own, w_own = whole(
        functools.partial(pack_kernel, raw, classes),
        [jax.ShapeDtypeStruct((depth + wide, own), BF16), jax.ShapeDtypeStruct((depth + wide, width), BF16)],
        inputs, probs, labels[None, :], proj_weight, phase, direction,
    )
    x_line = [x_own] + [along(x_own, k) for k in range(1, line)]
    x_peer = [swap_core(a) for a in x_line]
    cut = up(depth // 2, 128)
    ws = {(0, 0): [w_own]}
    for dy in range(1, ys):
        ws[dy, 0] = [across(w_own, dy, 0)]
    for dx in range(1, xs):
        ws[0, dx] = [across(w_own, 0, dx)]
    for dy in range(1, ys):
        for dx in range(1, xs):
            ws[dy, dx] = [across(ws[0, dx][0][:cut], dy, 0), across(ws[dy, 0][0][cut:], 0, dx)]

    blocks = x_peer + x_line
    samples = own * len(blocks)
    xt, resid = whole(
        functools.partial(turn_kernel, depth),
        [jax.ShapeDtypeStruct((samples, depth), BF16), jax.ShapeDtypeStruct((wide, samples), BF16)],
        *blocks,
    )
    feats, total = {}, None
    for at in offsets:
        last = at == offsets[-1]
        feats[at], *rest = make_features(xt, ws[at], depth, total, last, own)
        total = rest[0]
    t_other, t_own = rest
    t_got = swap_core(t_other)
    keep, *send = whole(
        spread_kernel,
        [jax.ShapeDtypeStruct((wide, own), F32)] + [jax.ShapeDtypeStruct((wide, own), BF16)] * (line - 1),
        t_own, t_got,
    )
    got = [along(a, -k) for k, a in enumerate(send, 1)]
    curv = whole(
        functools.partial(curve_kernel, classes), jax.ShapeDtypeStruct((wide, own), BF16), keep, *got, probs
    )
    c_line = [curv] + [along(curv, k) for k in range(1, line)]
    c_peer = [swap_core(a) for a in c_line]
    curvs = c_peer + c_line

    def reduce(lefts):
        out = None
        for dy, dx in offsets[:0:-1]:
            piece = across(make_share(lefts, feats[dy, dx], BF16, width // 2), -dy, -dx).astype(F32)
            out = piece if out is None else out + piece
        own_part = make_share(lefts, feats[0, 0], F32, width // 2)
        return (own_part + out if out is not None else own_part)[:classes]

    gradient = reduce([resid])
    hess_vec = reduce(curvs) + damping[0] * direction.astype(F32)
    return (hess_vec, gradient)


def solution(mesh):
    line, feat = mesh.shape["samp"], mesh.shape["feat"]
    ys = 2 if feat % 4 == 0 else 1
    xs = feat // (2 * ys)
    placed = (
        P(None, ("samp", "feat")),
        P(None, ("samp", "feat")),
        P(("samp", "feat")),
        P(None, ("feat", "samp")),
        P(None, ("feat", "samp")),
        P(None, ("feat", "samp")),
        P(),
    )
    return jax.shard_map(
        functools.partial(on_device, line, ys, xs),
        mesh=mesh,
        in_specs=placed,
        out_specs=(P(None, ("feat", "samp")), P(None, ("feat", "samp"))),
        check_vma=False,
    )
```

time: 577 us -> 142 us (0.25)
  matrix products: 282 us -> 0 us
  waiting for transfers between devices: 229 us -> 37.8 us
  Pallas kernels: 0 us -> 50 us
  blocking collectives: 40 us -> 0 us
  starting transfers between devices: 0.24 us -> 33.7 us
  between operations: 14.8 us -> 1.51 us
  local copies, waits for them, and re-layouts: 1.74 us -> 14 us
    dot_general x16 -> x0, matrix products: 282 us -> none  [the longest x4 132 us: second_early(): lax.dot_general(curv_block, feats, dims, preferred_element_type=jnp.float32)]
    all_gather x3 -> x0, waiting for transfers between devices: 107 us -> none  [the longest x1 72.6 us: on_device(): lax.all_gather(proj_weight, 'samp', axis=1, tiled=True)]
    reduce_scatter x2 -> x0, waiting for transfers between devices: 78.4 us -> none  [the longest x1 49.7 us: on_device(): lax.psum_scatter(grad_acc, 'samp', scatter_dimension=1, tiled=True)]
    pallas_call x0 -> x16, Pallas kernels: none -> 50 us  [the longest x4 38.3 us: make_features(): pl.pallas_call(functools.partial(feature_kernel, depth, [w.shape for w in...]
    psum x1 -> x0, waiting for transfers between devices: 40.6 us -> none  [on_device(): total = lax.psum(tangent.astype(jnp.bfloat16), 'feat').astype(jnp.float32)]
    all_gather x3 -> x0, blocking collectives: 40 us -> none  [the longest x1 15 us: on_device(): lax.all_gather(phase, 'samp', axis=1, tiled=True)]
    ppermute x0 -> x28, waiting for transfers between devices: none -> 37.8 us  [the longest x9 25.1 us: along(): return lax.ppermute(a, 'samp', [(i, (i + k) % line) for i in range(line)])]
    ppermute x0 -> x28, starting transfers between devices: none -> 33.7 us  [the longest x9 18.1 us: along(): return lax.ppermute(a, 'samp', [(i, (i + k) % line) for i in range(line)])]
  transfers between devices with their start and end apart: 6 -> 28, of which waited for: 6 -> 12; matrix products, arithmetic and copies ran while one was open for 0% -> 1% of each run, Pallas kernels for 0% -> 27%
where the time goes in v1:
time: 142 us; the launch traced here: 141 us
  Pallas kernels  50 us (35%)
  waiting for transfers between devices  37.8 us (27%)
  starting transfers between devices  33.7 us (24%)
  local copies, waits for them, and re-layouts  14 us (10%)
  other arithmetic  3.97 us (3%)
  between operations  1.51 us (1%)
    pallas_call x4, Pallas kernels, make_features(): pl.pallas_call(functools.partial(feature_kernel, depth, [w.shape for w in...  38.3 us
    ppermute x9, waiting for transfers between devices, along(): return lax.ppermute(a, 'samp', [(i, (i + k) % line) for i in range(line)])  25.1 us
    ppermute x9, starting transfers between devices, along(): return lax.ppermute(a, 'samp', [(i, (i + k) % line) for i in range(line)])  18.1 us
    ppermute x10, starting transfers between devices, across(): return lax.ppermute(a, 'feat', [(i, to(i)) for i in range(2 * xs * ys)])  14 us
    unnamed x34, local copies, waits for them, and re-layouts  13.9 us
    pallas_call x8, Pallas kernels, make_share(): pl.pallas_call(share_kernel, grid=(f // tile,), in_specs=[pl.BlockSpec(a....  10.8 us
    ppermute x10, waiting for transfers between devices, across(): return lax.ppermute(a, 'feat', [(i, to(i)) for i in range(2 * xs * ys)])  9.18 us
    ppermute x9, waiting for transfers between devices, swap_core(): return lax.ppermute(a, 'feat', [(i, i ^ 1) for i in range(2 * xs * ys)])  3.51 us
  transfers between devices with their start and end apart: 28, of which 12 were waited for; matrix products, arithmetic and copies ran while one was open for 1% of the time, Pallas kernels for 27%

profile of v1, /device:TPU:0, one launch (start us, length us, event | category | flops | bytes accessed | tf_op | source)
XLA Modules:
  0.0 141.0 jit_solution(10796315281167050446)
XLA Ops:
  0.6 1.0 copy-done.6
  1.6 1.2 copy-done.8
  2.8 0.9 copy-done.9
  3.7 0.9 copy-done.11
  4.6 0.7 copy-done.12
  5.3 0.7 copy-done.13
  6.1 3.0 %collective-permute-start.9 = (bf16[600,1024]{1,0:T(8,128)(2,1)S(1)}, bf16[600,1024]{1,0:T(8,128)(2,1)S(1)}, u32[]{:S(2)}, u32[]{:S(2)}) collective-permute-start(bf16[600,1024]{1,0:T(8,128)(2,1)S(1)} %get-tuple-element.21.refs_0_), channel_id=1, source_target_pairs={{0,4},{1,5},{2,6},{3,7},{4,0},{5,1},{6,2},{7,3},{8,12},{9,13},{10,... | collective-permute-start | bytes 3686408 | tf_op jit(solution)/shard_map/ppermute | solution.py:195
  9.1 1.5 %collective-permute-start.7 = (bf16[600,1024]{1,0:T(8,128)(2,1)S(1)}, bf16[600,1024]{1,0:T(8,128)(2,1)S(1)}, u32[]{:S(2)}, u32[]{:S(2)}) collective-permute-start(bf16[600,1024]{1,0:T(8,128)(2,1)S(1)} %get-tuple-element.21.refs_0_), channel_id=1, source_target_pairs={{0,2},{1,3},{2,0},{3,1},{4,6},{5,7},{6,4},{7,5},{8,10},{9,11},{10,... | collective-permute-start | bytes 3686408 | tf_op jit(solution)/shard_map/ppermute | solution.py:195
  10.6 1.6 %collective-permute-start.1 = (bf16[600,256]{1,0:T(8,128)(2,1)S(1)}, bf16[600,256]{1,0:T(8,128)(2,1)S(1)}, u32[]{:S(2)}, u32[]{:S(2)}) collective-permute-start(bf16[600,256]{1,0:T(8,128)(2,1)S(1)} %get-tuple-element.19.refs_4_), channel_id=1, source_target_pairs={{0,8},{8,16},{16,24},{24,0},{1,9},{9,17},{17,25},{25,1},{2,10},{10... | collective-permute-start | bytes 921608 | tf_op jit(solution)/shard_map/ppermute | solution.py:188
  12.2 2.6 %collective-permute-start.3 = (bf16[600,256]{1,0:T(8,128)(2,1)S(1)}, bf16[600,256]{1,0:T(8,128)(2,1)S(1)}, u32[]{:S(2)}, u32[]{:S(2)}) collective-permute-start(bf16[600,256]{1,0:T(8,128)(2,1)S(1)} %get-tuple-element.19.refs_4_), channel_id=1, source_target_pairs={{0,16},{8,24},{16,0},{24,8},{1,17},{9,25},{17,1},{25,9},{2,18},{10... | collective-permute-start | bytes 921608 | tf_op jit(solution)/shard_map/ppermute | solution.py:188
  14.8 1.3 collective-permute-start.5
  16.1 6.6 %collective-permute-done.1.refs_5_ = bf16[600,256]{1,0:T(8,128)(2,1)S(1)} collective-permute-done((bf16[600,256]{1,0:T(8,128)(2,1)S(1)}, bf16[600,256]{1,0:T(8,128)(2,1)S(1)}, u32[]{:S(2)}, u32[]{:S(2)}) %collective-permute-start.1) | collective-permute-done | bytes 307232 | tf_op jit(solution)/shard_map/ppermute | solution.py:188
  22.8 11.5 %collective-permute-done.3.refs_6_ = bf16[600,256]{1,0:T(8,128)(2,1)S(1)} collective-permute-done((bf16[600,256]{1,0:T(8,128)(2,1)S(1)}, bf16[600,256]{1,0:T(8,128)(2,1)S(1)}, u32[]{:S(2)}, u32[]{:S(2)}) %collective-permute-start.3) | collective-permute-done | bytes 307232 | tf_op jit(solution)/shard_map/ppermute | solution.py:188
  34.8 1.0 collective-permute-done.2.refs_1_
  36.7 0.6 shard_map.87
  37.4 0.6 collective-permute-start.10
  38.1 1.5 %collective-permute-start.8 = (bf16[256,1024]{1,0:T(8,128)(2,1)S(1)}, bf16[256,1024]{1,0:T(8,128)(2,1)S(1)}, u32[]{:S(2)}, u32[]{:S(2)}) collective-permute-start(bf16[256,1024]{1,0:T(8,128)(2,1)S(1)} %slice.16), channel_id=1, source_target_pairs={{0,4},{1,5},{2,6},{3,7},{4,0},{5,1},{6,2},{7,3},{8,12},{9,13},{10,... | collective-permute-start | bytes 1572872 | tf_op jit(solution)/shard_map/ppermute | solution.py:195
  39.6 8.0 %shard_map.88 = (bf16[2048,1024]{1,0:T(8,128)(2,1)}, f32[2048,152]{1,0:T(8,128)S(1)}) custom-call(bf16[2048,448]{1,0:T(8,128)(2,1)S(1)} %get-tuple-element.20.xt_ref, bf16[600,1024]{1,0:T(8,128)(2,1)S(1)} %get-tuple-element.21.refs_0_), custom_call_target="tpu_custom_call" | custom-call | flops 2516582400 | bytes 4194304 | tf_op jit(solution)/shard_map/pallas_call | solution.py:116
  47.6 1.3 copy-done.16
  49.0 9.4 %shard_map.89 = (bf16[2048,1024]{1,0:T(8,128)(2,1)}, f32[2048,152]{1,0:T(8,128)S(1)}) custom-call(bf16[2048,448]{1,0:T(8,128)(2,1)S(1)} %get-tuple-element.20.xt_ref, bf16[600,1024]{1,0:T(8,128)(2,1)S(1)} %collective-permute-done.7.refs_0_, f32[2048,152]{1,0:T(8,128)} %copy-done.16), custom_call_target="tpu_custom_call" | custom-call | flops 2516582400 | bytes 4194304 | tf_op jit(solution)/shard_map/pallas_call | solution.py:116
  58.4 1.3 copy-done.15
  59.7 9.4 %shard_map.90 = (bf16[2048,1024]{1,0:T(8,128)(2,1)}, f32[2048,152]{1,0:T(8,128)S(1)}) custom-call(bf16[2048,448]{1,0:T(8,128)(2,1)S(1)} %get-tuple-element.20.xt_ref, bf16[600,1024]{1,0:T(8,128)(2,1)S(1)} %collective-permute-done.9.refs_0_, f32[2048,152]{1,0:T(8,128)} %copy-done.15), custom_call_target="tpu_custom_call" | custom-call | flops 2516582400 | bytes 4194304 | tf_op jit(solution)/shard_map/pallas_call | solution.py:116
  69.0 1.3 copy-done.14
  70.4 11.4 %shard_map.91 = (bf16[2048,1024]{1,0:T(8,128)(2,1)}, bf16[152,1024]{1,0:T(8,128)(2,1)S(1)}, f32[152,1024]{1,0:T(8,128)S(1)}) custom-call(bf16[2048,448]{1,0:T(8,128)(2,1)S(1)} %get-tuple-element.20.xt_ref, bf16[256,1024]{1,0:T(8,128)(2,1)S(1)} %collective-permute-done.8.refs_0_, bf16[344,1024]{1,0:T(8,128)(2,1)S(1)} %collective-permute-done.10.refs_1_, ...), custom_call_target="tpu_custom_call" | custom-call | flops 2516582400 | bytes 4194304 | tf_op jit(solution)/shard_map/pallas_call | solution.py:116
  81.8 1.6 %collective-permute-done.11.got_ref = bf16[152,1024]{1,0:T(8,128)(2,1)S(1)} collective-permute-done((bf16[152,1024]{1,0:T(8,128)(2,1)S(1)}, bf16[152,1024]{1,0:T(8,128)(2,1)S(1)}, u32[]{:S(2)}, u32[]{:S(2)}) %collective-permute-start.11) | collective-permute-done | bytes 311328 | tf_op jit(solution)/shard_map/ppermute | solution.py:185
  83.5 7.2 %collective-permute-start.12 = (bf16[152,256]{1,0:T(8,128)(2,1)S(1)}, bf16[152,256]{1,0:T(8,128)(2,1)S(1)}, u32[]{:S(2)}, u32[]{:S(2)}) collective-permute-start(bf16[152,256]{1,0:T(8,128)(2,1)S(1)} %get-tuple-element.28), channel_id=1, source_target_pairs={{0,24},{8,0},{16,8},{24,16},{1,25},{9,1},{17,9},{25,17},{2,26},{10... | collective-permute-start | bytes 233480 | tf_op jit(solution)/shard_map/ppermute | solution.py:188
  90.7 0.6 collective-permute-start.14
  91.3 2.1 %collective-permute-done.12.refs_0_ = bf16[152,256]{1,0:T(8,128)(2,1)S(1)} collective-permute-done((bf16[152,256]{1,0:T(8,128)(2,1)S(1)}, bf16[152,256]{1,0:T(8,128)(2,1)S(1)}, u32[]{:S(2)}, u32[]{:S(2)}) %collective-permute-start.12) | collective-permute-done | bytes 77856 | tf_op jit(solution)/shard_map/ppermute | solution.py:188
  93.4 4.9 %collective-permute-done.13.refs_1_ = bf16[152,256]{1,0:T(8,128)(2,1)S(1)} collective-permute-done((bf16[152,256]{1,0:T(8,128)(2,1)S(1)}, bf16[152,256]{1,0:T(8,128)(2,1)S(1)}, u32[]{:S(2)}, u32[]{:S(2)}) %collective-permute-start.13) | collective-permute-done | bytes 77856 | tf_op jit(solution)/shard_map/ppermute | solution.py:188
  98.6 1.4 shard_map.100
  100.0 1.6 %collective-permute-start.26 = (bf16[152,1024]{1,0:T(8,128)(2,1)S(1)}, bf16[152,1024]{1,0:T(8,128)(2,1)S(1)}, u32[]{:S(2)}, u32[]{:S(2)}) collective-permute-start(bf16[152,1024]{1,0:T(8,128)(2,1)S(1)} %shard_map.100), channel_id=1, source_target_pairs={{0,4},{1,5},{2,6},{3,7},{4,0},{5,1},{6,2},{7,3},{8,12},{9,13},{10,... | collective-permute-start | bytes 933896 | tf_op jit(solution)/shard_map/ppermute | solution.py:195
  101.5 2.2 %collective-permute-start.18 = (bf16[152,256]{1,0:T(8,128)(2,1)S(1)}, bf16[152,256]{1,0:T(8,128)(2,1)S(1)}, u32[]{:S(2)}, u32[]{:S(2)}) collective-permute-start(bf16[152,256]{1,0:T(8,128)(2,1)S(1)} %shard_map.93.refs_4_), channel_id=1, source_target_pairs={{0,16},{8,24},{16,0},{24,8},{1,17},{9,25},{17,1},{25,9},{2,18},{10... | collective-permute-start | bytes 233480 | tf_op jit(solution)/shard_map/ppermute | solution.py:188
  103.8 2.4 %collective-permute-start.20 = (bf16[152,256]{1,0:T(8,128)(2,1)S(1)}, bf16[152,256]{1,0:T(8,128)(2,1)S(1)}, u32[]{:S(2)}, u32[]{:S(2)}) collective-permute-start(bf16[152,256]{1,0:T(8,128)(2,1)S(1)} %shard_map.93.refs_4_), channel_id=1, source_target_pairs={{0,24},{8,0},{16,8},{24,16},{1,25},{9,1},{17,9},{25,17},{2,26},{10... | collective-permute-start | bytes 233480 | tf_op jit(solution)/shard_map/ppermute | solution.py:188
  106.2 1.4 shard_map.101
  108.4 1.4 shard_map.99
  109.7 1.6 %collective-permute-start.27 = (bf16[152,1024]{1,0:T(8,128)(2,1)S(1)}, bf16[152,1024]{1,0:T(8,128)(2,1)S(1)}, u32[]{:S(2)}, u32[]{:S(2)}) collective-permute-start(bf16[152,1024]{1,0:T(8,128)(2,1)S(1)} %shard_map.101), channel_id=1, source_target_pairs={{0,2},{1,3},{2,0},{3,1},{4,6},{5,7},{6,4},{7,5},{8,10},{9,11},{10,... | collective-permute-start | bytes 933896 | tf_op jit(solution)/shard_map/ppermute | solution.py:195
  113.0 2.2 %copy-done.4 = bf16[2048,1024]{1,0:T(8,128)(2,1)S(1)} copy-done((bf16[2048,1024]{1,0:T(8,128)(2,1)S(1)}, bf16[2048,1024]{1,0:T(8,128)(2,1)}, u32[]{:S(2)}) %copy-start.4) | copy-done | bytes 4194328
  115.1 1.4 shard_map.98
  116.5 2.2 %copy-done.3 = bf16[2048,1024]{1,0:T(8,128)(2,1)S(1)} copy-done((bf16[2048,1024]{1,0:T(8,128)(2,1)S(1)}, bf16[2048,1024]{1,0:T(8,128)(2,1)}, u32[]{:S(2)}) %copy-start.3) | copy-done | bytes 4194328
  118.7 1.3 shard_map.95
  120.1 2.5 %collective-permute-start.22 = (bf16[152,1024]{1,0:T(8,128)(2,1)S(1)}, bf16[152,1024]{1,0:T(8,128)(2,1)}, u32[]{:S(2)}, u32[]{:S(2)}) collective-permute-start(bf16[152,1024]{1,0:T(8,128)(2,1)S(1)} %shard_map.95), channel_id=1, source_target_pairs={{0,6},{1,7},{2,4},{3,5},{4,2},{5,3},{6,0},{7,1},{8,14},{9,15},{10,... | collective-permute-start | bytes 933896 | tf_op jit(solution)/shard_map/ppermute | solution.py:195
  122.6 1.3 shard_map.96
  124.5 1.4 shard_map.97
  126.8 2.0 %slice_add_fusion = f32[147,1024]{1,0:T(8,128)} fusion(f32[152,1024]{1,0:T(8,128)S(1)} %shard_map.98, bf16[152,1024]{1,0:T(8,128)(2,1)S(1)} %collective-permute-done.27, bf16[152,1024]{1,0:T(8,128)(2,1)S(1)} %collective-permute-done.26, bf16[152,1024]{1,0:T(8,128)(2,1)} %collective-permute-done.25), kind=kLoop, calls=%fused_computation | loop fusion | flops 903168 | bytes 2107392 | tf_op jit(solution)/shard_map/add | solution.py:248
  128.8 1.4 shard_map.94
  130.1 3.4 %collective-permute-done.22 = bf16[152,1024]{1,0:T(8,128)(2,1)} collective-permute-done((bf16[152,1024]{1,0:T(8,128)(2,1)S(1)}, bf16[152,1024]{1,0:T(8,128)(2,1)}, u32[]{:S(2)}, u32[]{:S(2)}) %collective-permute-start.22) | collective-permute-done | bytes 311328 | tf_op jit(solution)/shard_map/ppermute | solution.py:195
  133.5 5.4 %collective-permute-done.23 = bf16[152,1024]{1,0:T(8,128)(2,1)S(1)} collective-permute-done((bf16[152,1024]{1,0:T(8,128)(2,1)S(1)}, bf16[152,1024]{1,0:T(8,128)(2,1)S(1)}, u32[]{:S(2)}, u32[]{:S(2)}) %collective-permute-start.23) | collective-permute-done | bytes 311328 | tf_op jit(solution)/shard_map/ppermute | solution.py:195
  139.0 2.0 %fusion = f32[147,1024]{1,0:T(8,128)} fusion(f32[152,1024]{1,0:T(8,128)S(1)} %shard_map.94, bf16[147,1024]{1,0:T(8,128)(2,1)S(1)} %copy-done.7, bf16[152,1024]{1,0:T(8,128)(2,1)S(1)} %collective-permute-done.24, bf16[152,1024]{1,0:T(8,128)(2,1)S(1)} %collective-permute-done.23, bf16[152,1024]{1,0:T(8,128)(2,1)} %collective-permute-done.22, f32[]{:T(128)} %bitcast.2), kind=kLoop, calls=%fused_computation.2 | loop fusion | flops 1354752 | bytes 2408452 | tf_op jit(solution)/shard_map/add | solution.py:251
  (62 shorter events, 5.5 us)
Async XLA Ops:
  0.6 1.0 copy-start.6
  1.6 1.2 copy-start.8
  2.8 0.9 copy-start.9
  3.7 0.9 copy-start.11
  4.6 0.7 copy-start.12
  5.3 0.7 copy-start.13
  6.1 31.3 %collective-permute-start.9 = (bf16[600,1024]{1,0:T(8,128)(2,1)S(1)}, bf16[600,1024]{1,0:T(8,128)(2,1)S(1)}, u32[]{:S(2)}, u32[]{:S(2)}) collective-permute-start(bf16[600,1024]{1,0:T(8,128)(2,1)S(1)} %get-tuple-element.21.refs_0_), channel_id=1, source_target_pairs={{0,4},{1,5},{2,6},{3,7},{4,0},{5,1},{6,2},{7,3},{8,12},{9,13},{10,... | collective-permute-start | bytes 3686408 | tf_op jit(solution)/shard_map/ppermute | solution.py:195
  9.1 28.9 %collective-permute-start.7 = (bf16[600,1024]{1,0:T(8,128)(2,1)S(1)}, bf16[600,1024]{1,0:T(8,128)(2,1)S(1)}, u32[]{:S(2)}, u32[]{:S(2)}) collective-permute-start(bf16[600,1024]{1,0:T(8,128)(2,1)S(1)} %get-tuple-element.21.refs_0_), channel_id=1, source_target_pairs={{0,2},{1,3},{2,0},{3,1},{4,6},{5,7},{6,4},{7,5},{8,10},{9,11},{10,... | collective-permute-start | bytes 3686408 | tf_op jit(solution)/shard_map/ppermute | solution.py:195
  10.6 12.1 %collective-permute-start.1 = (bf16[600,256]{1,0:T(8,128)(2,1)S(1)}, bf16[600,256]{1,0:T(8,128)(2,1)S(1)}, u32[]{:S(2)}, u32[]{:S(2)}) collective-permute-start(bf16[600,256]{1,0:T(8,128)(2,1)S(1)} %get-tuple-element.19.refs_4_), channel_id=1, source_target_pairs={{0,8},{8,16},{16,24},{24,0},{1,9},{9,17},{17,25},{25,1},{2,10},{10... | collective-permute-start | bytes 921608 | tf_op jit(solution)/shard_map/ppermute | solution.py:188
  12.2 22.0 %collective-permute-start.3 = (bf16[600,256]{1,0:T(8,128)(2,1)S(1)}, bf16[600,256]{1,0:T(8,128)(2,1)S(1)}, u32[]{:S(2)}, u32[]{:S(2)}) collective-permute-start(bf16[600,256]{1,0:T(8,128)(2,1)S(1)} %get-tuple-element.19.refs_4_), channel_id=1, source_target_pairs={{0,16},{8,24},{16,0},{24,8},{1,17},{9,25},{17,1},{25,9},{2,18},{10... | collective-permute-start | bytes 921608 | tf_op jit(solution)/shard_map/ppermute | solution.py:188
  14.8 19.5 %collective-permute-start.5 = (bf16[600,256]{1,0:T(8,128)(2,1)S(1)}, bf16[600,256]{1,0:T(8,128)(2,1)S(1)}, u32[]{:S(2)}, u32[]{:S(2)}) collective-permute-start(bf16[600,256]{1,0:T(8,128)(2,1)S(1)} %get-tuple-element.19.refs_4_), channel_id=1, source_target_pairs={{0,24},{8,0},{16,8},{24,16},{1,25},{9,1},{17,9},{25,17},{2,26},{10... | collective-permute-start | bytes 921608 | tf_op jit(solution)/shard_map/ppermute | solution.py:188
  22.8 12.0 %collective-permute-start = (bf16[600,256]{1,0:T(8,128)(2,1)S(1)}, bf16[600,256]{1,0:T(8,128)(2,1)S(1)}, u32[]{:S(2)}, u32[]{:S(2)}) collective-permute-start(bf16[600,256]{1,0:T(8,128)(2,1)S(1)} %get-tuple-element.19.refs_4_), channel_id=1, source_target_pairs={{0,1},{1,0},{2,3},{3,2},{4,5},{5,4},{6,7},{7,6},{8,9},{9,8},{10,11... | collective-permute-start | bytes 921608 | tf_op jit(solution)/shard_map/ppermute | solution.py:185
  34.2 1.6 %collective-permute-start.2 = (bf16[600,256]{1,0:T(8,128)(2,1)S(1)}, bf16[600,256]{1,0:T(8,128)(2,1)S(1)}, u32[]{:S(2)}, u32[]{:S(2)}) collective-permute-start(bf16[600,256]{1,0:T(8,128)(2,1)S(1)} %collective-permute-done.1.refs_5_), channel_id=1, source_target_pairs={{0,1},{1,0},{2,3},{3,2},{4,5},{5,4},{6,7},{7,6},{8,9},{9,8},{10,11... | collective-permute-start | bytes 921608 | tf_op jit(solution)/shard_map/ppermute | solution.py:185
  34.2 2.0 %collective-permute-start.4 = (bf16[600,256]{1,0:T(8,128)(2,1)S(1)}, bf16[600,256]{1,0:T(8,128)(2,1)S(1)}, u32[]{:S(2)}, u32[]{:S(2)}) collective-permute-start(bf16[600,256]{1,0:T(8,128)(2,1)S(1)} %collective-permute-done.3.refs_6_), channel_id=1, source_target_pairs={{0,1},{1,0},{2,3},{3,2},{4,5},{5,4},{6,7},{7,6},{8,9},{9,8},{10,11... | collective-permute-start | bytes 921608 | tf_op jit(solution)/shard_map/ppermute | solution.py:185
  34.7 2.0 %collective-permute-start.6 = (bf16[600,256]{1,0:T(8,128)(2,1)S(1)}, bf16[600,256]{1,0:T(8,128)(2,1)S(1)}, u32[]{:S(2)}, u32[]{:S(2)}) collective-permute-start(bf16[600,256]{1,0:T(8,128)(2,1)S(1)} %collective-permute-done.5.refs_7_), channel_id=1, source_target_pairs={{0,1},{1,0},{2,3},{3,2},{4,5},{5,4},{6,7},{7,6},{8,9},{9,8},{10,11... | collective-permute-start | bytes 921608 | tf_op jit(solution)/shard_map/ppermute | solution.py:185
  37.4 33.0 %collective-permute-start.10 = (bf16[344,1024]{1,0:T(8,128)(2,1)S(1)}, bf16[344,1024]{1,0:T(8,128)(2,1)S(1)}, u32[]{:S(2)}, u32[]{:S(2)}) collective-permute-start(bf16[344,1024]{1,0:T(8,128)(2,1)S(1)} %slice.17), channel_id=1, source_target_pairs={{0,2},{1,3},{2,0},{3,1},{4,6},{5,7},{6,4},{7,5},{8,10},{9,11},{10,... | collective-permute-start | bytes 2113544 | tf_op jit(solution)/shard_map/ppermute | solution.py:195
  38.1 32.3 %collective-permute-start.8 = (bf16[256,1024]{1,0:T(8,128)(2,1)S(1)}, bf16[256,1024]{1,0:T(8,128)(2,1)S(1)}, u32[]{:S(2)}, u32[]{:S(2)}) collective-permute-start(bf16[256,1024]{1,0:T(8,128)(2,1)S(1)} %slice.16), channel_id=1, source_target_pairs={{0,4},{1,5},{2,6},{3,7},{4,0},{5,1},{6,2},{7,3},{8,12},{9,13},{10,... | collective-permute-start | bytes 1572872 | tf_op jit(solution)/shard_map/ppermute | solution.py:195
  47.6 1.3 copy-start.16
  58.4 1.3 copy-start.15
  69.0 1.3 copy-start.14
  70.4 27.9 %copy-start.10 = (bf16[147,256]{1,0:T(8,128)(2,1)S(1)}, bf16[147,256]{1,0:T(8,128)(2,1)}, u32[]{:S(2)}) copy-start(bf16[147,256]{1,0:T(8,128)(2,1)} %refs_3_.1) | copy-start | bytes 225796
  70.4 28.2 %copy-start.1 = (bf16[2048,1024]{1,0:T(8,128)(2,1)S(1)}, bf16[2048,1024]{1,0:T(8,128)(2,1)}, u32[]{:S(2)}) copy-start(bf16[2048,1024]{1,0:T(8,128)(2,1)} %get-tuple-element.33.refs_8_.refs_1_) | copy-start | bytes 12582916
  81.8 1.6 %collective-permute-start.11 = (bf16[152,1024]{1,0:T(8,128)(2,1)S(1)}, bf16[152,1024]{1,0:T(8,128)(2,1)S(1)}, u32[]{:S(2)}, u32[]{:S(2)}) collective-permute-start(bf16[152,1024]{1,0:T(8,128)(2,1)S(1)} %get-tuple-element.26), channel_id=1, source_target_pairs={{0,1},{1,0},{2,3},{3,2},{4,5},{5,4},{6,7},{7,6},{8,9},{9,8},{10,11... | collective-permute-start | bytes 933896 | tf_op jit(solution)/shard_map/ppermute | solution.py:185
  83.5 9.9 %collective-permute-start.12 = (bf16[152,256]{1,0:T(8,128)(2,1)S(1)}, bf16[152,256]{1,0:T(8,128)(2,1)S(1)}, u32[]{:S(2)}, u32[]{:S(2)}) collective-permute-start(bf16[152,256]{1,0:T(8,128)(2,1)S(1)} %get-tuple-element.28), channel_id=1, source_target_pairs={{0,24},{8,0},{16,8},{24,16},{1,25},{9,1},{17,9},{25,17},{2,26},{10... | collective-permute-start | bytes 233480 | tf_op jit(solution)/shard_map/ppermute | solution.py:188
  90.7 7.7 %collective-permute-start.13 = (bf16[152,256]{1,0:T(8,128)(2,1)S(1)}, bf16[152,256]{1,0:T(8,128)(2,1)S(1)}, u32[]{:S(2)}, u32[]{:S(2)}) collective-permute-start(bf16[152,256]{1,0:T(8,128)(2,1)S(1)} %get-tuple-element.29), channel_id=1, source_target_pairs={{0,16},{8,24},{16,0},{24,8},{1,17},{9,25},{17,1},{25,9},{2,18},{10... | collective-permute-start | bytes 233480 | tf_op jit(solution)/shard_map/ppermute | solution.py:188
  90.7 7.7 %collective-permute-start.14 = (bf16[152,256]{1,0:T(8,128)(2,1)S(1)}, bf16[152,256]{1,0:T(8,128)(2,1)S(1)}, u32[]{:S(2)}, u32[]{:S(2)}) collective-permute-start(bf16[152,256]{1,0:T(8,128)(2,1)S(1)} %get-tuple-element.30), channel_id=1, source_target_pairs={{0,8},{8,16},{16,24},{24,0},{1,9},{9,17},{17,25},{25,1},{2,10},{10... | collective-permute-start | bytes 233480 | tf_op jit(solution)/shard_map/ppermute | solution.py:188
  98.4 9.2 %collective-permute-start.16 = (bf16[152,256]{1,0:T(8,128)(2,1)S(1)}, bf16[152,256]{1,0:T(8,128)(2,1)S(1)}, u32[]{:S(2)}, u32[]{:S(2)}) collective-permute-start(bf16[152,256]{1,0:T(8,128)(2,1)S(1)} %shard_map.93.refs_4_), channel_id=1, source_target_pairs={{0,8},{8,16},{16,24},{24,0},{1,9},{9,17},{17,25},{25,1},{2,10},{10... | collective-permute-start | bytes 233480 | tf_op jit(solution)/shard_map/ppermute | solution.py:188
  98.6 7.6 %copy-start = (bf16[2048,1024]{1,0:T(8,128)(2,1)S(1)}, bf16[2048,1024]{1,0:T(8,128)(2,1)}, u32[]{:S(2)}) copy-start(bf16[2048,1024]{1,0:T(8,128)(2,1)} %get-tuple-element.34.refs_8_.refs_1_) | copy-start | bytes 12582916
  100.0 25.9 %collective-permute-start.26 = (bf16[152,1024]{1,0:T(8,128)(2,1)S(1)}, bf16[152,1024]{1,0:T(8,128)(2,1)S(1)}, u32[]{:S(2)}, u32[]{:S(2)}) collective-permute-start(bf16[152,1024]{1,0:T(8,128)(2,1)S(1)} %shard_map.100), channel_id=1, source_target_pairs={{0,4},{1,5},{2,6},{3,7},{4,0},{5,1},{6,2},{7,3},{8,12},{9,13},{10,... | collective-permute-start | bytes 933896 | tf_op jit(solution)/shard_map/ppermute | solution.py:195
  101.5 8.2 %collective-permute-start.18 = (bf16[152,256]{1,0:T(8,128)(2,1)S(1)}, bf16[152,256]{1,0:T(8,128)(2,1)S(1)}, u32[]{:S(2)}, u32[]{:S(2)}) collective-permute-start(bf16[152,256]{1,0:T(8,128)(2,1)S(1)} %shard_map.93.refs_4_), channel_id=1, source_target_pairs={{0,16},{8,24},{16,0},{24,8},{1,17},{9,25},{17,1},{25,9},{2,18},{10... | collective-permute-start | bytes 233480 | tf_op jit(solution)/shard_map/ppermute | solution.py:188
  103.8 7.5 %collective-permute-start.20 = (bf16[152,256]{1,0:T(8,128)(2,1)S(1)}, bf16[152,256]{1,0:T(8,128)(2,1)S(1)}, u32[]{:S(2)}, u32[]{:S(2)}) collective-permute-start(bf16[152,256]{1,0:T(8,128)(2,1)S(1)} %shard_map.93.refs_4_), channel_id=1, source_target_pairs={{0,24},{8,0},{16,8},{24,16},{1,25},{9,1},{17,9},{25,17},{2,26},{10... | collective-permute-start | bytes 233480 | tf_op jit(solution)/shard_map/ppermute | solution.py:188
  106.2 2.2 %copy-start.2 = (bf16[2048,1024]{1,0:T(8,128)(2,1)S(1)}, bf16[2048,1024]{1,0:T(8,128)(2,1)}, u32[]{:S(2)}) copy-start(bf16[2048,1024]{1,0:T(8,128)(2,1)} %get-tuple-element.32.refs_8_.refs_1_) | copy-start | bytes 12582916
  107.5 4.2 %collective-permute-start.15 = (bf16[152,256]{1,0:T(8,128)(2,1)S(1)}, bf16[152,256]{1,0:T(8,128)(2,1)S(1)}, u32[]{:S(2)}, u32[]{:S(2)}) collective-permute-start(bf16[152,256]{1,0:T(8,128)(2,1)S(1)} %shard_map.93.refs_4_), channel_id=1, source_target_pairs={{0,1},{1,0},{2,3},{3,2},{4,5},{5,4},{6,7},{7,6},{8,9},{9,8},{10,11... | collective-permute-start | bytes 233480 | tf_op jit(solution)/shard_map/ppermute | solution.py:185
  107.6 4.2 %collective-permute-start.17 = (bf16[152,256]{1,0:T(8,128)(2,1)S(1)}, bf16[152,256]{1,0:T(8,128)(2,1)S(1)}, u32[]{:S(2)}, u32[]{:S(2)}) collective-permute-start(bf16[152,256]{1,0:T(8,128)(2,1)S(1)} %collective-permute-done.16.refs_5_), channel_id=1, source_target_pairs={{0,1},{1,0},{2,3},{3,2},{4,5},{5,4},{6,7},{7,6},{8,9},{9,8},{10,11... | collective-permute-start | bytes 233480 | tf_op jit(solution)/shard_map/ppermute | solution.py:185
  109.7 16.7 %collective-permute-start.27 = (bf16[152,1024]{1,0:T(8,128)(2,1)S(1)}, bf16[152,1024]{1,0:T(8,128)(2,1)S(1)}, u32[]{:S(2)}, u32[]{:S(2)}) collective-permute-start(bf16[152,1024]{1,0:T(8,128)(2,1)S(1)} %shard_map.101), channel_id=1, source_target_pairs={{0,2},{1,3},{2,0},{3,1},{4,6},{5,7},{6,4},{7,5},{8,10},{9,11},{10,... | collective-permute-start | bytes 933896 | tf_op jit(solution)/shard_map/ppermute | solution.py:195
  111.3 15.5 %collective-permute-start.25 = (bf16[152,1024]{1,0:T(8,128)(2,1)S(1)}, bf16[152,1024]{1,0:T(8,128)(2,1)}, u32[]{:S(2)}, u32[]{:S(2)}) collective-permute-start(bf16[152,1024]{1,0:T(8,128)(2,1)S(1)} %shard_map.99), channel_id=1, source_target_pairs={{0,6},{1,7},{2,4},{3,5},{4,2},{5,3},{6,0},{7,1},{8,14},{9,15},{10,... | collective-permute-start | bytes 933896 | tf_op jit(solution)/shard_map/ppermute | solution.py:195
  111.8 4.7 %collective-permute-start.19 = (bf16[152,256]{1,0:T(8,128)(2,1)S(1)}, bf16[152,256]{1,0:T(8,128)(2,1)S(1)}, u32[]{:S(2)}, u32[]{:S(2)}) collective-permute-start(bf16[152,256]{1,0:T(8,128)(2,1)S(1)} %collective-permute-done.18.refs_6_), channel_id=1, source_target_pairs={{0,1},{1,0},{2,3},{3,2},{4,5},{5,4},{6,7},{7,6},{8,9},{9,8},{10,11... | collective-permute-start | bytes 233480 | tf_op jit(solution)/shard_map/ppermute | solution.py:185
  111.8 4.7 %collective-permute-start.21 = (bf16[152,256]{1,0:T(8,128)(2,1)S(1)}, bf16[152,256]{1,0:T(8,128)(2,1)S(1)}, u32[]{:S(2)}, u32[]{:S(2)}) collective-permute-start(bf16[152,256]{1,0:T(8,128)(2,1)S(1)} %collective-permute-done.20.refs_7_), channel_id=1, source_target_pairs={{0,1},{1,0},{2,3},{3,2},{4,5},{5,4},{6,7},{7,6},{8,9},{9,8},{10,11... | collective-permute-start | bytes 233480 | tf_op jit(solution)/shard_map/ppermute | solution.py:185
  112.9 2.2 %copy-start.4 = (bf16[2048,1024]{1,0:T(8,128)(2,1)S(1)}, bf16[2048,1024]{1,0:T(8,128)(2,1)}, u32[]{:S(2)}) copy-start(bf16[2048,1024]{1,0:T(8,128)(2,1)} %get-tuple-element.31.refs_8_.refs_1_) | copy-start | bytes 12582916
  116.5 2.2 %copy-start.3 = (bf16[2048,1024]{1,0:T(8,128)(2,1)S(1)}, bf16[2048,1024]{1,0:T(8,128)(2,1)}, u32[]{:S(2)}) copy-start(bf16[2048,1024]{1,0:T(8,128)(2,1)} %get-tuple-element.32.refs_8_.refs_1_) | copy-start | bytes 12582916
  120.1 13.4 %collective-permute-start.22 = (bf16[152,1024]{1,0:T(8,128)(2,1)S(1)}, bf16[152,1024]{1,0:T(8,128)(2,1)}, u32[]{:S(2)}, u32[]{:S(2)}) collective-permute-start(bf16[152,1024]{1,0:T(8,128)(2,1)S(1)} %shard_map.95), channel_id=1, source_target_pairs={{0,6},{1,7},{2,4},{3,5},{4,2},{5,3},{6,0},{7,1},{8,14},{9,15},{10,... | collective-permute-start | bytes 933896 | tf_op jit(solution)/shard_map/ppermute | solution.py:195
  123.9 14.9 %collective-permute-start.23 = (bf16[152,1024]{1,0:T(8,128)(2,1)S(1)}, bf16[152,1024]{1,0:T(8,128)(2,1)S(1)}, u32[]{:S(2)}, u32[]{:S(2)}) collective-permute-start(bf16[152,1024]{1,0:T(8,128)(2,1)S(1)} %shard_map.96), channel_id=1, source_target_pairs={{0,4},{1,5},{2,6},{3,7},{4,0},{5,1},{6,2},{7,3},{8,12},{9,13},{10,... | collective-permute-start | bytes 933896 | tf_op jit(solution)/shard_map/ppermute | solution.py:195
  124.5 4.2 %copy-start.5 = (bf16[2048,1024]{1,0:T(8,128)(2,1)S(1)}, bf16[2048,1024]{1,0:T(8,128)(2,1)}, u32[]{:S(2)}) copy-start(bf16[2048,1024]{1,0:T(8,128)(2,1)} %get-tuple-element.31.refs_8_.refs_1_) | copy-start | bytes 12582916
  125.9 13.1 %collective-permute-start.24 = (bf16[152,1024]{1,0:T(8,128)(2,1)S(1)}, bf16[152,1024]{1,0:T(8,128)(2,1)S(1)}, u32[]{:S(2)}, u32[]{:S(2)}) collective-permute-start(bf16[152,1024]{1,0:T(8,128)(2,1)S(1)} %shard_map.97), channel_id=1, source_target_pairs={{0,2},{1,3},{2,0},{3,1},{4,6},{5,7},{6,4},{7,5},{8,10},{9,11},{10,... | collective-permute-start | bytes 933896 | tf_op jit(solution)/shard_map/ppermute | solution.py:195
  128.8 10.2 %copy-start.7 = (bf16[147,1024]{1,0:T(8,128)(2,1)S(1)}, bf16[147,1024]{1,0:T(8,128)(2,1)}, u32[]{:S(2)}) copy-start(bf16[147,1024]{1,0:T(8,128)(2,1)} %d_ref.1) | copy-start | bytes 903172

commit v2 on v1

v2 whole, which is shorter than its diff:
```python
import functools
import math

import jax
import jax.numpy as jnp
from jax import lax
from jax.experimental import pallas as pl
from jax.experimental.pallas import tpu as pltpu
from jax.sharding import PartitionSpec as P

F32, BF16 = jnp.float32, jnp.bfloat16
VMEM = 16 * 2**20
COEFS = (0.99999921, -19.73898036, 64.92865742, -85.27162153, 58.79049212, -21.07110563)
ROUNDER = 12582912.0


def up(value, step):
    return -(-value // step) * step


def params():
    return pltpu.CompilerParams(vmem_limit_bytes=VMEM)


def cosine(angle):
    turns = angle * (0.5 / math.pi)
    rest = turns - ((turns + ROUNDER) - ROUNDER)
    square = rest * rest
    total = square * COEFS[-1] + COEFS[-2]
    for coef in COEFS[-3::-1]:
        total = total * square + coef
    return total


def pack_weights_kernel(raw, depth, classes, w_ref, ph_ref, d_ref, o_ref):
    rows, f = o_ref.shape
    o_ref[:raw, :] = w_ref[...]
    head = lax.broadcasted_iota(jnp.int32, (depth - raw, f), 0) == 0
    o_ref[raw:depth, :] = jnp.where(head, ph_ref[...].astype(F32), 0.0).astype(BF16)
    o_ref[depth : depth + classes, :] = d_ref[...]
    o_ref[depth + classes :, :] = jnp.zeros((rows - depth - classes, f), BF16)


def pack_samples_kernel(raw, depth, classes, x_ref, p_ref, l_ref, o_ref):
    rows, n = o_ref.shape
    o_ref[:raw, :] = x_ref[...]
    head = lax.broadcasted_iota(jnp.int32, (depth - raw, n), 0) == 0
    o_ref[raw:depth, :] = jnp.where(head, 1.0, 0.0).astype(BF16)
    ids = lax.broadcasted_iota(jnp.int32, (classes, n), 0)
    onehot = (ids == l_ref[...]).astype(F32)
    o_ref[depth : depth + classes, :] = (p_ref[...].astype(F32) - onehot).astype(BF16)
    o_ref[depth + classes :, :] = jnp.zeros((rows - depth - classes, n), BF16)


def pack(kernel, shape, *args):
    return pl.pallas_call(
        kernel,
        grid=(1,),
        in_specs=[pl.BlockSpec(a.shape, lambda i: (0, 0)) for a in args],
        out_specs=pl.BlockSpec(shape, lambda i: (0, 0)),
        out_shape=jax.ShapeDtypeStruct(shape, BF16),
        compiler_params=params(),
    )(*args)


def one_block(xt, w_refs, depth):
    proj, spot = None, 0
    for w_ref in w_refs:
        end = min(spot + w_ref.shape[0], depth)
        part = jnp.dot(xt[:, spot:end], w_ref[: end - spot, :], preferred_element_type=F32)
        proj = part if proj is None else proj + part
        spot += w_ref.shape[0]
    direction = w_refs[-1][w_refs[-1].shape[0] - (spot - depth) :, :]
    feats = cosine(proj).astype(BF16)
    return feats, lax.dot_general(feats, direction, (((1,), (1,)), ((), ())), preferred_element_type=F32)


def first_kernel(depth, count, *refs):
    x_refs, w_ref = refs[:count], refs[count]
    xt_ref, f_ref, t_ref = refs[count + 1 :]
    n = x_refs[0].shape[1]
    for j in range(count):
        here = slice(j * n, (j + 1) * n)
        xt = x_refs[j][:depth, :].T
        xt_ref[here, :] = xt
        f_ref[here, :], t_ref[here, :] = one_block(xt, [w_ref], depth)


def next_kernel(depth, count, totals, pieces, block, last, *refs):
    refs = list(refs)
    xt_refs, t_refs = refs[:count], refs[count : count + totals]
    refs = refs[count + totals :]
    w_refs = [[refs.pop(0) for _ in range(k)] for k in pieces]
    f_refs = [refs.pop(0) for _ in pieces]
    spot = 0
    t_blocks = [(ref, at) for ref in t_refs for at in range(0, ref.shape[0], block)]
    for xt_ref in xt_refs:
        for at in range(0, xt_ref.shape[0], block):
            t_ref, t_at = t_blocks[spot // block]
            xt, total = xt_ref[at : at + block, :], t_ref[t_at : t_at + block, :]
            for ws, f_ref in zip(w_refs, f_refs, strict=True):
                f_ref[spot : spot + block, :], tangent = one_block(xt, ws, depth)
                total = total + tangent
            if not last:
                refs[0][spot : spot + block, :] = total
            else:
                pair, mine = spot // (2 * block), spot // block % 2
                here = slice(pair * block, (pair + 1) * block)
                if mine:
                    refs[1][:, here] = total.T
                else:
                    refs[0][:, here] = total.T.astype(BF16)
            spot += block


def make_next(xts, totals, pieces, depth, wide, block, last):
    n, f = sum(a.shape[0] for a in xts), pieces[0][0].shape[1]
    shapes = [jax.ShapeDtypeStruct((n, f), BF16)] * len(pieces)
    if last:
        shapes.append(jax.ShapeDtypeStruct((wide, n // 2), BF16))
        shapes.append(jax.ShapeDtypeStruct((wide, n // 2), F32))
    else:
        shapes.append(jax.ShapeDtypeStruct((n, wide), F32))
    kernel = functools.partial(next_kernel, depth, len(xts), len(totals), [len(ws) for ws in pieces], block, last)
    out = whole(kernel, shapes, *xts, *totals, *[w for ws in pieces for w in ws], flops=2 * n * f * len(pieces) * (depth + wide))
    return out[: len(pieces)], out[len(pieces) :]


def spread_kernel(own_ref, got_ref, keep_ref, *send_refs):
    n = keep_ref.shape[1]
    total = own_ref[...] + got_ref[...].astype(F32)
    keep_ref[...] = total[:, :n]
    for j, ref in enumerate(send_refs):
        ref[...] = total[:, (j + 1) * n : (j + 2) * n].astype(BF16)


def curve_kernel(classes, keep_ref, *refs):
    got_refs, p_ref, c_ref = refs[:-2], refs[-2], refs[-1]
    total = keep_ref[...]
    for ref in got_refs:
        total = total + ref[...].astype(F32)
    total = total[:classes, :]
    prob = p_ref[...].astype(F32)
    mixed = jnp.sum(prob * total, axis=0, keepdims=True)
    c_ref[:classes, :] = (prob * (total - mixed)).astype(BF16)
    c_ref[classes:, :] = jnp.zeros((c_ref.shape[0] - classes, c_ref.shape[1]), BF16)


def share_kernel(count, skip, block, *refs):
    left_refs, f_refs, o_ref = refs[:count], refs[count:-1], refs[-1]
    f_blocks = [(ref, at) for ref in f_refs for at in range(0, ref.shape[0], block)]
    total = None
    for left_ref, (f_ref, at) in zip(left_refs, f_blocks, strict=True):
        part = jnp.dot(left_ref[skip:, :], f_ref[at : at + block, :], preferred_element_type=F32)
        total = part if total is None else total + part
    o_ref[...] = total.astype(o_ref.dtype)


def make_share(lefts, skip, feats, dtype):
    block = lefts[0].shape[1]
    wide, n, f = lefts[0].shape[0] - skip, sum(a.shape[0] for a in feats), feats[0].shape[1]
    return whole(
        functools.partial(share_kernel, len(lefts), skip, block),
        jax.ShapeDtypeStruct((wide, f), dtype),
        *lefts, *feats, flops=2 * n * f * wide,
    )


def whole(kernel, shapes, *args, flops=0):
    size = sum(math.prod(a.shape) * a.dtype.itemsize for a in args)
    cost = pl.CostEstimate(flops=flops, bytes_accessed=size, transcendentals=0)
    return pl.pallas_call(kernel, out_shape=shapes, compiler_params=params(), cost_estimate=cost)(*args)


def on_device(line, ys, xs, inputs, probs, labels, proj_weight, phase, direction, damping):
    raw, own = inputs.shape
    classes = probs.shape[0]
    width = proj_weight.shape[1]
    depth = up(raw + 1, 16)
    wide = up(classes, 8)

    def swap_core(a):
        return lax.ppermute(a, "feat", [(i, i ^ 1) for i in range(2 * xs * ys)])

    def along(a, k):
        return lax.ppermute(a, "samp", [(i, (i + k) % line) for i in range(line)])

    def across(a, dy, dx):
        def to(i):
            y, x, c = i // (2 * xs), i // 2 % xs, i % 2
            return ((y + dy) % ys * xs + (x + dx) % xs) * 2 + c

        return lax.ppermute(a, "feat", [(i, to(i)) for i in range(2 * xs * ys)])

    offsets = [(dy, dx) for dy in range(ys) for dx in range(xs)]
    w_own = pack(
        functools.partial(pack_weights_kernel, raw, depth, classes), (depth + wide, width), proj_weight, phase, direction
    )
    ws = {(0, 0): [w_own]}
    for dy in range(1, ys):
        ws[dy, 0] = [across(w_own, dy, 0)]
    for dx in range(1, xs):
        ws[0, dx] = [across(w_own, 0, dx)]
    x_own = pack(
        functools.partial(pack_samples_kernel, raw, depth, classes), (depth + wide, own), inputs, probs, labels[None, :]
    )
    x_line = [x_own] + [along(x_own, k) for k in range(1, line)]
    blocks = [b for a in x_line for b in (swap_core(a), a)]
    cut = up(depth // 2, 128)
    for dy in range(1, ys):
        for dx in range(1, xs):
            ws[dy, dx] = [across(ws[0, dx][0][:cut], dy, 0), across(ws[dy, 0][0][cut:], 0, dx)]

    feats = {(0, 0): []}
    xts, totals = [], []
    for k in range(line):
        pair = 2 * own
        xt, part, total = whole(
            functools.partial(first_kernel, depth, 2),
            [
                jax.ShapeDtypeStruct((pair, depth), BF16),
                jax.ShapeDtypeStruct((pair, width), BF16),
                jax.ShapeDtypeStruct((pair, wide), F32),
            ],
            *blocks[2 * k : 2 * k + 2], w_own, flops=2 * pair * width * (depth + wide),
        )
        xts.append(xt)
        totals.append(total)
        feats[0, 0].append(part)
    near = [at for at in offsets[1:] if 0 in at]
    far = [at for at in offsets[1:] if 0 not in at]
    groups = [group for group in (near, far) if group]
    for group in groups:
        got, rest = make_next(xts, totals, [ws[at] for at in group], depth, wide, own, group is groups[-1])
        for at, piece in zip(group, got, strict=True):
            feats[at] = [piece]
        if group is not groups[-1]:
            totals = [rest[0]]
    t_other, t_own = rest
    t_got = swap_core(t_other)
    keep, *send = whole(
        spread_kernel,
        [jax.ShapeDtypeStruct((wide, own), F32)] + [jax.ShapeDtypeStruct((wide, own), BF16)] * (line - 1),
        t_own, t_got,
    )
    got = [along(a, -k) for k, a in enumerate(send, 1)]

    def collect(parts):
        out = parts[0, 0]
        for dy, dx in offsets[1:]:
            out = out + across(parts[dy, dx], -dy, -dx).astype(F32)
        return out[:classes]

    parts = {at: make_share(blocks, depth, feats[at], F32 if at == (0, 0) else BF16) for at in offsets[::-1]}
    keep, parts = lax.optimization_barrier((keep, parts))
    gradient = collect(parts)
    curv = whole(
        functools.partial(curve_kernel, classes), jax.ShapeDtypeStruct((wide, own), BF16), keep, *got, probs
    )
    c_line = [curv] + [along(curv, k) for k in range(1, line)]
    curvs = [b for a in c_line for b in (swap_core(a), a)]

    hess_parts = {at: make_share(curvs, 0, feats[at], F32 if at == (0, 0) else BF16) for at in offsets[::-1]}
    hess_vec = collect(hess_parts) + damping[0] * direction.astype(F32)
    return (hess_vec, gradient)


def solution(mesh):
    line, feat = mesh.shape["samp"], mesh.shape["feat"]
    ys = 2 if feat % 4 == 0 else 1
    xs = feat // (2 * ys)
    placed = (
        P(None, ("samp", "feat")),
        P(None, ("samp", "feat")),
        P(("samp", "feat")),
        P(None, ("feat", "samp")),
        P(None, ("feat", "samp")),
        P(None, ("feat", "samp")),
        P(),
    )
    return jax.shard_map(
        functools.partial(on_device, line, ys, xs),
        mesh=mesh,
        in_specs=placed,
        out_specs=(P(None, ("feat", "samp")), P(None, ("feat", "samp"))),
        check_vma=False,
    )
```

time: 142 us -> 117 us (0.82)
  Pallas kernels: 50 us -> 30.8 us
  local copies, waits for them, and re-layouts: 14 us -> 2.92 us
  waiting for transfers between devices: 37.8 us -> 45.8 us
  other arithmetic: 3.97 us -> 2.06 us
    pallas_call x16 -> x18, Pallas kernels: 50 us -> 30.8 us  [the longest x16 30.7 us: whole(): pl.pallas_call(kernel, out_shape=shapes, compiler_params=params(), cost_e...]
    unnamed x34 -> x14, local copies, waits for them, and re-layouts: 13.9 us -> 2.84 us
    ppermute x10, waiting for transfers between devices: 9.18 us -> 18.9 us  [across(): return lax.ppermute(a, 'feat', [(i, to(i)) for i in range(2 * xs * ys)])]
    ppermute x9, waiting for transfers between devices: 3.51 us -> 0.02 us  [swap_core(): return lax.ppermute(a, 'feat', [(i, i ^ 1) for i in range(2 * xs * ys)])]
    ppermute x10, starting transfers between devices: 14 us -> 16 us  [across(): return lax.ppermute(a, 'feat', [(i, to(i)) for i in range(2 * xs * ys)])]
    add x2, other arithmetic: 3.97 us -> 2.06 us  [the longest x1 1.05 us: on_device(): hess_vec = collect(hess_parts) + damping[0] * direction.astype(F32)]
    ppermute x9, waiting for transfers between devices: 25.1 us -> 26.9 us  [along(): return lax.ppermute(a, 'samp', [(i, (i + k) % line) for i in range(line)])]
    ppermute x9, starting transfers between devices: 18.1 us -> 16.6 us  [along(): return lax.ppermute(a, 'samp', [(i, (i + k) % line) for i in range(line)])]
  transfers between devices with their start and end apart: 28 -> 28, of which waited for: 12 -> 10; matrix products, arithmetic and copies ran while one was open for 1% -> 1% of each run, Pallas kernels for 27% -> 21%
where the time goes in v2:
time: 117 us
  waiting for transfers between devices  45.8 us (39%)
  starting transfers between devices  33.7 us (29%)
  Pallas kernels  30.8 us (26%)
  local copies, waits for them, and re-layouts  2.92 us (2%)
  other arithmetic  2.06 us (2%)
  between operations  1.53 us (1%)
    pallas_call x16, Pallas kernels, whole(): pl.pallas_call(kernel, out_shape=shapes, compiler_params=params(), cost_e...  30.7 us
    ppermute x9, waiting for transfers between devices, along(): return lax.ppermute(a, 'samp', [(i, (i + k) % line) for i in range(line)])  26.9 us
    ppermute x10, waiting for transfers between devices, across(): return lax.ppermute(a, 'feat', [(i, to(i)) for i in range(2 * xs * ys)])  18.9 us
    ppermute x9, starting transfers between devices, along(): return lax.ppermute(a, 'samp', [(i, (i + k) % line) for i in range(line)])  16.6 us
    ppermute x10, starting transfers between devices, across(): return lax.ppermute(a, 'feat', [(i, to(i)) for i in range(2 * xs * ys)])  16 us
    unnamed x14, local copies, waits for them, and re-layouts  2.84 us
  transfers between devices with their start and end apart: 28, of which 10 were waited for; matrix products, arithmetic and copies ran while one was open for 1% of the time, Pallas kernels for 21%

profile of v2, /device:TPU:0, one launch (start us, length us, event | category | flops | bytes accessed | tf_op | source)
XLA Modules:
  0.0 116.8 jit_solution(10013310740408361445)
XLA Ops:
  0.6 1.0 copy-done
  1.6 1.2 %copy-done.2 = bf16[440,1024]{1,0:T(8,128)(2,1)S(1)} copy-done((bf16[440,1024]{1,0:T(8,128)(2,1)S(1)}, bf16[440,1024]{1,0:T(8,128)(2,1)}, u32[]{:S(2)}) %copy-start.2) | copy-done | bytes 901144
  2.8 0.7 copy-done.5
  3.6 3.0 %collective-permute-start.8 = (bf16[600,1024]{1,0:T(8,128)(2,1)S(1)}, bf16[600,1024]{1,0:T(8,128)(2,1)S(1)}, u32[]{:S(2)}, u32[]{:S(2)}) collective-permute-start(bf16[600,1024]{1,0:T(8,128)(2,1)S(1)} %shard_map.87.refs_2_), channel_id=1, source_target_pairs={{0,4},{1,5},{2,6},{3,7},{4,0},{5,1},{6,2},{7,3},{8,12},{9,13},{10,... | collective-permute-start | bytes 3686408 | tf_op jit(solution)/shard_map/ppermute | solution.py:193
  6.6 1.5 %collective-permute-start.7 = (bf16[600,1024]{1,0:T(8,128)(2,1)S(1)}, bf16[600,1024]{1,0:T(8,128)(2,1)S(1)}, u32[]{:S(2)}, u32[]{:S(2)}) collective-permute-start(bf16[600,1024]{1,0:T(8,128)(2,1)S(1)} %shard_map.87.refs_2_), channel_id=1, source_target_pairs={{0,2},{1,3},{2,0},{3,1},{4,6},{5,7},{6,4},{7,5},{8,10},{9,11},{10,... | collective-permute-start | bytes 3686408 | tf_op jit(solution)/shard_map/ppermute | solution.py:193
  8.1 1.6 %collective-permute-start.1 = (bf16[600,256]{1,0:T(8,128)(2,1)S(1)}, bf16[600,256]{1,0:T(8,128)(2,1)S(1)}, u32[]{:S(2)}, u32[]{:S(2)}) collective-permute-start(bf16[600,256]{1,0:T(8,128)(2,1)S(1)} %shard_map.86.refs_1_), channel_id=1, source_target_pairs={{0,8},{8,16},{16,24},{24,0},{1,9},{9,17},{17,25},{25,1},{2,10},{10... | collective-permute-start | bytes 921608 | tf_op jit(solution)/shard_map/ppermute | solution.py:186
  9.8 2.6 %collective-permute-start.3 = (bf16[600,256]{1,0:T(8,128)(2,1)S(1)}, bf16[600,256]{1,0:T(8,128)(2,1)S(1)}, u32[]{:S(2)}, u32[]{:S(2)}) collective-permute-start(bf16[600,256]{1,0:T(8,128)(2,1)S(1)} %shard_map.86.refs_1_), channel_id=1, source_target_pairs={{0,16},{8,24},{16,0},{24,8},{1,17},{9,25},{17,1},{25,9},{2,18},{10... | collective-permute-start | bytes 921608 | tf_op jit(solution)/shard_map/ppermute | solution.py:186
  12.4 1.3 %collective-permute-start.5 = (bf16[600,256]{1,0:T(8,128)(2,1)S(1)}, bf16[600,256]{1,0:T(8,128)(2,1)S(1)}, u32[]{:S(2)}, u32[]{:S(2)}) collective-permute-start(bf16[600,256]{1,0:T(8,128)(2,1)S(1)} %shard_map.86.refs_1_), channel_id=1, source_target_pairs={{0,24},{8,0},{16,8},{24,16},{1,25},{9,1},{17,9},{25,17},{2,26},{10... | collective-permute-start | bytes 921608 | tf_op jit(solution)/shard_map/ppermute | solution.py:186
  13.7 6.6 %collective-permute-done.1.refs_1_.refs_3_ = bf16[600,256]{1,0:T(8,128)(2,1)S(1)} collective-permute-done((bf16[600,256]{1,0:T(8,128)(2,1)S(1)}, bf16[600,256]{1,0:T(8,128)(2,1)S(1)}, u32[]{:S(2)}, u32[]{:S(2)}) %collective-permute-start.1) | collective-permute-done | bytes 307232 | tf_op jit(solution)/shard_map/ppermute | solution.py:186
  20.4 11.5 %collective-permute-done.3.refs_1_.refs_5_ = bf16[600,256]{1,0:T(8,128)(2,1)S(1)} collective-permute-done((bf16[600,256]{1,0:T(8,128)(2,1)S(1)}, bf16[600,256]{1,0:T(8,128)(2,1)S(1)}, u32[]{:S(2)}, u32[]{:S(2)}) %collective-permute-start.3) | collective-permute-done | bytes 307232 | tf_op jit(solution)/shard_map/ppermute | solution.py:186
  31.8 0.5 collective-permute-start.4
  32.3 1.3 %collective-permute-done.8.refs_9_ = bf16[600,1024]{1,0:T(8,128)(2,1)S(1)} collective-permute-done((bf16[600,1024]{1,0:T(8,128)(2,1)S(1)}, bf16[600,1024]{1,0:T(8,128)(2,1)S(1)}, u32[]{:S(2)}, u32[]{:S(2)}) %collective-permute-start.8) | collective-permute-done | bytes 1228832 | tf_op jit(solution)/shard_map/ppermute | solution.py:193
  33.7 1.8 %collective-permute-start.10 = (bf16[344,1024]{1,0:T(8,128)(2,1)S(1)}, bf16[344,1024]{1,0:T(8,128)(2,1)S(1)}, u32[]{:S(2)}, u32[]{:S(2)}) collective-permute-start(bf16[344,1024]{1,0:T(8,128)(2,1)S(1)} %slice.17), channel_id=1, source_target_pairs={{0,2},{1,3},{2,0},{3,1},{4,6},{5,7},{6,4},{7,5},{8,10},{9,11},{10,... | collective-permute-start | bytes 2113544 | tf_op jit(solution)/shard_map/ppermute | solution.py:193
  35.5 1.6 %shard_map.88 = (bf16[512,448]{1,0:T(8,128)(2,1)S(1)}, bf16[512,1024]{1,0:T(8,128)(2,1)S(1)}, f32[512,152]{1,0:T(8,128)S(1)}) custom-call(bf16[600,256]{1,0:T(8,128)(2,1)S(1)} %collective-permute-done.refs_0_, bf16[600,256]{1,0:T(8,128)(2,1)S(1)} %shard_map.86.refs_1_, bf16[600,1024]{1,0:T(8,128)(2,1)S(1)} %shard_map.87.refs_2_), custom_call_target="tpu_custom_call" | custom-call | flops 629145600 | bytes 1843200 | tf_op jit(solution)/shard_map/pallas_call | solution.py:172
  37.1 1.6 %shard_map.89 = (bf16[512,448]{1,0:T(8,128)(2,1)S(1)}, bf16[512,1024]{1,0:T(8,128)(2,1)S(1)}, f32[512,152]{1,0:T(8,128)S(1)}) custom-call(bf16[600,256]{1,0:T(8,128)(2,1)S(1)} %collective-permute-done.2.refs_0_.refs_2_, bf16[600,256]{1,0:T(8,128)(2,1)S(1)} %collective-permute-done.1.refs_1_.refs_3_, bf16[600,1024]{1,0:T(8,128)(2,1)S(1)} %shard_map.87.refs_2_), custom_call_target="tpu_custom_call" | custom-call | flops 629145600 | bytes 1843200 | tf_op jit(solution)/shard_map/pallas_call | solution.py:172
  38.7 1.6 %shard_map.90 = (bf16[512,448]{1,0:T(8,128)(2,1)S(1)}, bf16[512,1024]{1,0:T(8,128)(2,1)S(1)}, f32[512,152]{1,0:T(8,128)S(1)}) custom-call(bf16[600,256]{1,0:T(8,128)(2,1)S(1)} %collective-permute-done.4.refs_0_.refs_4_, bf16[600,256]{1,0:T(8,128)(2,1)S(1)} %collective-permute-done.3.refs_1_.refs_5_, bf16[600,1024]{1,0:T(8,128)(2,1)S(1)} %shard_map.87.refs_2_), custom_call_target="tpu_custom_call" | custom-call | flops 629145600 | bytes 1843200 | tf_op jit(solution)/shard_map/pallas_call | solution.py:172
  40.4 1.6 %collective-permute-start.9 = (bf16[256,1024]{1,0:T(8,128)(2,1)S(1)}, bf16[256,1024]{1,0:T(8,128)(2,1)S(1)}, u32[]{:S(2)}, u32[]{:S(2)}) collective-permute-start(bf16[256,1024]{1,0:T(8,128)(2,1)S(1)} %slice.16), channel_id=1, source_target_pairs={{0,4},{1,5},{2,6},{3,7},{4,0},{5,1},{6,2},{7,3},{8,12},{9,13},{10,... | collective-permute-start | bytes 1572872 | tf_op jit(solution)/shard_map/ppermute | solution.py:193
  42.0 1.6 %shard_map.91 = (bf16[512,448]{1,0:T(8,128)(2,1)S(1)}, bf16[512,1024]{1,0:T(8,128)(2,1)S(1)}, f32[512,152]{1,0:T(8,128)S(1)}) custom-call(bf16[600,256]{1,0:T(8,128)(2,1)S(1)} %collective-permute-done.6.refs_0_.refs_6_, bf16[600,256]{1,0:T(8,128)(2,1)S(1)} %collective-permute-done.5.refs_1_.refs_7_, bf16[600,1024]{1,0:T(8,128)(2,1)S(1)} %shard_map.87.refs_2_), custom_call_target="tpu_custom_call" | custom-call | flops 629145600 | bytes 1843200 | tf_op jit(solution)/shard_map/pallas_call | solution.py:172
  43.6 11.0 %shard_map.92 = (bf16[2048,1024]{1,0:T(8,128)(2,1)S(1)}, bf16[2048,1024]{1,0:T(8,128)(2,1)S(1)}, f32[2048,152]{1,0:T(8,128)S(1)}) custom-call(bf16[512,448]{1,0:T(8,128)(2,1)S(1)} %get-tuple-element.29.refs_0_, bf16[512,448]{1,0:T(8,128)(2,1)S(1)} %get-tuple-element.30.refs_1_, bf16[512,448]{1,0:T(8,128)(2,1)S(1)} %get-tuple-element.31.refs_2_, ...), custom_call_target="tpu_custom_call" | custom-call | flops 5033164800 | bytes 5537792 | tf_op jit(solution)/shard_map/pallas_call | solution.py:172
  54.6 6.0 %shard_map.93 = (bf16[2048,1024]{1,0:T(8,128)(2,1)S(1)}, bf16[152,1024]{1,0:T(8,128)(2,1)S(1)}, f32[152,1024]{1,0:T(8,128)S(1)}) custom-call(bf16[512,448]{1,0:T(8,128)(2,1)S(1)} %get-tuple-element.29.refs_0_, bf16[512,448]{1,0:T(8,128)(2,1)S(1)} %get-tuple-element.30.refs_1_, bf16[512,448]{1,0:T(8,128)(2,1)S(1)} %get-tuple-element.31.refs_2_, ...), custom_call_target="tpu_custom_call" | custom-call | flops 2516582400 | bytes 4308992 | tf_op jit(solution)/shard_map/pallas_call | solution.py:172
  60.7 1.1 shard_map.95
  61.8 0.9 shard_map.96
  62.7 5.6 %collective-permute-start.12 = (bf16[152,256]{1,0:T(8,128)(2,1)S(1)}, bf16[152,256]{1,0:T(8,128)(2,1)S(1)}, u32[]{:S(2)}, u32[]{:S(2)}) collective-permute-start(bf16[152,256]{1,0:T(8,128)(2,1)S(1)} %get-tuple-element.49), channel_id=1, source_target_pairs={{0,24},{8,0},{16,8},{24,16},{1,25},{9,1},{17,9},{25,17},{2,26},{10... | collective-permute-start | bytes 233480 | tf_op jit(solution)/shard_map/ppermute | solution.py:186
  68.3 0.6 collective-permute-start.14
  69.0 0.9 shard_map.97
  69.8 0.9 shard_map.98
  70.7 0.3 collective-permute-done.12.refs_0_
  71.0 5.3 %collective-permute-done.13.refs_1_ = bf16[152,256]{1,0:T(8,128)(2,1)S(1)} collective-permute-done((bf16[152,256]{1,0:T(8,128)(2,1)S(1)}, bf16[152,256]{1,0:T(8,128)(2,1)S(1)}, u32[]{:S(2)}, u32[]{:S(2)}) %collective-permute-start.13) | collective-permute-done | bytes 77856 | tf_op jit(solution)/shard_map/ppermute | solution.py:186
  76.6 1.9 %collective-permute-start.18 = (bf16[152,256]{1,0:T(8,128)(2,1)S(1)}, bf16[152,256]{1,0:T(8,128)(2,1)S(1)}, u32[]{:S(2)}, u32[]{:S(2)}) collective-permute-start(bf16[152,256]{1,0:T(8,128)(2,1)S(1)} %shard_map.99.refs_1_), channel_id=1, source_target_pairs={{0,16},{8,24},{16,0},{24,8},{1,17},{9,25},{17,1},{25,9},{2,18},{10... | collective-permute-start | bytes 233480 | tf_op jit(solution)/shard_map/ppermute | solution.py:186
  78.5 2.7 %collective-permute-start.20 = (bf16[152,256]{1,0:T(8,128)(2,1)S(1)}, bf16[152,256]{1,0:T(8,128)(2,1)S(1)}, u32[]{:S(2)}, u32[]{:S(2)}) collective-permute-start(bf16[152,256]{1,0:T(8,128)(2,1)S(1)} %shard_map.99.refs_1_), channel_id=1, source_target_pairs={{0,24},{8,0},{16,8},{24,16},{1,25},{9,1},{17,9},{25,17},{2,26},{10... | collective-permute-start | bytes 233480 | tf_op jit(solution)/shard_map/ppermute | solution.py:186
  81.2 2.3 %collective-permute-done.16.refs_3_ = bf16[152,256]{1,0:T(8,128)(2,1)S(1)} collective-permute-done((bf16[152,256]{1,0:T(8,128)(2,1)S(1)}, bf16[152,256]{1,0:T(8,128)(2,1)S(1)}, u32[]{:S(2)}, u32[]{:S(2)}) %collective-permute-start.16) | collective-permute-done | bytes 77856 | tf_op jit(solution)/shard_map/ppermute | solution.py:186
  83.5 1.5 %collective-permute-start.25 = (bf16[152,1024]{1,0:T(8,128)(2,1)S(1)}, bf16[152,1024]{1,0:T(8,128)(2,1)S(1)}, u32[]{:S(2)}, u32[]{:S(2)}) collective-permute-start(bf16[152,1024]{1,0:T(8,128)(2,1)S(1)} %shard_map.96), channel_id=1, source_target_pairs={{0,2},{1,3},{2,0},{3,1},{4,6},{5,7},{6,4},{7,5},{8,10},{9,11},{10,... | collective-permute-start | bytes 933896 | tf_op jit(solution)/shard_map/ppermute | solution.py:193
  85.0 0.8 collective-permute-done.18.refs_5_
  85.8 0.5 collective-permute-start.21
  86.4 0.8 collective-permute-start.26
  87.2 2.1 %collective-permute-start.27 = (bf16[152,1024]{1,0:T(8,128)(2,1)S(1)}, bf16[152,1024]{1,0:T(8,128)(2,1)S(1)}, u32[]{:S(2)}, u32[]{:S(2)}) collective-permute-start(bf16[152,1024]{1,0:T(8,128)(2,1)S(1)} %shard_map.98), channel_id=1, source_target_pairs={{0,6},{1,7},{2,4},{3,5},{4,2},{5,3},{6,0},{7,1},{8,14},{9,15},{10,... | collective-permute-start | bytes 933896 | tf_op jit(solution)/shard_map/ppermute | solution.py:193
  90.0 0.9 shard_map.101
  90.9 0.6 collective-permute-start.22
  91.4 0.8 shard_map.102
  92.3 0.9 collective-permute-start.23
  93.2 0.8 shard_map.103
  94.1 2.2 %collective-permute-start.24 = (bf16[152,1024]{1,0:T(8,128)(2,1)S(1)}, bf16[152,1024]{1,0:T(8,128)(2,1)S(1)}, u32[]{:S(2)}, u32[]{:S(2)}) collective-permute-start(bf16[152,1024]{1,0:T(8,128)(2,1)S(1)} %shard_map.103), channel_id=1, source_target_pairs={{0,6},{1,7},{2,4},{3,5},{4,2},{5,3},{6,0},{7,1},{8,14},{9,15},{10,... | collective-permute-start | bytes 933896 | tf_op jit(solution)/shard_map/ppermute | solution.py:193
  96.3 0.8 shard_map.100
  97.1 6.1 %collective-permute-done.26 = bf16[152,1024]{1,0:T(8,128)(2,1)S(1)} collective-permute-done((bf16[152,1024]{1,0:T(8,128)(2,1)S(1)}, bf16[152,1024]{1,0:T(8,128)(2,1)S(1)}, u32[]{:S(2)}, u32[]{:S(2)}) %collective-permute-start.26) | collective-permute-done | bytes 311328 | tf_op jit(solution)/shard_map/ppermute | solution.py:193
  103.2 1.0 fusion.1
  104.3 2.8 %collective-permute-done.22 = bf16[152,1024]{1,0:T(8,128)(2,1)S(1)} collective-permute-done((bf16[152,1024]{1,0:T(8,128)(2,1)S(1)}, bf16[152,1024]{1,0:T(8,128)(2,1)S(1)}, u32[]{:S(2)}, u32[]{:S(2)}) %collective-permute-start.22) | collective-permute-done | bytes 311328 | tf_op jit(solution)/shard_map/ppermute | solution.py:193
  107.1 8.6 %collective-permute-done.23 = bf16[152,1024]{1,0:T(8,128)(2,1)S(1)} collective-permute-done((bf16[152,1024]{1,0:T(8,128)(2,1)S(1)}, bf16[152,1024]{1,0:T(8,128)(2,1)S(1)}, u32[]{:S(2)}, u32[]{:S(2)}) %collective-permute-start.23) | collective-permute-done | bytes 311328 | tf_op jit(solution)/shard_map/ppermute | solution.py:193
  115.7 1.1 fusion.4
  (44 shorter events, 0.7 us)
Async XLA Ops:
  0.6 1.0 copy-start
  1.6 1.2 %copy-start.2 = (bf16[440,1024]{1,0:T(8,128)(2,1)S(1)}, bf16[440,1024]{1,0:T(8,128)(2,1)}, u32[]{:S(2)}) copy-start(bf16[440,1024]{1,0:T(8,128)(2,1)} %w_ref.1) | copy-start | bytes 2703364
  2.8 0.7 copy-start.5
  3.5 4.6 %copy-start.3 = (bf16[147,256]{1,0:T(8,128)(2,1)S(1)}, bf16[147,256]{1,0:T(8,128)(2,1)}, u32[]{:S(2)}) copy-start(bf16[147,256]{1,0:T(8,128)(2,1)} %refs_3_.1) | copy-start | bytes 225796
  3.5 4.6 %copy-start.4 = (bf16[440,256]{1,0:T(8,128)(2,1)S(1)}, bf16[440,256]{1,0:T(8,128)(2,1)}, u32[]{:S(2)}) copy-start(bf16[440,256]{1,0:T(8,128)(2,1)} %x_ref.1) | copy-start | bytes 675844
  3.5 4.6 %copy-start.6 = (s32[256]{0:T(256)S(1)}, s32[256]{0:T(256)}, u32[]{:S(2)}) copy-start(s32[256]{0:T(256)} %param.9) | copy-start | bytes 3076
  3.6 30.1 %collective-permute-start.8 = (bf16[600,1024]{1,0:T(8,128)(2,1)S(1)}, bf16[600,1024]{1,0:T(8,128)(2,1)S(1)}, u32[]{:S(2)}, u32[]{:S(2)}) collective-permute-start(bf16[600,1024]{1,0:T(8,128)(2,1)S(1)} %shard_map.87.refs_2_), channel_id=1, source_target_pairs={{0,4},{1,5},{2,6},{3,7},{4,0},{5,1},{6,2},{7,3},{8,12},{9,13},{10,... | collective-permute-start | bytes 3686408 | tf_op jit(solution)/shard_map/ppermute | solution.py:193
  6.6 33.7 %collective-permute-start.7 = (bf16[600,1024]{1,0:T(8,128)(2,1)S(1)}, bf16[600,1024]{1,0:T(8,128)(2,1)S(1)}, u32[]{:S(2)}, u32[]{:S(2)}) collective-permute-start(bf16[600,1024]{1,0:T(8,128)(2,1)S(1)} %shard_map.87.refs_2_), channel_id=1, source_target_pairs={{0,2},{1,3},{2,0},{3,1},{4,6},{5,7},{6,4},{7,5},{8,10},{9,11},{10,... | collective-permute-start | bytes 3686408 | tf_op jit(solution)/shard_map/ppermute | solution.py:193
  8.1 12.2 %collective-permute-start.1 = (bf16[600,256]{1,0:T(8,128)(2,1)S(1)}, bf16[600,256]{1,0:T(8,128)(2,1)S(1)}, u32[]{:S(2)}, u32[]{:S(2)}) collective-permute-start(bf16[600,256]{1,0:T(8,128)(2,1)S(1)} %shard_map.86.refs_1_), channel_id=1, source_target_pairs={{0,8},{8,16},{16,24},{24,0},{1,9},{9,17},{17,25},{25,1},{2,10},{10... | collective-permute-start | bytes 921608 | tf_op jit(solution)/shard_map/ppermute | solution.py:186
  9.8 22.0 %collective-permute-start.3 = (bf16[600,256]{1,0:T(8,128)(2,1)S(1)}, bf16[600,256]{1,0:T(8,128)(2,1)S(1)}, u32[]{:S(2)}, u32[]{:S(2)}) collective-permute-start(bf16[600,256]{1,0:T(8,128)(2,1)S(1)} %shard_map.86.refs_1_), channel_id=1, source_target_pairs={{0,16},{8,24},{16,0},{24,8},{1,17},{9,25},{17,1},{25,9},{2,18},{10... | collective-permute-start | bytes 921608 | tf_op jit(solution)/shard_map/ppermute | solution.py:186
  12.4 19.5 %collective-permute-start.5 = (bf16[600,256]{1,0:T(8,128)(2,1)S(1)}, bf16[600,256]{1,0:T(8,128)(2,1)S(1)}, u32[]{:S(2)}, u32[]{:S(2)}) collective-permute-start(bf16[600,256]{1,0:T(8,128)(2,1)S(1)} %shard_map.86.refs_1_), channel_id=1, source_target_pairs={{0,24},{8,0},{16,8},{24,16},{1,25},{9,1},{17,9},{25,17},{2,26},{10... | collective-permute-start | bytes 921608 | tf_op jit(solution)/shard_map/ppermute | solution.py:186
  20.4 13.3 %collective-permute-start = (bf16[600,256]{1,0:T(8,128)(2,1)S(1)}, bf16[600,256]{1,0:T(8,128)(2,1)S(1)}, u32[]{:S(2)}, u32[]{:S(2)}) collective-permute-start(bf16[600,256]{1,0:T(8,128)(2,1)S(1)} %shard_map.86.refs_1_), channel_id=1, source_target_pairs={{0,1},{1,0},{2,3},{3,2},{4,5},{5,4},{6,7},{7,6},{8,9},{9,8},{10,11... | collective-permute-start | bytes 921608 | tf_op jit(solution)/shard_map/ppermute | solution.py:183
  31.8 5.3 %collective-permute-start.2 = (bf16[600,256]{1,0:T(8,128)(2,1)S(1)}, bf16[600,256]{1,0:T(8,128)(2,1)S(1)}, u32[]{:S(2)}, u32[]{:S(2)}) collective-permute-start(bf16[600,256]{1,0:T(8,128)(2,1)S(1)} %collective-permute-done.1.refs_1_.refs_3_), channel_id=1, source_target_pairs={{0,1},{1,0},{2,3},{3,2},{4,5},{5,4},{6,7},{7,6},{8,9},{9,8},{10,11... | collective-permute-start | bytes 921608 | tf_op jit(solution)/shard_map/ppermute | solution.py:183
  31.8 6.9 %collective-permute-start.4 = (bf16[600,256]{1,0:T(8,128)(2,1)S(1)}, bf16[600,256]{1,0:T(8,128)(2,1)S(1)}, u32[]{:S(2)}, u32[]{:S(2)}) collective-permute-start(bf16[600,256]{1,0:T(8,128)(2,1)S(1)} %collective-permute-done.3.refs_1_.refs_5_), channel_id=1, source_target_pairs={{0,1},{1,0},{2,3},{3,2},{4,5},{5,4},{6,7},{7,6},{8,9},{9,8},{10,11... | collective-permute-start | bytes 921608 | tf_op jit(solution)/shard_map/ppermute | solution.py:183
  33.6 8.3 %collective-permute-start.6 = (bf16[600,256]{1,0:T(8,128)(2,1)S(1)}, bf16[600,256]{1,0:T(8,128)(2,1)S(1)}, u32[]{:S(2)}, u32[]{:S(2)}) collective-permute-start(bf16[600,256]{1,0:T(8,128)(2,1)S(1)} %collective-permute-done.5.refs_1_.refs_7_), channel_id=1, source_target_pairs={{0,1},{1,0},{2,3},{3,2},{4,5},{5,4},{6,7},{7,6},{8,9},{9,8},{10,11... | collective-permute-start | bytes 921608 | tf_op jit(solution)/shard_map/ppermute | solution.py:183
  33.7 20.9 %collective-permute-start.10 = (bf16[344,1024]{1,0:T(8,128)(2,1)S(1)}, bf16[344,1024]{1,0:T(8,128)(2,1)S(1)}, u32[]{:S(2)}, u32[]{:S(2)}) collective-permute-start(bf16[344,1024]{1,0:T(8,128)(2,1)S(1)} %slice.17), channel_id=1, source_target_pairs={{0,2},{1,3},{2,0},{3,1},{4,6},{5,7},{6,4},{7,5},{8,10},{9,11},{10,... | collective-permute-start | bytes 2113544 | tf_op jit(solution)/shard_map/ppermute | solution.py:193
  40.4 14.2 %collective-permute-start.9 = (bf16[256,1024]{1,0:T(8,128)(2,1)S(1)}, bf16[256,1024]{1,0:T(8,128)(2,1)S(1)}, u32[]{:S(2)}, u32[]{:S(2)}) collective-permute-start(bf16[256,1024]{1,0:T(8,128)(2,1)S(1)} %slice.16), channel_id=1, source_target_pairs={{0,4},{1,5},{2,6},{3,7},{4,0},{5,1},{6,2},{7,3},{8,12},{9,13},{10,... | collective-permute-start | bytes 1572872 | tf_op jit(solution)/shard_map/ppermute | solution.py:193
  60.6 2.1 %collective-permute-start.11 = (bf16[152,1024]{1,0:T(8,128)(2,1)S(1)}, bf16[152,1024]{1,0:T(8,128)(2,1)S(1)}, u32[]{:S(2)}, u32[]{:S(2)}) collective-permute-start(bf16[152,1024]{1,0:T(8,128)(2,1)S(1)} %get-tuple-element.39), channel_id=1, source_target_pairs={{0,1},{1,0},{2,3},{3,2},{4,5},{5,4},{6,7},{7,6},{8,9},{9,8},{10,11... | collective-permute-start | bytes 933896 | tf_op jit(solution)/shard_map/ppermute | solution.py:183
  62.7 8.3 %collective-permute-start.12 = (bf16[152,256]{1,0:T(8,128)(2,1)S(1)}, bf16[152,256]{1,0:T(8,128)(2,1)S(1)}, u32[]{:S(2)}, u32[]{:S(2)}) collective-permute-start(bf16[152,256]{1,0:T(8,128)(2,1)S(1)} %get-tuple-element.49), channel_id=1, source_target_pairs={{0,24},{8,0},{16,8},{24,16},{1,25},{9,1},{17,9},{25,17},{2,26},{10... | collective-permute-start | bytes 233480 | tf_op jit(solution)/shard_map/ppermute | solution.py:186
  68.3 8.0 %collective-permute-start.13 = (bf16[152,256]{1,0:T(8,128)(2,1)S(1)}, bf16[152,256]{1,0:T(8,128)(2,1)S(1)}, u32[]{:S(2)}, u32[]{:S(2)}) collective-permute-start(bf16[152,256]{1,0:T(8,128)(2,1)S(1)} %get-tuple-element.50), channel_id=1, source_target_pairs={{0,16},{8,24},{16,0},{24,8},{1,17},{9,25},{17,1},{25,9},{2,18},{10... | collective-permute-start | bytes 233480 | tf_op jit(solution)/shard_map/ppermute | solution.py:186
  68.3 8.0 %collective-permute-start.14 = (bf16[152,256]{1,0:T(8,128)(2,1)S(1)}, bf16[152,256]{1,0:T(8,128)(2,1)S(1)}, u32[]{:S(2)}, u32[]{:S(2)}) collective-permute-start(bf16[152,256]{1,0:T(8,128)(2,1)S(1)} %get-tuple-element.51), channel_id=1, source_target_pairs={{0,8},{8,16},{16,24},{24,0},{1,9},{9,17},{17,25},{25,1},{2,10},{10... | collective-permute-start | bytes 233480 | tf_op jit(solution)/shard_map/ppermute | solution.py:186
  76.4 7.1 %collective-permute-start.16 = (bf16[152,256]{1,0:T(8,128)(2,1)S(1)}, bf16[152,256]{1,0:T(8,128)(2,1)S(1)}, u32[]{:S(2)}, u32[]{:S(2)}) collective-permute-start(bf16[152,256]{1,0:T(8,128)(2,1)S(1)} %shard_map.99.refs_1_), channel_id=1, source_target_pairs={{0,8},{8,16},{16,24},{24,0},{1,9},{9,17},{17,25},{25,1},{2,10},{10... | collective-permute-start | bytes 233480 | tf_op jit(solution)/shard_map/ppermute | solution.py:186
  76.6 9.2 %collective-permute-start.18 = (bf16[152,256]{1,0:T(8,128)(2,1)S(1)}, bf16[152,256]{1,0:T(8,128)(2,1)S(1)}, u32[]{:S(2)}, u32[]{:S(2)}) collective-permute-start(bf16[152,256]{1,0:T(8,128)(2,1)S(1)} %shard_map.99.refs_1_), channel_id=1, source_target_pairs={{0,16},{8,24},{16,0},{24,8},{1,17},{9,25},{17,1},{25,9},{2,18},{10... | collective-permute-start | bytes 233480 | tf_op jit(solution)/shard_map/ppermute | solution.py:186
  78.5 7.3 %collective-permute-start.20 = (bf16[152,256]{1,0:T(8,128)(2,1)S(1)}, bf16[152,256]{1,0:T(8,128)(2,1)S(1)}, u32[]{:S(2)}, u32[]{:S(2)}) collective-permute-start(bf16[152,256]{1,0:T(8,128)(2,1)S(1)} %shard_map.99.refs_1_), channel_id=1, source_target_pairs={{0,24},{8,0},{16,8},{24,16},{1,25},{9,1},{17,9},{25,17},{2,26},{10... | collective-permute-start | bytes 233480 | tf_op jit(solution)/shard_map/ppermute | solution.py:186
  81.2 5.1 %collective-permute-start.15 = (bf16[152,256]{1,0:T(8,128)(2,1)S(1)}, bf16[152,256]{1,0:T(8,128)(2,1)S(1)}, u32[]{:S(2)}, u32[]{:S(2)}) collective-permute-start(bf16[152,256]{1,0:T(8,128)(2,1)S(1)} %shard_map.99.refs_1_), channel_id=1, source_target_pairs={{0,1},{1,0},{2,3},{3,2},{4,5},{5,4},{6,7},{7,6},{8,9},{9,8},{10,11... | collective-permute-start | bytes 233480 | tf_op jit(solution)/shard_map/ppermute | solution.py:183
  83.5 3.7 %collective-permute-start.17 = (bf16[152,256]{1,0:T(8,128)(2,1)S(1)}, bf16[152,256]{1,0:T(8,128)(2,1)S(1)}, u32[]{:S(2)}, u32[]{:S(2)}) collective-permute-start(bf16[152,256]{1,0:T(8,128)(2,1)S(1)} %collective-permute-done.16.refs_3_), channel_id=1, source_target_pairs={{0,1},{1,0},{2,3},{3,2},{4,5},{5,4},{6,7},{7,6},{8,9},{9,8},{10,11... | collective-permute-start | bytes 233480 | tf_op jit(solution)/shard_map/ppermute | solution.py:183
  83.5 10.5 %collective-permute-start.25 = (bf16[152,1024]{1,0:T(8,128)(2,1)S(1)}, bf16[152,1024]{1,0:T(8,128)(2,1)S(1)}, u32[]{:S(2)}, u32[]{:S(2)}) collective-permute-start(bf16[152,1024]{1,0:T(8,128)(2,1)S(1)} %shard_map.96), channel_id=1, source_target_pairs={{0,2},{1,3},{2,0},{3,1},{4,6},{5,7},{6,4},{7,5},{8,10},{9,11},{10,... | collective-permute-start | bytes 933896 | tf_op jit(solution)/shard_map/ppermute | solution.py:193
  85.8 4.1 %collective-permute-start.19 = (bf16[152,256]{1,0:T(8,128)(2,1)S(1)}, bf16[152,256]{1,0:T(8,128)(2,1)S(1)}, u32[]{:S(2)}, u32[]{:S(2)}) collective-permute-start(bf16[152,256]{1,0:T(8,128)(2,1)S(1)} %collective-permute-done.18.refs_5_), channel_id=1, source_target_pairs={{0,1},{1,0},{2,3},{3,2},{4,5},{5,4},{6,7},{7,6},{8,9},{9,8},{10,11... | collective-permute-start | bytes 233480 | tf_op jit(solution)/shard_map/ppermute | solution.py:183
  85.8 4.1 %collective-permute-start.21 = (bf16[152,256]{1,0:T(8,128)(2,1)S(1)}, bf16[152,256]{1,0:T(8,128)(2,1)S(1)}, u32[]{:S(2)}, u32[]{:S(2)}) collective-permute-start(bf16[152,256]{1,0:T(8,128)(2,1)S(1)} %collective-permute-done.20.refs_7_), channel_id=1, source_target_pairs={{0,1},{1,0},{2,3},{3,2},{4,5},{5,4},{6,7},{7,6},{8,9},{9,8},{10,11... | collective-permute-start | bytes 233480 | tf_op jit(solution)/shard_map/ppermute | solution.py:183
  86.4 16.9 %collective-permute-start.26 = (bf16[152,1024]{1,0:T(8,128)(2,1)S(1)}, bf16[152,1024]{1,0:T(8,128)(2,1)S(1)}, u32[]{:S(2)}, u32[]{:S(2)}) collective-permute-start(bf16[152,1024]{1,0:T(8,128)(2,1)S(1)} %shard_map.97), channel_id=1, source_target_pairs={{0,4},{1,5},{2,6},{3,7},{4,0},{5,1},{6,2},{7,3},{8,12},{9,13},{10,... | collective-permute-start | bytes 933896 | tf_op jit(solution)/shard_map/ppermute | solution.py:193
  87.2 16.1 %collective-permute-start.27 = (bf16[152,1024]{1,0:T(8,128)(2,1)S(1)}, bf16[152,1024]{1,0:T(8,128)(2,1)S(1)}, u32[]{:S(2)}, u32[]{:S(2)}) collective-permute-start(bf16[152,1024]{1,0:T(8,128)(2,1)S(1)} %shard_map.98), channel_id=1, source_target_pairs={{0,6},{1,7},{2,4},{3,5},{4,2},{5,3},{6,0},{7,1},{8,14},{9,15},{10,... | collective-permute-start | bytes 933896 | tf_op jit(solution)/shard_map/ppermute | solution.py:193
  90.9 16.2 %collective-permute-start.22 = (bf16[152,1024]{1,0:T(8,128)(2,1)S(1)}, bf16[152,1024]{1,0:T(8,128)(2,1)S(1)}, u32[]{:S(2)}, u32[]{:S(2)}) collective-permute-start(bf16[152,1024]{1,0:T(8,128)(2,1)S(1)} %shard_map.101), channel_id=1, source_target_pairs={{0,2},{1,3},{2,0},{3,1},{4,6},{5,7},{6,4},{7,5},{8,10},{9,11},{10,... | collective-permute-start | bytes 933896 | tf_op jit(solution)/shard_map/ppermute | solution.py:193
  92.3 23.4 %collective-permute-start.23 = (bf16[152,1024]{1,0:T(8,128)(2,1)S(1)}, bf16[152,1024]{1,0:T(8,128)(2,1)S(1)}, u32[]{:S(2)}, u32[]{:S(2)}) collective-permute-start(bf16[152,1024]{1,0:T(8,128)(2,1)S(1)} %shard_map.102), channel_id=1, source_target_pairs={{0,4},{1,5},{2,6},{3,7},{4,0},{5,1},{6,2},{7,3},{8,12},{9,13},{10,... | collective-permute-start | bytes 933896 | tf_op jit(solution)/shard_map/ppermute | solution.py:193
  94.1 21.6 %collective-permute-start.24 = (bf16[152,1024]{1,0:T(8,128)(2,1)S(1)}, bf16[152,1024]{1,0:T(8,128)(2,1)S(1)}, u32[]{:S(2)}, u32[]{:S(2)}) collective-permute-start(bf16[152,1024]{1,0:T(8,128)(2,1)S(1)} %shard_map.103), channel_id=1, source_target_pairs={{0,6},{1,7},{2,4},{3,5},{4,2},{5,3},{6,0},{7,1},{8,14},{9,15},{10,... | collective-permute-start | bytes 933896 | tf_op jit(solution)/shard_map/ppermute | solution.py:193
  97.1 18.6 %copy-start.1 = (bf16[147,1024]{1,0:T(8,128)(2,1)S(1)}, bf16[147,1024]{1,0:T(8,128)(2,1)}, u32[]{:S(2)}) copy-start(bf16[147,1024]{1,0:T(8,128)(2,1)} %d_ref.1) | copy-start | bytes 903172

commit v3 on v2

v3 whole, which is shorter than its diff:
```python
import functools
import math

import jax
import jax.numpy as jnp
from jax import lax
from jax.experimental import pallas as pl
from jax.experimental.pallas import tpu as pltpu
from jax.sharding import PartitionSpec as P

F32, BF16 = jnp.float32, jnp.bfloat16
VMEM = 16 * 2**20
COEFS = (0.99999921, -19.73898036, 64.92865742, -85.27162153, 58.79049212, -21.07110563)
ROUNDER = 12582912.0


def up(value, step):
    return -(-value // step) * step


def params():
    return pltpu.CompilerParams(vmem_limit_bytes=VMEM)


def cosine(angle):
    turns = angle * (0.5 / math.pi)
    rest = turns - ((turns + ROUNDER) - ROUNDER)
    square = rest * rest
    total = square * COEFS[-1] + COEFS[-2]
    for coef in COEFS[-3::-1]:
        total = total * square + coef
    return total


def fetch(refs, bufs, sems):
    copies = [pltpu.make_async_copy(ref, buf, sems.at[j]) for j, (ref, buf) in enumerate(zip(refs, bufs, strict=True))]
    for copy in copies:
        copy.start()
    for copy in copies:
        copy.wait()


def pack_weights_kernel(raw, depth, classes, w_hbm, ph_hbm, d_hbm, *refs):
    o_refs, (w_ref, ph_ref, d_ref, sems) = refs[:-4], refs[-4:]
    fetch((w_hbm, ph_hbm, d_hbm), (w_ref, ph_ref, d_ref), sems)
    rows, f = o_refs[0].shape
    for j, o_ref in enumerate(o_refs):
        here = slice(j * f, (j + 1) * f)
        o_ref[:raw, :] = w_ref[:, here]
        head = lax.broadcasted_iota(jnp.int32, (depth - raw, f), 0) == 0
        o_ref[raw:depth, :] = jnp.where(head, ph_ref[:, here].astype(F32), 0.0).astype(BF16)
        o_ref[depth : depth + classes, :] = d_ref[:, here]
        o_ref[depth + classes :, :] = jnp.zeros((rows - depth - classes, f), BF16)


def pack_samples_kernel(raw, depth, classes, x_hbm, p_hbm, l_hbm, o_ref, x_ref, p_ref, l_ref, sems):
    fetch((x_hbm, p_hbm, l_hbm), (x_ref, p_ref, l_ref), sems)
    rows, n = o_ref.shape
    o_ref[:raw, :] = x_ref[...]
    head = lax.broadcasted_iota(jnp.int32, (depth - raw, n), 0) == 0
    o_ref[raw:depth, :] = jnp.where(head, 1.0, 0.0).astype(BF16)
    ids = lax.broadcasted_iota(jnp.int32, (classes, n), 0)
    onehot = (ids == l_ref[...]).astype(F32)
    o_ref[depth : depth + classes, :] = (p_ref[...].astype(F32) - onehot).astype(BF16)
    o_ref[depth + classes :, :] = jnp.zeros((rows - depth - classes, n), BF16)


def pack(kernel, shapes, *args):
    return pl.pallas_call(
        kernel,
        in_specs=[pl.BlockSpec(memory_space=pl.ANY)] * len(args),
        out_shape=shapes,
        scratch_shapes=[pltpu.VMEM(a.shape, a.dtype) for a in args] + [pltpu.SemaphoreType.DMA((len(args),))],
        compiler_params=params(),
    )(*args)


def one_block(xt, w_ref, depth):
    feats = cosine(jnp.dot(xt, w_ref[:depth, :], preferred_element_type=F32)).astype(BF16)
    dims = (((1,), (1,)), ((), ()))
    return feats, lax.dot_general(feats, w_ref[depth:, :], dims, preferred_element_type=F32)


def first_kernel(depth, count, parts, *refs):
    x_refs, w_refs = refs[:count], refs[count : count + parts]
    xt_ref, t_ref, *f_refs = refs[count + parts :]
    n = x_refs[0].shape[1]
    for j in range(count):
        here = slice(j * n, (j + 1) * n)
        xt = x_refs[j][:depth, :].T
        xt_ref[here, :] = xt
        total = None
        for w_ref, f_ref in zip(w_refs, f_refs, strict=True):
            f_ref[here, :], tangent = one_block(xt, w_ref, depth)
            total = tangent if total is None else total + tangent
        t_ref[here, :] = total


def next_kernel(depth, count, totals, parts, block, last, *refs):
    xt_refs, t_refs = refs[:count], refs[count : count + totals]
    refs = refs[count + totals :]
    w_refs, f_refs, out_refs = refs[:parts], refs[parts : 2 * parts], refs[2 * parts :]
    t_blocks = [(ref, at) for ref in t_refs for at in range(0, ref.shape[0], block)]
    spot = 0
    for xt_ref in xt_refs:
        for at in range(0, xt_ref.shape[0], block):
            t_ref, t_at = t_blocks[spot // block]
            xt, total = xt_ref[at : at + block, :], t_ref[t_at : t_at + block, :]
            for w_ref, f_ref in zip(w_refs, f_refs, strict=True):
                f_ref[spot : spot + block, :], tangent = one_block(xt, w_ref, depth)
                total = total + tangent
            if not last:
                out_refs[0][spot : spot + block, :] = total
            else:
                pair, mine = spot // (2 * block), spot // block % 2
                here = slice(pair * block, (pair + 1) * block)
                if mine:
                    out_refs[1][:, here] = total.T
                else:
                    out_refs[0][:, here] = total.T.astype(BF16)
            spot += block


def make_next(xts, totals, pieces, depth, wide, block, last):
    n, f = sum(a.shape[0] for a in xts), pieces[0].shape[1]
    shapes = [jax.ShapeDtypeStruct((n, f), BF16)] * len(pieces)
    if last:
        shapes.append(jax.ShapeDtypeStruct((wide, n // 2), BF16))
        shapes.append(jax.ShapeDtypeStruct((wide, n // 2), F32))
    else:
        shapes.append(jax.ShapeDtypeStruct((n, wide), F32))
    kernel = functools.partial(next_kernel, depth, len(xts), len(totals), len(pieces), block, last)
    out = whole(kernel, shapes, *xts, *totals, *pieces, flops=2 * n * f * len(pieces) * (depth + wide))
    return out[: len(pieces)], out[len(pieces) :]


def spread_kernel(own_ref, got_ref, keep_ref, *send_refs):
    n = keep_ref.shape[1]
    total = own_ref[...] + got_ref[...].astype(F32)
    keep_ref[...] = total[:, :n]
    for j, ref in enumerate(send_refs):
        ref[...] = total[:, (j + 1) * n : (j + 2) * n].astype(BF16)


def curve_kernel(classes, keep_ref, *refs):
    got_refs, p_ref, c_ref = refs[:-2], refs[-2], refs[-1]
    total = keep_ref[...]
    for ref in got_refs:
        total = total + ref[...].astype(F32)
    total = total[:classes, :]
    prob = p_ref[...].astype(F32)
    mixed = jnp.sum(prob * total, axis=0, keepdims=True)
    c_ref[:classes, :] = (prob * (total - mixed)).astype(BF16)
    c_ref[classes:, :] = jnp.zeros((c_ref.shape[0] - classes, c_ref.shape[1]), BF16)


def share_kernel(count, skip, block, halves, *refs):
    left_refs, f_refs, o_ref = refs[:count], refs[count:-1], refs[-1]
    each = len(f_refs) // halves
    f = f_refs[0].shape[1]
    for h in range(halves):
        f_blocks = [(ref, at) for ref in f_refs[h * each : (h + 1) * each] for at in range(0, ref.shape[0], block)]
        total = None
        for left_ref, (f_ref, at) in zip(left_refs, f_blocks, strict=True):
            part = jnp.dot(left_ref[skip:, :], f_ref[at : at + block, :], preferred_element_type=F32)
            total = part if total is None else total + part
        o_ref[:, h * f : (h + 1) * f] = total.astype(o_ref.dtype)


def make_share(lefts, skip, feats, dtype):
    block = lefts[0].shape[1]
    wide, n, f = lefts[0].shape[0] - skip, block * len(lefts), sum(h[0].shape[1] for h in feats)
    return whole(
        functools.partial(share_kernel, len(lefts), skip, block, len(feats)),
        jax.ShapeDtypeStruct((wide, f), dtype),
        *lefts, *[a for h in feats for a in h], flops=2 * n * f * wide,
    )


def whole(kernel, shapes, *args, flops=0):
    size = sum(math.prod(a.shape) * a.dtype.itemsize for a in args)
    cost = pl.CostEstimate(flops=flops, bytes_accessed=size, transcendentals=0)
    return pl.pallas_call(kernel, out_shape=shapes, compiler_params=params(), cost_estimate=cost)(*args)


def on_device(line, ys, xs, inputs, probs, labels, proj_weight, phase, direction, damping):
    raw, own = inputs.shape
    classes = probs.shape[0]
    width = proj_weight.shape[1]
    depth = up(raw + 1, 16)
    wide = up(classes, 8)

    def swap_core(a):
        return lax.ppermute(a, "feat", [(i, i ^ 1) for i in range(2 * xs * ys)])

    def along(a, k):
        return lax.ppermute(a, "samp", [(i, (i + k) % line) for i in range(line)])

    def across(a, dy, dx):
        def to(i):
            y, x, c = i // (2 * xs), i // 2 % xs, i % 2
            return ((y + dy) % ys * xs + (x + dx) % xs) * 2 + c

        return lax.ppermute(a, "feat", [(i, to(i)) for i in range(2 * xs * ys)])

    offsets = [(dy, dx) for dy in range(ys) for dx in range(xs)]
    rows, half = depth + wide, width // 2
    w_own = pack(
        functools.partial(pack_weights_kernel, raw, depth, classes),
        [jax.ShapeDtypeStruct((rows, half), BF16)] * 2,
        proj_weight, phase, direction,
    )
    ws = {(0, 0): w_own}
    for h in (0, 1):
        for dx in range(1, xs):
            ws[0, dx, h] = across(w_own[h], 0, dx)
        for dy in range(1, ys):
            ws[dy, 0, 1 - h] = across(w_own[1 - h], dy, 0)
    for dy in range(1, ys):
        for dx in range(1, xs):
            ws[dy, dx, 0] = across(ws[0, dx, 0], dy, 0)
            ws[dy, dx, 1] = across(ws[dy, 0, 1], 0, dx)
    x_own = pack(
        functools.partial(pack_samples_kernel, raw, depth, classes),
        jax.ShapeDtypeStruct((rows, own), BF16),
        inputs, probs, labels[None, :],
    )
    x_line = [x_own] + [along(x_own, k) for k in range(1, line)]

    feats = {at: [[], []] for at in offsets}
    xts, totals, blocks = [], [], []
    for k in range(line):
        pair = 2 * own
        blocks += [swap_core(x_line[k]), x_line[k]]
        xt, total, *part = whole(
            functools.partial(first_kernel, depth, 2, 2),
            [jax.ShapeDtypeStruct((pair, depth), BF16), jax.ShapeDtypeStruct((pair, wide), F32)]
            + [jax.ShapeDtypeStruct((pair, half), BF16)] * 2,
            *blocks[-2:], *w_own, flops=2 * pair * width * (depth + wide),
        )
        xts.append(xt)
        totals.append(total)
        for h in (0, 1):
            feats[0, 0][h].append(part[h])
        if k + 1 < line:
            x_line[k + 1], totals[k] = lax.optimization_barrier((x_line[k + 1], totals[k]))
    soon = [(0, dx, 0) for dx in range(1, xs)] + [(dy, 0, 1) for dy in range(1, ys)]
    near = [(0, dx, 1) for dx in range(1, xs)] + [(dy, 0, 0) for dy in range(1, ys)]
    far = [(dy, dx, h) for dy in range(1, ys) for dx in range(1, xs) for h in (0, 1)]
    groups = [group for group in (soon, near, far) if group]
    for group in groups:
        last = group is groups[-1]
        got, rest = make_next(xts, totals, [ws[at] for at in group], depth, wide, own, last)
        for (dy, dx, h), piece in zip(group, got, strict=True):
            feats[dy, dx][h] = [piece]
        if not last:
            totals = rest
    t_other, t_own = rest
    t_got = swap_core(t_other)
    keep, *send = whole(
        spread_kernel,
        [jax.ShapeDtypeStruct((wide, own), F32)] + [jax.ShapeDtypeStruct((wide, own), BF16)] * (line - 1),
        t_own, t_got,
    )
    got = [along(a, -k) for k, a in enumerate(send, 1)]

    def collect(parts):
        out = parts[0, 0]
        for dy, dx in offsets[1:]:
            out = out + parts[dy, dx].astype(F32)
        return out[:classes]

    def send_home(lefts, skip):
        parts = {at: make_share(lefts, skip, feats[at], F32 if at == (0, 0) else BF16) for at in offsets[::-1]}
        return parts, {(dy, dx): across(parts[dy, dx], -dy, -dx) for dy, dx in offsets[1:]}

    parts, arrived = send_home(blocks, depth)
    keep, parts = lax.optimization_barrier((keep, parts))
    curv = whole(
        functools.partial(curve_kernel, classes), jax.ShapeDtypeStruct((wide, own), BF16), keep, *got, probs
    )
    c_line = [curv] + [along(curv, k) for k in range(1, line)]
    curvs = [b for a in c_line for b in (swap_core(a), a)]
    curvs, arrived = lax.optimization_barrier((curvs, arrived))
    gradient = collect({(0, 0): parts[0, 0], **arrived})
    parts, arrived = send_home(curvs, 0)
    hess_vec = collect({(0, 0): parts[0, 0], **arrived}) + damping[0] * direction.astype(F32)
    return (hess_vec, gradient)


def solution(mesh):
    line, feat = mesh.shape["samp"], mesh.shape["feat"]
    ys = 2 if feat % 4 == 0 else 1
    xs = feat // (2 * ys)
    placed = (
        P(None, ("samp", "feat")),
        P(None, ("samp", "feat")),
        P(("samp", "feat")),
        P(None, ("feat", "samp")),
        P(None, ("feat", "samp")),
        P(None, ("feat", "samp")),
        P(),
    )
    return jax.shard_map(
        functools.partial(on_device, line, ys, xs),
        mesh=mesh,
        in_specs=placed,
        out_specs=(P(None, ("feat", "samp")), P(None, ("feat", "samp"))),
        check_vma=False,
    )
```

time: 117 us -> 118 us (level)
  starting transfers between devices: 33.7 us -> 28.2 us
  waiting for transfers between devices: 45.8 us -> 49.4 us
  local copies, waits for them, and re-layouts: 2.92 us -> 5.33 us
    ppermute x9, starting transfers between devices: 16.6 us -> 10.8 us  [along(): return lax.ppermute(a, 'samp', [(i, (i + k) % line) for i in range(line)])]
    ppermute x9, waiting for transfers between devices: 26.9 us -> 29.7 us  [along(): return lax.ppermute(a, 'samp', [(i, (i + k) % line) for i in range(line)])]
    unnamed x14 -> x16, local copies, waits for them, and re-layouts: 2.84 us -> 5.33 us
    pallas_call x16 -> x17, Pallas kernels: 30.7 us -> 30 us  [whole(): pl.pallas_call(kernel, out_shape=shapes, compiler_params=params(), cost_e...]
    ppermute x10 -> x12, waiting for transfers between devices: 18.9 us -> 19.5 us  [across(): return lax.ppermute(a, 'feat', [(i, to(i)) for i in range(2 * xs * ys)])]
    ppermute x10 -> x12, starting transfers between devices: 16 us -> 16.3 us  [across(): return lax.ppermute(a, 'feat', [(i, to(i)) for i in range(2 * xs * ys)])]
  transfers between devices with their start and end apart: 28 -> 30, of which waited for: 10 -> 15; matrix products, arithmetic and copies ran while one was open for 1% -> 1% of each run, Pallas kernels for 21% -> 19%
where the time goes in v3:
time: 118 us; the launch traced here: 117 us
  waiting for transfers between devices  49.4 us (42%)
  Pallas kernels  30.8 us (26%)
  starting transfers between devices  28.2 us (24%)
  local copies, waits for them, and re-layouts  5.33 us (5%)
  other arithmetic  2.06 us (2%)
  between operations  1.5 us (1%)
    pallas_call x17, Pallas kernels, whole(): pl.pallas_call(kernel, out_shape=shapes, compiler_params=params(), cost_e...  30 us
    ppermute x9, waiting for transfers between devices, along(): return lax.ppermute(a, 'samp', [(i, (i + k) % line) for i in range(line)])  29.7 us
    ppermute x12, waiting for transfers between devices, across(): return lax.ppermute(a, 'feat', [(i, to(i)) for i in range(2 * xs * ys)])  19.5 us
    ppermute x12, starting transfers between devices, across(): return lax.ppermute(a, 'feat', [(i, to(i)) for i in range(2 * xs * ys)])  16.3 us
    ppermute x9, starting transfers between devices, along(): return lax.ppermute(a, 'samp', [(i, (i + k) % line) for i in range(line)])  10.8 us
    unnamed x16, local copies, waits for them, and re-layouts  5.33 us
  transfers between devices with their start and end apart: 30, of which 15 were waited for; matrix products, arithmetic and copies ran while one was open for 1% of the time, Pallas kernels for 19%

profile of v3, /device:TPU:0, one launch (start us, length us, event | category | flops | bytes accessed | tf_op | source)
XLA Modules:
  0.0 117.4 jit_solution(10524627692390915375)
XLA Ops:
  0.6 0.9 copy-done.3
  1.5 0.9 copy-done.5
  4.1 2.6 %collective-permute-start.1 = (bf16[600,256]{1,0:T(8,128)(2,1)S(1)}, bf16[600,256]{1,0:T(8,128)(2,1)S(1)}, u32[]{:S(2)}, u32[]{:S(2)}) collective-permute-start(bf16[600,256]{1,0:T(8,128)(2,1)S(1)} %shard_map.86.refs_1_), channel_id=1, source_target_pairs={{0,8},{8,16},{16,24},{24,0},{1,9},{9,17},{17,25},{25,1},{2,10},{10... | collective-permute-start | bytes 921608 | tf_op jit(solution)/shard_map/ppermute | solution.py:197
  6.7 1.0 copy-done
  7.7 1.2 copy-done.2
  10.0 1.6 %shard_map.88 = (bf16[512,448]{1,0:T(8,128)(2,1)S(1)}, f32[512,152]{1,0:T(8,128)S(1)}, bf16[512,512]{1,0:T(8,128)(2,1)S(1)}, bf16[512,512]{1,0:T(8,128)(2,1)S(1)}) custom-call(bf16[600,256]{1,0:T(8,128)(2,1)S(1)} %collective-permute-done.refs_0_, bf16[600,256]{1,0:T(8,128)(2,1)S(1)} %shard_map.86.refs_1_, bf16[600,512]{1,0:T(8,128)(2,1)S(1)} %get-tuple-element.53.refs_2_, ...), custom_call_target="tpu_custom_call" | custom-call | flops 629145600 | bytes 1843200 | tf_op jit(solution)/shard_map/pallas_call | solution.py:183
  11.6 5.0 %collective-permute-done.1.refs_1_.refs_3_ = bf16[600,256]{1,0:T(8,128)(2,1)S(1)} collective-permute-done((bf16[600,256]{1,0:T(8,128)(2,1)S(1)}, bf16[600,256]{1,0:T(8,128)(2,1)S(1)}, u32[]{:S(2)}, u32[]{:S(2)}) %collective-permute-start.1) | collective-permute-done | bytes 307232 | tf_op jit(solution)/shard_map/ppermute | solution.py:197
  16.6 0.7 collective-permute-start.3
  17.4 1.5 %collective-permute-start.7 = (bf16[600,512]{1,0:T(8,128)(2,1)S(1)}, bf16[600,512]{1,0:T(8,128)(2,1)S(1)}, u32[]{:S(2)}, u32[]{:S(2)}) collective-permute-start(bf16[600,512]{1,0:T(8,128)(2,1)S(1)} %get-tuple-element.53.refs_2_), channel_id=1, source_target_pairs={{0,2},{1,3},{2,0},{3,1},{4,6},{5,7},{6,4},{7,5},{8,10},{9,11},{10,... | collective-permute-start | bytes 1843208 | tf_op jit(solution)/shard_map/ppermute | solution.py:204
  18.9 1.5 %collective-permute-start.8 = (bf16[600,512]{1,0:T(8,128)(2,1)S(1)}, bf16[600,512]{1,0:T(8,128)(2,1)S(1)}, u32[]{:S(2)}, u32[]{:S(2)}) collective-permute-start(bf16[600,512]{1,0:T(8,128)(2,1)S(1)} %get-tuple-element.54.refs_3_), channel_id=1, source_target_pairs={{0,4},{1,5},{2,6},{3,7},{4,0},{5,1},{6,2},{7,3},{8,12},{9,13},{10,... | collective-permute-start | bytes 1843208 | tf_op jit(solution)/shard_map/ppermute | solution.py:204
  20.4 1.6 %shard_map.89 = (bf16[512,448]{1,0:T(8,128)(2,1)S(1)}, f32[512,152]{1,0:T(8,128)S(1)}, bf16[512,512]{1,0:T(8,128)(2,1)S(1)}, bf16[512,512]{1,0:T(8,128)(2,1)S(1)}) custom-call(bf16[600,256]{1,0:T(8,128)(2,1)S(1)} %collective-permute-done.2.refs_0_.refs_2_, bf16[600,256]{1,0:T(8,128)(2,1)S(1)} %collective-permute-done.1.refs_1_.refs_3_, ...), custom_call_target="tpu_custom_call" | custom-call | flops 629145600 | bytes 1843200 | tf_op jit(solution)/shard_map/pallas_call | solution.py:183
  22.0 10.9 %collective-permute-done.3.refs_1_.refs_5_ = bf16[600,256]{1,0:T(8,128)(2,1)S(1)} collective-permute-done((bf16[600,256]{1,0:T(8,128)(2,1)S(1)}, bf16[600,256]{1,0:T(8,128)(2,1)S(1)}, u32[]{:S(2)}, u32[]{:S(2)}) %collective-permute-start.3) | collective-permute-done | bytes 307232 | tf_op jit(solution)/shard_map/ppermute | solution.py:197
  33.0 2.5 %collective-permute-start.5 = (bf16[600,256]{1,0:T(8,128)(2,1)S(1)}, bf16[600,256]{1,0:T(8,128)(2,1)S(1)}, u32[]{:S(2)}, u32[]{:S(2)}) collective-permute-start(bf16[600,256]{1,0:T(8,128)(2,1)S(1)} %shard_map.86.refs_1_), channel_id=1, source_target_pairs={{0,24},{8,0},{16,8},{24,16},{1,25},{9,1},{17,9},{25,17},{2,26},{10... | collective-permute-start | bytes 921608 | tf_op jit(solution)/shard_map/ppermute | solution.py:197
  35.5 1.5 %collective-permute-start.10 = (bf16[600,512]{1,0:T(8,128)(2,1)S(1)}, bf16[600,512]{1,0:T(8,128)(2,1)S(1)}, u32[]{:S(2)}, u32[]{:S(2)}) collective-permute-start(bf16[600,512]{1,0:T(8,128)(2,1)S(1)} %get-tuple-element.53.refs_2_), channel_id=1, source_target_pairs={{0,4},{1,5},{2,6},{3,7},{4,0},{5,1},{6,2},{7,3},{8,12},{9,13},{10,... | collective-permute-start | bytes 1843208 | tf_op jit(solution)/shard_map/ppermute | solution.py:204
  37.0 1.5 %collective-permute-start.9 = (bf16[600,512]{1,0:T(8,128)(2,1)S(1)}, bf16[600,512]{1,0:T(8,128)(2,1)S(1)}, u32[]{:S(2)}, u32[]{:S(2)}) collective-permute-start(bf16[600,512]{1,0:T(8,128)(2,1)S(1)} %get-tuple-element.54.refs_3_), channel_id=1, source_target_pairs={{0,2},{1,3},{2,0},{3,1},{4,6},{5,7},{6,4},{7,5},{8,10},{9,11},{10,... | collective-permute-start | bytes 1843208 | tf_op jit(solution)/shard_map/ppermute | solution.py:204
  38.5 1.6 %shard_map.90 = (bf16[512,448]{1,0:T(8,128)(2,1)S(1)}, f32[512,152]{1,0:T(8,128)S(1)}, bf16[512,512]{1,0:T(8,128)(2,1)S(1)}, bf16[512,512]{1,0:T(8,128)(2,1)S(1)}) custom-call(bf16[600,256]{1,0:T(8,128)(2,1)S(1)} %collective-permute-done.4.refs_0_.refs_4_, bf16[600,256]{1,0:T(8,128)(2,1)S(1)} %collective-permute-done.3.refs_1_.refs_5_, ...), custom_call_target="tpu_custom_call" | custom-call | flops 629145600 | bytes 1843200 | tf_op jit(solution)/shard_map/pallas_call | solution.py:183
  40.1 2.5 %collective-permute-done.5.refs_1_.refs_7_ = bf16[600,256]{1,0:T(8,128)(2,1)S(1)} collective-permute-done((bf16[600,256]{1,0:T(8,128)(2,1)S(1)}, bf16[600,256]{1,0:T(8,128)(2,1)S(1)}, u32[]{:S(2)}, u32[]{:S(2)}) %collective-permute-start.5) | collective-permute-done | bytes 307232 | tf_op jit(solution)/shard_map/ppermute | solution.py:197
  42.7 1.5 %collective-permute-start.11 = (bf16[600,512]{1,0:T(8,128)(2,1)S(1)}, bf16[600,512]{1,0:T(8,128)(2,1)S(1)}, u32[]{:S(2)}, u32[]{:S(2)}) collective-permute-start(bf16[600,512]{1,0:T(8,128)(2,1)S(1)} %collective-permute-done.7.refs_8_), channel_id=1, source_target_pairs={{0,4},{1,5},{2,6},{3,7},{4,0},{5,1},{6,2},{7,3},{8,12},{9,13},{10,... | collective-permute-start | bytes 1843208 | tf_op jit(solution)/shard_map/ppermute | solution.py:204
  44.2 1.5 %collective-permute-start.12 = (bf16[600,512]{1,0:T(8,128)(2,1)S(1)}, bf16[600,512]{1,0:T(8,128)(2,1)S(1)}, u32[]{:S(2)}, u32[]{:S(2)}) collective-permute-start(bf16[600,512]{1,0:T(8,128)(2,1)S(1)} %collective-permute-done.8.refs_9_), channel_id=1, source_target_pairs={{0,2},{1,3},{2,0},{3,1},{4,6},{5,7},{6,4},{7,5},{8,10},{9,11},{10,... | collective-permute-start | bytes 1843208 | tf_op jit(solution)/shard_map/ppermute | solution.py:204
  45.7 1.6 %shard_map.91 = (bf16[512,448]{1,0:T(8,128)(2,1)S(1)}, f32[512,152]{1,0:T(8,128)S(1)}, bf16[512,512]{1,0:T(8,128)(2,1)S(1)}, bf16[512,512]{1,0:T(8,128)(2,1)S(1)}) custom-call(bf16[600,256]{1,0:T(8,128)(2,1)S(1)} %collective-permute-done.6.refs_0_.refs_6_, bf16[600,256]{1,0:T(8,128)(2,1)S(1)} %collective-permute-done.5.refs_1_.refs_7_, ...), custom_call_target="tpu_custom_call" | custom-call | flops 629145600 | bytes 1843200 | tf_op jit(solution)/shard_map/pallas_call | solution.py:183
  47.3 5.4 %shard_map.92 = (bf16[2048,512]{1,0:T(8,128)(2,1)S(1)}, bf16[2048,512]{1,0:T(8,128)(2,1)S(1)}, f32[2048,152]{1,0:T(8,128)S(1)}) custom-call(bf16[512,448]{1,0:T(8,128)(2,1)S(1)} %get-tuple-element.55.refs_0_, bf16[512,448]{1,0:T(8,128)(2,1)S(1)} %get-tuple-element.58.refs_1_, bf16[512,448]{1,0:T(8,128)(2,1)S(1)} %get-tuple-element.61.refs_2_, ...), custom_call_target="tpu_custom_call" | custom-call | flops 2516582400 | bytes 4308992 | tf_op jit(solution)/shard_map/pallas_call | solution.py:183
  52.8 1.0 collective-permute-done.9.refs_5_
  53.8 5.7 %shard_map.93 = (bf16[2048,512]{1,0:T(8,128)(2,1)S(1)}, bf16[2048,512]{1,0:T(8,128)(2,1)S(1)}, f32[2048,152]{1,0:T(8,128)S(1)}) custom-call(bf16[512,448]{1,0:T(8,128)(2,1)S(1)} %get-tuple-element.55.refs_0_, bf16[512,448]{1,0:T(8,128)(2,1)S(1)} %get-tuple-element.58.refs_1_, bf16[512,448]{1,0:T(8,128)(2,1)S(1)} %get-tuple-element.61.refs_2_, ...), custom_call_target="tpu_custom_call" | custom-call | flops 2516582400 | bytes 4308992 | tf_op jit(solution)/shard_map/pallas_call | solution.py:183
  59.4 5.2 %collective-permute-done.11.refs_5_ = bf16[600,512]{1,0:T(8,128)(2,1)S(1)} collective-permute-done((bf16[600,512]{1,0:T(8,128)(2,1)S(1)}, bf16[600,512]{1,0:T(8,128)(2,1)S(1)}, u32[]{:S(2)}, u32[]{:S(2)}) %collective-permute-start.11) | collective-permute-done | bytes 614432 | tf_op jit(solution)/shard_map/ppermute | solution.py:204
  64.6 1.2 %collective-permute-done.12.refs_6_ = bf16[600,512]{1,0:T(8,128)(2,1)S(1)} collective-permute-done((bf16[600,512]{1,0:T(8,128)(2,1)S(1)}, bf16[600,512]{1,0:T(8,128)(2,1)S(1)}, u32[]{:S(2)}, u32[]{:S(2)}) %collective-permute-start.12) | collective-permute-done | bytes 614432 | tf_op jit(solution)/shard_map/ppermute | solution.py:204
  65.8 5.5 %shard_map.94 = (bf16[2048,512]{1,0:T(8,128)(2,1)S(1)}, bf16[2048,512]{1,0:T(8,128)(2,1)S(1)}, bf16[152,1024]{1,0:T(8,128)(2,1)S(1)}, f32[152,1024]{1,0:T(8,128)S(1)}) custom-call(bf16[512,448]{1,0:T(8,128)(2,1)S(1)} %get-tuple-element.55.refs_0_, bf16[512,448]{1,0:T(8,128)(2,1)S(1)} %get-tuple-element.58.refs_1_, ...), custom_call_target="tpu_custom_call" | custom-call | flops 2516582400 | bytes 4308992 | tf_op jit(solution)/shard_map/pallas_call | solution.py:183
  71.5 0.8 shard_map.99
  72.3 1.5 %collective-permute-start.26 = (bf16[152,1024]{1,0:T(8,128)(2,1)S(1)}, bf16[152,1024]{1,0:T(8,128)(2,1)S(1)}, u32[]{:S(2)}, u32[]{:S(2)}) collective-permute-start(bf16[152,1024]{1,0:T(8,128)(2,1)S(1)} %shard_map.99), channel_id=1, source_target_pairs={{0,6},{1,7},{2,4},{3,5},{4,2},{5,3},{6,0},{7,1},{8,14},{9,15},{10,... | collective-permute-start | bytes 933896 | tf_op jit(solution)/shard_map/ppermute | solution.py:204
  73.8 0.8 shard_map.98
  74.7 1.6 %collective-permute-start.25 = (bf16[152,1024]{1,0:T(8,128)(2,1)S(1)}, bf16[152,1024]{1,0:T(8,128)(2,1)S(1)}, u32[]{:S(2)}, u32[]{:S(2)}) collective-permute-start(bf16[152,1024]{1,0:T(8,128)(2,1)S(1)} %shard_map.98), channel_id=1, source_target_pairs={{0,4},{1,5},{2,6},{3,7},{4,0},{5,1},{6,2},{7,3},{8,12},{9,13},{10,... | collective-permute-start | bytes 933896 | tf_op jit(solution)/shard_map/ppermute | solution.py:204
  76.6 0.8 shard_map.97
  78.8 1.9 %collective-permute-done.14.refs_0_ = bf16[152,256]{1,0:T(8,128)(2,1)S(1)} collective-permute-done((bf16[152,256]{1,0:T(8,128)(2,1)S(1)}, bf16[152,256]{1,0:T(8,128)(2,1)S(1)}, u32[]{:S(2)}, u32[]{:S(2)}) %collective-permute-start.14) | collective-permute-done | bytes 77856 | tf_op jit(solution)/shard_map/ppermute | solution.py:197
  80.8 0.8 shard_map.96
  81.6 2.2 %collective-permute-done.15.refs_1_ = bf16[152,256]{1,0:T(8,128)(2,1)S(1)} collective-permute-done((bf16[152,256]{1,0:T(8,128)(2,1)S(1)}, bf16[152,256]{1,0:T(8,128)(2,1)S(1)}, u32[]{:S(2)}, u32[]{:S(2)}) %collective-permute-start.15) | collective-permute-done | bytes 77856 | tf_op jit(solution)/shard_map/ppermute | solution.py:197
  83.8 3.1 %collective-permute-done.16.refs_2_ = bf16[152,256]{1,0:T(8,128)(2,1)S(1)} collective-permute-done((bf16[152,256]{1,0:T(8,128)(2,1)S(1)}, bf16[152,256]{1,0:T(8,128)(2,1)S(1)}, u32[]{:S(2)}, u32[]{:S(2)}) %collective-permute-start.16) | collective-permute-done | bytes 77856 | tf_op jit(solution)/shard_map/ppermute | solution.py:197
  87.1 1.2 %collective-permute-start.20 = (bf16[152,256]{1,0:T(8,128)(2,1)S(1)}, bf16[152,256]{1,0:T(8,128)(2,1)S(1)}, u32[]{:S(2)}, u32[]{:S(2)}) collective-permute-start(bf16[152,256]{1,0:T(8,128)(2,1)S(1)} %shard_map.100.refs_1_), channel_id=1, source_target_pairs={{0,16},{8,24},{16,0},{24,8},{1,17},{9,25},{17,1},{25,9},{2,18},{10... | collective-permute-start | bytes 233480 | tf_op jit(solution)/shard_map/ppermute | solution.py:197
  88.3 2.6 %collective-permute-start.22 = (bf16[152,256]{1,0:T(8,128)(2,1)S(1)}, bf16[152,256]{1,0:T(8,128)(2,1)S(1)}, u32[]{:S(2)}, u32[]{:S(2)}) collective-permute-start(bf16[152,256]{1,0:T(8,128)(2,1)S(1)} %shard_map.100.refs_1_), channel_id=1, source_target_pairs={{0,24},{8,0},{16,8},{24,16},{1,25},{9,1},{17,9},{25,17},{2,26},{10... | collective-permute-start | bytes 233480 | tf_op jit(solution)/shard_map/ppermute | solution.py:197
  90.9 2.5 %collective-permute-done.18.refs_3_ = bf16[152,256]{1,0:T(8,128)(2,1)S(1)} collective-permute-done((bf16[152,256]{1,0:T(8,128)(2,1)S(1)}, bf16[152,256]{1,0:T(8,128)(2,1)S(1)}, u32[]{:S(2)}, u32[]{:S(2)}) %collective-permute-start.18) | collective-permute-done | bytes 77856 | tf_op jit(solution)/shard_map/ppermute | solution.py:197
  93.4 1.4 %collective-permute-done.20.refs_5_ = bf16[152,256]{1,0:T(8,128)(2,1)S(1)} collective-permute-done((bf16[152,256]{1,0:T(8,128)(2,1)S(1)}, bf16[152,256]{1,0:T(8,128)(2,1)S(1)}, u32[]{:S(2)}, u32[]{:S(2)}) %collective-permute-start.20) | collective-permute-done | bytes 77856 | tf_op jit(solution)/shard_map/ppermute | solution.py:197
  96.3 0.8 shard_map.102
  97.1 0.8 shard_map.103
  98.0 0.8 shard_map.104
  99.5 2.6 %collective-permute-start.28 = (bf16[152,1024]{1,0:T(8,128)(2,1)S(1)}, bf16[152,1024]{1,0:T(8,128)(2,1)S(1)}, u32[]{:S(2)}, u32[]{:S(2)}) collective-permute-start(bf16[152,1024]{1,0:T(8,128)(2,1)S(1)} %shard_map.103), channel_id=1, source_target_pairs={{0,4},{1,5},{2,6},{3,7},{4,0},{5,1},{6,2},{7,3},{8,12},{9,13},{10,... | collective-permute-start | bytes 933896 | tf_op jit(solution)/shard_map/ppermute | solution.py:204
  102.4 0.8 shard_map.101
  103.2 1.0 fusion.1
  104.2 4.8 %collective-permute-done.27 = bf16[152,1024]{1,0:T(8,128)(2,1)S(1)} collective-permute-done((bf16[152,1024]{1,0:T(8,128)(2,1)S(1)}, bf16[152,1024]{1,0:T(8,128)(2,1)S(1)}, u32[]{:S(2)}, u32[]{:S(2)}) %collective-permute-start.27) | collective-permute-done | bytes 311328 | tf_op jit(solution)/shard_map/ppermute | solution.py:204
  109.1 7.2 %collective-permute-done.28 = bf16[152,1024]{1,0:T(8,128)(2,1)S(1)} collective-permute-done((bf16[152,1024]{1,0:T(8,128)(2,1)S(1)}, bf16[152,1024]{1,0:T(8,128)(2,1)S(1)}, u32[]{:S(2)}, u32[]{:S(2)}) %collective-permute-start.28) | collective-permute-done | bytes 311328 | tf_op jit(solution)/shard_map/ppermute | solution.py:204
  116.3 1.1 fusion.4
  (49 shorter events, 6.5 us)
Async XLA Ops:
  0.6 0.9 copy-start.3
  1.5 0.9 copy-start.5
  2.5 0.7 copy-start.7
  3.6 6.4 %collective-permute-start = (bf16[600,256]{1,0:T(8,128)(2,1)S(1)}, bf16[600,256]{1,0:T(8,128)(2,1)S(1)}, u32[]{:S(2)}, u32[]{:S(2)}) collective-permute-start(bf16[600,256]{1,0:T(8,128)(2,1)S(1)} %shard_map.86.refs_1_), channel_id=1, source_target_pairs={{0,1},{1,0},{2,3},{3,2},{4,5},{5,4},{6,7},{7,6},{8,9},{9,8},{10,11... | collective-permute-start | bytes 921608 | tf_op jit(solution)/shard_map/ppermute | solution.py:194
  4.1 12.5 %collective-permute-start.1 = (bf16[600,256]{1,0:T(8,128)(2,1)S(1)}, bf16[600,256]{1,0:T(8,128)(2,1)S(1)}, u32[]{:S(2)}, u32[]{:S(2)}) collective-permute-start(bf16[600,256]{1,0:T(8,128)(2,1)S(1)} %shard_map.86.refs_1_), channel_id=1, source_target_pairs={{0,8},{8,16},{16,24},{24,0},{1,9},{9,17},{17,25},{25,1},{2,10},{10... | collective-permute-start | bytes 921608 | tf_op jit(solution)/shard_map/ppermute | solution.py:197
  6.7 1.0 copy-start
  7.7 1.2 copy-start.2
  8.9 0.7 copy-start.6
  16.6 3.7 %collective-permute-start.2 = (bf16[600,256]{1,0:T(8,128)(2,1)S(1)}, bf16[600,256]{1,0:T(8,128)(2,1)S(1)}, u32[]{:S(2)}, u32[]{:S(2)}) collective-permute-start(bf16[600,256]{1,0:T(8,128)(2,1)S(1)} %collective-permute-done.1.refs_1_.refs_3_), channel_id=1, source_target_pairs={{0,1},{1,0},{2,3},{3,2},{4,5},{5,4},{6,7},{7,6},{8,9},{9,8},{10,11... | collective-permute-start | bytes 921608 | tf_op jit(solution)/shard_map/ppermute | solution.py:194
  16.6 16.3 %collective-permute-start.3 = (bf16[600,256]{1,0:T(8,128)(2,1)S(1)}, bf16[600,256]{1,0:T(8,128)(2,1)S(1)}, u32[]{:S(2)}, u32[]{:S(2)}) collective-permute-start(bf16[600,256]{1,0:T(8,128)(2,1)S(1)} %shard_map.86.refs_1_), channel_id=1, source_target_pairs={{0,16},{8,24},{16,0},{24,8},{1,17},{9,25},{17,1},{25,9},{2,18},{10... | collective-permute-start | bytes 921608 | tf_op jit(solution)/shard_map/ppermute | solution.py:197
  17.4 25.3 %collective-permute-start.7 = (bf16[600,512]{1,0:T(8,128)(2,1)S(1)}, bf16[600,512]{1,0:T(8,128)(2,1)S(1)}, u32[]{:S(2)}, u32[]{:S(2)}) collective-permute-start(bf16[600,512]{1,0:T(8,128)(2,1)S(1)} %get-tuple-element.53.refs_2_), channel_id=1, source_target_pairs={{0,2},{1,3},{2,0},{3,1},{4,6},{5,7},{6,4},{7,5},{8,10},{9,11},{10,... | collective-permute-start | bytes 1843208 | tf_op jit(solution)/shard_map/ppermute | solution.py:204
  18.9 25.3 %collective-permute-start.8 = (bf16[600,512]{1,0:T(8,128)(2,1)S(1)}, bf16[600,512]{1,0:T(8,128)(2,1)S(1)}, u32[]{:S(2)}, u32[]{:S(2)}) collective-permute-start(bf16[600,512]{1,0:T(8,128)(2,1)S(1)} %get-tuple-element.54.refs_3_), channel_id=1, source_target_pairs={{0,4},{1,5},{2,6},{3,7},{4,0},{5,1},{6,2},{7,3},{8,12},{9,13},{10,... | collective-permute-start | bytes 1843208 | tf_op jit(solution)/shard_map/ppermute | solution.py:204
  33.0 4.1 %collective-permute-start.4 = (bf16[600,256]{1,0:T(8,128)(2,1)S(1)}, bf16[600,256]{1,0:T(8,128)(2,1)S(1)}, u32[]{:S(2)}, u32[]{:S(2)}) collective-permute-start(bf16[600,256]{1,0:T(8,128)(2,1)S(1)} %collective-permute-done.3.refs_1_.refs_5_), channel_id=1, source_target_pairs={{0,1},{1,0},{2,3},{3,2},{4,5},{5,4},{6,7},{7,6},{8,9},{9,8},{10,11... | collective-permute-start | bytes 921608 | tf_op jit(solution)/shard_map/ppermute | solution.py:194
  33.0 9.6 %collective-permute-start.5 = (bf16[600,256]{1,0:T(8,128)(2,1)S(1)}, bf16[600,256]{1,0:T(8,128)(2,1)S(1)}, u32[]{:S(2)}, u32[]{:S(2)}) collective-permute-start(bf16[600,256]{1,0:T(8,128)(2,1)S(1)} %shard_map.86.refs_1_), channel_id=1, source_target_pairs={{0,24},{8,0},{16,8},{24,16},{1,25},{9,1},{17,9},{25,17},{2,26},{10... | collective-permute-start | bytes 921608 | tf_op jit(solution)/shard_map/ppermute | solution.py:197
  35.5 17.2 %collective-permute-start.10 = (bf16[600,512]{1,0:T(8,128)(2,1)S(1)}, bf16[600,512]{1,0:T(8,128)(2,1)S(1)}, u32[]{:S(2)}, u32[]{:S(2)}) collective-permute-start(bf16[600,512]{1,0:T(8,128)(2,1)S(1)} %get-tuple-element.53.refs_2_), channel_id=1, source_target_pairs={{0,4},{1,5},{2,6},{3,7},{4,0},{5,1},{6,2},{7,3},{8,12},{9,13},{10,... | collective-permute-start | bytes 1843208 | tf_op jit(solution)/shard_map/ppermute | solution.py:204
  37.0 16.7 %collective-permute-start.9 = (bf16[600,512]{1,0:T(8,128)(2,1)S(1)}, bf16[600,512]{1,0:T(8,128)(2,1)S(1)}, u32[]{:S(2)}, u32[]{:S(2)}) collective-permute-start(bf16[600,512]{1,0:T(8,128)(2,1)S(1)} %get-tuple-element.54.refs_3_), channel_id=1, source_target_pairs={{0,2},{1,3},{2,0},{3,1},{4,6},{5,7},{6,4},{7,5},{8,10},{9,11},{10,... | collective-permute-start | bytes 1843208 | tf_op jit(solution)/shard_map/ppermute | solution.py:204
  42.7 3.0 %collective-permute-start.6 = (bf16[600,256]{1,0:T(8,128)(2,1)S(1)}, bf16[600,256]{1,0:T(8,128)(2,1)S(1)}, u32[]{:S(2)}, u32[]{:S(2)}) collective-permute-start(bf16[600,256]{1,0:T(8,128)(2,1)S(1)} %collective-permute-done.5.refs_1_.refs_7_), channel_id=1, source_target_pairs={{0,1},{1,0},{2,3},{3,2},{4,5},{5,4},{6,7},{7,6},{8,9},{9,8},{10,11... | collective-permute-start | bytes 921608 | tf_op jit(solution)/shard_map/ppermute | solution.py:194
  42.7 21.9 %collective-permute-start.11 = (bf16[600,512]{1,0:T(8,128)(2,1)S(1)}, bf16[600,512]{1,0:T(8,128)(2,1)S(1)}, u32[]{:S(2)}, u32[]{:S(2)}) collective-permute-start(bf16[600,512]{1,0:T(8,128)(2,1)S(1)} %collective-permute-done.7.refs_8_), channel_id=1, source_target_pairs={{0,4},{1,5},{2,6},{3,7},{4,0},{5,1},{6,2},{7,3},{8,12},{9,13},{10,... | collective-permute-start | bytes 1843208 | tf_op jit(solution)/shard_map/ppermute | solution.py:204
  44.2 21.7 %collective-permute-start.12 = (bf16[600,512]{1,0:T(8,128)(2,1)S(1)}, bf16[600,512]{1,0:T(8,128)(2,1)S(1)}, u32[]{:S(2)}, u32[]{:S(2)}) collective-permute-start(bf16[600,512]{1,0:T(8,128)(2,1)S(1)} %collective-permute-done.8.refs_9_), channel_id=1, source_target_pairs={{0,2},{1,3},{2,0},{3,1},{4,6},{5,7},{6,4},{7,5},{8,10},{9,11},{10,... | collective-permute-start | bytes 1843208 | tf_op jit(solution)/shard_map/ppermute | solution.py:204
  71.4 4.9 %collective-permute-start.13 = (bf16[152,1024]{1,0:T(8,128)(2,1)S(1)}, bf16[152,1024]{1,0:T(8,128)(2,1)S(1)}, u32[]{:S(2)}, u32[]{:S(2)}) collective-permute-start(bf16[152,1024]{1,0:T(8,128)(2,1)S(1)} %get-tuple-element.72), channel_id=1, source_target_pairs={{0,1},{1,0},{2,3},{3,2},{4,5},{5,4},{6,7},{7,6},{8,9},{9,8},{10,11... | collective-permute-start | bytes 933896 | tf_op jit(solution)/shard_map/ppermute | solution.py:194
  72.3 16.0 %collective-permute-start.26 = (bf16[152,1024]{1,0:T(8,128)(2,1)S(1)}, bf16[152,1024]{1,0:T(8,128)(2,1)S(1)}, u32[]{:S(2)}, u32[]{:S(2)}) collective-permute-start(bf16[152,1024]{1,0:T(8,128)(2,1)S(1)} %shard_map.99), channel_id=1, source_target_pairs={{0,6},{1,7},{2,4},{3,5},{4,2},{5,3},{6,0},{7,1},{8,14},{9,15},{10,... | collective-permute-start | bytes 933896 | tf_op jit(solution)/shard_map/ppermute | solution.py:204
  74.7 16.3 %collective-permute-start.25 = (bf16[152,1024]{1,0:T(8,128)(2,1)S(1)}, bf16[152,1024]{1,0:T(8,128)(2,1)S(1)}, u32[]{:S(2)}, u32[]{:S(2)}) collective-permute-start(bf16[152,1024]{1,0:T(8,128)(2,1)S(1)} %shard_map.98), channel_id=1, source_target_pairs={{0,4},{1,5},{2,6},{3,7},{4,0},{5,1},{6,2},{7,3},{8,12},{9,13},{10,... | collective-permute-start | bytes 933896 | tf_op jit(solution)/shard_map/ppermute | solution.py:204
  76.3 4.5 %collective-permute-start.14 = (bf16[152,256]{1,0:T(8,128)(2,1)S(1)}, bf16[152,256]{1,0:T(8,128)(2,1)S(1)}, u32[]{:S(2)}, u32[]{:S(2)}) collective-permute-start(bf16[152,256]{1,0:T(8,128)(2,1)S(1)} %get-tuple-element.89), channel_id=1, source_target_pairs={{0,24},{8,0},{16,8},{24,16},{1,25},{9,1},{17,9},{25,17},{2,26},{10... | collective-permute-start | bytes 233480 | tf_op jit(solution)/shard_map/ppermute | solution.py:197
  77.5 18.5 %collective-permute-start.24 = (bf16[152,1024]{1,0:T(8,128)(2,1)S(1)}, bf16[152,1024]{1,0:T(8,128)(2,1)S(1)}, u32[]{:S(2)}, u32[]{:S(2)}) collective-permute-start(bf16[152,1024]{1,0:T(8,128)(2,1)S(1)} %shard_map.97), channel_id=1, source_target_pairs={{0,2},{1,3},{2,0},{3,1},{4,6},{5,7},{6,4},{7,5},{8,10},{9,11},{10,... | collective-permute-start | bytes 933896 | tf_op jit(solution)/shard_map/ppermute | solution.py:204
  78.1 5.7 %collective-permute-start.15 = (bf16[152,256]{1,0:T(8,128)(2,1)S(1)}, bf16[152,256]{1,0:T(8,128)(2,1)S(1)}, u32[]{:S(2)}, u32[]{:S(2)}) collective-permute-start(bf16[152,256]{1,0:T(8,128)(2,1)S(1)} %get-tuple-element.90), channel_id=1, source_target_pairs={{0,16},{8,24},{16,0},{24,8},{1,17},{9,25},{17,1},{25,9},{2,18},{10... | collective-permute-start | bytes 233480 | tf_op jit(solution)/shard_map/ppermute | solution.py:197
  80.8 6.2 %collective-permute-start.16 = (bf16[152,256]{1,0:T(8,128)(2,1)S(1)}, bf16[152,256]{1,0:T(8,128)(2,1)S(1)}, u32[]{:S(2)}, u32[]{:S(2)}) collective-permute-start(bf16[152,256]{1,0:T(8,128)(2,1)S(1)} %get-tuple-element.91), channel_id=1, source_target_pairs={{0,8},{8,16},{16,24},{24,0},{1,9},{9,17},{17,25},{25,1},{2,10},{10... | collective-permute-start | bytes 233480 | tf_op jit(solution)/shard_map/ppermute | solution.py:197
  80.8 6.2 %copy-start.4 = (bf16[147,256]{1,0:T(8,128)(2,1)S(1)}, bf16[147,256]{1,0:T(8,128)(2,1)}, u32[]{:S(2)}) copy-start(bf16[147,256]{1,0:T(8,128)(2,1)} %refs_3_.1) | copy-start | bytes 225796
  87.0 6.4 %collective-permute-start.18 = (bf16[152,256]{1,0:T(8,128)(2,1)S(1)}, bf16[152,256]{1,0:T(8,128)(2,1)S(1)}, u32[]{:S(2)}, u32[]{:S(2)}) collective-permute-start(bf16[152,256]{1,0:T(8,128)(2,1)S(1)} %shard_map.100.refs_1_), channel_id=1, source_target_pairs={{0,8},{8,16},{16,24},{24,0},{1,9},{9,17},{17,25},{25,1},{2,10},{10... | collective-permute-start | bytes 233480 | tf_op jit(solution)/shard_map/ppermute | solution.py:197
  87.1 7.7 %collective-permute-start.20 = (bf16[152,256]{1,0:T(8,128)(2,1)S(1)}, bf16[152,256]{1,0:T(8,128)(2,1)S(1)}, u32[]{:S(2)}, u32[]{:S(2)}) collective-permute-start(bf16[152,256]{1,0:T(8,128)(2,1)S(1)} %shard_map.100.refs_1_), channel_id=1, source_target_pairs={{0,16},{8,24},{16,0},{24,8},{1,17},{9,25},{17,1},{25,9},{2,18},{10... | collective-permute-start | bytes 233480 | tf_op jit(solution)/shard_map/ppermute | solution.py:197
  88.3 6.5 %collective-permute-start.22 = (bf16[152,256]{1,0:T(8,128)(2,1)S(1)}, bf16[152,256]{1,0:T(8,128)(2,1)S(1)}, u32[]{:S(2)}, u32[]{:S(2)}) collective-permute-start(bf16[152,256]{1,0:T(8,128)(2,1)S(1)} %shard_map.100.refs_1_), channel_id=1, source_target_pairs={{0,24},{8,0},{16,8},{24,16},{1,25},{9,1},{17,9},{25,17},{2,26},{10... | collective-permute-start | bytes 233480 | tf_op jit(solution)/shard_map/ppermute | solution.py:197
  90.9 5.1 %collective-permute-start.17 = (bf16[152,256]{1,0:T(8,128)(2,1)S(1)}, bf16[152,256]{1,0:T(8,128)(2,1)S(1)}, u32[]{:S(2)}, u32[]{:S(2)}) collective-permute-start(bf16[152,256]{1,0:T(8,128)(2,1)S(1)} %shard_map.100.refs_1_), channel_id=1, source_target_pairs={{0,1},{1,0},{2,3},{3,2},{4,5},{5,4},{6,7},{7,6},{8,9},{9,8},{10,11... | collective-permute-start | bytes 233480 | tf_op jit(solution)/shard_map/ppermute | solution.py:194
  93.4 2.6 %collective-permute-start.19 = (bf16[152,256]{1,0:T(8,128)(2,1)S(1)}, bf16[152,256]{1,0:T(8,128)(2,1)S(1)}, u32[]{:S(2)}, u32[]{:S(2)}) collective-permute-start(bf16[152,256]{1,0:T(8,128)(2,1)S(1)} %collective-permute-done.18.refs_3_), channel_id=1, source_target_pairs={{0,1},{1,0},{2,3},{3,2},{4,5},{5,4},{6,7},{7,6},{8,9},{9,8},{10,11... | collective-permute-start | bytes 233480 | tf_op jit(solution)/shard_map/ppermute | solution.py:194
  94.8 1.3 %collective-permute-start.21 = (bf16[152,256]{1,0:T(8,128)(2,1)S(1)}, bf16[152,256]{1,0:T(8,128)(2,1)S(1)}, u32[]{:S(2)}, u32[]{:S(2)}) collective-permute-start(bf16[152,256]{1,0:T(8,128)(2,1)S(1)} %collective-permute-done.20.refs_5_), channel_id=1, source_target_pairs={{0,1},{1,0},{2,3},{3,2},{4,5},{5,4},{6,7},{7,6},{8,9},{9,8},{10,11... | collective-permute-start | bytes 233480 | tf_op jit(solution)/shard_map/ppermute | solution.py:194
  94.9 1.4 %collective-permute-start.23 = (bf16[152,256]{1,0:T(8,128)(2,1)S(1)}, bf16[152,256]{1,0:T(8,128)(2,1)S(1)}, u32[]{:S(2)}, u32[]{:S(2)}) collective-permute-start(bf16[152,256]{1,0:T(8,128)(2,1)S(1)} %collective-permute-done.22.refs_7_), channel_id=1, source_target_pairs={{0,1},{1,0},{2,3},{3,2},{4,5},{5,4},{6,7},{7,6},{8,9},{9,8},{10,11... | collective-permute-start | bytes 233480 | tf_op jit(solution)/shard_map/ppermute | solution.py:194
  98.8 10.2 %collective-permute-start.27 = (bf16[152,1024]{1,0:T(8,128)(2,1)S(1)}, bf16[152,1024]{1,0:T(8,128)(2,1)S(1)}, u32[]{:S(2)}, u32[]{:S(2)}) collective-permute-start(bf16[152,1024]{1,0:T(8,128)(2,1)S(1)} %shard_map.102), channel_id=1, source_target_pairs={{0,2},{1,3},{2,0},{3,1},{4,6},{5,7},{6,4},{7,5},{8,10},{9,11},{10,... | collective-permute-start | bytes 933896 | tf_op jit(solution)/shard_map/ppermute | solution.py:204
  99.5 16.8 %collective-permute-start.28 = (bf16[152,1024]{1,0:T(8,128)(2,1)S(1)}, bf16[152,1024]{1,0:T(8,128)(2,1)S(1)}, u32[]{:S(2)}, u32[]{:S(2)}) collective-permute-start(bf16[152,1024]{1,0:T(8,128)(2,1)S(1)} %shard_map.103), channel_id=1, source_target_pairs={{0,4},{1,5},{2,6},{3,7},{4,0},{5,1},{6,2},{7,3},{8,12},{9,13},{10,... | collective-permute-start | bytes 933896 | tf_op jit(solution)/shard_map/ppermute | solution.py:204
  102.1 14.3 %collective-permute-start.29 = (bf16[152,1024]{1,0:T(8,128)(2,1)S(1)}, bf16[152,1024]{1,0:T(8,128)(2,1)S(1)}, u32[]{:S(2)}, u32[]{:S(2)}) collective-permute-start(bf16[152,1024]{1,0:T(8,128)(2,1)S(1)} %shard_map.104), channel_id=1, source_target_pairs={{0,6},{1,7},{2,4},{3,5},{4,2},{5,3},{6,0},{7,1},{8,14},{9,15},{10,... | collective-permute-start | bytes 933896 | tf_op jit(solution)/shard_map/ppermute | solution.py:204
  103.2 13.1 %copy-start.1 = (bf16[147,1024]{1,0:T(8,128)(2,1)S(1)}, bf16[147,1024]{1,0:T(8,128)(2,1)}, u32[]{:S(2)}) copy-start(bf16[147,1024]{1,0:T(8,128)(2,1)} %d_hbm.1) | copy-start | bytes 903172

commit v4 on v3

--- a/solution.py
+++ b/solution.py
@@ -68,7 +68,7 @@
 def pack(kernel, shapes, *args):
     return pl.pallas_call(
         kernel,
-        in_specs=[pl.BlockSpec(memory_space=pl.ANY)] * len(args),
+        in_specs=[pl.BlockSpec(memory_space=pltpu.HBM)] * len(args),
         out_shape=shapes,
         scratch_shapes=[pltpu.VMEM(a.shape, a.dtype) for a in args] + [pltpu.SemaphoreType.DMA((len(args),))],
         compiler_params=params(),
@@ -112,12 +112,9 @@
             if not last:
                 out_refs[0][spot : spot + block, :] = total
             else:
-                pair, mine = spot // (2 * block), spot // block % 2
-                here = slice(pair * block, (pair + 1) * block)
-                if mine:
-                    out_refs[1][:, here] = total.T
-                else:
-                    out_refs[0][:, here] = total.T.astype(BF16)
+                out_ref = out_refs[spot // out_refs[0].shape[1]]
+                at_out = spot % out_ref.shape[1]
+                out_ref[:, at_out : at_out + block] = total.T.astype(out_ref.dtype)
             spot += block
 
 
@@ -125,8 +122,8 @@
     n, f = sum(a.shape[0] for a in xts), pieces[0].shape[1]
     shapes = [jax.ShapeDtypeStruct((n, f), BF16)] * len(pieces)
     if last:
+        shapes.append(jax.ShapeDtypeStruct((wide, n // 2), F32))
         shapes.append(jax.ShapeDtypeStruct((wide, n // 2), BF16))
-        shapes.append(jax.ShapeDtypeStruct((wide, n // 2), F32))
     else:
         shapes.append(jax.ShapeDtypeStruct((n, wide), F32))
     kernel = functools.partial(next_kernel, depth, len(xts), len(totals), len(pieces), block, last)
@@ -205,21 +202,17 @@
 
     offsets = [(dy, dx) for dy in range(ys) for dx in range(xs)]
     rows, half = depth + wide, width // 2
-    w_own = pack(
+    (w_own,) = pack(
         functools.partial(pack_weights_kernel, raw, depth, classes),
-        [jax.ShapeDtypeStruct((rows, half), BF16)] * 2,
+        [jax.ShapeDtypeStruct((rows, width), BF16)],
         proj_weight, phase, direction,
     )
-    ws = {(0, 0): w_own}
-    for h in (0, 1):
-        for dx in range(1, xs):
-            ws[0, dx, h] = across(w_own[h], 0, dx)
-        for dy in range(1, ys):
-            ws[dy, 0, 1 - h] = across(w_own[1 - h], dy, 0)
-    for dy in range(1, ys):
-        for dx in range(1, xs):
-            ws[dy, dx, 0] = across(ws[0, dx, 0], dy, 0)
-            ws[dy, dx, 1] = across(ws[dy, 0, 1], 0, dx)
+    ws = {(0, dx): across(w_own, 0, dx) for dx in range(1, xs)}
+    ws.update({(dy, 0): across(w_own, dy, 0) for dy in range(1, ys)})
+    far = [(dy, dx) for dy in range(1, ys) for dx in range(1, xs)]
+    halves = {}
+    for dy, dx in far:
+        halves[dy, dx] = [across(ws[0, dx][:, :half], dy, 0), across(ws[dy, 0][:, half:], 0, dx)]
     x_own = pack(
         functools.partial(pack_samples_kernel, raw, depth, classes),
         jax.ShapeDtypeStruct((rows, own), BF16),
@@ -227,36 +220,40 @@
     )
     x_line = [x_own] + [along(x_own, k) for k in range(1, line)]
 
-    feats = {at: [[], []] for at in offsets}
-    xts, totals, blocks = [], [], []
-    for k in range(line):
-        pair = 2 * own
-        blocks += [swap_core(x_line[k]), x_line[k]]
+    feats = {at: [[]] for at in offsets}
+    xts, totals = [], []
+
+    def first(some):
+        n = own * len(some)
         xt, total, *part = whole(
-            functools.partial(first_kernel, depth, 2, 2),
-            [jax.ShapeDtypeStruct((pair, depth), BF16), jax.ShapeDtypeStruct((pair, wide), F32)]
-            + [jax.ShapeDtypeStruct((pair, half), BF16)] * 2,
-            *blocks[-2:], *w_own, flops=2 * pair * width * (depth + wide),
+            functools.partial(first_kernel, depth, len(some), 1),
+            [jax.ShapeDtypeStruct((n, depth), BF16), jax.ShapeDtypeStruct((n, wide), F32)]
+            + [jax.ShapeDtypeStruct((n, width), BF16)],
+            *some, w_own, flops=2 * n * width * (depth + wide),
         )
         xts.append(xt)
         totals.append(total)
-        for h in (0, 1):
-            feats[0, 0][h].append(part[h])
+        feats[0, 0][0] += part
+
+    for k in range(line):
+        first(x_line[k : k + 1])
         if k + 1 < line:
             x_line[k + 1], totals[k] = lax.optimization_barrier((x_line[k + 1], totals[k]))
-    soon = [(0, dx, 0) for dx in range(1, xs)] + [(dy, 0, 1) for dy in range(1, ys)]
-    near = [(0, dx, 1) for dx in range(1, xs)] + [(dy, 0, 0) for dy in range(1, ys)]
-    far = [(dy, dx, h) for dy in range(1, ys) for dx in range(1, xs) for h in (0, 1)]
-    groups = [group for group in (soon, near, far) if group]
-    for group in groups:
-        last = group is groups[-1]
-        got, rest = make_next(xts, totals, [ws[at] for at in group], depth, wide, own, last)
-        for (dy, dx, h), piece in zip(group, got, strict=True):
-            feats[dy, dx][h] = [piece]
-        if not last:
+    x_peer = [swap_core(a) for a in x_line]
+    first(x_peer)
+    blocks = x_line + x_peer
+    near = list(ws)
+    for group in (near, far):
+        if group:
+            last = group is far or not far
+            pieces = [ws[at] for at in near] if group is near else [w for at in far for w in halves[at]]
+            got, rest = make_next(xts, totals, pieces, depth, wide, own, last)
+            for j, at in enumerate(group):
+                feats[at] = [[got[j]]] if group is near else [[got[2 * j]], [got[2 * j + 1]]]
             totals = rest
-    t_other, t_own = rest
+    t_own, t_other = rest
     t_got = swap_core(t_other)
+    lefts = blocks
     keep, *send = whole(
         spread_kernel,
         [jax.ShapeDtypeStruct((wide, own), F32)] + [jax.ShapeDtypeStruct((wide, own), BF16)] * (line - 1),
@@ -274,14 +271,14 @@
         parts = {at: make_share(lefts, skip, feats[at], F32 if at == (0, 0) else BF16) for at in offsets[::-1]}
         return parts, {(dy, dx): across(parts[dy, dx], -dy, -dx) for dy, dx in offsets[1:]}
 
-    parts, arrived = send_home(blocks, depth)
+    parts, arrived = send_home(lefts, depth)
     keep, parts = lax.optimization_barrier((keep, parts))
     curv = whole(
         functools.partial(curve_kernel, classes), jax.ShapeDtypeStruct((wide, own), BF16), keep, *got, probs
     )
     c_line = [curv] + [along(curv, k) for k in range(1, line)]
-    curvs = [b for a in c_line for b in (swap_core(a), a)]
-    curvs, arrived = lax.optimization_barrier((curvs, arrived))
+    c_line, arrived = lax.optimization_barrier((c_line, arrived))
+    curvs = c_line + [swap_core(a) for a in c_line]
     gradient = collect({(0, 0): parts[0, 0], **arrived})
     parts, arrived = send_home(curvs, 0)
     hess_vec = collect({(0, 0): parts[0, 0], **arrived}) + damping[0] * direction.astype(F32)

time: 118 us -> 111 us (0.941)
  waiting for transfers between devices: 49.4 us -> 41 us
  starting transfers between devices: 28.2 us -> 31.9 us
  local copies, waits for them, and re-layouts: 5.33 us -> 2.93 us
    ppermute x12 -> x10, waiting for transfers between devices: 19.5 us -> 12.4 us  [across(): return lax.ppermute(a, 'feat', [(i, to(i)) for i in range(2 * xs * ys)])]
    ppermute x9, starting transfers between devices: 10.8 us -> 16.2 us  [along(): return lax.ppermute(a, 'samp', [(i, (i + k) % line) for i in range(line)])]
    unnamed x16 -> x14, local copies, waits for them, and re-layouts: 5.33 us -> 2.84 us
    ppermute x12 -> x10, starting transfers between devices: 16.3 us -> 14 us  [across(): return lax.ppermute(a, 'feat', [(i, to(i)) for i in range(2 * xs * ys)])]
    ppermute x9, waiting for transfers between devices: 29.7 us -> 28.4 us  [along(): return lax.ppermute(a, 'samp', [(i, (i + k) % line) for i in range(line)])]
  transfers between devices with their start and end apart: 30 -> 28, of which waited for: 15 -> 12; matrix products, arithmetic and copies ran while one was open for 1% -> 1% of each run, Pallas kernels for 19% -> 22%
where the time goes in v4:
time: 111 us; the launch traced here: 110 us
  waiting for transfers between devices  41 us (37%)
  starting transfers between devices  31.9 us (29%)
  Pallas kernels  31 us (28%)
  local copies, waits for them, and re-layouts  2.93 us (3%)
  other arithmetic  2.04 us (2%)
  between operations  1.54 us (1%)
    pallas_call x17, Pallas kernels, whole(): pl.pallas_call(kernel, out_shape=shapes, compiler_params=params(), cost_e...  30.1 us
    ppermute x9, waiting for transfers between devices, along(): return lax.ppermute(a, 'samp', [(i, (i + k) % line) for i in range(line)])  28.4 us
    ppermute x9, starting transfers between devices, along(): return lax.ppermute(a, 'samp', [(i, (i + k) % line) for i in range(line)])  16.2 us
    ppermute x10, starting transfers between devices, across(): return lax.ppermute(a, 'feat', [(i, to(i)) for i in range(2 * xs * ys)])  14 us
    ppermute x10, waiting for transfers between devices, across(): return lax.ppermute(a, 'feat', [(i, to(i)) for i in range(2 * xs * ys)])  12.4 us
    unnamed x14, local copies, waits for them, and re-layouts  2.84 us
  transfers between devices with their start and end apart: 28, of which 12 were waited for; matrix products, arithmetic and copies ran while one was open for 1% of the time, Pallas kernels for 22%

profile of v4, /device:TPU:0, one launch (start us, length us, event | category | flops | bytes accessed | tf_op | source)
XLA Modules:
  0.0 110.4 jit_solution(10877804039450460620)
XLA Ops:
  0.6 1.0 copy-done
  1.6 1.2 %copy-done.2 = bf16[440,1024]{1,0:T(8,128)(2,1)S(1)} copy-done((bf16[440,1024]{1,0:T(8,128)(2,1)S(1)}, bf16[440,1024]{1,0:T(8,128)(2,1)}, u32[]{:S(2)}) %copy-start.2) | copy-done | bytes 901144
  2.8 0.7 copy-done.5
  3.9 3.0 %collective-permute-start.8 = (bf16[600,1024]{1,0:T(8,128)(2,1)S(1)}, bf16[600,1024]{1,0:T(8,128)(2,1)S(1)}, u32[]{:S(2)}, u32[]{:S(2)}) collective-permute-start(bf16[600,1024]{1,0:T(8,128)(2,1)S(1)} %shard_map.87.refs_1_.refs_4_), channel_id=1, source_target_pairs={{0,4},{1,5},{2,6},{3,7},{4,0},{5,1},{6,2},{7,3},{8,12},{9,13},{10,... | collective-permute-start | bytes 3686408 | tf_op jit(solution)/shard_map/ppermute | solution.py:201
  6.9 1.5 %collective-permute-start.7 = (bf16[600,1024]{1,0:T(8,128)(2,1)S(1)}, bf16[600,1024]{1,0:T(8,128)(2,1)S(1)}, u32[]{:S(2)}, u32[]{:S(2)}) collective-permute-start(bf16[600,1024]{1,0:T(8,128)(2,1)S(1)} %shard_map.87.refs_1_.refs_4_), channel_id=1, source_target_pairs={{0,2},{1,3},{2,0},{3,1},{4,6},{5,7},{6,4},{7,5},{8,10},{9,11},{10,... | collective-permute-start | bytes 3686408 | tf_op jit(solution)/shard_map/ppermute | solution.py:201
  8.9 1.6 %collective-permute-start = (bf16[600,256]{1,0:T(8,128)(2,1)S(1)}, bf16[600,256]{1,0:T(8,128)(2,1)S(1)}, u32[]{:S(2)}, u32[]{:S(2)}) collective-permute-start(bf16[600,256]{1,0:T(8,128)(2,1)S(1)} %shard_map.86.refs_0_), channel_id=1, source_target_pairs={{0,8},{8,16},{16,24},{24,0},{1,9},{9,17},{17,25},{25,1},{2,10},{10... | collective-permute-start | bytes 921608 | tf_op jit(solution)/shard_map/ppermute | solution.py:194
  10.5 2.6 %collective-permute-start.1 = (bf16[600,256]{1,0:T(8,128)(2,1)S(1)}, bf16[600,256]{1,0:T(8,128)(2,1)S(1)}, u32[]{:S(2)}, u32[]{:S(2)}) collective-permute-start(bf16[600,256]{1,0:T(8,128)(2,1)S(1)} %shard_map.86.refs_0_), channel_id=1, source_target_pairs={{0,16},{8,24},{16,0},{24,8},{1,17},{9,25},{17,1},{25,9},{2,18},{10... | collective-permute-start | bytes 921608 | tf_op jit(solution)/shard_map/ppermute | solution.py:194
  13.1 1.3 %collective-permute-start.2 = (bf16[600,256]{1,0:T(8,128)(2,1)S(1)}, bf16[600,256]{1,0:T(8,128)(2,1)S(1)}, u32[]{:S(2)}, u32[]{:S(2)}) collective-permute-start(bf16[600,256]{1,0:T(8,128)(2,1)S(1)} %shard_map.86.refs_0_), channel_id=1, source_target_pairs={{0,24},{8,0},{16,8},{24,16},{1,25},{9,1},{17,9},{25,17},{2,26},{10... | collective-permute-start | bytes 921608 | tf_op jit(solution)/shard_map/ppermute | solution.py:194
  14.5 0.9 shard_map.88
  15.4 5.7 %collective-permute-done.refs_0_.refs_1_ = bf16[600,256]{1,0:T(8,128)(2,1)S(1)} collective-permute-done((bf16[600,256]{1,0:T(8,128)(2,1)S(1)}, bf16[600,256]{1,0:T(8,128)(2,1)S(1)}, u32[]{:S(2)}, u32[]{:S(2)}) %collective-permute-start) | collective-permute-done | bytes 307232 | tf_op jit(solution)/shard_map/ppermute | solution.py:194
  21.1 0.9 shard_map.89
  22.1 10.5 %collective-permute-done.1.refs_0_.refs_2_ = bf16[600,256]{1,0:T(8,128)(2,1)S(1)} collective-permute-done((bf16[600,256]{1,0:T(8,128)(2,1)S(1)}, bf16[600,256]{1,0:T(8,128)(2,1)S(1)}, u32[]{:S(2)}, u32[]{:S(2)}) %collective-permute-start.1) | collective-permute-done | bytes 307232 | tf_op jit(solution)/shard_map/ppermute | solution.py:194
  32.6 1.0 shard_map.90
  33.5 0.6 collective-permute-start.6
  34.2 1.1 %collective-permute-done.7.refs_10_ = bf16[600,1024]{1,0:T(8,128)(2,1)S(1)} collective-permute-done((bf16[600,1024]{1,0:T(8,128)(2,1)S(1)}, bf16[600,1024]{1,0:T(8,128)(2,1)S(1)}, u32[]{:S(2)}, u32[]{:S(2)}) %collective-permute-start.7) | collective-permute-done | bytes 1228832 | tf_op jit(solution)/shard_map/ppermute | solution.py:201
  35.4 1.5 %collective-permute-start.10 = (bf16[600,512]{1,0:T(8,128)(2,1)S(1)}, bf16[600,512]{1,0:T(8,128)(2,1)S(1)}, u32[]{:S(2)}, u32[]{:S(2)}) collective-permute-start(bf16[600,512]{1,0:T(8,128)(2,1)S(1)} %slice.17), channel_id=1, source_target_pairs={{0,2},{1,3},{2,0},{3,1},{4,6},{5,7},{6,4},{7,5},{8,10},{9,11},{10,... | collective-permute-start | bytes 1843208 | tf_op jit(solution)/shard_map/ppermute | solution.py:201
  36.9 0.6 collective-permute-start.9
  37.5 1.0 shard_map.91
  38.5 2.9 %shard_map.92 = (bf16[1024,448]{1,0:T(8,128)(2,1)S(1)}, f32[1024,152]{1,0:T(8,128)S(1)}, bf16[1024,1024]{1,0:T(8,128)(2,1)S(1)}) custom-call(bf16[600,256]{1,0:T(8,128)(2,1)S(1)} %collective-permute-done.3.refs_0_.refs_4_, bf16[600,256]{1,0:T(8,128)(2,1)S(1)} %collective-permute-done.4.refs_1_.refs_5_, ...), custom_call_target="tpu_custom_call" | custom-call | flops 1258291200 | bytes 2457600 | tf_op jit(solution)/shard_map/pallas_call | solution.py:180
  41.4 10.8 %shard_map.93 = (bf16[2048,1024]{1,0:T(8,128)(2,1)S(1)}, bf16[2048,1024]{1,0:T(8,128)(2,1)S(1)}, f32[2048,152]{1,0:T(8,128)S(1)}) custom-call(bf16[256,448]{1,0:T(8,128)(2,1)S(1)} %get-tuple-element.43.refs_0_, bf16[256,448]{1,0:T(8,128)(2,1)S(1)} %get-tuple-element.46.refs_1_, bf16[256,448]{1,0:T(8,128)(2,1)S(1)} %get-tuple-element.49.refs_2_, ...), custom_call_target="tpu_custom_call" | custom-call | flops 5033164800 | bytes 5537792 | tf_op jit(solution)/shard_map/pallas_call | solution.py:180
  52.3 5.5 %shard_map.94 = (bf16[2048,512]{1,0:T(8,128)(2,1)S(1)}, bf16[2048,512]{1,0:T(8,128)(2,1)S(1)}, f32[152,1024]{1,0:T(8,128)S(1)}, bf16[152,1024]{1,0:T(8,128)(2,1)S(1)}) custom-call(bf16[256,448]{1,0:T(8,128)(2,1)S(1)} %get-tuple-element.43.refs_0_, bf16[256,448]{1,0:T(8,128)(2,1)S(1)} %get-tuple-element.46.refs_1_, ...), custom_call_target="tpu_custom_call" | custom-call | flops 2516582400 | bytes 4308992 | tf_op jit(solution)/shard_map/pallas_call | solution.py:180
  57.8 1.0 shard_map.98
  58.9 1.6 %collective-permute-start.19 = (bf16[152,1024]{1,0:T(8,128)(2,1)S(1)}, bf16[152,1024]{1,0:T(8,128)(2,1)S(1)}, u32[]{:S(2)}, u32[]{:S(2)}) collective-permute-start(bf16[152,1024]{1,0:T(8,128)(2,1)S(1)} %shard_map.98), channel_id=1, source_target_pairs={{0,4},{1,5},{2,6},{3,7},{4,0},{5,1},{6,2},{7,3},{8,12},{9,13},{10,... | collective-permute-start | bytes 933896 | tf_op jit(solution)/shard_map/ppermute | solution.py:201
  60.4 0.8 shard_map.97
  61.3 0.6 collective-permute-start.18
  61.9 0.8 shard_map.99
  62.8 1.5 %collective-permute-start.20 = (bf16[152,1024]{1,0:T(8,128)(2,1)S(1)}, bf16[152,1024]{1,0:T(8,128)(2,1)S(1)}, u32[]{:S(2)}, u32[]{:S(2)}) collective-permute-start(bf16[152,1024]{1,0:T(8,128)(2,1)S(1)} %shard_map.99), channel_id=1, source_target_pairs={{0,6},{1,7},{2,4},{3,5},{4,2},{5,3},{6,0},{7,1},{8,14},{9,15},{10,... | collective-permute-start | bytes 933896 | tf_op jit(solution)/shard_map/ppermute | solution.py:201
  64.3 6.8 %collective-permute-start.12 = (bf16[152,256]{1,0:T(8,128)(2,1)S(1)}, bf16[152,256]{1,0:T(8,128)(2,1)S(1)}, u32[]{:S(2)}, u32[]{:S(2)}) collective-permute-start(bf16[152,256]{1,0:T(8,128)(2,1)S(1)} %get-tuple-element.73), channel_id=1, source_target_pairs={{0,24},{8,0},{16,8},{24,16},{1,25},{9,1},{17,9},{25,17},{2,26},{10... | collective-permute-start | bytes 233480 | tf_op jit(solution)/shard_map/ppermute | solution.py:194
  71.1 2.8 %collective-permute-done.12.refs_0_ = bf16[152,256]{1,0:T(8,128)(2,1)S(1)} collective-permute-done((bf16[152,256]{1,0:T(8,128)(2,1)S(1)}, bf16[152,256]{1,0:T(8,128)(2,1)S(1)}, u32[]{:S(2)}, u32[]{:S(2)}) %collective-permute-start.12) | collective-permute-done | bytes 77856 | tf_op jit(solution)/shard_map/ppermute | solution.py:194
  73.9 0.8 shard_map.96
  74.8 1.7 %collective-permute-done.13.refs_1_ = bf16[152,256]{1,0:T(8,128)(2,1)S(1)} collective-permute-done((bf16[152,256]{1,0:T(8,128)(2,1)S(1)}, bf16[152,256]{1,0:T(8,128)(2,1)S(1)}, u32[]{:S(2)}, u32[]{:S(2)}) %collective-permute-start.13) | collective-permute-done | bytes 77856 | tf_op jit(solution)/shard_map/ppermute | solution.py:194
  76.5 4.1 %collective-permute-done.14.refs_2_ = bf16[152,256]{1,0:T(8,128)(2,1)S(1)} collective-permute-done((bf16[152,256]{1,0:T(8,128)(2,1)S(1)}, bf16[152,256]{1,0:T(8,128)(2,1)S(1)}, u32[]{:S(2)}, u32[]{:S(2)}) %collective-permute-start.14) | collective-permute-done | bytes 77856 | tf_op jit(solution)/shard_map/ppermute | solution.py:194
  80.7 3.0 %collective-permute-start.16 = (bf16[152,256]{1,0:T(8,128)(2,1)S(1)}, bf16[152,256]{1,0:T(8,128)(2,1)S(1)}, u32[]{:S(2)}, u32[]{:S(2)}) collective-permute-start(bf16[152,256]{1,0:T(8,128)(2,1)S(1)} %shard_map.100.refs_0_), channel_id=1, source_target_pairs={{0,16},{8,24},{16,0},{24,8},{1,17},{9,25},{17,1},{25,9},{2,18},{10... | collective-permute-start | bytes 233480 | tf_op jit(solution)/shard_map/ppermute | solution.py:194
  83.7 0.8 collective-permute-start.17
  84.5 2.4 %collective-permute-done.15.refs_1_ = bf16[152,256]{1,0:T(8,128)(2,1)S(1)} collective-permute-done((bf16[152,256]{1,0:T(8,128)(2,1)S(1)}, bf16[152,256]{1,0:T(8,128)(2,1)S(1)}, u32[]{:S(2)}, u32[]{:S(2)}) %collective-permute-start.15) | collective-permute-done | bytes 77856 | tf_op jit(solution)/shard_map/ppermute | solution.py:194
  86.9 1.2 %collective-permute-done.17.refs_3_ = bf16[152,256]{1,0:T(8,128)(2,1)S(1)} collective-permute-done((bf16[152,256]{1,0:T(8,128)(2,1)S(1)}, bf16[152,256]{1,0:T(8,128)(2,1)S(1)}, u32[]{:S(2)}, u32[]{:S(2)}) %collective-permute-start.17) | collective-permute-done | bytes 77856 | tf_op jit(solution)/shard_map/ppermute | solution.py:194
  88.1 0.5 collective-permute-start.22
  90.0 0.8 shard_map.102
  90.9 1.6 %collective-permute-start.25 = (bf16[152,1024]{1,0:T(8,128)(2,1)S(1)}, bf16[152,1024]{1,0:T(8,128)(2,1)S(1)}, u32[]{:S(2)}, u32[]{:S(2)}) collective-permute-start(bf16[152,1024]{1,0:T(8,128)(2,1)S(1)} %shard_map.102), channel_id=1, source_target_pairs={{0,2},{1,3},{2,0},{3,1},{4,6},{5,7},{6,4},{7,5},{8,10},{9,11},{10,... | collective-permute-start | bytes 933896 | tf_op jit(solution)/shard_map/ppermute | solution.py:201
  92.4 0.8 shard_map.103
  93.3 0.9 collective-permute-start.26
  94.2 0.8 shard_map.104
  95.1 1.2 %collective-permute-start.27 = (bf16[152,1024]{1,0:T(8,128)(2,1)S(1)}, bf16[152,1024]{1,0:T(8,128)(2,1)S(1)}, u32[]{:S(2)}, u32[]{:S(2)}) collective-permute-start(bf16[152,1024]{1,0:T(8,128)(2,1)S(1)} %shard_map.104), channel_id=1, source_target_pairs={{0,6},{1,7},{2,4},{3,5},{4,2},{5,3},{6,0},{7,1},{8,14},{9,15},{10,... | collective-permute-start | bytes 933896 | tf_op jit(solution)/shard_map/ppermute | solution.py:201
  96.3 1.0 fusion.1
  97.3 0.8 shard_map.101
  98.1 3.0 %collective-permute-done.25 = bf16[152,1024]{1,0:T(8,128)(2,1)S(1)} collective-permute-done((bf16[152,1024]{1,0:T(8,128)(2,1)S(1)}, bf16[152,1024]{1,0:T(8,128)(2,1)S(1)}, u32[]{:S(2)}, u32[]{:S(2)}) %collective-permute-start.25) | collective-permute-done | bytes 311328 | tf_op jit(solution)/shard_map/ppermute | solution.py:201
  101.1 8.2 %collective-permute-done.26 = bf16[152,1024]{1,0:T(8,128)(2,1)S(1)} collective-permute-done((bf16[152,1024]{1,0:T(8,128)(2,1)S(1)}, bf16[152,1024]{1,0:T(8,128)(2,1)S(1)}, u32[]{:S(2)}, u32[]{:S(2)}) %collective-permute-start.26) | collective-permute-done | bytes 311328 | tf_op jit(solution)/shard_map/ppermute | solution.py:201
  109.4 1.1 fusion.4
  (45 shorter events, 2.2 us)
Async XLA Ops:
  0.6 1.0 copy-start
  1.6 1.2 %copy-start.2 = (bf16[440,1024]{1,0:T(8,128)(2,1)S(1)}, bf16[440,1024]{1,0:T(8,128)(2,1)}, u32[]{:S(2)}) copy-start(bf16[440,1024]{1,0:T(8,128)(2,1)} %w_hbm.1) | copy-start | bytes 2703364
  2.8 0.7 copy-start.5
  3.5 4.9 %copy-start.3 = (bf16[147,256]{1,0:T(8,128)(2,1)S(1)}, bf16[147,256]{1,0:T(8,128)(2,1)}, u32[]{:S(2)}) copy-start(bf16[147,256]{1,0:T(8,128)(2,1)} %refs_3_.1) | copy-start | bytes 225796
  3.5 4.9 %copy-start.4 = (bf16[440,256]{1,0:T(8,128)(2,1)S(1)}, bf16[440,256]{1,0:T(8,128)(2,1)}, u32[]{:S(2)}) copy-start(bf16[440,256]{1,0:T(8,128)(2,1)} %x_hbm.1) | copy-start | bytes 675844
  3.5 4.9 %copy-start.6 = (s32[256]{0:T(256)S(1)}, s32[256]{0:T(256)}, u32[]{:S(2)}) copy-start(s32[256]{0:T(256)} %param.9) | copy-start | bytes 3076
  3.9 30.2 %collective-permute-start.8 = (bf16[600,1024]{1,0:T(8,128)(2,1)S(1)}, bf16[600,1024]{1,0:T(8,128)(2,1)S(1)}, u32[]{:S(2)}, u32[]{:S(2)}) collective-permute-start(bf16[600,1024]{1,0:T(8,128)(2,1)S(1)} %shard_map.87.refs_1_.refs_4_), channel_id=1, source_target_pairs={{0,4},{1,5},{2,6},{3,7},{4,0},{5,1},{6,2},{7,3},{8,12},{9,13},{10,... | collective-permute-start | bytes 3686408 | tf_op jit(solution)/shard_map/ppermute | solution.py:201
  6.9 28.5 %collective-permute-start.7 = (bf16[600,1024]{1,0:T(8,128)(2,1)S(1)}, bf16[600,1024]{1,0:T(8,128)(2,1)S(1)}, u32[]{:S(2)}, u32[]{:S(2)}) collective-permute-start(bf16[600,1024]{1,0:T(8,128)(2,1)S(1)} %shard_map.87.refs_1_.refs_4_), channel_id=1, source_target_pairs={{0,2},{1,3},{2,0},{3,1},{4,6},{5,7},{6,4},{7,5},{8,10},{9,11},{10,... | collective-permute-start | bytes 3686408 | tf_op jit(solution)/shard_map/ppermute | solution.py:201
  8.9 12.2 %collective-permute-start = (bf16[600,256]{1,0:T(8,128)(2,1)S(1)}, bf16[600,256]{1,0:T(8,128)(2,1)S(1)}, u32[]{:S(2)}, u32[]{:S(2)}) collective-permute-start(bf16[600,256]{1,0:T(8,128)(2,1)S(1)} %shard_map.86.refs_0_), channel_id=1, source_target_pairs={{0,8},{8,16},{16,24},{24,0},{1,9},{9,17},{17,25},{25,1},{2,10},{10... | collective-permute-start | bytes 921608 | tf_op jit(solution)/shard_map/ppermute | solution.py:194
  10.5 22.0 %collective-permute-start.1 = (bf16[600,256]{1,0:T(8,128)(2,1)S(1)}, bf16[600,256]{1,0:T(8,128)(2,1)S(1)}, u32[]{:S(2)}, u32[]{:S(2)}) collective-permute-start(bf16[600,256]{1,0:T(8,128)(2,1)S(1)} %shard_map.86.refs_0_), channel_id=1, source_target_pairs={{0,16},{8,24},{16,0},{24,8},{1,17},{9,25},{17,1},{25,9},{2,18},{10... | collective-permute-start | bytes 921608 | tf_op jit(solution)/shard_map/ppermute | solution.py:194
  13.1 20.4 %collective-permute-start.2 = (bf16[600,256]{1,0:T(8,128)(2,1)S(1)}, bf16[600,256]{1,0:T(8,128)(2,1)S(1)}, u32[]{:S(2)}, u32[]{:S(2)}) collective-permute-start(bf16[600,256]{1,0:T(8,128)(2,1)S(1)} %shard_map.86.refs_0_), channel_id=1, source_target_pairs={{0,24},{8,0},{16,8},{24,16},{1,25},{9,1},{17,9},{25,17},{2,26},{10... | collective-permute-start | bytes 921608 | tf_op jit(solution)/shard_map/ppermute | solution.py:194
  21.1 15.8 %collective-permute-start.3 = (bf16[600,256]{1,0:T(8,128)(2,1)S(1)}, bf16[600,256]{1,0:T(8,128)(2,1)S(1)}, u32[]{:S(2)}, u32[]{:S(2)}) collective-permute-start(bf16[600,256]{1,0:T(8,128)(2,1)S(1)} %shard_map.86.refs_0_), channel_id=1, source_target_pairs={{0,1},{1,0},{2,3},{3,2},{4,5},{5,4},{6,7},{7,6},{8,9},{9,8},{10,11... | collective-permute-start | bytes 921608 | tf_op jit(solution)/shard_map/ppermute | solution.py:191
  32.6 5.9 %collective-permute-start.5 = (bf16[600,256]{1,0:T(8,128)(2,1)S(1)}, bf16[600,256]{1,0:T(8,128)(2,1)S(1)}, u32[]{:S(2)}, u32[]{:S(2)}) collective-permute-start(bf16[600,256]{1,0:T(8,128)(2,1)S(1)} %collective-permute-done.1.refs_0_.refs_2_), channel_id=1, source_target_pairs={{0,1},{1,0},{2,3},{3,2},{4,5},{5,4},{6,7},{7,6},{8,9},{9,8},{10,11... | collective-permute-start | bytes 921608 | tf_op jit(solution)/shard_map/ppermute | solution.py:191
  33.5 4.9 %collective-permute-start.6 = (bf16[600,256]{1,0:T(8,128)(2,1)S(1)}, bf16[600,256]{1,0:T(8,128)(2,1)S(1)}, u32[]{:S(2)}, u32[]{:S(2)}) collective-permute-start(bf16[600,256]{1,0:T(8,128)(2,1)S(1)} %collective-permute-done.2.refs_0_.refs_3_), channel_id=1, source_target_pairs={{0,1},{1,0},{2,3},{3,2},{4,5},{5,4},{6,7},{7,6},{8,9},{9,8},{10,11... | collective-permute-start | bytes 921608 | tf_op jit(solution)/shard_map/ppermute | solution.py:191
  34.1 4.4 %collective-permute-start.4 = (bf16[600,256]{1,0:T(8,128)(2,1)S(1)}, bf16[600,256]{1,0:T(8,128)(2,1)S(1)}, u32[]{:S(2)}, u32[]{:S(2)}) collective-permute-start(bf16[600,256]{1,0:T(8,128)(2,1)S(1)} %collective-permute-done.refs_0_.refs_1_), channel_id=1, source_target_pairs={{0,1},{1,0},{2,3},{3,2},{4,5},{5,4},{6,7},{7,6},{8,9},{9,8},{10,11... | collective-permute-start | bytes 921608 | tf_op jit(solution)/shard_map/ppermute | solution.py:191
  35.4 16.8 %collective-permute-start.10 = (bf16[600,512]{1,0:T(8,128)(2,1)S(1)}, bf16[600,512]{1,0:T(8,128)(2,1)S(1)}, u32[]{:S(2)}, u32[]{:S(2)}) collective-permute-start(bf16[600,512]{1,0:T(8,128)(2,1)S(1)} %slice.17), channel_id=1, source_target_pairs={{0,2},{1,3},{2,0},{3,1},{4,6},{5,7},{6,4},{7,5},{8,10},{9,11},{10,... | collective-permute-start | bytes 1843208 | tf_op jit(solution)/shard_map/ppermute | solution.py:201
  36.9 15.3 %collective-permute-start.9 = (bf16[600,512]{1,0:T(8,128)(2,1)S(1)}, bf16[600,512]{1,0:T(8,128)(2,1)S(1)}, u32[]{:S(2)}, u32[]{:S(2)}) collective-permute-start(bf16[600,512]{1,0:T(8,128)(2,1)S(1)} %slice.16), channel_id=1, source_target_pairs={{0,4},{1,5},{2,6},{3,7},{4,0},{5,1},{6,2},{7,3},{8,12},{9,13},{10,... | collective-permute-start | bytes 1843208 | tf_op jit(solution)/shard_map/ppermute | solution.py:201
  57.8 6.5 %collective-permute-start.11 = (bf16[152,1024]{1,0:T(8,128)(2,1)S(1)}, bf16[152,1024]{1,0:T(8,128)(2,1)S(1)}, u32[]{:S(2)}, u32[]{:S(2)}) collective-permute-start(bf16[152,1024]{1,0:T(8,128)(2,1)S(1)} %get-tuple-element.61), channel_id=1, source_target_pairs={{0,1},{1,0},{2,3},{3,2},{4,5},{5,4},{6,7},{7,6},{8,9},{9,8},{10,11... | collective-permute-start | bytes 933896 | tf_op jit(solution)/shard_map/ppermute | solution.py:191
  58.9 24.8 %collective-permute-start.19 = (bf16[152,1024]{1,0:T(8,128)(2,1)S(1)}, bf16[152,1024]{1,0:T(8,128)(2,1)S(1)}, u32[]{:S(2)}, u32[]{:S(2)}) collective-permute-start(bf16[152,1024]{1,0:T(8,128)(2,1)S(1)} %shard_map.98), channel_id=1, source_target_pairs={{0,4},{1,5},{2,6},{3,7},{4,0},{5,1},{6,2},{7,3},{8,12},{9,13},{10,... | collective-permute-start | bytes 933896 | tf_op jit(solution)/shard_map/ppermute | solution.py:201
  61.3 23.2 %collective-permute-start.18 = (bf16[152,1024]{1,0:T(8,128)(2,1)S(1)}, bf16[152,1024]{1,0:T(8,128)(2,1)S(1)}, u32[]{:S(2)}, u32[]{:S(2)}) collective-permute-start(bf16[152,1024]{1,0:T(8,128)(2,1)S(1)} %shard_map.97), channel_id=1, source_target_pairs={{0,2},{1,3},{2,0},{3,1},{4,6},{5,7},{6,4},{7,5},{8,10},{9,11},{10,... | collective-permute-start | bytes 933896 | tf_op jit(solution)/shard_map/ppermute | solution.py:201
  62.8 21.8 %collective-permute-start.20 = (bf16[152,1024]{1,0:T(8,128)(2,1)S(1)}, bf16[152,1024]{1,0:T(8,128)(2,1)S(1)}, u32[]{:S(2)}, u32[]{:S(2)}) collective-permute-start(bf16[152,1024]{1,0:T(8,128)(2,1)S(1)} %shard_map.99), channel_id=1, source_target_pairs={{0,6},{1,7},{2,4},{3,5},{4,2},{5,3},{6,0},{7,1},{8,14},{9,15},{10,... | collective-permute-start | bytes 933896 | tf_op jit(solution)/shard_map/ppermute | solution.py:201
  64.3 9.6 %collective-permute-start.12 = (bf16[152,256]{1,0:T(8,128)(2,1)S(1)}, bf16[152,256]{1,0:T(8,128)(2,1)S(1)}, u32[]{:S(2)}, u32[]{:S(2)}) collective-permute-start(bf16[152,256]{1,0:T(8,128)(2,1)S(1)} %get-tuple-element.73), channel_id=1, source_target_pairs={{0,24},{8,0},{16,8},{24,16},{1,25},{9,1},{17,9},{25,17},{2,26},{10... | collective-permute-start | bytes 233480 | tf_op jit(solution)/shard_map/ppermute | solution.py:194
  71.1 5.4 %collective-permute-start.13 = (bf16[152,256]{1,0:T(8,128)(2,1)S(1)}, bf16[152,256]{1,0:T(8,128)(2,1)S(1)}, u32[]{:S(2)}, u32[]{:S(2)}) collective-permute-start(bf16[152,256]{1,0:T(8,128)(2,1)S(1)} %get-tuple-element.74), channel_id=1, source_target_pairs={{0,16},{8,24},{16,0},{24,8},{1,17},{9,25},{17,1},{25,9},{2,18},{10... | collective-permute-start | bytes 233480 | tf_op jit(solution)/shard_map/ppermute | solution.py:194
  73.9 6.7 %collective-permute-start.14 = (bf16[152,256]{1,0:T(8,128)(2,1)S(1)}, bf16[152,256]{1,0:T(8,128)(2,1)S(1)}, u32[]{:S(2)}, u32[]{:S(2)}) collective-permute-start(bf16[152,256]{1,0:T(8,128)(2,1)S(1)} %get-tuple-element.75), channel_id=1, source_target_pairs={{0,8},{8,16},{16,24},{24,0},{1,9},{9,17},{17,25},{25,1},{2,10},{10... | collective-permute-start | bytes 233480 | tf_op jit(solution)/shard_map/ppermute | solution.py:194
  80.6 6.3 %collective-permute-start.15 = (bf16[152,256]{1,0:T(8,128)(2,1)S(1)}, bf16[152,256]{1,0:T(8,128)(2,1)S(1)}, u32[]{:S(2)}, u32[]{:S(2)}) collective-permute-start(bf16[152,256]{1,0:T(8,128)(2,1)S(1)} %shard_map.100.refs_0_), channel_id=1, source_target_pairs={{0,8},{8,16},{16,24},{24,0},{1,9},{9,17},{17,25},{25,1},{2,10},{10... | collective-permute-start | bytes 233480 | tf_op jit(solution)/shard_map/ppermute | solution.py:194
  80.7 6.2 %collective-permute-start.16 = (bf16[152,256]{1,0:T(8,128)(2,1)S(1)}, bf16[152,256]{1,0:T(8,128)(2,1)S(1)}, u32[]{:S(2)}, u32[]{:S(2)}) collective-permute-start(bf16[152,256]{1,0:T(8,128)(2,1)S(1)} %shard_map.100.refs_0_), channel_id=1, source_target_pairs={{0,16},{8,24},{16,0},{24,8},{1,17},{9,25},{17,1},{25,9},{2,18},{10... | collective-permute-start | bytes 233480 | tf_op jit(solution)/shard_map/ppermute | solution.py:194
  83.7 4.4 %collective-permute-start.17 = (bf16[152,256]{1,0:T(8,128)(2,1)S(1)}, bf16[152,256]{1,0:T(8,128)(2,1)S(1)}, u32[]{:S(2)}, u32[]{:S(2)}) collective-permute-start(bf16[152,256]{1,0:T(8,128)(2,1)S(1)} %shard_map.100.refs_0_), channel_id=1, source_target_pairs={{0,24},{8,0},{16,8},{24,16},{1,25},{9,1},{17,9},{25,17},{2,26},{10... | collective-permute-start | bytes 233480 | tf_op jit(solution)/shard_map/ppermute | solution.py:194
  88.1 1.7 %collective-permute-start.21 = (bf16[152,256]{1,0:T(8,128)(2,1)S(1)}, bf16[152,256]{1,0:T(8,128)(2,1)S(1)}, u32[]{:S(2)}, u32[]{:S(2)}) collective-permute-start(bf16[152,256]{1,0:T(8,128)(2,1)S(1)} %shard_map.100.refs_0_), channel_id=1, source_target_pairs={{0,1},{1,0},{2,3},{3,2},{4,5},{5,4},{6,7},{7,6},{8,9},{9,8},{10,11... | collective-permute-start | bytes 233480 | tf_op jit(solution)/shard_map/ppermute | solution.py:191
  88.1 1.7 %collective-permute-start.22 = (bf16[152,256]{1,0:T(8,128)(2,1)S(1)}, bf16[152,256]{1,0:T(8,128)(2,1)S(1)}, u32[]{:S(2)}, u32[]{:S(2)}) collective-permute-start(bf16[152,256]{1,0:T(8,128)(2,1)S(1)} %collective-permute-done.15.refs_1_), channel_id=1, source_target_pairs={{0,1},{1,0},{2,3},{3,2},{4,5},{5,4},{6,7},{7,6},{8,9},{9,8},{10,11... | collective-permute-start | bytes 233480 | tf_op jit(solution)/shard_map/ppermute | solution.py:191
  88.6 1.3 %collective-permute-start.23 = (bf16[152,256]{1,0:T(8,128)(2,1)S(1)}, bf16[152,256]{1,0:T(8,128)(2,1)S(1)}, u32[]{:S(2)}, u32[]{:S(2)}) collective-permute-start(bf16[152,256]{1,0:T(8,128)(2,1)S(1)} %collective-permute-done.16.refs_2_), channel_id=1, source_target_pairs={{0,1},{1,0},{2,3},{3,2},{4,5},{5,4},{6,7},{7,6},{8,9},{9,8},{10,11... | collective-permute-start | bytes 233480 | tf_op jit(solution)/shard_map/ppermute | solution.py:191
  88.6 1.4 %collective-permute-start.24 = (bf16[152,256]{1,0:T(8,128)(2,1)S(1)}, bf16[152,256]{1,0:T(8,128)(2,1)S(1)}, u32[]{:S(2)}, u32[]{:S(2)}) collective-permute-start(bf16[152,256]{1,0:T(8,128)(2,1)S(1)} %collective-permute-done.17.refs_3_), channel_id=1, source_target_pairs={{0,1},{1,0},{2,3},{3,2},{4,5},{5,4},{6,7},{7,6},{8,9},{9,8},{10,11... | collective-permute-start | bytes 233480 | tf_op jit(solution)/shard_map/ppermute | solution.py:191
  90.9 10.3 %collective-permute-start.25 = (bf16[152,1024]{1,0:T(8,128)(2,1)S(1)}, bf16[152,1024]{1,0:T(8,128)(2,1)S(1)}, u32[]{:S(2)}, u32[]{:S(2)}) collective-permute-start(bf16[152,1024]{1,0:T(8,128)(2,1)S(1)} %shard_map.102), channel_id=1, source_target_pairs={{0,2},{1,3},{2,0},{3,1},{4,6},{5,7},{6,4},{7,5},{8,10},{9,11},{10,... | collective-permute-start | bytes 933896 | tf_op jit(solution)/shard_map/ppermute | solution.py:201
  93.3 16.1 %collective-permute-start.26 = (bf16[152,1024]{1,0:T(8,128)(2,1)S(1)}, bf16[152,1024]{1,0:T(8,128)(2,1)S(1)}, u32[]{:S(2)}, u32[]{:S(2)}) collective-permute-start(bf16[152,1024]{1,0:T(8,128)(2,1)S(1)} %shard_map.103), channel_id=1, source_target_pairs={{0,4},{1,5},{2,6},{3,7},{4,0},{5,1},{6,2},{7,3},{8,12},{9,13},{10,... | collective-permute-start | bytes 933896 | tf_op jit(solution)/shard_map/ppermute | solution.py:201
  95.1 14.3 %collective-permute-start.27 = (bf16[152,1024]{1,0:T(8,128)(2,1)S(1)}, bf16[152,1024]{1,0:T(8,128)(2,1)S(1)}, u32[]{:S(2)}, u32[]{:S(2)}) collective-permute-start(bf16[152,1024]{1,0:T(8,128)(2,1)S(1)} %shard_map.104), channel_id=1, source_target_pairs={{0,6},{1,7},{2,4},{3,5},{4,2},{5,3},{6,0},{7,1},{8,14},{9,15},{10,... | collective-permute-start | bytes 933896 | tf_op jit(solution)/shard_map/ppermute | solution.py:201
  97.3 12.1 %copy-start.1 = (bf16[147,1024]{1,0:T(8,128)(2,1)S(1)}, bf16[147,1024]{1,0:T(8,128)(2,1)}, u32[]{:S(2)}) copy-start(bf16[147,1024]{1,0:T(8,128)(2,1)} %d_hbm.1) | copy-start | bytes 903172

commit v5 on v4

--- a/solution.py
+++ b/solution.py
@@ -10,7 +10,7 @@
 
 F32, BF16 = jnp.float32, jnp.bfloat16
 VMEM = 16 * 2**20
-COEFS = (0.99999921, -19.73898036, 64.92865742, -85.27162153, 58.79049212, -21.07110563)
+COEFS = (0.99995902, -19.73094237, 64.67144178, -82.39080631, 45.6210511)
 ROUNDER = 12582912.0
 
 
@@ -24,7 +24,7 @@
 
 def cosine(angle):
     turns = angle * (0.5 / math.pi)
-    rest = turns - ((turns + ROUNDER) - ROUNDER)
+    rest = turns - jnp.round(turns)
     square = rest * rest
     total = square * COEFS[-1] + COEFS[-2]
     for coef in COEFS[-3::-1]:
@@ -110,23 +110,21 @@
                 f_ref[spot : spot + block, :], tangent = one_block(xt, w_ref, depth)
                 total = total + tangent
             if not last:
-                out_refs[0][spot : spot + block, :] = total
+                here = spot % out_refs[0].shape[0]
+                out_refs[spot // out_refs[0].shape[0]][here : here + block, :] = total
             else:
-                out_ref = out_refs[spot // out_refs[0].shape[1]]
-                at_out = spot % out_ref.shape[1]
-                out_ref[:, at_out : at_out + block] = total.T.astype(out_ref.dtype)
+                out_refs[0][:, spot : spot + block] = total.T.astype(out_refs[0].dtype)
             spot += block
 
 
-def make_next(xts, totals, pieces, depth, wide, block, last):
+def make_next(xts, totals, pieces, depth, wide, block, last=None):
     n, f = sum(a.shape[0] for a in xts), pieces[0].shape[1]
     shapes = [jax.ShapeDtypeStruct((n, f), BF16)] * len(pieces)
-    if last:
-        shapes.append(jax.ShapeDtypeStruct((wide, n // 2), F32))
-        shapes.append(jax.ShapeDtypeStruct((wide, n // 2), BF16))
+    if last is None:
+        shapes += [jax.ShapeDtypeStruct((n // 2, wide), F32)] * 2
     else:
-        shapes.append(jax.ShapeDtypeStruct((n, wide), F32))
-    kernel = functools.partial(next_kernel, depth, len(xts), len(totals), len(pieces), block, last)
+        shapes.append(jax.ShapeDtypeStruct((wide, n), last))
+    kernel = functools.partial(next_kernel, depth, len(xts), len(totals), len(pieces), block, last is not None)
     out = whole(kernel, shapes, *xts, *totals, *pieces, flops=2 * n * f * len(pieces) * (depth + wide))
     return out[: len(pieces)], out[len(pieces) :]
 
@@ -151,8 +149,8 @@
     c_ref[classes:, :] = jnp.zeros((c_ref.shape[0] - classes, c_ref.shape[1]), BF16)
 
 
-def share_kernel(count, skip, block, halves, *refs):
-    left_refs, f_refs, o_ref = refs[:count], refs[count:-1], refs[-1]
+def share_kernel(count, skip, block, halves, outs, *refs):
+    left_refs, f_refs, o_refs = refs[:count], refs[count:-outs], refs[-outs:]
     each = len(f_refs) // halves
     f = f_refs[0].shape[1]
     for h in range(halves):
@@ -161,15 +159,29 @@
         for left_ref, (f_ref, at) in zip(left_refs, f_blocks, strict=True):
             part = jnp.dot(left_ref[skip:, :], f_ref[at : at + block, :], preferred_element_type=F32)
             total = part if total is None else total + part
-        o_ref[:, h * f : (h + 1) * f] = total.astype(o_ref.dtype)
-
-
-def make_share(lefts, skip, feats, dtype):
+        if outs == 1:
+            o_refs[0][:, h * f : (h + 1) * f] = total.astype(o_refs[0].dtype)
+        else:
+            o_refs[h][...] = total.astype(o_refs[h].dtype)
+
+
+def add_kernel(side, own_ref, *refs):
+    add_refs, o_ref = refs[:-1], refs[-1]
+    half = own_ref.shape[1] // 2
+    for h in (0, 1):
+        here = slice(h * half, (h + 1) * half)
+        total = own_ref[:, here]
+        for ref in add_refs if h == side else ():
+            total = total + ref[...].astype(F32)
+        o_ref[:, here] = total.astype(o_ref.dtype)
+
+
+def make_share(lefts, skip, feats, dtype, apart=False):
     block = lefts[0].shape[1]
     wide, n, f = lefts[0].shape[0] - skip, block * len(lefts), sum(h[0].shape[1] for h in feats)
     return whole(
-        functools.partial(share_kernel, len(lefts), skip, block, len(feats)),
-        jax.ShapeDtypeStruct((wide, f), dtype),
+        functools.partial(share_kernel, len(lefts), skip, block, len(feats), len(feats) if apart else 1),
+        [jax.ShapeDtypeStruct((wide, f // 2), dtype)] * 2 if apart else jax.ShapeDtypeStruct((wide, f), dtype),
         *lefts, *[a for h in feats for a in h], flops=2 * n * f * wide,
     )
 
@@ -191,7 +203,12 @@
         return lax.ppermute(a, "feat", [(i, i ^ 1) for i in range(2 * xs * ys)])
 
     def along(a, k):
-        return lax.ppermute(a, "samp", [(i, (i + k) % line) for i in range(line)])
+        def to(i):
+            return i ^ abs(k) if line & (line - 1) == 0 else (i + k) % line
+
+        return lax.ppermute(a, "samp", [(i, to(i)) for i in range(line)])
+
+    places = (1, 2, 3) if line == 4 else range(1, line)
 
     def across(a, dy, dx):
         def to(i):
@@ -218,7 +235,7 @@
         jax.ShapeDtypeStruct((rows, own), BF16),
         inputs, probs, labels[None, :],
     )
-    x_line = [x_own] + [along(x_own, k) for k in range(1, line)]
+    x_line = [x_own] + [along(x_own, k) for k in places]
 
     feats = {at: [[]] for at in offsets}
     xts, totals = [], []
@@ -243,45 +260,64 @@
     first(x_peer)
     blocks = x_line + x_peer
     near = list(ws)
-    for group in (near, far):
-        if group:
-            last = group is far or not far
-            pieces = [ws[at] for at in near] if group is near else [w for at in far for w in halves[at]]
-            got, rest = make_next(xts, totals, pieces, depth, wide, own, last)
-            for j, at in enumerate(group):
-                feats[at] = [[got[j]]] if group is near else [[got[2 * j]], [got[2 * j + 1]]]
-            totals = rest
-    t_own, t_other = rest
+    got, totals = make_next(xts, totals, [ws[at] for at in near], depth, wide, own)
+    for at, piece in zip(near, got, strict=True):
+        feats[at] = [[piece]]
+
+    def share(at, lefts, skip):
+        return make_share(lefts, skip, feats[at], F32 if at == (0, 0) else BF16)
+
+    def home(at, part):
+        return across(part, -at[0], -at[1])
+
+    parts = {at: share(at, blocks, depth) for at in near}
+    totals, parts = lax.optimization_barrier((totals, parts))
+    arrived = {at: home(at, parts[at]) for at in near}
+    turned = []
+    pieces = [w for at in far for w in halves[at]]
+    for some, total, dtype in ((xts[-1:], totals[1], BF16), (xts[:-1], totals[0], F32)):
+        got, (out,) = make_next(some, [total], pieces, depth, wide, own, dtype)
+        turned.append((got, out))
+    for j, at in enumerate(far):
+        feats[at] = [[turned[1][0][2 * j + h], turned[0][0][2 * j + h]] for h in (0, 1)]
+    t_other, t_own = turned[0][1], turned[1][1]
     t_got = swap_core(t_other)
-    lefts = blocks
     keep, *send = whole(
         spread_kernel,
         [jax.ShapeDtypeStruct((wide, own), F32)] + [jax.ShapeDtypeStruct((wide, own), BF16)] * (line - 1),
         t_own, t_got,
     )
-    got = [along(a, -k) for k, a in enumerate(send, 1)]
-
-    def collect(parts):
+    got = [along(a, -k) for k, a in zip(places, send, strict=True)]
+
+    def collect(parts, some):
         out = parts[0, 0]
-        for dy, dx in offsets[1:]:
+        for dy, dx in some:
             out = out + parts[dy, dx].astype(F32)
         return out[:classes]
 
-    def send_home(lefts, skip):
-        parts = {at: make_share(lefts, skip, feats[at], F32 if at == (0, 0) else BF16) for at in offsets[::-1]}
-        return parts, {(dy, dx): across(parts[dy, dx], -dy, -dx) for dy, dx in offsets[1:]}
-
-    parts, arrived = send_home(lefts, depth)
+    parts.update({at: share(at, blocks, depth) for at in far + [(0, 0)]})
+    arrived.update({at: home(at, parts[at]) for at in far})
     keep, parts = lax.optimization_barrier((keep, parts))
     curv = whole(
         functools.partial(curve_kernel, classes), jax.ShapeDtypeStruct((wide, own), BF16), keep, *got, probs
     )
-    c_line = [curv] + [along(curv, k) for k in range(1, line)]
+    c_line = [curv] + [along(curv, k) for k in places]
     c_line, arrived = lax.optimization_barrier((c_line, arrived))
     curvs = c_line + [swap_core(a) for a in c_line]
-    gradient = collect({(0, 0): parts[0, 0], **arrived})
-    parts, arrived = send_home(curvs, 0)
-    hess_vec = collect({(0, 0): parts[0, 0], **arrived}) + damping[0] * direction.astype(F32)
+    gradient = collect({(0, 0): parts[0, 0], **arrived}, offsets[1:])
+    thirds = {at: make_share(curvs, 0, feats[at], BF16, apart=True) for at in far}
+    curvs, thirds = lax.optimization_barrier((curvs, thirds))
+    first_half = {(dy, dx): across(thirds[dy, dx][0], 0, -dx) for dy, dx in far}
+    second_half = {(dy, dx): across(thirds[dy, dx][1], -dy, 0) for dy, dx in far}
+    parts, arrived = {}, {}
+    for at in near:
+        plain = make_share(curvs, 0, feats[at], F32)
+        others = [first_half[f] if at[0] else second_half[f] for f in far if at[0] in (0, f[0]) and at[1] in (0, f[1])]
+        h = 0 if at[0] else 1
+        parts[at] = whole(functools.partial(add_kernel, h), jax.ShapeDtypeStruct(plain.shape, BF16), plain, *others)
+        arrived[at] = home(at, parts[at])
+    parts[0, 0] = share((0, 0), curvs, 0)
+    hess_vec = collect({(0, 0): parts[0, 0], **arrived}, near) + damping[0] * direction.astype(F32)
     return (hess_vec, gradient)
 
 

time: 111 us -> 106 us (0.955)
  Pallas kernels: 31 us -> 28.4 us
  waiting for transfers between devices: 41 us -> 39.7 us
    ppermute x10 -> x11, waiting for transfers between devices: 12.4 us -> 9.68 us  [across(): return lax.ppermute(a, 'feat', [(i, to(i)) for i in range(2 * xs * ys)])]
    pallas_call x17 -> x20, Pallas kernels: 30.1 us -> 27.5 us  [whole(): pl.pallas_call(kernel, out_shape=shapes, compiler_params=params(), cost_e...]
    ppermute x10 -> x11, starting transfers between devices: 14 us -> 13.5 us  [across(): return lax.ppermute(a, 'feat', [(i, to(i)) for i in range(2 * xs * ys)])]
  transfers between devices with their start and end apart: 28 -> 29, of which waited for: 12 -> 16; matrix products, arithmetic and copies ran while one was open for 1% -> 1% of each run, Pallas kernels for 22% -> 23%
where the time goes in v5:
time: 106 us
  waiting for transfers between devices  39.7 us (37%)
  starting transfers between devices  31.4 us (30%)
  Pallas kernels  28.4 us (27%)
  local copies, waits for them, and re-layouts  2.93 us (3%)
  other arithmetic  2 us (2%)
  between operations  1.52 us (1%)
    ppermute x9, waiting for transfers between devices, along(): return lax.ppermute(a, 'samp', [(i, to(i)) for i in range(line)])  29.1 us
    pallas_call x20, Pallas kernels, whole(): pl.pallas_call(kernel, out_shape=shapes, compiler_params=params(), cost_e...  27.5 us
    ppermute x9, starting transfers between devices, along(): return lax.ppermute(a, 'samp', [(i, to(i)) for i in range(line)])  16.1 us
    ppermute x11, starting transfers between devices, across(): return lax.ppermute(a, 'feat', [(i, to(i)) for i in range(2 * xs * ys)])  13.5 us
    ppermute x11, waiting for transfers between devices, across(): return lax.ppermute(a, 'feat', [(i, to(i)) for i in range(2 * xs * ys)])  9.68 us
    unnamed x14, local copies, waits for them, and re-layouts  2.84 us
  transfers between devices with their start and end apart: 29, of which 16 were waited for; matrix products, arithmetic and copies ran while one was open for 1% of the time, Pallas kernels for 23%

profile of v5, /device:TPU:0, one launch (start us, length us, event | category | flops | bytes accessed | tf_op | source)
XLA Modules:
  0.0 106.0 jit_solution(9999291038155961383)
XLA Ops:
  0.6 1.0 copy-done
  1.6 1.2 %copy-done.2 = bf16[440,1024]{1,0:T(8,128)(2,1)S(1)} copy-done((bf16[440,1024]{1,0:T(8,128)(2,1)S(1)}, bf16[440,1024]{1,0:T(8,128)(2,1)}, u32[]{:S(2)}) %copy-start.2) | copy-done | bytes 901144
  2.8 0.7 copy-done.5
  3.9 3.0 %collective-permute-start.8 = (bf16[600,1024]{1,0:T(8,128)(2,1)S(1)}, bf16[600,1024]{1,0:T(8,128)(2,1)S(1)}, u32[]{:S(2)}, u32[]{:S(2)}) collective-permute-start(bf16[600,1024]{1,0:T(8,128)(2,1)S(1)} %shard_map.87.refs_1_.refs_4_), channel_id=1, source_target_pairs={{0,4},{1,5},{2,6},{3,7},{4,0},{5,1},{6,2},{7,3},{8,12},{9,13},{10,... | collective-permute-start | bytes 3686408 | tf_op jit(solution)/shard_map/ppermute | solution.py:218
  6.9 1.5 %collective-permute-start.7 = (bf16[600,1024]{1,0:T(8,128)(2,1)S(1)}, bf16[600,1024]{1,0:T(8,128)(2,1)S(1)}, u32[]{:S(2)}, u32[]{:S(2)}) collective-permute-start(bf16[600,1024]{1,0:T(8,128)(2,1)S(1)} %shard_map.87.refs_1_.refs_4_), channel_id=1, source_target_pairs={{0,2},{1,3},{2,0},{3,1},{4,6},{5,7},{6,4},{7,5},{8,10},{9,11},{10,... | collective-permute-start | bytes 3686408 | tf_op jit(solution)/shard_map/ppermute | solution.py:218
  8.9 1.6 %collective-permute-start = (bf16[600,256]{1,0:T(8,128)(2,1)S(1)}, bf16[600,256]{1,0:T(8,128)(2,1)S(1)}, u32[]{:S(2)}, u32[]{:S(2)}) collective-permute-start(bf16[600,256]{1,0:T(8,128)(2,1)S(1)} %shard_map.86.refs_0_), channel_id=1, source_target_pairs={{0,8},{8,0},{16,24},{24,16},{1,9},{9,1},{17,25},{25,17},{2,10},{10... | collective-permute-start | bytes 921608 | tf_op jit(solution)/shard_map/ppermute | solution.py:209
  10.5 2.6 %collective-permute-start.1 = (bf16[600,256]{1,0:T(8,128)(2,1)S(1)}, bf16[600,256]{1,0:T(8,128)(2,1)S(1)}, u32[]{:S(2)}, u32[]{:S(2)}) collective-permute-start(bf16[600,256]{1,0:T(8,128)(2,1)S(1)} %shard_map.86.refs_0_), channel_id=1, source_target_pairs={{0,16},{8,24},{16,0},{24,8},{1,17},{9,25},{17,1},{25,9},{2,18},{10... | collective-permute-start | bytes 921608 | tf_op jit(solution)/shard_map/ppermute | solution.py:209
  13.3 0.8 shard_map.88
  14.2 8.8 %collective-permute-done.refs_0_.refs_1_ = bf16[600,256]{1,0:T(8,128)(2,1)S(1)} collective-permute-done((bf16[600,256]{1,0:T(8,128)(2,1)S(1)}, bf16[600,256]{1,0:T(8,128)(2,1)S(1)}, u32[]{:S(2)}, u32[]{:S(2)}) %collective-permute-start) | collective-permute-done | bytes 307232 | tf_op jit(solution)/shard_map/ppermute | solution.py:209
  22.9 0.8 shard_map.89
  23.8 11.0 %collective-permute-done.1.refs_0_.refs_2_ = bf16[600,256]{1,0:T(8,128)(2,1)S(1)} collective-permute-done((bf16[600,256]{1,0:T(8,128)(2,1)S(1)}, bf16[600,256]{1,0:T(8,128)(2,1)S(1)}, u32[]{:S(2)}, u32[]{:S(2)}) %collective-permute-start.1) | collective-permute-done | bytes 307232 | tf_op jit(solution)/shard_map/ppermute | solution.py:209
  34.8 0.8 shard_map.90
  36.3 0.8 shard_map.91
  37.2 0.6 collective-permute-start.10
  38.5 2.5 %shard_map.92 = (bf16[1024,448]{1,0:T(8,128)(2,1)S(1)}, f32[1024,152]{1,0:T(8,128)S(1)}, bf16[1024,1024]{1,0:T(8,128)(2,1)S(1)}) custom-call(bf16[600,256]{1,0:T(8,128)(2,1)S(1)} %collective-permute-done.3.refs_0_.refs_4_, bf16[600,256]{1,0:T(8,128)(2,1)S(1)} %collective-permute-done.4.refs_1_.refs_5_, ...), custom_call_target="tpu_custom_call" | custom-call | flops 1258291200 | bytes 2457600 | tf_op jit(solution)/shard_map/pallas_call | solution.py:192
  41.0 9.6 %shard_map.93 = (bf16[2048,1024]{1,0:T(8,128)(2,1)S(1)}, bf16[2048,1024]{1,0:T(8,128)(2,1)S(1)}, f32[1024,152]{1,0:T(8,128)S(1)}, f32[1024,152]{1,0:T(8,128)S(1)}) custom-call(bf16[256,448]{1,0:T(8,128)(2,1)S(1)} %get-tuple-element.62.refs_0_, bf16[256,448]{1,0:T(8,128)(2,1)S(1)} %get-tuple-element.65.refs_1_, ...), custom_call_target="tpu_custom_call" | custom-call | flops 5033164800 | bytes 5537792 | tf_op jit(solution)/shard_map/pallas_call | solution.py:192
  50.6 0.8 shard_map.95
  51.4 0.9 shard_map.94
  52.3 1.2 %collective-permute-done.10.refs_6_.refs_3_ = bf16[600,512]{1,0:T(8,128)(2,1)S(1)} collective-permute-done((bf16[600,512]{1,0:T(8,128)(2,1)S(1)}, bf16[600,512]{1,0:T(8,128)(2,1)S(1)}, u32[]{:S(2)}, u32[]{:S(2)}) %collective-permute-start.10) | collective-permute-done | bytes 614432 | tf_op jit(solution)/shard_map/ppermute | solution.py:218
  53.9 2.5 %shard_map.97 = (bf16[1024,512]{1,0:T(8,128)(2,1)S(1)}, bf16[1024,512]{1,0:T(8,128)(2,1)S(1)}, bf16[152,1024]{1,0:T(8,128)(2,1)S(1)}) custom-call(bf16[1024,448]{1,0:T(8,128)(2,1)S(1)} %get-tuple-element.72.refs_4_.refs_0_, f32[1024,152]{1,0:T(8,128)S(1)} %get-tuple-element.84.refs_1_, bf16[600,512]{1,0:T(8,128)(2,1)S(1)} %collective-permute-done.9.refs_5_.refs_2_, ...), custom_call_target="tpu_custom_call" | custom-call | flops 1258291200 | bytes 2768896 | tf_op jit(solution)/shard_map/pallas_call | solution.py:192
  56.5 1.6 %collective-permute-start.18 = (bf16[152,1024]{1,0:T(8,128)(2,1)S(1)}, bf16[152,1024]{1,0:T(8,128)(2,1)S(1)}, u32[]{:S(2)}, u32[]{:S(2)}) collective-permute-start(bf16[152,1024]{1,0:T(8,128)(2,1)S(1)} %shard_map.94), channel_id=1, source_target_pairs={{0,2},{1,3},{2,0},{3,1},{4,6},{5,7},{6,4},{7,5},{8,10},{9,11},{10,... | collective-permute-start | bytes 933896 | tf_op jit(solution)/shard_map/ppermute | solution.py:218
  58.6 2.5 %shard_map.96 = (bf16[1024,512]{1,0:T(8,128)(2,1)S(1)}, bf16[1024,512]{1,0:T(8,128)(2,1)S(1)}, f32[152,1024]{1,0:T(8,128)S(1)}) custom-call(bf16[256,448]{1,0:T(8,128)(2,1)S(1)} %get-tuple-element.62.refs_0_, bf16[256,448]{1,0:T(8,128)(2,1)S(1)} %get-tuple-element.65.refs_1_, bf16[256,448]{1,0:T(8,128)(2,1)S(1)} %get-tuple-element.68.refs_2_, ...), custom_call_target="tpu_custom_call" | custom-call | flops 1258291200 | bytes 2768896 | tf_op jit(solution)/shard_map/pallas_call | solution.py:192
  61.1 0.8 shard_map.100
  62.0 1.6 %collective-permute-start.20 = (bf16[152,1024]{1,0:T(8,128)(2,1)S(1)}, bf16[152,1024]{1,0:T(8,128)(2,1)S(1)}, u32[]{:S(2)}, u32[]{:S(2)}) collective-permute-start(bf16[152,1024]{1,0:T(8,128)(2,1)S(1)} %shard_map.100), channel_id=1, source_target_pairs={{0,6},{1,7},{2,4},{3,5},{4,2},{5,3},{6,0},{7,1},{8,14},{9,15},{10,... | collective-permute-start | bytes 933896 | tf_op jit(solution)/shard_map/ppermute | solution.py:218
  63.6 3.8 %collective-permute-start.12 = (bf16[152,256]{1,0:T(8,128)(2,1)S(1)}, bf16[152,256]{1,0:T(8,128)(2,1)S(1)}, u32[]{:S(2)}, u32[]{:S(2)}) collective-permute-start(bf16[152,256]{1,0:T(8,128)(2,1)S(1)} %get-tuple-element.99), channel_id=1, source_target_pairs={{0,8},{8,0},{16,24},{24,16},{1,9},{9,1},{17,25},{25,17},{2,10},{10... | collective-permute-start | bytes 233480 | tf_op jit(solution)/shard_map/ppermute | solution.py:209
  67.4 1.1 %collective-permute-start.13 = (bf16[152,256]{1,0:T(8,128)(2,1)S(1)}, bf16[152,256]{1,0:T(8,128)(2,1)S(1)}, u32[]{:S(2)}, u32[]{:S(2)}) collective-permute-start(bf16[152,256]{1,0:T(8,128)(2,1)S(1)} %get-tuple-element.100), channel_id=1, source_target_pairs={{0,16},{8,24},{16,0},{24,8},{1,17},{9,25},{17,1},{25,9},{2,18},{10... | collective-permute-start | bytes 233480 | tf_op jit(solution)/shard_map/ppermute | solution.py:209
  68.5 1.4 %collective-permute-done.12.refs_0_ = bf16[152,256]{1,0:T(8,128)(2,1)S(1)} collective-permute-done((bf16[152,256]{1,0:T(8,128)(2,1)S(1)}, bf16[152,256]{1,0:T(8,128)(2,1)S(1)}, u32[]{:S(2)}, u32[]{:S(2)}) %collective-permute-start.12) | collective-permute-done | bytes 77856 | tf_op jit(solution)/shard_map/ppermute | solution.py:209
  69.8 2.4 %collective-permute-start.14 = (bf16[152,256]{1,0:T(8,128)(2,1)S(1)}, bf16[152,256]{1,0:T(8,128)(2,1)S(1)}, u32[]{:S(2)}, u32[]{:S(2)}) collective-permute-start(bf16[152,256]{1,0:T(8,128)(2,1)S(1)} %get-tuple-element.101), channel_id=1, source_target_pairs={{0,24},{8,16},{16,8},{24,0},{1,25},{9,17},{17,9},{25,1},{2,26},{10... | collective-permute-start | bytes 233480 | tf_op jit(solution)/shard_map/ppermute | solution.py:209
  72.2 0.8 shard_map.99
  73.1 1.5 %collective-permute-done.13.refs_1_ = bf16[152,256]{1,0:T(8,128)(2,1)S(1)} collective-permute-done((bf16[152,256]{1,0:T(8,128)(2,1)S(1)}, bf16[152,256]{1,0:T(8,128)(2,1)S(1)}, u32[]{:S(2)}, u32[]{:S(2)}) %collective-permute-start.13) | collective-permute-done | bytes 77856 | tf_op jit(solution)/shard_map/ppermute | solution.py:209
  74.6 1.5 %collective-permute-done.14.refs_2_ = bf16[152,256]{1,0:T(8,128)(2,1)S(1)} collective-permute-done((bf16[152,256]{1,0:T(8,128)(2,1)S(1)}, bf16[152,256]{1,0:T(8,128)(2,1)S(1)}, u32[]{:S(2)}, u32[]{:S(2)}) %collective-permute-start.14) | collective-permute-done | bytes 77856 | tf_op jit(solution)/shard_map/ppermute | solution.py:209
  76.2 1.4 %collective-permute-start.15 = (bf16[152,256]{1,0:T(8,128)(2,1)S(1)}, bf16[152,256]{1,0:T(8,128)(2,1)S(1)}, u32[]{:S(2)}, u32[]{:S(2)}) collective-permute-start(bf16[152,256]{1,0:T(8,128)(2,1)S(1)} %shard_map.101.refs_0_), channel_id=1, source_target_pairs={{0,8},{8,0},{16,24},{24,16},{1,9},{9,1},{17,25},{25,17},{2,10},{10... | collective-permute-start | bytes 233480 | tf_op jit(solution)/shard_map/ppermute | solution.py:209
  77.6 1.6 %collective-permute-start.16 = (bf16[152,256]{1,0:T(8,128)(2,1)S(1)}, bf16[152,256]{1,0:T(8,128)(2,1)S(1)}, u32[]{:S(2)}, u32[]{:S(2)}) collective-permute-start(bf16[152,256]{1,0:T(8,128)(2,1)S(1)} %shard_map.101.refs_0_), channel_id=1, source_target_pairs={{0,16},{8,24},{16,0},{24,8},{1,17},{9,25},{17,1},{25,9},{2,18},{10... | collective-permute-start | bytes 233480 | tf_op jit(solution)/shard_map/ppermute | solution.py:209
  79.2 1.4 %collective-permute-start.17 = (bf16[152,256]{1,0:T(8,128)(2,1)S(1)}, bf16[152,256]{1,0:T(8,128)(2,1)S(1)}, u32[]{:S(2)}, u32[]{:S(2)}) collective-permute-start(bf16[152,256]{1,0:T(8,128)(2,1)S(1)} %shard_map.101.refs_0_), channel_id=1, source_target_pairs={{0,24},{8,16},{16,8},{24,0},{1,25},{9,17},{17,9},{25,1},{2,26},{10... | collective-permute-start | bytes 233480 | tf_op jit(solution)/shard_map/ppermute | solution.py:209
  80.7 3.6 %collective-permute-done.16.refs_2_ = bf16[152,256]{1,0:T(8,128)(2,1)S(1)} collective-permute-done((bf16[152,256]{1,0:T(8,128)(2,1)S(1)}, bf16[152,256]{1,0:T(8,128)(2,1)S(1)}, u32[]{:S(2)}, u32[]{:S(2)}) %collective-permute-start.16) | collective-permute-done | bytes 77856 | tf_op jit(solution)/shard_map/ppermute | solution.py:209
  84.3 1.3 %collective-permute-done.17.refs_3_ = bf16[152,256]{1,0:T(8,128)(2,1)S(1)} collective-permute-done((bf16[152,256]{1,0:T(8,128)(2,1)S(1)}, bf16[152,256]{1,0:T(8,128)(2,1)S(1)}, u32[]{:S(2)}, u32[]{:S(2)}) %collective-permute-start.17) | collective-permute-done | bytes 77856 | tf_op jit(solution)/shard_map/ppermute | solution.py:209
  87.5 0.8 shard_map.102
  88.9 1.5 %collective-permute-start.27 = (bf16[152,512]{1,0:T(8,128)(2,1)S(1)}, bf16[152,512]{1,0:T(8,128)(2,1)S(1)}, u32[]{:S(2)}, u32[]{:S(2)}) collective-permute-start(bf16[152,512]{1,0:T(8,128)(2,1)S(1)} %get-tuple-element.117), channel_id=1, source_target_pairs={{0,2},{1,3},{2,0},{3,1},{4,6},{5,7},{6,4},{7,5},{8,10},{9,11},{10,... | collective-permute-start | bytes 466952 | tf_op jit(solution)/shard_map/ppermute | solution.py:218
  91.1 0.9 shard_map.104.own_ref
  91.9 0.9 shard_map.106.own_ref
  92.8 1.9 %collective-permute-done.25.refs_0_ = bf16[152,512]{1,0:T(8,128)(2,1)S(1)} collective-permute-done((bf16[152,512]{1,0:T(8,128)(2,1)S(1)}, bf16[152,512]{1,0:T(8,128)(2,1)S(1)}, u32[]{:S(2)}, u32[]{:S(2)}) %collective-permute-start.25) | collective-permute-done | bytes 155680 | tf_op jit(solution)/shard_map/ppermute | solution.py:218
  94.7 1.6 %collective-permute-start.26 = (bf16[152,1024]{1,0:T(8,128)(2,1)S(1)}, bf16[152,1024]{1,0:T(8,128)(2,1)S(1)}, u32[]{:S(2)}, u32[]{:S(2)}) collective-permute-start(bf16[152,1024]{1,0:T(8,128)(2,1)S(1)} %shard_map.105), channel_id=1, source_target_pairs={{0,2},{1,3},{2,0},{3,1},{4,6},{5,7},{6,4},{7,5},{8,10},{9,11},{10,... | collective-permute-start | bytes 933896 | tf_op jit(solution)/shard_map/ppermute | solution.py:218
  96.4 0.6 collective-permute-start.28
  96.9 1.0 fusion.1
  97.9 0.8 shard_map.103
  98.8 4.8 %collective-permute-done.26 = bf16[152,1024]{1,0:T(8,128)(2,1)S(1)} collective-permute-done((bf16[152,1024]{1,0:T(8,128)(2,1)S(1)}, bf16[152,1024]{1,0:T(8,128)(2,1)S(1)}, u32[]{:S(2)}, u32[]{:S(2)}) %collective-permute-start.26) | collective-permute-done | bytes 311328 | tf_op jit(solution)/shard_map/ppermute | solution.py:218
  103.6 1.3 %collective-permute-done.28 = bf16[152,1024]{1,0:T(8,128)(2,1)S(1)} collective-permute-done((bf16[152,1024]{1,0:T(8,128)(2,1)S(1)}, bf16[152,1024]{1,0:T(8,128)(2,1)S(1)}, u32[]{:S(2)}, u32[]{:S(2)}) %collective-permute-start.28) | collective-permute-done | bytes 311328 | tf_op jit(solution)/shard_map/ppermute | solution.py:218
  105.0 1.0 fusion.3
  (50 shorter events, 6.2 us)
Async XLA Ops:
  0.6 1.0 copy-start
  1.6 1.2 %copy-start.2 = (bf16[440,1024]{1,0:T(8,128)(2,1)S(1)}, bf16[440,1024]{1,0:T(8,128)(2,1)}, u32[]{:S(2)}) copy-start(bf16[440,1024]{1,0:T(8,128)(2,1)} %w_hbm.1) | copy-start | bytes 2703364
  2.8 0.7 copy-start.5
  3.5 4.9 %copy-start.3 = (bf16[147,256]{1,0:T(8,128)(2,1)S(1)}, bf16[147,256]{1,0:T(8,128)(2,1)}, u32[]{:S(2)}) copy-start(bf16[147,256]{1,0:T(8,128)(2,1)} %refs_3_.1) | copy-start | bytes 225796
  3.5 4.9 %copy-start.4 = (bf16[440,256]{1,0:T(8,128)(2,1)S(1)}, bf16[440,256]{1,0:T(8,128)(2,1)}, u32[]{:S(2)}) copy-start(bf16[440,256]{1,0:T(8,128)(2,1)} %x_hbm.1) | copy-start | bytes 675844
  3.5 4.9 %copy-start.6 = (s32[256]{0:T(256)S(1)}, s32[256]{0:T(256)}, u32[]{:S(2)}) copy-start(s32[256]{0:T(256)} %param.9) | copy-start | bytes 3076
  3.9 32.4 %collective-permute-start.8 = (bf16[600,1024]{1,0:T(8,128)(2,1)S(1)}, bf16[600,1024]{1,0:T(8,128)(2,1)S(1)}, u32[]{:S(2)}, u32[]{:S(2)}) collective-permute-start(bf16[600,1024]{1,0:T(8,128)(2,1)S(1)} %shard_map.87.refs_1_.refs_4_), channel_id=1, source_target_pairs={{0,4},{1,5},{2,6},{3,7},{4,0},{5,1},{6,2},{7,3},{8,12},{9,13},{10,... | collective-permute-start | bytes 3686408 | tf_op jit(solution)/shard_map/ppermute | solution.py:218
  6.9 30.3 %collective-permute-start.7 = (bf16[600,1024]{1,0:T(8,128)(2,1)S(1)}, bf16[600,1024]{1,0:T(8,128)(2,1)S(1)}, u32[]{:S(2)}, u32[]{:S(2)}) collective-permute-start(bf16[600,1024]{1,0:T(8,128)(2,1)S(1)} %shard_map.87.refs_1_.refs_4_), channel_id=1, source_target_pairs={{0,2},{1,3},{2,0},{3,1},{4,6},{5,7},{6,4},{7,5},{8,10},{9,11},{10,... | collective-permute-start | bytes 3686408 | tf_op jit(solution)/shard_map/ppermute | solution.py:218
  8.9 14.0 %collective-permute-start = (bf16[600,256]{1,0:T(8,128)(2,1)S(1)}, bf16[600,256]{1,0:T(8,128)(2,1)S(1)}, u32[]{:S(2)}, u32[]{:S(2)}) collective-permute-start(bf16[600,256]{1,0:T(8,128)(2,1)S(1)} %shard_map.86.refs_0_), channel_id=1, source_target_pairs={{0,8},{8,0},{16,24},{24,16},{1,9},{9,1},{17,25},{25,17},{2,10},{10... | collective-permute-start | bytes 921608 | tf_op jit(solution)/shard_map/ppermute | solution.py:209
  10.5 24.3 %collective-permute-start.1 = (bf16[600,256]{1,0:T(8,128)(2,1)S(1)}, bf16[600,256]{1,0:T(8,128)(2,1)S(1)}, u32[]{:S(2)}, u32[]{:S(2)}) collective-permute-start(bf16[600,256]{1,0:T(8,128)(2,1)S(1)} %shard_map.86.refs_0_), channel_id=1, source_target_pairs={{0,16},{8,24},{16,0},{24,8},{1,17},{9,25},{17,1},{25,9},{2,18},{10... | collective-permute-start | bytes 921608 | tf_op jit(solution)/shard_map/ppermute | solution.py:209
  13.1 22.5 %collective-permute-start.2 = (bf16[600,256]{1,0:T(8,128)(2,1)S(1)}, bf16[600,256]{1,0:T(8,128)(2,1)S(1)}, u32[]{:S(2)}, u32[]{:S(2)}) collective-permute-start(bf16[600,256]{1,0:T(8,128)(2,1)S(1)} %shard_map.86.refs_0_), channel_id=1, source_target_pairs={{0,24},{8,16},{16,8},{24,0},{1,25},{9,17},{17,9},{25,1},{2,26},{10... | collective-permute-start | bytes 921608 | tf_op jit(solution)/shard_map/ppermute | solution.py:209
  22.9 14.9 %collective-permute-start.3 = (bf16[600,256]{1,0:T(8,128)(2,1)S(1)}, bf16[600,256]{1,0:T(8,128)(2,1)S(1)}, u32[]{:S(2)}, u32[]{:S(2)}) collective-permute-start(bf16[600,256]{1,0:T(8,128)(2,1)S(1)} %shard_map.86.refs_0_), channel_id=1, source_target_pairs={{0,1},{1,0},{2,3},{3,2},{4,5},{5,4},{6,7},{7,6},{8,9},{9,8},{10,11... | collective-permute-start | bytes 921608 | tf_op jit(solution)/shard_map/ppermute | solution.py:203
  34.8 3.7 %collective-permute-start.5 = (bf16[600,256]{1,0:T(8,128)(2,1)S(1)}, bf16[600,256]{1,0:T(8,128)(2,1)S(1)}, u32[]{:S(2)}, u32[]{:S(2)}) collective-permute-start(bf16[600,256]{1,0:T(8,128)(2,1)S(1)} %collective-permute-done.1.refs_0_.refs_2_), channel_id=1, source_target_pairs={{0,1},{1,0},{2,3},{3,2},{4,5},{5,4},{6,7},{7,6},{8,9},{9,8},{10,11... | collective-permute-start | bytes 921608 | tf_op jit(solution)/shard_map/ppermute | solution.py:203
  35.7 2.8 %collective-permute-start.6 = (bf16[600,256]{1,0:T(8,128)(2,1)S(1)}, bf16[600,256]{1,0:T(8,128)(2,1)S(1)}, u32[]{:S(2)}, u32[]{:S(2)}) collective-permute-start(bf16[600,256]{1,0:T(8,128)(2,1)S(1)} %collective-permute-done.2.refs_0_.refs_3_), channel_id=1, source_target_pairs={{0,1},{1,0},{2,3},{3,2},{4,5},{5,4},{6,7},{7,6},{8,9},{9,8},{10,11... | collective-permute-start | bytes 921608 | tf_op jit(solution)/shard_map/ppermute | solution.py:203
  36.2 2.2 %collective-permute-start.4 = (bf16[600,256]{1,0:T(8,128)(2,1)S(1)}, bf16[600,256]{1,0:T(8,128)(2,1)S(1)}, u32[]{:S(2)}, u32[]{:S(2)}) collective-permute-start(bf16[600,256]{1,0:T(8,128)(2,1)S(1)} %collective-permute-done.refs_0_.refs_1_), channel_id=1, source_target_pairs={{0,1},{1,0},{2,3},{3,2},{4,5},{5,4},{6,7},{7,6},{8,9},{9,8},{10,11... | collective-permute-start | bytes 921608 | tf_op jit(solution)/shard_map/ppermute | solution.py:203
  37.2 16.3 %collective-permute-start.10 = (bf16[600,512]{1,0:T(8,128)(2,1)S(1)}, bf16[600,512]{1,0:T(8,128)(2,1)S(1)}, u32[]{:S(2)}, u32[]{:S(2)}) collective-permute-start(bf16[600,512]{1,0:T(8,128)(2,1)S(1)} %slice.17), channel_id=1, source_target_pairs={{0,2},{1,3},{2,0},{3,1},{4,6},{5,7},{6,4},{7,5},{8,10},{9,11},{10,... | collective-permute-start | bytes 1843208 | tf_op jit(solution)/shard_map/ppermute | solution.py:218
  37.9 16.0 %collective-permute-start.9 = (bf16[600,512]{1,0:T(8,128)(2,1)S(1)}, bf16[600,512]{1,0:T(8,128)(2,1)S(1)}, u32[]{:S(2)}, u32[]{:S(2)}) collective-permute-start(bf16[600,512]{1,0:T(8,128)(2,1)S(1)} %slice.16), channel_id=1, source_target_pairs={{0,4},{1,5},{2,6},{3,7},{4,0},{5,1},{6,2},{7,3},{8,12},{9,13},{10,... | collective-permute-start | bytes 1843208 | tf_op jit(solution)/shard_map/ppermute | solution.py:218
  56.4 7.1 %collective-permute-start.11 = (bf16[152,1024]{1,0:T(8,128)(2,1)S(1)}, bf16[152,1024]{1,0:T(8,128)(2,1)S(1)}, u32[]{:S(2)}, u32[]{:S(2)}) collective-permute-start(bf16[152,1024]{1,0:T(8,128)(2,1)S(1)} %get-tuple-element.85), channel_id=1, source_target_pairs={{0,1},{1,0},{2,3},{3,2},{4,5},{5,4},{6,7},{7,6},{8,9},{9,8},{10,11... | collective-permute-start | bytes 933896 | tf_op jit(solution)/shard_map/ppermute | solution.py:203
  56.5 22.7 %collective-permute-start.18 = (bf16[152,1024]{1,0:T(8,128)(2,1)S(1)}, bf16[152,1024]{1,0:T(8,128)(2,1)S(1)}, u32[]{:S(2)}, u32[]{:S(2)}) collective-permute-start(bf16[152,1024]{1,0:T(8,128)(2,1)S(1)} %shard_map.94), channel_id=1, source_target_pairs={{0,2},{1,3},{2,0},{3,1},{4,6},{5,7},{6,4},{7,5},{8,10},{9,11},{10,... | collective-permute-start | bytes 933896 | tf_op jit(solution)/shard_map/ppermute | solution.py:218
  58.1 22.6 %collective-permute-start.19 = (bf16[152,1024]{1,0:T(8,128)(2,1)S(1)}, bf16[152,1024]{1,0:T(8,128)(2,1)S(1)}, u32[]{:S(2)}, u32[]{:S(2)}) collective-permute-start(bf16[152,1024]{1,0:T(8,128)(2,1)S(1)} %shard_map.95), channel_id=1, source_target_pairs={{0,4},{1,5},{2,6},{3,7},{4,0},{5,1},{6,2},{7,3},{8,12},{9,13},{10,... | collective-permute-start | bytes 933896 | tf_op jit(solution)/shard_map/ppermute | solution.py:218
  62.0 18.7 %collective-permute-start.20 = (bf16[152,1024]{1,0:T(8,128)(2,1)S(1)}, bf16[152,1024]{1,0:T(8,128)(2,1)S(1)}, u32[]{:S(2)}, u32[]{:S(2)}) collective-permute-start(bf16[152,1024]{1,0:T(8,128)(2,1)S(1)} %shard_map.100), channel_id=1, source_target_pairs={{0,6},{1,7},{2,4},{3,5},{4,2},{5,3},{6,0},{7,1},{8,14},{9,15},{10,... | collective-permute-start | bytes 933896 | tf_op jit(solution)/shard_map/ppermute | solution.py:218
  63.6 6.3 %collective-permute-start.12 = (bf16[152,256]{1,0:T(8,128)(2,1)S(1)}, bf16[152,256]{1,0:T(8,128)(2,1)S(1)}, u32[]{:S(2)}, u32[]{:S(2)}) collective-permute-start(bf16[152,256]{1,0:T(8,128)(2,1)S(1)} %get-tuple-element.99), channel_id=1, source_target_pairs={{0,8},{8,0},{16,24},{24,16},{1,9},{9,1},{17,25},{25,17},{2,10},{10... | collective-permute-start | bytes 233480 | tf_op jit(solution)/shard_map/ppermute | solution.py:209
  67.4 7.2 %collective-permute-start.13 = (bf16[152,256]{1,0:T(8,128)(2,1)S(1)}, bf16[152,256]{1,0:T(8,128)(2,1)S(1)}, u32[]{:S(2)}, u32[]{:S(2)}) collective-permute-start(bf16[152,256]{1,0:T(8,128)(2,1)S(1)} %get-tuple-element.100), channel_id=1, source_target_pairs={{0,16},{8,24},{16,0},{24,8},{1,17},{9,25},{17,1},{25,9},{2,18},{10... | collective-permute-start | bytes 233480 | tf_op jit(solution)/shard_map/ppermute | solution.py:209
  69.8 6.3 %collective-permute-start.14 = (bf16[152,256]{1,0:T(8,128)(2,1)S(1)}, bf16[152,256]{1,0:T(8,128)(2,1)S(1)}, u32[]{:S(2)}, u32[]{:S(2)}) collective-permute-start(bf16[152,256]{1,0:T(8,128)(2,1)S(1)} %get-tuple-element.101), channel_id=1, source_target_pairs={{0,24},{8,16},{16,8},{24,0},{1,25},{9,17},{17,9},{25,1},{2,26},{10... | collective-permute-start | bytes 233480 | tf_op jit(solution)/shard_map/ppermute | solution.py:209
  76.2 4.5 %collective-permute-start.15 = (bf16[152,256]{1,0:T(8,128)(2,1)S(1)}, bf16[152,256]{1,0:T(8,128)(2,1)S(1)}, u32[]{:S(2)}, u32[]{:S(2)}) collective-permute-start(bf16[152,256]{1,0:T(8,128)(2,1)S(1)} %shard_map.101.refs_0_), channel_id=1, source_target_pairs={{0,8},{8,0},{16,24},{24,16},{1,9},{9,1},{17,25},{25,17},{2,10},{10... | collective-permute-start | bytes 233480 | tf_op jit(solution)/shard_map/ppermute | solution.py:209
  77.6 6.7 %collective-permute-start.16 = (bf16[152,256]{1,0:T(8,128)(2,1)S(1)}, bf16[152,256]{1,0:T(8,128)(2,1)S(1)}, u32[]{:S(2)}, u32[]{:S(2)}) collective-permute-start(bf16[152,256]{1,0:T(8,128)(2,1)S(1)} %shard_map.101.refs_0_), channel_id=1, source_target_pairs={{0,16},{8,24},{16,0},{24,8},{1,17},{9,25},{17,1},{25,9},{2,18},{10... | collective-permute-start | bytes 233480 | tf_op jit(solution)/shard_map/ppermute | solution.py:209
  79.2 6.3 %collective-permute-start.17 = (bf16[152,256]{1,0:T(8,128)(2,1)S(1)}, bf16[152,256]{1,0:T(8,128)(2,1)S(1)}, u32[]{:S(2)}, u32[]{:S(2)}) collective-permute-start(bf16[152,256]{1,0:T(8,128)(2,1)S(1)} %shard_map.101.refs_0_), channel_id=1, source_target_pairs={{0,24},{8,16},{16,8},{24,0},{1,25},{9,17},{17,9},{25,1},{2,26},{10... | collective-permute-start | bytes 233480 | tf_op jit(solution)/shard_map/ppermute | solution.py:209
  85.5 1.3 %collective-permute-start.21 = (bf16[152,256]{1,0:T(8,128)(2,1)S(1)}, bf16[152,256]{1,0:T(8,128)(2,1)S(1)}, u32[]{:S(2)}, u32[]{:S(2)}) collective-permute-start(bf16[152,256]{1,0:T(8,128)(2,1)S(1)} %shard_map.101.refs_0_), channel_id=1, source_target_pairs={{0,1},{1,0},{2,3},{3,2},{4,5},{5,4},{6,7},{7,6},{8,9},{9,8},{10,11... | collective-permute-start | bytes 233480 | tf_op jit(solution)/shard_map/ppermute | solution.py:203
  85.5 1.4 %collective-permute-start.22 = (bf16[152,256]{1,0:T(8,128)(2,1)S(1)}, bf16[152,256]{1,0:T(8,128)(2,1)S(1)}, u32[]{:S(2)}, u32[]{:S(2)}) collective-permute-start(bf16[152,256]{1,0:T(8,128)(2,1)S(1)} %collective-permute-done.15.refs_1_), channel_id=1, source_target_pairs={{0,1},{1,0},{2,3},{3,2},{4,5},{5,4},{6,7},{7,6},{8,9},{9,8},{10,11... | collective-permute-start | bytes 233480 | tf_op jit(solution)/shard_map/ppermute | solution.py:203
  86.1 1.3 %collective-permute-start.23 = (bf16[152,256]{1,0:T(8,128)(2,1)S(1)}, bf16[152,256]{1,0:T(8,128)(2,1)S(1)}, u32[]{:S(2)}, u32[]{:S(2)}) collective-permute-start(bf16[152,256]{1,0:T(8,128)(2,1)S(1)} %collective-permute-done.16.refs_2_), channel_id=1, source_target_pairs={{0,1},{1,0},{2,3},{3,2},{4,5},{5,4},{6,7},{7,6},{8,9},{9,8},{10,11... | collective-permute-start | bytes 233480 | tf_op jit(solution)/shard_map/ppermute | solution.py:203
  86.1 1.4 %collective-permute-start.24 = (bf16[152,256]{1,0:T(8,128)(2,1)S(1)}, bf16[152,256]{1,0:T(8,128)(2,1)S(1)}, u32[]{:S(2)}, u32[]{:S(2)}) collective-permute-start(bf16[152,256]{1,0:T(8,128)(2,1)S(1)} %collective-permute-done.17.refs_3_), channel_id=1, source_target_pairs={{0,1},{1,0},{2,3},{3,2},{4,5},{5,4},{6,7},{7,6},{8,9},{9,8},{10,11... | collective-permute-start | bytes 233480 | tf_op jit(solution)/shard_map/ppermute | solution.py:203
  88.3 6.3 %collective-permute-start.25 = (bf16[152,512]{1,0:T(8,128)(2,1)S(1)}, bf16[152,512]{1,0:T(8,128)(2,1)S(1)}, u32[]{:S(2)}, u32[]{:S(2)}) collective-permute-start(bf16[152,512]{1,0:T(8,128)(2,1)S(1)} %get-tuple-element.116), channel_id=1, source_target_pairs={{0,4},{1,5},{2,6},{3,7},{4,0},{5,1},{6,2},{7,3},{8,12},{9,13},{10,... | collective-permute-start | bytes 466952 | tf_op jit(solution)/shard_map/ppermute | solution.py:218
  88.9 7.4 %collective-permute-start.27 = (bf16[152,512]{1,0:T(8,128)(2,1)S(1)}, bf16[152,512]{1,0:T(8,128)(2,1)S(1)}, u32[]{:S(2)}, u32[]{:S(2)}) collective-permute-start(bf16[152,512]{1,0:T(8,128)(2,1)S(1)} %get-tuple-element.117), channel_id=1, source_target_pairs={{0,2},{1,3},{2,0},{3,1},{4,6},{5,7},{6,4},{7,5},{8,10},{9,11},{10,... | collective-permute-start | bytes 466952 | tf_op jit(solution)/shard_map/ppermute | solution.py:218
  94.7 8.9 %collective-permute-start.26 = (bf16[152,1024]{1,0:T(8,128)(2,1)S(1)}, bf16[152,1024]{1,0:T(8,128)(2,1)S(1)}, u32[]{:S(2)}, u32[]{:S(2)}) collective-permute-start(bf16[152,1024]{1,0:T(8,128)(2,1)S(1)} %shard_map.105), channel_id=1, source_target_pairs={{0,2},{1,3},{2,0},{3,1},{4,6},{5,7},{6,4},{7,5},{8,10},{9,11},{10,... | collective-permute-start | bytes 933896 | tf_op jit(solution)/shard_map/ppermute | solution.py:218
  96.4 8.6 %collective-permute-start.28 = (bf16[152,1024]{1,0:T(8,128)(2,1)S(1)}, bf16[152,1024]{1,0:T(8,128)(2,1)S(1)}, u32[]{:S(2)}, u32[]{:S(2)}) collective-permute-start(bf16[152,1024]{1,0:T(8,128)(2,1)S(1)} %shard_map.107), channel_id=1, source_target_pairs={{0,4},{1,5},{2,6},{3,7},{4,0},{5,1},{6,2},{7,3},{8,12},{9,13},{10,... | collective-permute-start | bytes 933896 | tf_op jit(solution)/shard_map/ppermute | solution.py:218
  97.9 7.0 %copy-start.1 = (bf16[147,1024]{1,0:T(8,128)(2,1)S(1)}, bf16[147,1024]{1,0:T(8,128)(2,1)}, u32[]{:S(2)}) copy-start(bf16[147,1024]{1,0:T(8,128)(2,1)} %d_hbm.1) | copy-start | bytes 903172

commit v6 on v5

--- a/solution.py
+++ b/solution.py
@@ -149,46 +149,46 @@
     c_ref[classes:, :] = jnp.zeros((c_ref.shape[0] - classes, c_ref.shape[1]), BF16)
 
 
-def share_kernel(count, skip, block, halves, outs, *refs):
+def share_kernel(count, start, skip, block, halves, outs, seeded, *refs):
     left_refs, f_refs, o_refs = refs[:count], refs[count:-outs], refs[-outs:]
+    seed_ref, f_refs = (f_refs[0], f_refs[1:]) if seeded else (None, f_refs)
     each = len(f_refs) // halves
     f = f_refs[0].shape[1]
     for h in range(halves):
         f_blocks = [(ref, at) for ref in f_refs[h * each : (h + 1) * each] for at in range(0, ref.shape[0], block)]
-        total = None
-        for left_ref, (f_ref, at) in zip(left_refs, f_blocks, strict=True):
+        total = seed_ref[:, h * f : (h + 1) * f] if seeded else None
+        for left_ref, (f_ref, at) in zip(left_refs, f_blocks[start : start + count], strict=True):
             part = jnp.dot(left_ref[skip:, :], f_ref[at : at + block, :], preferred_element_type=F32)
             total = part if total is None else total + part
         if outs == 1:
             o_refs[0][:, h * f : (h + 1) * f] = total.astype(o_refs[0].dtype)
         else:
-            o_refs[h][...] = total.astype(o_refs[h].dtype)
-
-
-def add_kernel(side, own_ref, *refs):
-    add_refs, o_ref = refs[:-1], refs[-1]
-    half = own_ref.shape[1] // 2
-    for h in (0, 1):
-        here = slice(h * half, (h + 1) * half)
-        total = own_ref[:, here]
-        for ref in add_refs if h == side else ():
-            total = total + ref[...].astype(F32)
-        o_ref[:, here] = total.astype(o_ref.dtype)
-
-
-def make_share(lefts, skip, feats, dtype, apart=False):
+            for j in range(outs // halves):
+                wide = f * halves // outs
+                o_refs[h * (outs // halves) + j][...] = total[:, j * wide : (j + 1) * wide].astype(o_refs[0].dtype)
+
+
+def add_kernel(*refs):
+    total = refs[0][...].astype(F32)
+    for ref in refs[1:-1]:
+        total = total + ref[...].astype(F32)
+    refs[-1][...] = total.astype(refs[-1].dtype)
+
+
+def make_share(lefts, skip, feats, dtype, start=0, seed=None, outs=1):
     block = lefts[0].shape[1]
     wide, n, f = lefts[0].shape[0] - skip, block * len(lefts), sum(h[0].shape[1] for h in feats)
+    shapes = [jax.ShapeDtypeStruct((wide, f // outs), dtype)] * outs
     return whole(
-        functools.partial(share_kernel, len(lefts), skip, block, len(feats), len(feats) if apart else 1),
-        [jax.ShapeDtypeStruct((wide, f // 2), dtype)] * 2 if apart else jax.ShapeDtypeStruct((wide, f), dtype),
-        *lefts, *[a for h in feats for a in h], flops=2 * n * f * wide,
-    )
-
-
-def whole(kernel, shapes, *args, flops=0):
+        functools.partial(share_kernel, len(lefts), start, skip, block, len(feats), outs, seed is not None),
+        shapes if outs > 1 else shapes[0],
+        *lefts, *([] if seed is None else [seed]), *[a for h in feats for a in h], flops=2 * n * f * wide,
+    )
+
+
+def whole(kernel, shapes, *args, flops=0, weight=1):
     size = sum(math.prod(a.shape) * a.dtype.itemsize for a in args)
-    cost = pl.CostEstimate(flops=flops, bytes_accessed=size, transcendentals=0)
+    cost = pl.CostEstimate(flops=weight * flops, bytes_accessed=weight * size, transcendentals=0)
     return pl.pallas_call(kernel, out_shape=shapes, compiler_params=params(), cost_estimate=cost)(*args)
 
 
@@ -219,10 +219,12 @@
 
     offsets = [(dy, dx) for dy in range(ys) for dx in range(xs)]
     rows, half = depth + wide, width // 2
-    (w_own,) = pack(
-        functools.partial(pack_weights_kernel, raw, depth, classes),
-        [jax.ShapeDtypeStruct((rows, width), BF16)],
-        proj_weight, phase, direction,
+    w_own = jnp.concatenate(
+        [
+            proj_weight,
+            jnp.pad(phase, ((0, depth - raw - 1), (0, 0))),
+            jnp.pad(direction, ((0, wide - classes), (0, 0))),
+        ]
     )
     ws = {(0, dx): across(w_own, 0, dx) for dx in range(1, xs)}
     ws.update({(dy, 0): across(w_own, dy, 0) for dy in range(1, ys)})
@@ -230,10 +232,15 @@
     halves = {}
     for dy, dx in far:
         halves[dy, dx] = [across(ws[0, dx][:, :half], dy, 0), across(ws[dy, 0][:, half:], 0, dx)]
-    x_own = pack(
-        functools.partial(pack_samples_kernel, raw, depth, classes),
-        jax.ShapeDtypeStruct((rows, own), BF16),
-        inputs, probs, labels[None, :],
+    onehot = lax.broadcasted_iota(jnp.int32, probs.shape, 0) == labels[None, :]
+    resid = (probs.astype(F32) - onehot.astype(F32)).astype(BF16)
+    x_own = jnp.concatenate(
+        [
+            inputs,
+            jnp.ones((1, own), BF16),
+            jnp.zeros((depth - raw - 1, own), BF16),
+            jnp.pad(resid, ((0, wide - classes), (0, 0))),
+        ]
     )
     x_line = [x_own] + [along(x_own, k) for k in places]
 
@@ -295,29 +302,40 @@
             out = out + parts[dy, dx].astype(F32)
         return out[:classes]
 
-    parts.update({at: share(at, blocks, depth) for at in far + [(0, 0)]})
+    parts[0, 0] = share((0, 0), blocks, depth)
+    keep, parts = lax.optimization_barrier((keep, parts))
+    got, after = lax.optimization_barrier((got, blocks))
+    parts.update({at: share(at, after, depth) for at in far})
     arrived.update({at: home(at, parts[at]) for at in far})
-    keep, parts = lax.optimization_barrier((keep, parts))
     curv = whole(
         functools.partial(curve_kernel, classes), jax.ShapeDtypeStruct((wide, own), BF16), keep, *got, probs
     )
     c_line = [curv] + [along(curv, k) for k in places]
-    c_line, arrived = lax.optimization_barrier((c_line, arrived))
-    curvs = c_line + [swap_core(a) for a in c_line]
-    gradient = collect({(0, 0): parts[0, 0], **arrived}, offsets[1:])
-    thirds = {at: make_share(curvs, 0, feats[at], BF16, apart=True) for at in far}
-    curvs, thirds = lax.optimization_barrier((curvs, thirds))
+    c_line, ready = lax.optimization_barrier((c_line, {at: arrived[at] for at in near}))
+    c_peer = [swap_core(a) for a in c_line]
+    seeds = {at: make_share(c_line, 0, feats[at], F32) for at in offsets[::-1]}
+
+    def total_share(at, dtype, outs=1):
+        return make_share(c_peer, 0, feats[at], dtype, line, seeds[at], outs)
+
+    thirds = {at: total_share(at, BF16, 2) for at in far}
+    c_peer, thirds = lax.optimization_barrier((c_peer, thirds))
     first_half = {(dy, dx): across(thirds[dy, dx][0], 0, -dx) for dy, dx in far}
     second_half = {(dy, dx): across(thirds[dy, dx][1], -dy, 0) for dy, dx in far}
-    parts, arrived = {}, {}
+    rest = {at: arrived[at] for at in far}
+    first_half, second_half, rest = lax.optimization_barrier((first_half, second_half, rest))
+    arrived = {**ready, **rest}
+    gradient = collect({(0, 0): parts[0, 0], **arrived}, offsets[1:])
+    hess = total_share((0, 0), F32)
+    sides = [hess[:classes, :half], hess[:classes, half:]]
     for at in near:
-        plain = make_share(curvs, 0, feats[at], F32)
+        h = 0 if at[0] else 1
+        plain = total_share(at, BF16, 2)
         others = [first_half[f] if at[0] else second_half[f] for f in far if at[0] in (0, f[0]) and at[1] in (0, f[1])]
-        h = 0 if at[0] else 1
-        parts[at] = whole(functools.partial(add_kernel, h), jax.ShapeDtypeStruct(plain.shape, BF16), plain, *others)
-        arrived[at] = home(at, parts[at])
-    parts[0, 0] = share((0, 0), curvs, 0)
-    hess_vec = collect({(0, 0): parts[0, 0], **arrived}, near) + damping[0] * direction.astype(F32)
+        mixed = whole(add_kernel, jax.ShapeDtypeStruct(plain[h].shape, BF16), plain[h], *others)
+        for side, piece in ((1 - h, home(at, plain[1 - h])), (h, home(at, mixed))):
+            sides[side] = sides[side] + piece[:classes].astype(F32)
+    hess_vec = jnp.concatenate(sides, axis=1) + damping[0] * direction.astype(F32)
     return (hess_vec, gradient)
 
 

time: 106 us -> 101 us (0.953)
  waiting for transfers between devices: 39.7 us -> 33.7 us
  local copies, waits for them, and re-layouts: 2.93 us -> 0.27 us
  other arithmetic: 2 us -> 4.41 us
  starting transfers between devices: 31.4 us -> 32.7 us
    ppermute x11 -> x13, waiting for transfers between devices: 9.68 us -> 5.82 us  [across(): return lax.ppermute(a, 'feat', [(i, to(i)) for i in range(2 * xs * ys)])]
    unnamed x14 -> x6, local copies, waits for them, and re-layouts: 2.84 us -> 0.01 us
    ppermute x11 -> x13, starting transfers between devices: 13.5 us -> 15.7 us  [across(): return lax.ppermute(a, 'feat', [(i, to(i)) for i in range(2 * xs * ys)])]
    concatenate x0 -> x2, other arithmetic: none -> 1.68 us  [the longest x1 1.45 us: on_device(): jnp.concatenate([proj_weight, jnp.pad(phase, ((0, depth - raw - 1), (0, 0...]
    ppermute x9, waiting for transfers between devices: 29.1 us -> 27.9 us  [along(): return lax.ppermute(a, 'samp', [(i, to(i)) for i in range(line)])]
    pallas_call x20 -> x24, Pallas kernels: 27.5 us -> 28.4 us  [whole(): pl.pallas_call(kernel, out_shape=shapes, compiler_params=params(), cost_e...]
  transfers between devices with their start and end apart: 29 -> 31, of which waited for: 16 -> 8; matrix products, arithmetic and copies ran while one was open for 1% -> 2% of each run, Pallas kernels for 23% -> 26%
where the time goes in v6:
time: 101 us
  waiting for transfers between devices  33.7 us (33%)
  starting transfers between devices  32.7 us (32%)
  Pallas kernels  28.4 us (28%)
  other arithmetic  4.41 us (4%)
  between operations  1.66 us (2%)
    pallas_call x24, Pallas kernels, whole(): pl.pallas_call(kernel, out_shape=shapes, compiler_params=params(), cost_e...  28.4 us
    ppermute x9, waiting for transfers between devices, along(): return lax.ppermute(a, 'samp', [(i, to(i)) for i in range(line)])  27.9 us
    ppermute x13, starting transfers between devices, across(): return lax.ppermute(a, 'feat', [(i, to(i)) for i in range(2 * xs * ys)])  15.7 us
    ppermute x9, starting transfers between devices, along(): return lax.ppermute(a, 'samp', [(i, to(i)) for i in range(line)])  15.2 us
    ppermute x13, waiting for transfers between devices, across(): return lax.ppermute(a, 'feat', [(i, to(i)) for i in range(2 * xs * ys)])  5.82 us
  transfers between devices with their start and end apart: 31, of which 8 were waited for; matrix products, arithmetic and copies ran while one was open for 2% of the time, Pallas kernels for 26%

profile of v6, /device:TPU:0, one launch (start us, length us, event | category | flops | bytes accessed | tf_op | source)
XLA Modules:
  0.0 101.1 jit_solution(1791762589355308960)
XLA Ops:
  0.7 1.5 %fusion.4.refs_1_.refs_4_ = bf16[600,1024]{1,0:T(8,128)(2,1)S(1)} fusion(bf16[147,1024]{1,0:T(8,128)(2,1)} %param.12, bf16[1,1024]{1,0:T(2,128)(2,1)} %param.11, bf16[440,1024]{1,0:T(8,128)(2,1)} %param.10), kind=kLoop, calls=%fused_computation.7 | loop fusion | flops 7372800 | bytes 2433024 | tf_op jit(solution)/shard_map/concatenate | solution.py:222
  2.1 3.0 %collective-permute-start.8 = (bf16[600,1024]{1,0:T(8,128)(2,1)S(1)}, bf16[600,1024]{1,0:T(8,128)(2,1)S(1)}, u32[]{:S(2)}, u32[]{:S(2)}) collective-permute-start(bf16[600,1024]{1,0:T(8,128)(2,1)S(1)} %fusion.4.refs_1_.refs_4_), channel_id=1, source_target_pairs={{0,4},{1,5},{2,6},{3,7},{4,0},{5,1},{6,2},{7,3},{8,12},{9,13},{10,... | collective-permute-start | bytes 3686408 | tf_op jit(solution)/shard_map/ppermute | solution.py:218
  5.1 1.5 %collective-permute-start.7 = (bf16[600,1024]{1,0:T(8,128)(2,1)S(1)}, bf16[600,1024]{1,0:T(8,128)(2,1)S(1)}, u32[]{:S(2)}, u32[]{:S(2)}) collective-permute-start(bf16[600,1024]{1,0:T(8,128)(2,1)S(1)} %fusion.4.refs_1_.refs_4_), channel_id=1, source_target_pairs={{0,2},{1,3},{2,0},{3,1},{4,6},{5,7},{6,4},{7,5},{8,10},{9,11},{10,... | collective-permute-start | bytes 3686408 | tf_op jit(solution)/shard_map/ppermute | solution.py:218
  6.8 0.7 subtract_convert_fusion
  7.7 1.6 %collective-permute-start = (bf16[600,256]{1,0:T(8,128)(2,1)S(1)}, bf16[600,256]{1,0:T(8,128)(2,1)S(1)}, u32[]{:S(2)}, u32[]{:S(2)}) collective-permute-start(bf16[600,256]{1,0:T(8,128)(2,1)S(1)} %fusion.10.refs_0_), channel_id=1, source_target_pairs={{0,8},{8,0},{16,24},{24,16},{1,9},{9,1},{17,25},{25,17},{2,10},{10... | collective-permute-start | bytes 921608 | tf_op jit(solution)/shard_map/ppermute | solution.py:209
  9.4 2.6 %collective-permute-start.1 = (bf16[600,256]{1,0:T(8,128)(2,1)S(1)}, bf16[600,256]{1,0:T(8,128)(2,1)S(1)}, u32[]{:S(2)}, u32[]{:S(2)}) collective-permute-start(bf16[600,256]{1,0:T(8,128)(2,1)S(1)} %fusion.10.refs_0_), channel_id=1, source_target_pairs={{0,16},{8,24},{16,0},{24,8},{1,17},{9,25},{17,1},{25,9},{2,18},{10... | collective-permute-start | bytes 921608 | tf_op jit(solution)/shard_map/ppermute | solution.py:209
  12.2 0.8 shard_map.86
  13.0 8.8 %collective-permute-done.refs_0_.refs_1_ = bf16[600,256]{1,0:T(8,128)(2,1)S(1)} collective-permute-done((bf16[600,256]{1,0:T(8,128)(2,1)S(1)}, bf16[600,256]{1,0:T(8,128)(2,1)S(1)}, u32[]{:S(2)}, u32[]{:S(2)}) %collective-permute-start) | collective-permute-done | bytes 307232 | tf_op jit(solution)/shard_map/ppermute | solution.py:209
  21.8 0.8 shard_map.87
  22.6 11.0 %collective-permute-done.1.refs_0_.refs_2_ = bf16[600,256]{1,0:T(8,128)(2,1)S(1)} collective-permute-done((bf16[600,256]{1,0:T(8,128)(2,1)S(1)}, bf16[600,256]{1,0:T(8,128)(2,1)S(1)}, u32[]{:S(2)}, u32[]{:S(2)}) %collective-permute-start.1) | collective-permute-done | bytes 307232 | tf_op jit(solution)/shard_map/ppermute | solution.py:209
  33.7 0.8 shard_map.88
  34.5 0.6 collective-permute-start.6
  35.2 0.8 shard_map.89
  36.1 0.6 collective-permute-start.10
  36.7 0.6 collective-permute-start.9
  37.3 2.5 %shard_map.90 = (bf16[1024,448]{1,0:T(8,128)(2,1)S(1)}, f32[1024,152]{1,0:T(8,128)S(1)}, bf16[1024,1024]{1,0:T(8,128)(2,1)S(1)}) custom-call(bf16[600,256]{1,0:T(8,128)(2,1)S(1)} %collective-permute-done.3.refs_0_.refs_4_, bf16[600,256]{1,0:T(8,128)(2,1)S(1)} %collective-permute-done.4.refs_1_.refs_5_, ...), custom_call_target="tpu_custom_call" | custom-call | flops 1258291200 | bytes 2457600 | tf_op jit(solution)/shard_map/pallas_call | solution.py:192
  39.8 9.5 %shard_map.91 = (bf16[2048,1024]{1,0:T(8,128)(2,1)S(1)}, bf16[2048,1024]{1,0:T(8,128)(2,1)S(1)}, f32[1024,152]{1,0:T(8,128)S(1)}, f32[1024,152]{1,0:T(8,128)S(1)}) custom-call(bf16[256,448]{1,0:T(8,128)(2,1)S(1)} %get-tuple-element.75.refs_0_, bf16[256,448]{1,0:T(8,128)(2,1)S(1)} %get-tuple-element.78.refs_1_, ...), custom_call_target="tpu_custom_call" | custom-call | flops 5033164800 | bytes 5537792 | tf_op jit(solution)/shard_map/pallas_call | solution.py:192
  49.4 0.9 shard_map.93
  50.2 0.9 shard_map.92
  51.1 1.3 %collective-permute-done.10.refs_6_.refs_3_ = bf16[600,512]{1,0:T(8,128)(2,1)S(1)} collective-permute-done((bf16[600,512]{1,0:T(8,128)(2,1)S(1)}, bf16[600,512]{1,0:T(8,128)(2,1)S(1)}, u32[]{:S(2)}, u32[]{:S(2)}) %collective-permute-start.10) | collective-permute-done | bytes 614432 | tf_op jit(solution)/shard_map/ppermute | solution.py:218
  52.7 2.5 %shard_map.95 = (bf16[1024,512]{1,0:T(8,128)(2,1)S(1)}, bf16[1024,512]{1,0:T(8,128)(2,1)S(1)}, bf16[152,1024]{1,0:T(8,128)(2,1)S(1)}) custom-call(bf16[1024,448]{1,0:T(8,128)(2,1)S(1)} %get-tuple-element.85.refs_4_.refs_0_, f32[1024,152]{1,0:T(8,128)S(1)} %get-tuple-element.97.refs_1_, bf16[600,512]{1,0:T(8,128)(2,1)S(1)} %collective-permute-done.9.refs_5_.refs_2_, ...), custom_call_target="tpu_custom_call" | custom-call | flops 1258291200 | bytes 2768896 | tf_op jit(solution)/shard_map/pallas_call | solution.py:192
  55.4 1.6 %collective-permute-start.18 = (bf16[152,1024]{1,0:T(8,128)(2,1)S(1)}, bf16[152,1024]{1,0:T(8,128)(2,1)S(1)}, u32[]{:S(2)}, u32[]{:S(2)}) collective-permute-start(bf16[152,1024]{1,0:T(8,128)(2,1)S(1)} %shard_map.92), channel_id=1, source_target_pairs={{0,2},{1,3},{2,0},{3,1},{4,6},{5,7},{6,4},{7,5},{8,10},{9,11},{10,... | collective-permute-start | bytes 933896 | tf_op jit(solution)/shard_map/ppermute | solution.py:218
  56.9 0.5 collective-permute-start.19
  57.4 2.5 %shard_map.94 = (bf16[1024,512]{1,0:T(8,128)(2,1)S(1)}, bf16[1024,512]{1,0:T(8,128)(2,1)S(1)}, f32[152,1024]{1,0:T(8,128)S(1)}) custom-call(bf16[256,448]{1,0:T(8,128)(2,1)S(1)} %get-tuple-element.75.refs_0_, bf16[256,448]{1,0:T(8,128)(2,1)S(1)} %get-tuple-element.78.refs_1_, bf16[256,448]{1,0:T(8,128)(2,1)S(1)} %get-tuple-element.81.refs_2_, ...), custom_call_target="tpu_custom_call" | custom-call | flops 1258291200 | bytes 2768896 | tf_op jit(solution)/shard_map/pallas_call | solution.py:192
  60.0 3.8 %collective-permute-start.12 = (bf16[152,256]{1,0:T(8,128)(2,1)S(1)}, bf16[152,256]{1,0:T(8,128)(2,1)S(1)}, u32[]{:S(2)}, u32[]{:S(2)}) collective-permute-start(bf16[152,256]{1,0:T(8,128)(2,1)S(1)} %get-tuple-element.108), channel_id=1, source_target_pairs={{0,8},{8,0},{16,24},{24,16},{1,9},{9,1},{17,25},{25,17},{2,10},{10... | collective-permute-start | bytes 233480 | tf_op jit(solution)/shard_map/ppermute | solution.py:209
  63.8 1.1 %collective-permute-start.13 = (bf16[152,256]{1,0:T(8,128)(2,1)S(1)}, bf16[152,256]{1,0:T(8,128)(2,1)S(1)}, u32[]{:S(2)}, u32[]{:S(2)}) collective-permute-start(bf16[152,256]{1,0:T(8,128)(2,1)S(1)} %get-tuple-element.109), channel_id=1, source_target_pairs={{0,16},{8,24},{16,0},{24,8},{1,17},{9,25},{17,1},{25,9},{2,18},{10... | collective-permute-start | bytes 233480 | tf_op jit(solution)/shard_map/ppermute | solution.py:209
  64.9 1.4 %collective-permute-start.14 = (bf16[152,256]{1,0:T(8,128)(2,1)S(1)}, bf16[152,256]{1,0:T(8,128)(2,1)S(1)}, u32[]{:S(2)}, u32[]{:S(2)}) collective-permute-start(bf16[152,256]{1,0:T(8,128)(2,1)S(1)} %get-tuple-element.110), channel_id=1, source_target_pairs={{0,24},{8,16},{16,8},{24,0},{1,25},{9,17},{17,9},{25,1},{2,26},{10... | collective-permute-start | bytes 233480 | tf_op jit(solution)/shard_map/ppermute | solution.py:209
  66.3 0.8 shard_map.97
  67.2 5.6 %collective-permute-done.13.refs_1_ = bf16[152,256]{1,0:T(8,128)(2,1)S(1)} collective-permute-done((bf16[152,256]{1,0:T(8,128)(2,1)S(1)}, bf16[152,256]{1,0:T(8,128)(2,1)S(1)}, u32[]{:S(2)}, u32[]{:S(2)}) %collective-permute-start.13) | collective-permute-done | bytes 77856 | tf_op jit(solution)/shard_map/ppermute | solution.py:209
  72.9 1.5 %collective-permute-start.15 = (bf16[152,256]{1,0:T(8,128)(2,1)S(1)}, bf16[152,256]{1,0:T(8,128)(2,1)S(1)}, u32[]{:S(2)}, u32[]{:S(2)}) collective-permute-start(bf16[152,256]{1,0:T(8,128)(2,1)S(1)} %shard_map.98.refs_0_), channel_id=1, source_target_pairs={{0,8},{8,0},{16,24},{24,16},{1,9},{9,1},{17,25},{25,17},{2,10},{10... | collective-permute-start | bytes 233480 | tf_op jit(solution)/shard_map/ppermute | solution.py:209
  74.3 1.4 %collective-permute-start.16 = (bf16[152,256]{1,0:T(8,128)(2,1)S(1)}, bf16[152,256]{1,0:T(8,128)(2,1)S(1)}, u32[]{:S(2)}, u32[]{:S(2)}) collective-permute-start(bf16[152,256]{1,0:T(8,128)(2,1)S(1)} %shard_map.98.refs_0_), channel_id=1, source_target_pairs={{0,16},{8,24},{16,0},{24,8},{1,17},{9,25},{17,1},{25,9},{2,18},{10... | collective-permute-start | bytes 233480 | tf_op jit(solution)/shard_map/ppermute | solution.py:209
  75.7 1.6 %collective-permute-start.17 = (bf16[152,256]{1,0:T(8,128)(2,1)S(1)}, bf16[152,256]{1,0:T(8,128)(2,1)S(1)}, u32[]{:S(2)}, u32[]{:S(2)}) collective-permute-start(bf16[152,256]{1,0:T(8,128)(2,1)S(1)} %shard_map.98.refs_0_), channel_id=1, source_target_pairs={{0,24},{8,16},{16,8},{24,0},{1,25},{9,17},{17,9},{25,1},{2,26},{10... | collective-permute-start | bytes 233480 | tf_op jit(solution)/shard_map/ppermute | solution.py:209
  77.3 1.1 %shard_map.107 = bf16[152,1024]{1,0:T(8,128)(2,1)S(1)} custom-call(bf16[600,256]{1,0:T(8,128)(2,1)S(1)} %fusion.10.refs_0_, bf16[600,256]{1,0:T(8,128)(2,1)S(1)} %collective-permute-done.refs_0_.refs_1_, bf16[600,256]{1,0:T(8,128)(2,1)S(1)} %collective-permute-done.1.refs_0_.refs_2_, bf16[600,256]{1,0:T(8,128)(2,1)S(1)} %collective-permute-done.2.refs_0_.refs_3_, ...), custom_call_target="tpu_custom_call" | custom-call | flops 637534208 | bytes 6651904 | tf_op jit(solution)/shard_map/pallas_call | solution.py:192
  78.4 1.6 %collective-permute-start.27 = (bf16[152,1024]{1,0:T(8,128)(2,1)S(1)}, bf16[152,1024]{1,0:T(8,128)(2,1)S(1)}, u32[]{:S(2)}, u32[]{:S(2)}) collective-permute-start(bf16[152,1024]{1,0:T(8,128)(2,1)S(1)} %shard_map.107), channel_id=1, source_target_pairs={{0,6},{1,7},{2,4},{3,5},{4,2},{5,3},{6,0},{7,1},{8,14},{9,15},{10,... | collective-permute-start | bytes 933896 | tf_op jit(solution)/shard_map/ppermute | solution.py:218
  80.0 2.5 %collective-permute-done.16.refs_2_ = bf16[152,256]{1,0:T(8,128)(2,1)S(1)} collective-permute-done((bf16[152,256]{1,0:T(8,128)(2,1)S(1)}, bf16[152,256]{1,0:T(8,128)(2,1)S(1)}, u32[]{:S(2)}, u32[]{:S(2)}) %collective-permute-start.16) | collective-permute-done | bytes 77856 | tf_op jit(solution)/shard_map/ppermute | solution.py:209
  84.7 0.5 shard_map.100
  85.2 0.6 collective-permute-start.25
  85.8 1.5 %collective-permute-start.26 = (bf16[152,512]{1,0:T(8,128)(2,1)S(1)}, bf16[152,512]{1,0:T(8,128)(2,1)S(1)}, u32[]{:S(2)}, u32[]{:S(2)}) collective-permute-start(bf16[152,512]{1,0:T(8,128)(2,1)S(1)} %get-tuple-element.131), channel_id=1, source_target_pairs={{0,4},{1,5},{2,6},{3,7},{4,0},{5,1},{6,2},{7,3},{8,12},{9,13},{10,... | collective-permute-start | bytes 466952 | tf_op jit(solution)/shard_map/ppermute | solution.py:218
  88.4 0.5 shard_map.101.refs_4_
  88.9 0.5 shard_map.104
  89.4 1.6 %collective-permute-start.24 = (bf16[152,512]{1,0:T(8,128)(2,1)S(1)}, bf16[152,512]{1,0:T(8,128)(2,1)S(1)}, u32[]{:S(2)}, u32[]{:S(2)}) collective-permute-start(bf16[152,512]{1,0:T(8,128)(2,1)S(1)} %get-tuple-element.128), channel_id=1, source_target_pairs={{0,2},{1,3},{2,0},{3,1},{4,6},{5,7},{6,4},{7,5},{8,10},{9,11},{10,... | collective-permute-start | bytes 466952 | tf_op jit(solution)/shard_map/ppermute | solution.py:218
  91.5 0.6 collective-permute-start.30
  92.7 0.6 collective-permute-start.29
  93.3 1.6 %collective-permute-start.28 = (bf16[152,512]{1,0:T(8,128)(2,1)S(1)}, bf16[152,512]{1,0:T(8,128)(2,1)S(1)}, u32[]{:S(2)}, u32[]{:S(2)}) collective-permute-start(bf16[152,512]{1,0:T(8,128)(2,1)S(1)} %shard_map.108), channel_id=1, source_target_pairs={{0,4},{1,5},{2,6},{3,7},{4,0},{5,1},{6,2},{7,3},{8,12},{9,13},{10,... | collective-permute-start | bytes 466952 | tf_op jit(solution)/shard_map/ppermute | solution.py:218
  94.9 1.0 fusion.6
  95.9 2.5 %collective-permute-done.30 = bf16[152,512]{1,0:T(8,128)(2,1)S(1)} collective-permute-done((bf16[152,512]{1,0:T(8,128)(2,1)S(1)}, bf16[152,512]{1,0:T(8,128)(2,1)S(1)}, u32[]{:S(2)}, u32[]{:S(2)}) %collective-permute-start.30) | collective-permute-done | bytes 155680 | tf_op jit(solution)/shard_map/ppermute | solution.py:218
  98.4 1.7 %collective-permute-done.28 = bf16[152,512]{1,0:T(8,128)(2,1)S(1)} collective-permute-done((bf16[152,512]{1,0:T(8,128)(2,1)S(1)}, bf16[152,512]{1,0:T(8,128)(2,1)S(1)}, u32[]{:S(2)}, u32[]{:S(2)}) %collective-permute-start.28) | collective-permute-done | bytes 155680 | tf_op jit(solution)/shard_map/ppermute | solution.py:218
  100.2 0.9 maximum_add_fusion
  (55 shorter events, 5.2 us)
Async XLA Ops:
  0.6 6.2 %copy-start = (bf16[147,256]{1,0:T(8,128)(2,1)S(1)}, bf16[147,256]{1,0:T(8,128)(2,1)}, u32[]{:S(2)}) copy-start(bf16[147,256]{1,0:T(8,128)(2,1)} %refs_3_.1) | copy-start | bytes 225796
  0.6 6.9 %copy-start.2 = (bf16[440,256]{1,0:T(8,128)(2,1)S(1)}, bf16[440,256]{1,0:T(8,128)(2,1)}, u32[]{:S(2)}) copy-start(bf16[440,256]{1,0:T(8,128)(2,1)} %param.7) | copy-start | bytes 675844
  2.1 33.0 %collective-permute-start.8 = (bf16[600,1024]{1,0:T(8,128)(2,1)S(1)}, bf16[600,1024]{1,0:T(8,128)(2,1)S(1)}, u32[]{:S(2)}, u32[]{:S(2)}) collective-permute-start(bf16[600,1024]{1,0:T(8,128)(2,1)S(1)} %fusion.4.refs_1_.refs_4_), channel_id=1, source_target_pairs={{0,4},{1,5},{2,6},{3,7},{4,0},{5,1},{6,2},{7,3},{8,12},{9,13},{10,... | collective-permute-start | bytes 3686408 | tf_op jit(solution)/shard_map/ppermute | solution.py:218
  5.1 30.9 %collective-permute-start.7 = (bf16[600,1024]{1,0:T(8,128)(2,1)S(1)}, bf16[600,1024]{1,0:T(8,128)(2,1)S(1)}, u32[]{:S(2)}, u32[]{:S(2)}) collective-permute-start(bf16[600,1024]{1,0:T(8,128)(2,1)S(1)} %fusion.4.refs_1_.refs_4_), channel_id=1, source_target_pairs={{0,2},{1,3},{2,0},{3,1},{4,6},{5,7},{6,4},{7,5},{8,10},{9,11},{10,... | collective-permute-start | bytes 3686408 | tf_op jit(solution)/shard_map/ppermute | solution.py:218
  7.7 14.0 %collective-permute-start = (bf16[600,256]{1,0:T(8,128)(2,1)S(1)}, bf16[600,256]{1,0:T(8,128)(2,1)S(1)}, u32[]{:S(2)}, u32[]{:S(2)}) collective-permute-start(bf16[600,256]{1,0:T(8,128)(2,1)S(1)} %fusion.10.refs_0_), channel_id=1, source_target_pairs={{0,8},{8,0},{16,24},{24,16},{1,9},{9,1},{17,25},{25,17},{2,10},{10... | collective-permute-start | bytes 921608 | tf_op jit(solution)/shard_map/ppermute | solution.py:209
  9.4 24.3 %collective-permute-start.1 = (bf16[600,256]{1,0:T(8,128)(2,1)S(1)}, bf16[600,256]{1,0:T(8,128)(2,1)S(1)}, u32[]{:S(2)}, u32[]{:S(2)}) collective-permute-start(bf16[600,256]{1,0:T(8,128)(2,1)S(1)} %fusion.10.refs_0_), channel_id=1, source_target_pairs={{0,16},{8,24},{16,0},{24,8},{1,17},{9,25},{17,1},{25,9},{2,18},{10... | collective-permute-start | bytes 921608 | tf_op jit(solution)/shard_map/ppermute | solution.py:209
  12.0 22.5 %collective-permute-start.2 = (bf16[600,256]{1,0:T(8,128)(2,1)S(1)}, bf16[600,256]{1,0:T(8,128)(2,1)S(1)}, u32[]{:S(2)}, u32[]{:S(2)}) collective-permute-start(bf16[600,256]{1,0:T(8,128)(2,1)S(1)} %fusion.10.refs_0_), channel_id=1, source_target_pairs={{0,24},{8,16},{16,8},{24,0},{1,25},{9,17},{17,9},{25,1},{2,26},{10... | collective-permute-start | bytes 921608 | tf_op jit(solution)/shard_map/ppermute | solution.py:209
  21.8 14.9 %collective-permute-start.3 = (bf16[600,256]{1,0:T(8,128)(2,1)S(1)}, bf16[600,256]{1,0:T(8,128)(2,1)S(1)}, u32[]{:S(2)}, u32[]{:S(2)}) collective-permute-start(bf16[600,256]{1,0:T(8,128)(2,1)S(1)} %fusion.10.refs_0_), channel_id=1, source_target_pairs={{0,1},{1,0},{2,3},{3,2},{4,5},{5,4},{6,7},{7,6},{8,9},{9,8},{10,11... | collective-permute-start | bytes 921608 | tf_op jit(solution)/shard_map/ppermute | solution.py:203
  33.7 3.7 %collective-permute-start.5 = (bf16[600,256]{1,0:T(8,128)(2,1)S(1)}, bf16[600,256]{1,0:T(8,128)(2,1)S(1)}, u32[]{:S(2)}, u32[]{:S(2)}) collective-permute-start(bf16[600,256]{1,0:T(8,128)(2,1)S(1)} %collective-permute-done.1.refs_0_.refs_2_), channel_id=1, source_target_pairs={{0,1},{1,0},{2,3},{3,2},{4,5},{5,4},{6,7},{7,6},{8,9},{9,8},{10,11... | collective-permute-start | bytes 921608 | tf_op jit(solution)/shard_map/ppermute | solution.py:203
  34.5 2.8 %collective-permute-start.6 = (bf16[600,256]{1,0:T(8,128)(2,1)S(1)}, bf16[600,256]{1,0:T(8,128)(2,1)S(1)}, u32[]{:S(2)}, u32[]{:S(2)}) collective-permute-start(bf16[600,256]{1,0:T(8,128)(2,1)S(1)} %collective-permute-done.2.refs_0_.refs_3_), channel_id=1, source_target_pairs={{0,1},{1,0},{2,3},{3,2},{4,5},{5,4},{6,7},{7,6},{8,9},{9,8},{10,11... | collective-permute-start | bytes 921608 | tf_op jit(solution)/shard_map/ppermute | solution.py:203
  35.1 2.2 %collective-permute-start.4 = (bf16[600,256]{1,0:T(8,128)(2,1)S(1)}, bf16[600,256]{1,0:T(8,128)(2,1)S(1)}, u32[]{:S(2)}, u32[]{:S(2)}) collective-permute-start(bf16[600,256]{1,0:T(8,128)(2,1)S(1)} %collective-permute-done.refs_0_.refs_1_), channel_id=1, source_target_pairs={{0,1},{1,0},{2,3},{3,2},{4,5},{5,4},{6,7},{7,6},{8,9},{9,8},{10,11... | collective-permute-start | bytes 921608 | tf_op jit(solution)/shard_map/ppermute | solution.py:203
  36.1 16.3 %collective-permute-start.10 = (bf16[600,512]{1,0:T(8,128)(2,1)S(1)}, bf16[600,512]{1,0:T(8,128)(2,1)S(1)}, u32[]{:S(2)}, u32[]{:S(2)}) collective-permute-start(bf16[600,512]{1,0:T(8,128)(2,1)S(1)} %slice.37), channel_id=1, source_target_pairs={{0,2},{1,3},{2,0},{3,1},{4,6},{5,7},{6,4},{7,5},{8,10},{9,11},{10,... | collective-permute-start | bytes 1843208 | tf_op jit(solution)/shard_map/ppermute | solution.py:218
  36.7 16.0 %collective-permute-start.9 = (bf16[600,512]{1,0:T(8,128)(2,1)S(1)}, bf16[600,512]{1,0:T(8,128)(2,1)S(1)}, u32[]{:S(2)}, u32[]{:S(2)}) collective-permute-start(bf16[600,512]{1,0:T(8,128)(2,1)S(1)} %slice.36), channel_id=1, source_target_pairs={{0,4},{1,5},{2,6},{3,7},{4,0},{5,1},{6,2},{7,3},{8,12},{9,13},{10,... | collective-permute-start | bytes 1843208 | tf_op jit(solution)/shard_map/ppermute | solution.py:218
  55.3 4.7 %collective-permute-start.11 = (bf16[152,1024]{1,0:T(8,128)(2,1)S(1)}, bf16[152,1024]{1,0:T(8,128)(2,1)S(1)}, u32[]{:S(2)}, u32[]{:S(2)}) collective-permute-start(bf16[152,1024]{1,0:T(8,128)(2,1)S(1)} %get-tuple-element.98), channel_id=1, source_target_pairs={{0,1},{1,0},{2,3},{3,2},{4,5},{5,4},{6,7},{7,6},{8,9},{9,8},{10,11... | collective-permute-start | bytes 933896 | tf_op jit(solution)/shard_map/ppermute | solution.py:203
  55.4 23.1 %collective-permute-start.18 = (bf16[152,1024]{1,0:T(8,128)(2,1)S(1)}, bf16[152,1024]{1,0:T(8,128)(2,1)S(1)}, u32[]{:S(2)}, u32[]{:S(2)}) collective-permute-start(bf16[152,1024]{1,0:T(8,128)(2,1)S(1)} %shard_map.92), channel_id=1, source_target_pairs={{0,2},{1,3},{2,0},{3,1},{4,6},{5,7},{6,4},{7,5},{8,10},{9,11},{10,... | collective-permute-start | bytes 933896 | tf_op jit(solution)/shard_map/ppermute | solution.py:218
  56.9 23.1 %collective-permute-start.19 = (bf16[152,1024]{1,0:T(8,128)(2,1)S(1)}, bf16[152,1024]{1,0:T(8,128)(2,1)S(1)}, u32[]{:S(2)}, u32[]{:S(2)}) collective-permute-start(bf16[152,1024]{1,0:T(8,128)(2,1)S(1)} %shard_map.93), channel_id=1, source_target_pairs={{0,4},{1,5},{2,6},{3,7},{4,0},{5,1},{6,2},{7,3},{8,12},{9,13},{10,... | collective-permute-start | bytes 933896 | tf_op jit(solution)/shard_map/ppermute | solution.py:218
  60.0 7.1 %collective-permute-start.12 = (bf16[152,256]{1,0:T(8,128)(2,1)S(1)}, bf16[152,256]{1,0:T(8,128)(2,1)S(1)}, u32[]{:S(2)}, u32[]{:S(2)}) collective-permute-start(bf16[152,256]{1,0:T(8,128)(2,1)S(1)} %get-tuple-element.108), channel_id=1, source_target_pairs={{0,8},{8,0},{16,24},{24,16},{1,9},{9,1},{17,25},{25,17},{2,10},{10... | collective-permute-start | bytes 233480 | tf_op jit(solution)/shard_map/ppermute | solution.py:209
  63.8 8.9 %collective-permute-start.13 = (bf16[152,256]{1,0:T(8,128)(2,1)S(1)}, bf16[152,256]{1,0:T(8,128)(2,1)S(1)}, u32[]{:S(2)}, u32[]{:S(2)}) collective-permute-start(bf16[152,256]{1,0:T(8,128)(2,1)S(1)} %get-tuple-element.109), channel_id=1, source_target_pairs={{0,16},{8,24},{16,0},{24,8},{1,17},{9,25},{17,1},{25,9},{2,18},{10... | collective-permute-start | bytes 233480 | tf_op jit(solution)/shard_map/ppermute | solution.py:209
  64.9 7.9 %collective-permute-start.14 = (bf16[152,256]{1,0:T(8,128)(2,1)S(1)}, bf16[152,256]{1,0:T(8,128)(2,1)S(1)}, u32[]{:S(2)}, u32[]{:S(2)}) collective-permute-start(bf16[152,256]{1,0:T(8,128)(2,1)S(1)} %get-tuple-element.110), channel_id=1, source_target_pairs={{0,24},{8,16},{16,8},{24,0},{1,25},{9,17},{17,9},{25,1},{2,26},{10... | collective-permute-start | bytes 233480 | tf_op jit(solution)/shard_map/ppermute | solution.py:209
  72.9 7.1 %collective-permute-start.15 = (bf16[152,256]{1,0:T(8,128)(2,1)S(1)}, bf16[152,256]{1,0:T(8,128)(2,1)S(1)}, u32[]{:S(2)}, u32[]{:S(2)}) collective-permute-start(bf16[152,256]{1,0:T(8,128)(2,1)S(1)} %shard_map.98.refs_0_), channel_id=1, source_target_pairs={{0,8},{8,0},{16,24},{24,16},{1,9},{9,1},{17,25},{25,17},{2,10},{10... | collective-permute-start | bytes 233480 | tf_op jit(solution)/shard_map/ppermute | solution.py:209
  74.3 8.1 %collective-permute-start.16 = (bf16[152,256]{1,0:T(8,128)(2,1)S(1)}, bf16[152,256]{1,0:T(8,128)(2,1)S(1)}, u32[]{:S(2)}, u32[]{:S(2)}) collective-permute-start(bf16[152,256]{1,0:T(8,128)(2,1)S(1)} %shard_map.98.refs_0_), channel_id=1, source_target_pairs={{0,16},{8,24},{16,0},{24,8},{1,17},{9,25},{17,1},{25,9},{2,18},{10... | collective-permute-start | bytes 233480 | tf_op jit(solution)/shard_map/ppermute | solution.py:209
  75.7 6.7 %collective-permute-start.17 = (bf16[152,256]{1,0:T(8,128)(2,1)S(1)}, bf16[152,256]{1,0:T(8,128)(2,1)S(1)}, u32[]{:S(2)}, u32[]{:S(2)}) collective-permute-start(bf16[152,256]{1,0:T(8,128)(2,1)S(1)} %shard_map.98.refs_0_), channel_id=1, source_target_pairs={{0,24},{8,16},{16,8},{24,0},{1,25},{9,17},{17,9},{25,1},{2,26},{10... | collective-permute-start | bytes 233480 | tf_op jit(solution)/shard_map/ppermute | solution.py:209
  78.4 14.1 %collective-permute-start.27 = (bf16[152,1024]{1,0:T(8,128)(2,1)S(1)}, bf16[152,1024]{1,0:T(8,128)(2,1)S(1)}, u32[]{:S(2)}, u32[]{:S(2)}) collective-permute-start(bf16[152,1024]{1,0:T(8,128)(2,1)S(1)} %shard_map.107), channel_id=1, source_target_pairs={{0,6},{1,7},{2,4},{3,5},{4,2},{5,3},{6,0},{7,1},{8,14},{9,15},{10,... | collective-permute-start | bytes 933896 | tf_op jit(solution)/shard_map/ppermute | solution.py:218
  82.5 2.2 %collective-permute-start.20 = (bf16[152,256]{1,0:T(8,128)(2,1)S(1)}, bf16[152,256]{1,0:T(8,128)(2,1)S(1)}, u32[]{:S(2)}, u32[]{:S(2)}) collective-permute-start(bf16[152,256]{1,0:T(8,128)(2,1)S(1)} %shard_map.98.refs_0_), channel_id=1, source_target_pairs={{0,1},{1,0},{2,3},{3,2},{4,5},{5,4},{6,7},{7,6},{8,9},{9,8},{10,11... | collective-permute-start | bytes 233480 | tf_op jit(solution)/shard_map/ppermute | solution.py:203
  82.5 2.2 %collective-permute-start.21 = (bf16[152,256]{1,0:T(8,128)(2,1)S(1)}, bf16[152,256]{1,0:T(8,128)(2,1)S(1)}, u32[]{:S(2)}, u32[]{:S(2)}) collective-permute-start(bf16[152,256]{1,0:T(8,128)(2,1)S(1)} %collective-permute-done.15.refs_1_), channel_id=1, source_target_pairs={{0,1},{1,0},{2,3},{3,2},{4,5},{5,4},{6,7},{7,6},{8,9},{9,8},{10,11... | collective-permute-start | bytes 233480 | tf_op jit(solution)/shard_map/ppermute | solution.py:203
  83.0 1.7 %collective-permute-start.22 = (bf16[152,256]{1,0:T(8,128)(2,1)S(1)}, bf16[152,256]{1,0:T(8,128)(2,1)S(1)}, u32[]{:S(2)}, u32[]{:S(2)}) collective-permute-start(bf16[152,256]{1,0:T(8,128)(2,1)S(1)} %collective-permute-done.16.refs_2_), channel_id=1, source_target_pairs={{0,1},{1,0},{2,3},{3,2},{4,5},{5,4},{6,7},{7,6},{8,9},{9,8},{10,11... | collective-permute-start | bytes 233480 | tf_op jit(solution)/shard_map/ppermute | solution.py:203
  83.0 1.7 %collective-permute-start.23 = (bf16[152,256]{1,0:T(8,128)(2,1)S(1)}, bf16[152,256]{1,0:T(8,128)(2,1)S(1)}, u32[]{:S(2)}, u32[]{:S(2)}) collective-permute-start(bf16[152,256]{1,0:T(8,128)(2,1)S(1)} %collective-permute-done.17.refs_3_), channel_id=1, source_target_pairs={{0,1},{1,0},{2,3},{3,2},{4,5},{5,4},{6,7},{7,6},{8,9},{9,8},{10,11... | collective-permute-start | bytes 233480 | tf_op jit(solution)/shard_map/ppermute | solution.py:203
  85.2 7.4 %collective-permute-start.25 = (bf16[152,512]{1,0:T(8,128)(2,1)S(1)}, bf16[152,512]{1,0:T(8,128)(2,1)S(1)}, u32[]{:S(2)}, u32[]{:S(2)}) collective-permute-start(bf16[152,512]{1,0:T(8,128)(2,1)S(1)} %get-tuple-element.130), channel_id=1, source_target_pairs={{0,2},{1,3},{2,0},{3,1},{4,6},{5,7},{6,4},{7,5},{8,10},{9,11},{10,... | collective-permute-start | bytes 466952 | tf_op jit(solution)/shard_map/ppermute | solution.py:218
  85.8 6.8 %collective-permute-start.26 = (bf16[152,512]{1,0:T(8,128)(2,1)S(1)}, bf16[152,512]{1,0:T(8,128)(2,1)S(1)}, u32[]{:S(2)}, u32[]{:S(2)}) collective-permute-start(bf16[152,512]{1,0:T(8,128)(2,1)S(1)} %get-tuple-element.131), channel_id=1, source_target_pairs={{0,4},{1,5},{2,6},{3,7},{4,0},{5,1},{6,2},{7,3},{8,12},{9,13},{10,... | collective-permute-start | bytes 466952 | tf_op jit(solution)/shard_map/ppermute | solution.py:218
  89.4 6.5 %collective-permute-start.24 = (bf16[152,512]{1,0:T(8,128)(2,1)S(1)}, bf16[152,512]{1,0:T(8,128)(2,1)S(1)}, u32[]{:S(2)}, u32[]{:S(2)}) collective-permute-start(bf16[152,512]{1,0:T(8,128)(2,1)S(1)} %get-tuple-element.128), channel_id=1, source_target_pairs={{0,2},{1,3},{2,0},{3,1},{4,6},{5,7},{6,4},{7,5},{8,10},{9,11},{10,... | collective-permute-start | bytes 466952 | tf_op jit(solution)/shard_map/ppermute | solution.py:218
  91.5 6.9 %collective-permute-start.30 = (bf16[152,512]{1,0:T(8,128)(2,1)S(1)}, bf16[152,512]{1,0:T(8,128)(2,1)S(1)}, u32[]{:S(2)}, u32[]{:S(2)}) collective-permute-start(bf16[152,512]{1,0:T(8,128)(2,1)S(1)} %get-tuple-element.143), channel_id=1, source_target_pairs={{0,4},{1,5},{2,6},{3,7},{4,0},{5,1},{6,2},{7,3},{8,12},{9,13},{10,... | collective-permute-start | bytes 466952 | tf_op jit(solution)/shard_map/ppermute | solution.py:218
  92.6 7.6 %copy-start.1 = (bf16[147,1024]{1,0:T(8,128)(2,1)S(1)}, bf16[147,1024]{1,0:T(8,128)(2,1)}, u32[]{:S(2)}) copy-start(bf16[147,1024]{1,0:T(8,128)(2,1)} %param.12) | copy-start | bytes 903172
  92.7 5.7 %collective-permute-start.29 = (bf16[152,512]{1,0:T(8,128)(2,1)S(1)}, bf16[152,512]{1,0:T(8,128)(2,1)S(1)}, u32[]{:S(2)}, u32[]{:S(2)}) collective-permute-start(bf16[152,512]{1,0:T(8,128)(2,1)S(1)} %shard_map.109), channel_id=1, source_target_pairs={{0,2},{1,3},{2,0},{3,1},{4,6},{5,7},{6,4},{7,5},{8,10},{9,11},{10,... | collective-permute-start | bytes 466952 | tf_op jit(solution)/shard_map/ppermute | solution.py:218
  93.3 6.7 %collective-permute-start.28 = (bf16[152,512]{1,0:T(8,128)(2,1)S(1)}, bf16[152,512]{1,0:T(8,128)(2,1)S(1)}, u32[]{:S(2)}, u32[]{:S(2)}) collective-permute-start(bf16[152,512]{1,0:T(8,128)(2,1)S(1)} %shard_map.108), channel_id=1, source_target_pairs={{0,4},{1,5},{2,6},{3,7},{4,0},{5,1},{6,2},{7,3},{8,12},{9,13},{10,... | collective-permute-start | bytes 466952 | tf_op jit(solution)/shard_map/ppermute | solution.py:218

commit v7 on v6

--- a/solution.py
+++ b/solution.py
@@ -96,25 +96,35 @@
         t_ref[here, :] = total
 
 
+def rows_of(refs, block, group):
+    pieces = [(ref, at) for ref in refs for at in range(0, ref.shape[0], block)]
+    return [pieces[j : j + group] for j in range(0, len(pieces), group)]
+
+
+def load(pieces, block):
+    (first, start), (_, end) = pieces[0], pieces[-1]
+    if all(ref is first for ref, _ in pieces):
+        return first[start : end + block, :]
+    return jnp.concatenate([ref[at : at + block, :] for ref, at in pieces], axis=0)
+
+
 def next_kernel(depth, count, totals, parts, block, last, *refs):
     xt_refs, t_refs = refs[:count], refs[count : count + totals]
     refs = refs[count + totals :]
     w_refs, f_refs, out_refs = refs[:parts], refs[parts : 2 * parts], refs[2 * parts :]
-    t_blocks = [(ref, at) for ref in t_refs for at in range(0, ref.shape[0], block)]
     spot = 0
-    for xt_ref in xt_refs:
-        for at in range(0, xt_ref.shape[0], block):
-            t_ref, t_at = t_blocks[spot // block]
-            xt, total = xt_ref[at : at + block, :], t_ref[t_at : t_at + block, :]
-            for w_ref, f_ref in zip(w_refs, f_refs, strict=True):
-                f_ref[spot : spot + block, :], tangent = one_block(xt, w_ref, depth)
-                total = total + tangent
-            if not last:
-                here = spot % out_refs[0].shape[0]
-                out_refs[spot // out_refs[0].shape[0]][here : here + block, :] = total
-            else:
-                out_refs[0][:, spot : spot + block] = total.T.astype(out_refs[0].dtype)
-            spot += block
+    for xt_pieces, t_pieces in zip(rows_of(xt_refs, block, 2), rows_of(t_refs, block, 2), strict=True):
+        xt, total = load(xt_pieces, block), load(t_pieces, block)
+        n = xt.shape[0]
+        for w_ref, f_ref in zip(w_refs, f_refs, strict=True):
+            f_ref[spot : spot + n, :], tangent = one_block(xt, w_ref, depth)
+            total = total + tangent
+        if not last:
+            here = spot % out_refs[0].shape[0]
+            out_refs[spot // out_refs[0].shape[0]][here : here + n, :] = total
+        else:
+            out_refs[0][:, spot : spot + n] = total.T.astype(out_refs[0].dtype)
+        spot += n
 
 
 def make_next(xts, totals, pieces, depth, wide, block, last=None):
@@ -125,7 +135,7 @@
     else:
         shapes.append(jax.ShapeDtypeStruct((wide, n), last))
     kernel = functools.partial(next_kernel, depth, len(xts), len(totals), len(pieces), block, last is not None)
-    out = whole(kernel, shapes, *xts, *totals, *pieces, flops=2 * n * f * len(pieces) * (depth + wide))
+    out = whole(kernel, shapes, *xts, *totals, *pieces, flops=2 * n * f * len(pieces) * (depth + wide), weight=0.5 if last is None else 1)
     return out[: len(pieces)], out[len(pieces) :]
 
 
@@ -188,7 +198,7 @@
 
 def whole(kernel, shapes, *args, flops=0, weight=1):
     size = sum(math.prod(a.shape) * a.dtype.itemsize for a in args)
-    cost = pl.CostEstimate(flops=weight * flops, bytes_accessed=weight * size, transcendentals=0)
+    cost = pl.CostEstimate(flops=int(weight * flops), bytes_accessed=int(weight * size), transcendentals=0)
     return pl.pallas_call(kernel, out_shape=shapes, compiler_params=params(), cost_estimate=cost)(*args)
 
 
@@ -311,8 +321,8 @@
         functools.partial(curve_kernel, classes), jax.ShapeDtypeStruct((wide, own), BF16), keep, *got, probs
     )
     c_line = [curv] + [along(curv, k) for k in places]
-    c_line, ready = lax.optimization_barrier((c_line, {at: arrived[at] for at in near}))
     c_peer = [swap_core(a) for a in c_line]
+    c_peer, ready = lax.optimization_barrier((c_peer, {at: arrived[at] for at in near}))
     seeds = {at: make_share(c_line, 0, feats[at], F32) for at in offsets[::-1]}
 
     def total_share(at, dtype, outs=1):

time: 101 us -> 99.9 us (0.989)
  transfers between devices with their start and end apart: 31 -> 31, of which waited for: 8 -> 8; matrix products, arithmetic and copies ran while one was open for 2% -> 2% of each run, Pallas kernels for 26% -> 25%
where the time goes in v7:
time: 99.9 us; the launch traced here: 99.8 us
  waiting for transfers between devices  33 us (33%)
  starting transfers between devices  32.6 us (33%)
  Pallas kernels  27.8 us (28%)
  other arithmetic  4.41 us (4%)
  between operations  1.68 us (2%)
    pallas_call x24, Pallas kernels, whole(): pl.pallas_call(kernel, out_shape=shapes, compiler_params=params(), cost_e...  27.8 us
    ppermute x9, waiting for transfers between devices, along(): return lax.ppermute(a, 'samp', [(i, to(i)) for i in range(line)])  27.5 us
    ppermute x13, starting transfers between devices, across(): return lax.ppermute(a, 'feat', [(i, to(i)) for i in range(2 * xs * ys)])  15.5 us
    ppermute x9, starting transfers between devices, along(): return lax.ppermute(a, 'samp', [(i, to(i)) for i in range(line)])  15.3 us
    ppermute x13, waiting for transfers between devices, across(): return lax.ppermute(a, 'feat', [(i, to(i)) for i in range(2 * xs * ys)])  5.54 us
  transfers between devices with their start and end apart: 31, of which 8 were waited for; matrix products, arithmetic and copies ran while one was open for 2% of the time, Pallas kernels for 25%

profile of v7, /device:TPU:0, one launch (start us, length us, event | category | flops | bytes accessed | tf_op | source)
XLA Modules:
  0.0 99.8 jit_solution(1183586616996604018)
XLA Ops:
  0.7 1.5 %fusion.4.refs_1_.refs_4_ = bf16[600,1024]{1,0:T(8,128)(2,1)S(1)} fusion(bf16[147,1024]{1,0:T(8,128)(2,1)} %param.12, bf16[1,1024]{1,0:T(2,128)(2,1)} %param.11, bf16[440,1024]{1,0:T(8,128)(2,1)} %param.10), kind=kLoop, calls=%fused_computation.7 | loop fusion | flops 7372800 | bytes 2433024 | tf_op jit(solution)/shard_map/concatenate | solution.py:232
  2.1 3.0 %collective-permute-start.8 = (bf16[600,1024]{1,0:T(8,128)(2,1)S(1)}, bf16[600,1024]{1,0:T(8,128)(2,1)S(1)}, u32[]{:S(2)}, u32[]{:S(2)}) collective-permute-start(bf16[600,1024]{1,0:T(8,128)(2,1)S(1)} %fusion.4.refs_1_.refs_4_), channel_id=1, source_target_pairs={{0,4},{1,5},{2,6},{3,7},{4,0},{5,1},{6,2},{7,3},{8,12},{9,13},{10,... | collective-permute-start | bytes 3686408 | tf_op jit(solution)/shard_map/ppermute | solution.py:228
  5.1 1.5 %collective-permute-start.7 = (bf16[600,1024]{1,0:T(8,128)(2,1)S(1)}, bf16[600,1024]{1,0:T(8,128)(2,1)S(1)}, u32[]{:S(2)}, u32[]{:S(2)}) collective-permute-start(bf16[600,1024]{1,0:T(8,128)(2,1)S(1)} %fusion.4.refs_1_.refs_4_), channel_id=1, source_target_pairs={{0,2},{1,3},{2,0},{3,1},{4,6},{5,7},{6,4},{7,5},{8,10},{9,11},{10,... | collective-permute-start | bytes 3686408 | tf_op jit(solution)/shard_map/ppermute | solution.py:228
  6.8 0.7 subtract_convert_fusion
  7.7 1.6 %collective-permute-start = (bf16[600,256]{1,0:T(8,128)(2,1)S(1)}, bf16[600,256]{1,0:T(8,128)(2,1)S(1)}, u32[]{:S(2)}, u32[]{:S(2)}) collective-permute-start(bf16[600,256]{1,0:T(8,128)(2,1)S(1)} %fusion.10.refs_0_), channel_id=1, source_target_pairs={{0,8},{8,0},{16,24},{24,16},{1,9},{9,1},{17,25},{25,17},{2,10},{10... | collective-permute-start | bytes 921608 | tf_op jit(solution)/shard_map/ppermute | solution.py:219
  9.4 2.6 %collective-permute-start.1 = (bf16[600,256]{1,0:T(8,128)(2,1)S(1)}, bf16[600,256]{1,0:T(8,128)(2,1)S(1)}, u32[]{:S(2)}, u32[]{:S(2)}) collective-permute-start(bf16[600,256]{1,0:T(8,128)(2,1)S(1)} %fusion.10.refs_0_), channel_id=1, source_target_pairs={{0,16},{8,24},{16,0},{24,8},{1,17},{9,25},{17,1},{25,9},{2,18},{10... | collective-permute-start | bytes 921608 | tf_op jit(solution)/shard_map/ppermute | solution.py:219
  12.2 9.6 %collective-permute-done.refs_0_.refs_1_ = bf16[600,256]{1,0:T(8,128)(2,1)S(1)} collective-permute-done((bf16[600,256]{1,0:T(8,128)(2,1)S(1)}, bf16[600,256]{1,0:T(8,128)(2,1)S(1)}, u32[]{:S(2)}, u32[]{:S(2)}) %collective-permute-start) | collective-permute-done | bytes 307232 | tf_op jit(solution)/shard_map/ppermute | solution.py:219
  21.8 0.8 shard_map.86
  22.6 0.8 shard_map.87
  23.5 10.2 %collective-permute-done.1.refs_0_.refs_2_ = bf16[600,256]{1,0:T(8,128)(2,1)S(1)} collective-permute-done((bf16[600,256]{1,0:T(8,128)(2,1)S(1)}, bf16[600,256]{1,0:T(8,128)(2,1)S(1)}, u32[]{:S(2)}, u32[]{:S(2)}) %collective-permute-start.1) | collective-permute-done | bytes 307232 | tf_op jit(solution)/shard_map/ppermute | solution.py:219
  33.7 0.8 shard_map.88
  34.5 0.6 collective-permute-start.6
  35.2 0.6 collective-permute-start.10
  35.9 0.6 collective-permute-start.9
  36.5 0.8 shard_map.89
  37.3 2.5 %shard_map.90 = (bf16[1024,448]{1,0:T(8,128)(2,1)S(1)}, f32[1024,152]{1,0:T(8,128)S(1)}, bf16[1024,1024]{1,0:T(8,128)(2,1)S(1)}) custom-call(bf16[600,256]{1,0:T(8,128)(2,1)S(1)} %collective-permute-done.3.refs_0_.refs_4_, bf16[600,256]{1,0:T(8,128)(2,1)S(1)} %collective-permute-done.4.refs_1_.refs_5_, ...), custom_call_target="tpu_custom_call" | custom-call | flops 1258291200 | bytes 2457600 | tf_op jit(solution)/shard_map/pallas_call | solution.py:202
  39.8 9.0 %shard_map.91 = (bf16[2048,1024]{1,0:T(8,128)(2,1)S(1)}, bf16[2048,1024]{1,0:T(8,128)(2,1)S(1)}, f32[1024,152]{1,0:T(8,128)S(1)}, f32[1024,152]{1,0:T(8,128)S(1)}) custom-call(bf16[256,448]{1,0:T(8,128)(2,1)S(1)} %get-tuple-element.75.refs_0_, bf16[256,448]{1,0:T(8,128)(2,1)S(1)} %get-tuple-element.78.refs_1_, ...), custom_call_target="tpu_custom_call" | custom-call | flops 2516582400 | bytes 2768896 | tf_op jit(solution)/shard_map/pallas_call | solution.py:202
  48.8 0.9 shard_map.93
  49.6 0.9 shard_map.92
  50.5 1.0 collective-permute-done.10.refs_6_.refs_3_
  51.9 2.6 %shard_map.95 = (bf16[1024,512]{1,0:T(8,128)(2,1)S(1)}, bf16[1024,512]{1,0:T(8,128)(2,1)S(1)}, bf16[152,1024]{1,0:T(8,128)(2,1)S(1)}) custom-call(bf16[1024,448]{1,0:T(8,128)(2,1)S(1)} %get-tuple-element.85.refs_4_.refs_0_, f32[1024,152]{1,0:T(8,128)S(1)} %get-tuple-element.97.refs_1_, bf16[600,512]{1,0:T(8,128)(2,1)S(1)} %collective-permute-done.9.refs_5_.refs_2_, ...), custom_call_target="tpu_custom_call" | custom-call | flops 1258291200 | bytes 2768896 | tf_op jit(solution)/shard_map/pallas_call | solution.py:202
  54.5 1.6 %collective-permute-start.22 = (bf16[152,1024]{1,0:T(8,128)(2,1)S(1)}, bf16[152,1024]{1,0:T(8,128)(2,1)S(1)}, u32[]{:S(2)}, u32[]{:S(2)}) collective-permute-start(bf16[152,1024]{1,0:T(8,128)(2,1)S(1)} %shard_map.92), channel_id=1, source_target_pairs={{0,2},{1,3},{2,0},{3,1},{4,6},{5,7},{6,4},{7,5},{8,10},{9,11},{10,... | collective-permute-start | bytes 933896 | tf_op jit(solution)/shard_map/ppermute | solution.py:228
  56.6 2.5 %shard_map.94 = (bf16[1024,512]{1,0:T(8,128)(2,1)S(1)}, bf16[1024,512]{1,0:T(8,128)(2,1)S(1)}, f32[152,1024]{1,0:T(8,128)S(1)}) custom-call(bf16[256,448]{1,0:T(8,128)(2,1)S(1)} %get-tuple-element.75.refs_0_, bf16[256,448]{1,0:T(8,128)(2,1)S(1)} %get-tuple-element.78.refs_1_, bf16[256,448]{1,0:T(8,128)(2,1)S(1)} %get-tuple-element.81.refs_2_, ...), custom_call_target="tpu_custom_call" | custom-call | flops 1258291200 | bytes 2768896 | tf_op jit(solution)/shard_map/pallas_call | solution.py:202
  59.2 3.9 %collective-permute-start.12 = (bf16[152,256]{1,0:T(8,128)(2,1)S(1)}, bf16[152,256]{1,0:T(8,128)(2,1)S(1)}, u32[]{:S(2)}, u32[]{:S(2)}) collective-permute-start(bf16[152,256]{1,0:T(8,128)(2,1)S(1)} %get-tuple-element.108), channel_id=1, source_target_pairs={{0,8},{8,0},{16,24},{24,16},{1,9},{9,1},{17,25},{25,17},{2,10},{10... | collective-permute-start | bytes 233480 | tf_op jit(solution)/shard_map/ppermute | solution.py:219
  63.1 1.1 %collective-permute-start.13 = (bf16[152,256]{1,0:T(8,128)(2,1)S(1)}, bf16[152,256]{1,0:T(8,128)(2,1)S(1)}, u32[]{:S(2)}, u32[]{:S(2)}) collective-permute-start(bf16[152,256]{1,0:T(8,128)(2,1)S(1)} %get-tuple-element.109), channel_id=1, source_target_pairs={{0,16},{8,24},{16,0},{24,8},{1,17},{9,25},{17,1},{25,9},{2,18},{10... | collective-permute-start | bytes 233480 | tf_op jit(solution)/shard_map/ppermute | solution.py:219
  64.2 1.4 %collective-permute-start.14 = (bf16[152,256]{1,0:T(8,128)(2,1)S(1)}, bf16[152,256]{1,0:T(8,128)(2,1)S(1)}, u32[]{:S(2)}, u32[]{:S(2)}) collective-permute-start(bf16[152,256]{1,0:T(8,128)(2,1)S(1)} %get-tuple-element.110), channel_id=1, source_target_pairs={{0,24},{8,16},{16,8},{24,0},{1,25},{9,17},{17,9},{25,1},{2,26},{10... | collective-permute-start | bytes 233480 | tf_op jit(solution)/shard_map/ppermute | solution.py:219
  65.6 0.8 shard_map.97
  66.5 5.6 %collective-permute-done.13.refs_1_ = bf16[152,256]{1,0:T(8,128)(2,1)S(1)} collective-permute-done((bf16[152,256]{1,0:T(8,128)(2,1)S(1)}, bf16[152,256]{1,0:T(8,128)(2,1)S(1)}, u32[]{:S(2)}, u32[]{:S(2)}) %collective-permute-start.13) | collective-permute-done | bytes 77856 | tf_op jit(solution)/shard_map/ppermute | solution.py:219
  72.2 1.5 %collective-permute-start.16 = (bf16[152,256]{1,0:T(8,128)(2,1)S(1)}, bf16[152,256]{1,0:T(8,128)(2,1)S(1)}, u32[]{:S(2)}, u32[]{:S(2)}) collective-permute-start(bf16[152,256]{1,0:T(8,128)(2,1)S(1)} %shard_map.98.refs_0_), channel_id=1, source_target_pairs={{0,8},{8,0},{16,24},{24,16},{1,9},{9,1},{17,25},{25,17},{2,10},{10... | collective-permute-start | bytes 233480 | tf_op jit(solution)/shard_map/ppermute | solution.py:219
  73.6 1.4 %collective-permute-start.18 = (bf16[152,256]{1,0:T(8,128)(2,1)S(1)}, bf16[152,256]{1,0:T(8,128)(2,1)S(1)}, u32[]{:S(2)}, u32[]{:S(2)}) collective-permute-start(bf16[152,256]{1,0:T(8,128)(2,1)S(1)} %shard_map.98.refs_0_), channel_id=1, source_target_pairs={{0,16},{8,24},{16,0},{24,8},{1,17},{9,25},{17,1},{25,9},{2,18},{10... | collective-permute-start | bytes 233480 | tf_op jit(solution)/shard_map/ppermute | solution.py:219
  75.0 1.6 %collective-permute-start.20 = (bf16[152,256]{1,0:T(8,128)(2,1)S(1)}, bf16[152,256]{1,0:T(8,128)(2,1)S(1)}, u32[]{:S(2)}, u32[]{:S(2)}) collective-permute-start(bf16[152,256]{1,0:T(8,128)(2,1)S(1)} %shard_map.98.refs_0_), channel_id=1, source_target_pairs={{0,24},{8,16},{16,8},{24,0},{1,25},{9,17},{17,9},{25,1},{2,26},{10... | collective-permute-start | bytes 233480 | tf_op jit(solution)/shard_map/ppermute | solution.py:219
  76.6 1.1 %shard_map.107 = bf16[152,1024]{1,0:T(8,128)(2,1)S(1)} custom-call(bf16[600,256]{1,0:T(8,128)(2,1)S(1)} %fusion.10.refs_0_, bf16[600,256]{1,0:T(8,128)(2,1)S(1)} %collective-permute-done.refs_0_.refs_1_, bf16[600,256]{1,0:T(8,128)(2,1)S(1)} %collective-permute-done.1.refs_0_.refs_2_, bf16[600,256]{1,0:T(8,128)(2,1)S(1)} %collective-permute-done.2.refs_0_.refs_3_, ...), custom_call_target="tpu_custom_call" | custom-call | flops 637534208 | bytes 6651904 | tf_op jit(solution)/shard_map/pallas_call | solution.py:202
  77.7 1.4 %collective-permute-start.27 = (bf16[152,1024]{1,0:T(8,128)(2,1)S(1)}, bf16[152,1024]{1,0:T(8,128)(2,1)S(1)}, u32[]{:S(2)}, u32[]{:S(2)}) collective-permute-start(bf16[152,1024]{1,0:T(8,128)(2,1)S(1)} %shard_map.107), channel_id=1, source_target_pairs={{0,6},{1,7},{2,4},{3,5},{4,2},{5,3},{6,0},{7,1},{8,14},{9,15},{10,... | collective-permute-start | bytes 933896 | tf_op jit(solution)/shard_map/ppermute | solution.py:228
  79.7 2.1 %collective-permute-done.18.refs_2_ = bf16[152,256]{1,0:T(8,128)(2,1)S(1)} collective-permute-done((bf16[152,256]{1,0:T(8,128)(2,1)S(1)}, bf16[152,256]{1,0:T(8,128)(2,1)S(1)}, u32[]{:S(2)}, u32[]{:S(2)}) %collective-permute-start.18) | collective-permute-done | bytes 77856 | tf_op jit(solution)/shard_map/ppermute | solution.py:219
  83.5 0.5 shard_map.100
  84.0 0.6 collective-permute-start.25
  84.6 1.4 %collective-permute-start.26 = (bf16[152,512]{1,0:T(8,128)(2,1)S(1)}, bf16[152,512]{1,0:T(8,128)(2,1)S(1)}, u32[]{:S(2)}, u32[]{:S(2)}) collective-permute-start(bf16[152,512]{1,0:T(8,128)(2,1)S(1)} %get-tuple-element.131), channel_id=1, source_target_pairs={{0,4},{1,5},{2,6},{3,7},{4,0},{5,1},{6,2},{7,3},{8,12},{9,13},{10,... | collective-permute-start | bytes 466952 | tf_op jit(solution)/shard_map/ppermute | solution.py:228
  87.0 0.5 shard_map.101.refs_4_
  87.6 0.5 shard_map.104
  88.1 1.6 %collective-permute-start.24 = (bf16[152,512]{1,0:T(8,128)(2,1)S(1)}, bf16[152,512]{1,0:T(8,128)(2,1)S(1)}, u32[]{:S(2)}, u32[]{:S(2)}) collective-permute-start(bf16[152,512]{1,0:T(8,128)(2,1)S(1)} %get-tuple-element.128), channel_id=1, source_target_pairs={{0,2},{1,3},{2,0},{3,1},{4,6},{5,7},{6,4},{7,5},{8,10},{9,11},{10,... | collective-permute-start | bytes 466952 | tf_op jit(solution)/shard_map/ppermute | solution.py:228
  90.1 0.7 collective-permute-start.30
  90.8 0.5 shard_map.102
  91.4 0.6 collective-permute-start.29
  92.1 1.5 %collective-permute-start.28 = (bf16[152,512]{1,0:T(8,128)(2,1)S(1)}, bf16[152,512]{1,0:T(8,128)(2,1)S(1)}, u32[]{:S(2)}, u32[]{:S(2)}) collective-permute-start(bf16[152,512]{1,0:T(8,128)(2,1)S(1)} %shard_map.108), channel_id=1, source_target_pairs={{0,4},{1,5},{2,6},{3,7},{4,0},{5,1},{6,2},{7,3},{8,12},{9,13},{10,... | collective-permute-start | bytes 466952 | tf_op jit(solution)/shard_map/ppermute | solution.py:228
  93.6 1.0 fusion.6
  94.5 2.5 %collective-permute-done.30 = bf16[152,512]{1,0:T(8,128)(2,1)S(1)} collective-permute-done((bf16[152,512]{1,0:T(8,128)(2,1)S(1)}, bf16[152,512]{1,0:T(8,128)(2,1)S(1)}, u32[]{:S(2)}, u32[]{:S(2)}) %collective-permute-start.30) | collective-permute-done | bytes 155680 | tf_op jit(solution)/shard_map/ppermute | solution.py:228
  97.0 1.7 %collective-permute-done.28 = bf16[152,512]{1,0:T(8,128)(2,1)S(1)} collective-permute-done((bf16[152,512]{1,0:T(8,128)(2,1)S(1)}, bf16[152,512]{1,0:T(8,128)(2,1)S(1)}, u32[]{:S(2)}, u32[]{:S(2)}) %collective-permute-start.28) | collective-permute-done | bytes 155680 | tf_op jit(solution)/shard_map/ppermute | solution.py:228
  98.8 0.9 maximum_add_fusion
  (55 shorter events, 5.2 us)
Async XLA Ops:
  0.6 6.2 %copy-start = (bf16[147,256]{1,0:T(8,128)(2,1)S(1)}, bf16[147,256]{1,0:T(8,128)(2,1)}, u32[]{:S(2)}) copy-start(bf16[147,256]{1,0:T(8,128)(2,1)} %refs_3_.1) | copy-start | bytes 225796
  0.6 6.9 %copy-start.2 = (bf16[440,256]{1,0:T(8,128)(2,1)S(1)}, bf16[440,256]{1,0:T(8,128)(2,1)}, u32[]{:S(2)}) copy-start(bf16[440,256]{1,0:T(8,128)(2,1)} %param.7) | copy-start | bytes 675844
  2.1 33.0 %collective-permute-start.8 = (bf16[600,1024]{1,0:T(8,128)(2,1)S(1)}, bf16[600,1024]{1,0:T(8,128)(2,1)S(1)}, u32[]{:S(2)}, u32[]{:S(2)}) collective-permute-start(bf16[600,1024]{1,0:T(8,128)(2,1)S(1)} %fusion.4.refs_1_.refs_4_), channel_id=1, source_target_pairs={{0,4},{1,5},{2,6},{3,7},{4,0},{5,1},{6,2},{7,3},{8,12},{9,13},{10,... | collective-permute-start | bytes 3686408 | tf_op jit(solution)/shard_map/ppermute | solution.py:228
  5.1 30.1 %collective-permute-start.7 = (bf16[600,1024]{1,0:T(8,128)(2,1)S(1)}, bf16[600,1024]{1,0:T(8,128)(2,1)S(1)}, u32[]{:S(2)}, u32[]{:S(2)}) collective-permute-start(bf16[600,1024]{1,0:T(8,128)(2,1)S(1)} %fusion.4.refs_1_.refs_4_), channel_id=1, source_target_pairs={{0,2},{1,3},{2,0},{3,1},{4,6},{5,7},{6,4},{7,5},{8,10},{9,11},{10,... | collective-permute-start | bytes 3686408 | tf_op jit(solution)/shard_map/ppermute | solution.py:228
  7.7 14.0 %collective-permute-start = (bf16[600,256]{1,0:T(8,128)(2,1)S(1)}, bf16[600,256]{1,0:T(8,128)(2,1)S(1)}, u32[]{:S(2)}, u32[]{:S(2)}) collective-permute-start(bf16[600,256]{1,0:T(8,128)(2,1)S(1)} %fusion.10.refs_0_), channel_id=1, source_target_pairs={{0,8},{8,0},{16,24},{24,16},{1,9},{9,1},{17,25},{25,17},{2,10},{10... | collective-permute-start | bytes 921608 | tf_op jit(solution)/shard_map/ppermute | solution.py:219
  9.4 24.3 %collective-permute-start.1 = (bf16[600,256]{1,0:T(8,128)(2,1)S(1)}, bf16[600,256]{1,0:T(8,128)(2,1)S(1)}, u32[]{:S(2)}, u32[]{:S(2)}) collective-permute-start(bf16[600,256]{1,0:T(8,128)(2,1)S(1)} %fusion.10.refs_0_), channel_id=1, source_target_pairs={{0,16},{8,24},{16,0},{24,8},{1,17},{9,25},{17,1},{25,9},{2,18},{10... | collective-permute-start | bytes 921608 | tf_op jit(solution)/shard_map/ppermute | solution.py:219
  12.0 22.5 %collective-permute-start.2 = (bf16[600,256]{1,0:T(8,128)(2,1)S(1)}, bf16[600,256]{1,0:T(8,128)(2,1)S(1)}, u32[]{:S(2)}, u32[]{:S(2)}) collective-permute-start(bf16[600,256]{1,0:T(8,128)(2,1)S(1)} %fusion.10.refs_0_), channel_id=1, source_target_pairs={{0,24},{8,16},{16,8},{24,0},{1,25},{9,17},{17,9},{25,1},{2,26},{10... | collective-permute-start | bytes 921608 | tf_op jit(solution)/shard_map/ppermute | solution.py:219
  21.8 14.1 %collective-permute-start.3 = (bf16[600,256]{1,0:T(8,128)(2,1)S(1)}, bf16[600,256]{1,0:T(8,128)(2,1)S(1)}, u32[]{:S(2)}, u32[]{:S(2)}) collective-permute-start(bf16[600,256]{1,0:T(8,128)(2,1)S(1)} %fusion.10.refs_0_), channel_id=1, source_target_pairs={{0,1},{1,0},{2,3},{3,2},{4,5},{5,4},{6,7},{7,6},{8,9},{9,8},{10,11... | collective-permute-start | bytes 921608 | tf_op jit(solution)/shard_map/ppermute | solution.py:213
  33.7 3.7 %collective-permute-start.5 = (bf16[600,256]{1,0:T(8,128)(2,1)S(1)}, bf16[600,256]{1,0:T(8,128)(2,1)S(1)}, u32[]{:S(2)}, u32[]{:S(2)}) collective-permute-start(bf16[600,256]{1,0:T(8,128)(2,1)S(1)} %collective-permute-done.1.refs_0_.refs_2_), channel_id=1, source_target_pairs={{0,1},{1,0},{2,3},{3,2},{4,5},{5,4},{6,7},{7,6},{8,9},{9,8},{10,11... | collective-permute-start | bytes 921608 | tf_op jit(solution)/shard_map/ppermute | solution.py:213
  34.5 2.8 %collective-permute-start.6 = (bf16[600,256]{1,0:T(8,128)(2,1)S(1)}, bf16[600,256]{1,0:T(8,128)(2,1)S(1)}, u32[]{:S(2)}, u32[]{:S(2)}) collective-permute-start(bf16[600,256]{1,0:T(8,128)(2,1)S(1)} %collective-permute-done.2.refs_0_.refs_3_), channel_id=1, source_target_pairs={{0,1},{1,0},{2,3},{3,2},{4,5},{5,4},{6,7},{7,6},{8,9},{9,8},{10,11... | collective-permute-start | bytes 921608 | tf_op jit(solution)/shard_map/ppermute | solution.py:213
  35.1 2.2 %collective-permute-start.4 = (bf16[600,256]{1,0:T(8,128)(2,1)S(1)}, bf16[600,256]{1,0:T(8,128)(2,1)S(1)}, u32[]{:S(2)}, u32[]{:S(2)}) collective-permute-start(bf16[600,256]{1,0:T(8,128)(2,1)S(1)} %collective-permute-done.refs_0_.refs_1_), channel_id=1, source_target_pairs={{0,1},{1,0},{2,3},{3,2},{4,5},{5,4},{6,7},{7,6},{8,9},{9,8},{10,11... | collective-permute-start | bytes 921608 | tf_op jit(solution)/shard_map/ppermute | solution.py:213
  35.2 16.3 %collective-permute-start.10 = (bf16[600,512]{1,0:T(8,128)(2,1)S(1)}, bf16[600,512]{1,0:T(8,128)(2,1)S(1)}, u32[]{:S(2)}, u32[]{:S(2)}) collective-permute-start(bf16[600,512]{1,0:T(8,128)(2,1)S(1)} %slice.37), channel_id=1, source_target_pairs={{0,2},{1,3},{2,0},{3,1},{4,6},{5,7},{6,4},{7,5},{8,10},{9,11},{10,... | collective-permute-start | bytes 1843208 | tf_op jit(solution)/shard_map/ppermute | solution.py:228
  35.9 16.0 %collective-permute-start.9 = (bf16[600,512]{1,0:T(8,128)(2,1)S(1)}, bf16[600,512]{1,0:T(8,128)(2,1)S(1)}, u32[]{:S(2)}, u32[]{:S(2)}) collective-permute-start(bf16[600,512]{1,0:T(8,128)(2,1)S(1)} %slice.36), channel_id=1, source_target_pairs={{0,4},{1,5},{2,6},{3,7},{4,0},{5,1},{6,2},{7,3},{8,12},{9,13},{10,... | collective-permute-start | bytes 1843208 | tf_op jit(solution)/shard_map/ppermute | solution.py:228
  54.4 4.7 %collective-permute-start.11 = (bf16[152,1024]{1,0:T(8,128)(2,1)S(1)}, bf16[152,1024]{1,0:T(8,128)(2,1)S(1)}, u32[]{:S(2)}, u32[]{:S(2)}) collective-permute-start(bf16[152,1024]{1,0:T(8,128)(2,1)S(1)} %get-tuple-element.98), channel_id=1, source_target_pairs={{0,1},{1,0},{2,3},{3,2},{4,5},{5,4},{6,7},{7,6},{8,9},{9,8},{10,11... | collective-permute-start | bytes 933896 | tf_op jit(solution)/shard_map/ppermute | solution.py:213
  54.5 23.2 %collective-permute-start.22 = (bf16[152,1024]{1,0:T(8,128)(2,1)S(1)}, bf16[152,1024]{1,0:T(8,128)(2,1)S(1)}, u32[]{:S(2)}, u32[]{:S(2)}) collective-permute-start(bf16[152,1024]{1,0:T(8,128)(2,1)S(1)} %shard_map.92), channel_id=1, source_target_pairs={{0,2},{1,3},{2,0},{3,1},{4,6},{5,7},{6,4},{7,5},{8,10},{9,11},{10,... | collective-permute-start | bytes 933896 | tf_op jit(solution)/shard_map/ppermute | solution.py:228
  56.1 23.1 %collective-permute-start.23 = (bf16[152,1024]{1,0:T(8,128)(2,1)S(1)}, bf16[152,1024]{1,0:T(8,128)(2,1)S(1)}, u32[]{:S(2)}, u32[]{:S(2)}) collective-permute-start(bf16[152,1024]{1,0:T(8,128)(2,1)S(1)} %shard_map.93), channel_id=1, source_target_pairs={{0,4},{1,5},{2,6},{3,7},{4,0},{5,1},{6,2},{7,3},{8,12},{9,13},{10,... | collective-permute-start | bytes 933896 | tf_op jit(solution)/shard_map/ppermute | solution.py:228
  59.2 7.2 %collective-permute-start.12 = (bf16[152,256]{1,0:T(8,128)(2,1)S(1)}, bf16[152,256]{1,0:T(8,128)(2,1)S(1)}, u32[]{:S(2)}, u32[]{:S(2)}) collective-permute-start(bf16[152,256]{1,0:T(8,128)(2,1)S(1)} %get-tuple-element.108), channel_id=1, source_target_pairs={{0,8},{8,0},{16,24},{24,16},{1,9},{9,1},{17,25},{25,17},{2,10},{10... | collective-permute-start | bytes 233480 | tf_op jit(solution)/shard_map/ppermute | solution.py:219
  63.1 9.0 %collective-permute-start.13 = (bf16[152,256]{1,0:T(8,128)(2,1)S(1)}, bf16[152,256]{1,0:T(8,128)(2,1)S(1)}, u32[]{:S(2)}, u32[]{:S(2)}) collective-permute-start(bf16[152,256]{1,0:T(8,128)(2,1)S(1)} %get-tuple-element.109), channel_id=1, source_target_pairs={{0,16},{8,24},{16,0},{24,8},{1,17},{9,25},{17,1},{25,9},{2,18},{10... | collective-permute-start | bytes 233480 | tf_op jit(solution)/shard_map/ppermute | solution.py:219
  64.2 7.9 %collective-permute-start.14 = (bf16[152,256]{1,0:T(8,128)(2,1)S(1)}, bf16[152,256]{1,0:T(8,128)(2,1)S(1)}, u32[]{:S(2)}, u32[]{:S(2)}) collective-permute-start(bf16[152,256]{1,0:T(8,128)(2,1)S(1)} %get-tuple-element.110), channel_id=1, source_target_pairs={{0,24},{8,16},{16,8},{24,0},{1,25},{9,17},{17,9},{25,1},{2,26},{10... | collective-permute-start | bytes 233480 | tf_op jit(solution)/shard_map/ppermute | solution.py:219
  72.2 7.0 %collective-permute-start.16 = (bf16[152,256]{1,0:T(8,128)(2,1)S(1)}, bf16[152,256]{1,0:T(8,128)(2,1)S(1)}, u32[]{:S(2)}, u32[]{:S(2)}) collective-permute-start(bf16[152,256]{1,0:T(8,128)(2,1)S(1)} %shard_map.98.refs_0_), channel_id=1, source_target_pairs={{0,8},{8,0},{16,24},{24,16},{1,9},{9,1},{17,25},{25,17},{2,10},{10... | collective-permute-start | bytes 233480 | tf_op jit(solution)/shard_map/ppermute | solution.py:219
  73.6 8.1 %collective-permute-start.18 = (bf16[152,256]{1,0:T(8,128)(2,1)S(1)}, bf16[152,256]{1,0:T(8,128)(2,1)S(1)}, u32[]{:S(2)}, u32[]{:S(2)}) collective-permute-start(bf16[152,256]{1,0:T(8,128)(2,1)S(1)} %shard_map.98.refs_0_), channel_id=1, source_target_pairs={{0,16},{8,24},{16,0},{24,8},{1,17},{9,25},{17,1},{25,9},{2,18},{10... | collective-permute-start | bytes 233480 | tf_op jit(solution)/shard_map/ppermute | solution.py:219
  75.0 6.7 %collective-permute-start.20 = (bf16[152,256]{1,0:T(8,128)(2,1)S(1)}, bf16[152,256]{1,0:T(8,128)(2,1)S(1)}, u32[]{:S(2)}, u32[]{:S(2)}) collective-permute-start(bf16[152,256]{1,0:T(8,128)(2,1)S(1)} %shard_map.98.refs_0_), channel_id=1, source_target_pairs={{0,24},{8,16},{16,8},{24,0},{1,25},{9,17},{17,9},{25,1},{2,26},{10... | collective-permute-start | bytes 233480 | tf_op jit(solution)/shard_map/ppermute | solution.py:219
  77.7 13.6 %collective-permute-start.27 = (bf16[152,1024]{1,0:T(8,128)(2,1)S(1)}, bf16[152,1024]{1,0:T(8,128)(2,1)S(1)}, u32[]{:S(2)}, u32[]{:S(2)}) collective-permute-start(bf16[152,1024]{1,0:T(8,128)(2,1)S(1)} %shard_map.107), channel_id=1, source_target_pairs={{0,6},{1,7},{2,4},{3,5},{4,2},{5,3},{6,0},{7,1},{8,14},{9,15},{10,... | collective-permute-start | bytes 933896 | tf_op jit(solution)/shard_map/ppermute | solution.py:228
  79.2 4.3 %collective-permute-start.15 = (bf16[152,256]{1,0:T(8,128)(2,1)S(1)}, bf16[152,256]{1,0:T(8,128)(2,1)S(1)}, u32[]{:S(2)}, u32[]{:S(2)}) collective-permute-start(bf16[152,256]{1,0:T(8,128)(2,1)S(1)} %shard_map.98.refs_0_), channel_id=1, source_target_pairs={{0,1},{1,0},{2,3},{3,2},{4,5},{5,4},{6,7},{7,6},{8,9},{9,8},{10,11... | collective-permute-start | bytes 233480 | tf_op jit(solution)/shard_map/ppermute | solution.py:213
  79.2 4.3 %collective-permute-start.17 = (bf16[152,256]{1,0:T(8,128)(2,1)S(1)}, bf16[152,256]{1,0:T(8,128)(2,1)S(1)}, u32[]{:S(2)}, u32[]{:S(2)}) collective-permute-start(bf16[152,256]{1,0:T(8,128)(2,1)S(1)} %collective-permute-done.16.refs_1_), channel_id=1, source_target_pairs={{0,1},{1,0},{2,3},{3,2},{4,5},{5,4},{6,7},{7,6},{8,9},{9,8},{10,11... | collective-permute-start | bytes 233480 | tf_op jit(solution)/shard_map/ppermute | solution.py:213
  81.8 1.7 %collective-permute-start.19 = (bf16[152,256]{1,0:T(8,128)(2,1)S(1)}, bf16[152,256]{1,0:T(8,128)(2,1)S(1)}, u32[]{:S(2)}, u32[]{:S(2)}) collective-permute-start(bf16[152,256]{1,0:T(8,128)(2,1)S(1)} %collective-permute-done.18.refs_2_), channel_id=1, source_target_pairs={{0,1},{1,0},{2,3},{3,2},{4,5},{5,4},{6,7},{7,6},{8,9},{9,8},{10,11... | collective-permute-start | bytes 233480 | tf_op jit(solution)/shard_map/ppermute | solution.py:213
  81.8 1.7 %collective-permute-start.21 = (bf16[152,256]{1,0:T(8,128)(2,1)S(1)}, bf16[152,256]{1,0:T(8,128)(2,1)S(1)}, u32[]{:S(2)}, u32[]{:S(2)}) collective-permute-start(bf16[152,256]{1,0:T(8,128)(2,1)S(1)} %collective-permute-done.20.refs_3_), channel_id=1, source_target_pairs={{0,1},{1,0},{2,3},{3,2},{4,5},{5,4},{6,7},{7,6},{8,9},{9,8},{10,11... | collective-permute-start | bytes 233480 | tf_op jit(solution)/shard_map/ppermute | solution.py:213
  84.0 7.4 %collective-permute-start.25 = (bf16[152,512]{1,0:T(8,128)(2,1)S(1)}, bf16[152,512]{1,0:T(8,128)(2,1)S(1)}, u32[]{:S(2)}, u32[]{:S(2)}) collective-permute-start(bf16[152,512]{1,0:T(8,128)(2,1)S(1)} %get-tuple-element.130), channel_id=1, source_target_pairs={{0,2},{1,3},{2,0},{3,1},{4,6},{5,7},{6,4},{7,5},{8,10},{9,11},{10,... | collective-permute-start | bytes 466952 | tf_op jit(solution)/shard_map/ppermute | solution.py:228
  84.6 6.8 %collective-permute-start.26 = (bf16[152,512]{1,0:T(8,128)(2,1)S(1)}, bf16[152,512]{1,0:T(8,128)(2,1)S(1)}, u32[]{:S(2)}, u32[]{:S(2)}) collective-permute-start(bf16[152,512]{1,0:T(8,128)(2,1)S(1)} %get-tuple-element.131), channel_id=1, source_target_pairs={{0,4},{1,5},{2,6},{3,7},{4,0},{5,1},{6,2},{7,3},{8,12},{9,13},{10,... | collective-permute-start | bytes 466952 | tf_op jit(solution)/shard_map/ppermute | solution.py:228
  88.1 6.5 %collective-permute-start.24 = (bf16[152,512]{1,0:T(8,128)(2,1)S(1)}, bf16[152,512]{1,0:T(8,128)(2,1)S(1)}, u32[]{:S(2)}, u32[]{:S(2)}) collective-permute-start(bf16[152,512]{1,0:T(8,128)(2,1)S(1)} %get-tuple-element.128), channel_id=1, source_target_pairs={{0,2},{1,3},{2,0},{3,1},{4,6},{5,7},{6,4},{7,5},{8,10},{9,11},{10,... | collective-permute-start | bytes 466952 | tf_op jit(solution)/shard_map/ppermute | solution.py:228
  90.1 6.9 %collective-permute-start.30 = (bf16[152,512]{1,0:T(8,128)(2,1)S(1)}, bf16[152,512]{1,0:T(8,128)(2,1)S(1)}, u32[]{:S(2)}, u32[]{:S(2)}) collective-permute-start(bf16[152,512]{1,0:T(8,128)(2,1)S(1)} %get-tuple-element.143), channel_id=1, source_target_pairs={{0,4},{1,5},{2,6},{3,7},{4,0},{5,1},{6,2},{7,3},{8,12},{9,13},{10,... | collective-permute-start | bytes 466952 | tf_op jit(solution)/shard_map/ppermute | solution.py:228
  91.4 7.5 %copy-start.1 = (bf16[147,1024]{1,0:T(8,128)(2,1)S(1)}, bf16[147,1024]{1,0:T(8,128)(2,1)}, u32[]{:S(2)}) copy-start(bf16[147,1024]{1,0:T(8,128)(2,1)} %param.12) | copy-start | bytes 903172
  91.4 5.6 %collective-permute-start.29 = (bf16[152,512]{1,0:T(8,128)(2,1)S(1)}, bf16[152,512]{1,0:T(8,128)(2,1)S(1)}, u32[]{:S(2)}, u32[]{:S(2)}) collective-permute-start(bf16[152,512]{1,0:T(8,128)(2,1)S(1)} %shard_map.109), channel_id=1, source_target_pairs={{0,2},{1,3},{2,0},{3,1},{4,6},{5,7},{6,4},{7,5},{8,10},{9,11},{10,... | collective-permute-start | bytes 466952 | tf_op jit(solution)/shard_map/ppermute | solution.py:228
  92.1 6.6 %collective-permute-start.28 = (bf16[152,512]{1,0:T(8,128)(2,1)S(1)}, bf16[152,512]{1,0:T(8,128)(2,1)S(1)}, u32[]{:S(2)}, u32[]{:S(2)}) collective-permute-start(bf16[152,512]{1,0:T(8,128)(2,1)S(1)} %shard_map.108), channel_id=1, source_target_pairs={{0,4},{1,5},{2,6},{3,7},{4,0},{5,1},{6,2},{7,3},{8,12},{9,13},{10,... | collective-permute-start | bytes 466952 | tf_op jit(solution)/shard_map/ppermute | solution.py:228

commit v8 on v7

--- a/solution.py
+++ b/solution.py
@@ -218,7 +218,7 @@
 
         return lax.ppermute(a, "samp", [(i, to(i)) for i in range(line)])
 
-    places = (1, 2, 3) if line == 4 else range(1, line)
+    places = (2, 1, 3) if line == 4 else range(1, line)
 
     def across(a, dy, dx):
         def to(i):

time: 99.9 us -> 98.2 us (0.983)
  waiting for transfers between devices: 33 us -> 31 us
    ppermute x9, waiting for transfers between devices: 27.5 us -> 25.6 us  [along(): return lax.ppermute(a, 'samp', [(i, to(i)) for i in range(line)])]
  transfers between devices with their start and end apart: 31 -> 31, of which waited for: 8 -> 11; matrix products, arithmetic and copies ran while one was open for 2% -> 2% of each run, Pallas kernels for 25% -> 26%
where the time goes in v8:
time: 98.2 us; the launch traced here: 98 us
  starting transfers between devices  32.9 us (34%)
  waiting for transfers between devices  31 us (32%)
  Pallas kernels  27.8 us (28%)
  other arithmetic  4.41 us (4%)
  between operations  1.68 us (2%)
    pallas_call x24, Pallas kernels, whole(): pl.pallas_call(kernel, out_shape=shapes, compiler_params=params(), cost_e...  27.8 us
    ppermute x9, waiting for transfers between devices, along(): return lax.ppermute(a, 'samp', [(i, to(i)) for i in range(line)])  25.6 us
    ppermute x13, starting transfers between devices, across(): return lax.ppermute(a, 'feat', [(i, to(i)) for i in range(2 * xs * ys)])  15.8 us
    ppermute x9, starting transfers between devices, along(): return lax.ppermute(a, 'samp', [(i, to(i)) for i in range(line)])  15.3 us
    ppermute x13, waiting for transfers between devices, across(): return lax.ppermute(a, 'feat', [(i, to(i)) for i in range(2 * xs * ys)])  5.31 us
  transfers between devices with their start and end apart: 31, of which 11 were waited for; matrix products, arithmetic and copies ran while one was open for 2% of the time, Pallas kernels for 26%

profile of v8, /device:TPU:0, one launch (start us, length us, event | category | flops | bytes accessed | tf_op | source)
XLA Modules:
  0.0 98.0 jit_solution(5206465198827536260)
XLA Ops:
  0.7 1.5 %fusion.4.refs_1_.refs_4_ = bf16[600,1024]{1,0:T(8,128)(2,1)S(1)} fusion(bf16[147,1024]{1,0:T(8,128)(2,1)} %param.12, bf16[1,1024]{1,0:T(2,128)(2,1)} %param.11, bf16[440,1024]{1,0:T(8,128)(2,1)} %param.10), kind=kLoop, calls=%fused_computation.7 | loop fusion | flops 7372800 | bytes 2433024 | tf_op jit(solution)/shard_map/concatenate | solution.py:232
  2.1 3.0 %collective-permute-start.8 = (bf16[600,1024]{1,0:T(8,128)(2,1)S(1)}, bf16[600,1024]{1,0:T(8,128)(2,1)S(1)}, u32[]{:S(2)}, u32[]{:S(2)}) collective-permute-start(bf16[600,1024]{1,0:T(8,128)(2,1)S(1)} %fusion.4.refs_1_.refs_4_), channel_id=1, source_target_pairs={{0,4},{1,5},{2,6},{3,7},{4,0},{5,1},{6,2},{7,3},{8,12},{9,13},{10,... | collective-permute-start | bytes 3686408 | tf_op jit(solution)/shard_map/ppermute | solution.py:228
  5.1 1.5 %collective-permute-start.7 = (bf16[600,1024]{1,0:T(8,128)(2,1)S(1)}, bf16[600,1024]{1,0:T(8,128)(2,1)S(1)}, u32[]{:S(2)}, u32[]{:S(2)}) collective-permute-start(bf16[600,1024]{1,0:T(8,128)(2,1)S(1)} %fusion.4.refs_1_.refs_4_), channel_id=1, source_target_pairs={{0,2},{1,3},{2,0},{3,1},{4,6},{5,7},{6,4},{7,5},{8,10},{9,11},{10,... | collective-permute-start | bytes 3686408 | tf_op jit(solution)/shard_map/ppermute | solution.py:228
  6.8 0.7 subtract_convert_fusion
  7.7 2.7 %collective-permute-start = (bf16[600,256]{1,0:T(8,128)(2,1)S(1)}, bf16[600,256]{1,0:T(8,128)(2,1)S(1)}, u32[]{:S(2)}, u32[]{:S(2)}) collective-permute-start(bf16[600,256]{1,0:T(8,128)(2,1)S(1)} %fusion.10.refs_0_), channel_id=1, source_target_pairs={{0,16},{8,24},{16,0},{24,8},{1,17},{9,25},{17,1},{25,9},{2,18},{10... | collective-permute-start | bytes 921608 | tf_op jit(solution)/shard_map/ppermute | solution.py:219
  10.4 1.6 %collective-permute-start.1 = (bf16[600,256]{1,0:T(8,128)(2,1)S(1)}, bf16[600,256]{1,0:T(8,128)(2,1)S(1)}, u32[]{:S(2)}, u32[]{:S(2)}) collective-permute-start(bf16[600,256]{1,0:T(8,128)(2,1)S(1)} %fusion.10.refs_0_), channel_id=1, source_target_pairs={{0,8},{8,0},{16,24},{24,16},{1,9},{9,1},{17,25},{25,17},{2,10},{10... | collective-permute-start | bytes 921608 | tf_op jit(solution)/shard_map/ppermute | solution.py:219
  12.2 19.3 %collective-permute-done.refs_0_.refs_1_ = bf16[600,256]{1,0:T(8,128)(2,1)S(1)} collective-permute-done((bf16[600,256]{1,0:T(8,128)(2,1)S(1)}, bf16[600,256]{1,0:T(8,128)(2,1)S(1)}, u32[]{:S(2)}, u32[]{:S(2)}) %collective-permute-start) | collective-permute-done | bytes 307232 | tf_op jit(solution)/shard_map/ppermute | solution.py:219
  31.5 0.8 shard_map.86
  32.4 0.8 shard_map.87
  33.2 0.6 collective-permute-start.5
  33.8 0.8 shard_map.88
  35.3 0.6 collective-permute-start.10
  36.0 0.6 collective-permute-start.9
  36.5 0.8 shard_map.89
  37.4 2.5 %shard_map.90 = (bf16[1024,448]{1,0:T(8,128)(2,1)S(1)}, f32[1024,152]{1,0:T(8,128)S(1)}, bf16[1024,1024]{1,0:T(8,128)(2,1)S(1)}) custom-call(bf16[600,256]{1,0:T(8,128)(2,1)S(1)} %collective-permute-done.3.refs_0_.refs_4_, bf16[600,256]{1,0:T(8,128)(2,1)S(1)} %collective-permute-done.4.refs_1_.refs_5_, ...), custom_call_target="tpu_custom_call" | custom-call | flops 1258291200 | bytes 2457600 | tf_op jit(solution)/shard_map/pallas_call | solution.py:202
  39.9 9.0 %shard_map.91 = (bf16[2048,1024]{1,0:T(8,128)(2,1)S(1)}, bf16[2048,1024]{1,0:T(8,128)(2,1)S(1)}, f32[1024,152]{1,0:T(8,128)S(1)}, f32[1024,152]{1,0:T(8,128)S(1)}) custom-call(bf16[256,448]{1,0:T(8,128)(2,1)S(1)} %get-tuple-element.75.refs_0_, bf16[256,448]{1,0:T(8,128)(2,1)S(1)} %get-tuple-element.78.refs_1_, ...), custom_call_target="tpu_custom_call" | custom-call | flops 2516582400 | bytes 2768896 | tf_op jit(solution)/shard_map/pallas_call | solution.py:202
  48.8 0.9 shard_map.93
  49.7 0.9 shard_map.92
  50.6 0.6 collective-permute-done.10.refs_6_.refs_3_
  51.6 2.6 %shard_map.95 = (bf16[1024,512]{1,0:T(8,128)(2,1)S(1)}, bf16[1024,512]{1,0:T(8,128)(2,1)S(1)}, bf16[152,1024]{1,0:T(8,128)(2,1)S(1)}) custom-call(bf16[1024,448]{1,0:T(8,128)(2,1)S(1)} %get-tuple-element.85.refs_4_.refs_0_, f32[1024,152]{1,0:T(8,128)S(1)} %get-tuple-element.97.refs_1_, bf16[600,512]{1,0:T(8,128)(2,1)S(1)} %collective-permute-done.9.refs_5_.refs_2_, ...), custom_call_target="tpu_custom_call" | custom-call | flops 1258291200 | bytes 2768896 | tf_op jit(solution)/shard_map/pallas_call | solution.py:202
  54.2 1.6 %collective-permute-start.22 = (bf16[152,1024]{1,0:T(8,128)(2,1)S(1)}, bf16[152,1024]{1,0:T(8,128)(2,1)S(1)}, u32[]{:S(2)}, u32[]{:S(2)}) collective-permute-start(bf16[152,1024]{1,0:T(8,128)(2,1)S(1)} %shard_map.92), channel_id=1, source_target_pairs={{0,2},{1,3},{2,0},{3,1},{4,6},{5,7},{6,4},{7,5},{8,10},{9,11},{10,... | collective-permute-start | bytes 933896 | tf_op jit(solution)/shard_map/ppermute | solution.py:228
  55.8 0.5 collective-permute-start.23
  56.3 2.6 %shard_map.94 = (bf16[1024,512]{1,0:T(8,128)(2,1)S(1)}, bf16[1024,512]{1,0:T(8,128)(2,1)S(1)}, f32[152,1024]{1,0:T(8,128)S(1)}) custom-call(bf16[256,448]{1,0:T(8,128)(2,1)S(1)} %get-tuple-element.75.refs_0_, bf16[256,448]{1,0:T(8,128)(2,1)S(1)} %get-tuple-element.78.refs_1_, bf16[256,448]{1,0:T(8,128)(2,1)S(1)} %get-tuple-element.81.refs_2_, ...), custom_call_target="tpu_custom_call" | custom-call | flops 1258291200 | bytes 2768896 | tf_op jit(solution)/shard_map/pallas_call | solution.py:202
  59.0 4.8 %collective-permute-start.12 = (bf16[152,256]{1,0:T(8,128)(2,1)S(1)}, bf16[152,256]{1,0:T(8,128)(2,1)S(1)}, u32[]{:S(2)}, u32[]{:S(2)}) collective-permute-start(bf16[152,256]{1,0:T(8,128)(2,1)S(1)} %get-tuple-element.108), channel_id=1, source_target_pairs={{0,16},{8,24},{16,0},{24,8},{1,17},{9,25},{17,1},{25,9},{2,18},{10... | collective-permute-start | bytes 233480 | tf_op jit(solution)/shard_map/ppermute | solution.py:219
  63.8 1.5 %collective-permute-start.14 = (bf16[152,256]{1,0:T(8,128)(2,1)S(1)}, bf16[152,256]{1,0:T(8,128)(2,1)S(1)}, u32[]{:S(2)}, u32[]{:S(2)}) collective-permute-start(bf16[152,256]{1,0:T(8,128)(2,1)S(1)} %get-tuple-element.110), channel_id=1, source_target_pairs={{0,24},{8,16},{16,8},{24,0},{1,25},{9,17},{17,9},{25,1},{2,26},{10... | collective-permute-start | bytes 233480 | tf_op jit(solution)/shard_map/ppermute | solution.py:219
  65.3 0.8 shard_map.97
  66.2 2.2 %collective-permute-done.12.refs_0_ = bf16[152,256]{1,0:T(8,128)(2,1)S(1)} collective-permute-done((bf16[152,256]{1,0:T(8,128)(2,1)S(1)}, bf16[152,256]{1,0:T(8,128)(2,1)S(1)}, u32[]{:S(2)}, u32[]{:S(2)}) %collective-permute-start.12) | collective-permute-done | bytes 77856 | tf_op jit(solution)/shard_map/ppermute | solution.py:219
  68.4 2.1 %collective-permute-done.13.refs_1_ = bf16[152,256]{1,0:T(8,128)(2,1)S(1)} collective-permute-done((bf16[152,256]{1,0:T(8,128)(2,1)S(1)}, bf16[152,256]{1,0:T(8,128)(2,1)S(1)}, u32[]{:S(2)}, u32[]{:S(2)}) %collective-permute-start.13) | collective-permute-done | bytes 77856 | tf_op jit(solution)/shard_map/ppermute | solution.py:219
  70.6 0.9 collective-permute-start.16
  71.5 2.3 %collective-permute-start.18 = (bf16[152,256]{1,0:T(8,128)(2,1)S(1)}, bf16[152,256]{1,0:T(8,128)(2,1)S(1)}, u32[]{:S(2)}, u32[]{:S(2)}) collective-permute-start(bf16[152,256]{1,0:T(8,128)(2,1)S(1)} %shard_map.98.refs_0_), channel_id=1, source_target_pairs={{0,8},{8,0},{16,24},{24,16},{1,9},{9,1},{17,25},{25,17},{2,10},{10... | collective-permute-start | bytes 233480 | tf_op jit(solution)/shard_map/ppermute | solution.py:219
  73.8 1.2 %collective-permute-start.20 = (bf16[152,256]{1,0:T(8,128)(2,1)S(1)}, bf16[152,256]{1,0:T(8,128)(2,1)S(1)}, u32[]{:S(2)}, u32[]{:S(2)}) collective-permute-start(bf16[152,256]{1,0:T(8,128)(2,1)S(1)} %shard_map.98.refs_0_), channel_id=1, source_target_pairs={{0,24},{8,16},{16,8},{24,0},{1,25},{9,17},{17,9},{25,1},{2,26},{10... | collective-permute-start | bytes 233480 | tf_op jit(solution)/shard_map/ppermute | solution.py:219
  75.0 1.1 %shard_map.107 = bf16[152,1024]{1,0:T(8,128)(2,1)S(1)} custom-call(bf16[600,256]{1,0:T(8,128)(2,1)S(1)} %fusion.10.refs_0_, bf16[600,256]{1,0:T(8,128)(2,1)S(1)} %collective-permute-done.refs_0_.refs_1_, bf16[600,256]{1,0:T(8,128)(2,1)S(1)} %collective-permute-done.1.refs_0_.refs_2_, bf16[600,256]{1,0:T(8,128)(2,1)S(1)} %collective-permute-done.2.refs_0_.refs_3_, ...), custom_call_target="tpu_custom_call" | custom-call | flops 637534208 | bytes 6651904 | tf_op jit(solution)/shard_map/pallas_call | solution.py:202
  76.1 1.5 %collective-permute-start.27 = (bf16[152,1024]{1,0:T(8,128)(2,1)S(1)}, bf16[152,1024]{1,0:T(8,128)(2,1)S(1)}, u32[]{:S(2)}, u32[]{:S(2)}) collective-permute-start(bf16[152,1024]{1,0:T(8,128)(2,1)S(1)} %shard_map.107), channel_id=1, source_target_pairs={{0,6},{1,7},{2,4},{3,5},{4,2},{5,3},{6,0},{7,1},{8,14},{9,15},{10,... | collective-permute-start | bytes 933896 | tf_op jit(solution)/shard_map/ppermute | solution.py:228
  77.6 1.0 collective-permute-done.16.refs_1_
  79.1 1.0 %collective-permute-done.20.refs_3_ = bf16[152,256]{1,0:T(8,128)(2,1)S(1)} collective-permute-done((bf16[152,256]{1,0:T(8,128)(2,1)S(1)}, bf16[152,256]{1,0:T(8,128)(2,1)S(1)}, u32[]{:S(2)}, u32[]{:S(2)}) %collective-permute-start.20) | collective-permute-done | bytes 77856 | tf_op jit(solution)/shard_map/ppermute | solution.py:219
  81.9 0.6 collective-permute-start.25
  82.5 1.4 %collective-permute-start.26 = (bf16[152,512]{1,0:T(8,128)(2,1)S(1)}, bf16[152,512]{1,0:T(8,128)(2,1)S(1)}, u32[]{:S(2)}, u32[]{:S(2)}) collective-permute-start(bf16[152,512]{1,0:T(8,128)(2,1)S(1)} %get-tuple-element.131), channel_id=1, source_target_pairs={{0,4},{1,5},{2,6},{3,7},{4,0},{5,1},{6,2},{7,3},{8,12},{9,13},{10,... | collective-permute-start | bytes 466952 | tf_op jit(solution)/shard_map/ppermute | solution.py:228
  84.9 0.5 shard_map.101.refs_4_
  85.4 0.5 shard_map.104
  86.0 1.6 %collective-permute-start.24 = (bf16[152,512]{1,0:T(8,128)(2,1)S(1)}, bf16[152,512]{1,0:T(8,128)(2,1)S(1)}, u32[]{:S(2)}, u32[]{:S(2)}) collective-permute-start(bf16[152,512]{1,0:T(8,128)(2,1)S(1)} %get-tuple-element.128), channel_id=1, source_target_pairs={{0,2},{1,3},{2,0},{3,1},{4,6},{5,7},{6,4},{7,5},{8,10},{9,11},{10,... | collective-permute-start | bytes 466952 | tf_op jit(solution)/shard_map/ppermute | solution.py:228
  87.5 0.5 shard_map.106
  88.0 0.7 collective-permute-start.30
  89.3 0.9 collective-permute-start.29
  90.2 1.5 %collective-permute-start.28 = (bf16[152,512]{1,0:T(8,128)(2,1)S(1)}, bf16[152,512]{1,0:T(8,128)(2,1)S(1)}, u32[]{:S(2)}, u32[]{:S(2)}) collective-permute-start(bf16[152,512]{1,0:T(8,128)(2,1)S(1)} %shard_map.108), channel_id=1, source_target_pairs={{0,4},{1,5},{2,6},{3,7},{4,0},{5,1},{6,2},{7,3},{8,12},{9,13},{10,... | collective-permute-start | bytes 466952 | tf_op jit(solution)/shard_map/ppermute | solution.py:228
  91.7 1.0 %fusion.6 = f32[147,1024]{1,0:T(8,128)} fusion(f32[152,1024]{1,0:T(8,128)S(1)} %shard_map.97, bf16[152,1024]{1,0:T(8,128)(2,1)S(1)} %collective-permute-done.27, bf16[152,1024]{1,0:T(8,128)(2,1)S(1)} %collective-permute-done.23, bf16[152,1024]{1,0:T(8,128)(2,1)S(1)} %collective-permute-done.22), kind=kLoop, calls=%fused_computation.10 | loop fusion | flops 903168 | bytes 2107392 | tf_op jit(solution)/shard_map/add | solution.py:312
  92.7 2.3 %collective-permute-done.30 = bf16[152,512]{1,0:T(8,128)(2,1)S(1)} collective-permute-done((bf16[152,512]{1,0:T(8,128)(2,1)S(1)}, bf16[152,512]{1,0:T(8,128)(2,1)S(1)}, u32[]{:S(2)}, u32[]{:S(2)}) %collective-permute-start.30) | collective-permute-done | bytes 155680 | tf_op jit(solution)/shard_map/ppermute | solution.py:228
  95.2 1.8 %collective-permute-done.28 = bf16[152,512]{1,0:T(8,128)(2,1)S(1)} collective-permute-done((bf16[152,512]{1,0:T(8,128)(2,1)S(1)}, bf16[152,512]{1,0:T(8,128)(2,1)S(1)}, u32[]{:S(2)}, u32[]{:S(2)}) %collective-permute-start.28) | collective-permute-done | bytes 155680 | tf_op jit(solution)/shard_map/ppermute | solution.py:228
  97.1 0.9 maximum_add_fusion
  (55 shorter events, 5.4 us)
Async XLA Ops:
  0.6 6.2 %copy-start = (bf16[147,256]{1,0:T(8,128)(2,1)S(1)}, bf16[147,256]{1,0:T(8,128)(2,1)}, u32[]{:S(2)}) copy-start(bf16[147,256]{1,0:T(8,128)(2,1)} %refs_3_.1) | copy-start | bytes 225796
  0.6 6.9 %copy-start.2 = (bf16[440,256]{1,0:T(8,128)(2,1)S(1)}, bf16[440,256]{1,0:T(8,128)(2,1)}, u32[]{:S(2)}) copy-start(bf16[440,256]{1,0:T(8,128)(2,1)} %param.7) | copy-start | bytes 675844
  2.1 32.6 %collective-permute-start.8 = (bf16[600,1024]{1,0:T(8,128)(2,1)S(1)}, bf16[600,1024]{1,0:T(8,128)(2,1)S(1)}, u32[]{:S(2)}, u32[]{:S(2)}) collective-permute-start(bf16[600,1024]{1,0:T(8,128)(2,1)S(1)} %fusion.4.refs_1_.refs_4_), channel_id=1, source_target_pairs={{0,4},{1,5},{2,6},{3,7},{4,0},{5,1},{6,2},{7,3},{8,12},{9,13},{10,... | collective-permute-start | bytes 3686408 | tf_op jit(solution)/shard_map/ppermute | solution.py:228
  5.1 30.1 %collective-permute-start.7 = (bf16[600,1024]{1,0:T(8,128)(2,1)S(1)}, bf16[600,1024]{1,0:T(8,128)(2,1)S(1)}, u32[]{:S(2)}, u32[]{:S(2)}) collective-permute-start(bf16[600,1024]{1,0:T(8,128)(2,1)S(1)} %fusion.4.refs_1_.refs_4_), channel_id=1, source_target_pairs={{0,2},{1,3},{2,0},{3,1},{4,6},{5,7},{6,4},{7,5},{8,10},{9,11},{10,... | collective-permute-start | bytes 3686408 | tf_op jit(solution)/shard_map/ppermute | solution.py:228
  7.7 23.8 %collective-permute-start = (bf16[600,256]{1,0:T(8,128)(2,1)S(1)}, bf16[600,256]{1,0:T(8,128)(2,1)S(1)}, u32[]{:S(2)}, u32[]{:S(2)}) collective-permute-start(bf16[600,256]{1,0:T(8,128)(2,1)S(1)} %fusion.10.refs_0_), channel_id=1, source_target_pairs={{0,16},{8,24},{16,0},{24,8},{1,17},{9,25},{17,1},{25,9},{2,18},{10... | collective-permute-start | bytes 921608 | tf_op jit(solution)/shard_map/ppermute | solution.py:219
  10.4 22.8 %collective-permute-start.1 = (bf16[600,256]{1,0:T(8,128)(2,1)S(1)}, bf16[600,256]{1,0:T(8,128)(2,1)S(1)}, u32[]{:S(2)}, u32[]{:S(2)}) collective-permute-start(bf16[600,256]{1,0:T(8,128)(2,1)S(1)} %fusion.10.refs_0_), channel_id=1, source_target_pairs={{0,8},{8,0},{16,24},{24,16},{1,9},{9,1},{17,25},{25,17},{2,10},{10... | collective-permute-start | bytes 921608 | tf_op jit(solution)/shard_map/ppermute | solution.py:219
  12.0 22.7 %collective-permute-start.2 = (bf16[600,256]{1,0:T(8,128)(2,1)S(1)}, bf16[600,256]{1,0:T(8,128)(2,1)S(1)}, u32[]{:S(2)}, u32[]{:S(2)}) collective-permute-start(bf16[600,256]{1,0:T(8,128)(2,1)S(1)} %fusion.10.refs_0_), channel_id=1, source_target_pairs={{0,24},{8,16},{16,8},{24,0},{1,25},{9,17},{17,9},{25,1},{2,26},{10... | collective-permute-start | bytes 921608 | tf_op jit(solution)/shard_map/ppermute | solution.py:219
  31.5 4.4 %collective-permute-start.3 = (bf16[600,256]{1,0:T(8,128)(2,1)S(1)}, bf16[600,256]{1,0:T(8,128)(2,1)S(1)}, u32[]{:S(2)}, u32[]{:S(2)}) collective-permute-start(bf16[600,256]{1,0:T(8,128)(2,1)S(1)} %fusion.10.refs_0_), channel_id=1, source_target_pairs={{0,1},{1,0},{2,3},{3,2},{4,5},{5,4},{6,7},{7,6},{8,9},{9,8},{10,11... | collective-permute-start | bytes 921608 | tf_op jit(solution)/shard_map/ppermute | solution.py:213
  33.2 4.1 %collective-permute-start.5 = (bf16[600,256]{1,0:T(8,128)(2,1)S(1)}, bf16[600,256]{1,0:T(8,128)(2,1)S(1)}, u32[]{:S(2)}, u32[]{:S(2)}) collective-permute-start(bf16[600,256]{1,0:T(8,128)(2,1)S(1)} %collective-permute-done.1.refs_0_.refs_2_), channel_id=1, source_target_pairs={{0,1},{1,0},{2,3},{3,2},{4,5},{5,4},{6,7},{7,6},{8,9},{9,8},{10,11... | collective-permute-start | bytes 921608 | tf_op jit(solution)/shard_map/ppermute | solution.py:213
  34.7 2.7 %collective-permute-start.6 = (bf16[600,256]{1,0:T(8,128)(2,1)S(1)}, bf16[600,256]{1,0:T(8,128)(2,1)S(1)}, u32[]{:S(2)}, u32[]{:S(2)}) collective-permute-start(bf16[600,256]{1,0:T(8,128)(2,1)S(1)} %collective-permute-done.2.refs_0_.refs_3_), channel_id=1, source_target_pairs={{0,1},{1,0},{2,3},{3,2},{4,5},{5,4},{6,7},{7,6},{8,9},{9,8},{10,11... | collective-permute-start | bytes 921608 | tf_op jit(solution)/shard_map/ppermute | solution.py:213
  34.7 2.6 %collective-permute-start.4 = (bf16[600,256]{1,0:T(8,128)(2,1)S(1)}, bf16[600,256]{1,0:T(8,128)(2,1)S(1)}, u32[]{:S(2)}, u32[]{:S(2)}) collective-permute-start(bf16[600,256]{1,0:T(8,128)(2,1)S(1)} %collective-permute-done.refs_0_.refs_1_), channel_id=1, source_target_pairs={{0,1},{1,0},{2,3},{3,2},{4,5},{5,4},{6,7},{7,6},{8,9},{9,8},{10,11... | collective-permute-start | bytes 921608 | tf_op jit(solution)/shard_map/ppermute | solution.py:213
  35.3 15.9 %collective-permute-start.10 = (bf16[600,512]{1,0:T(8,128)(2,1)S(1)}, bf16[600,512]{1,0:T(8,128)(2,1)S(1)}, u32[]{:S(2)}, u32[]{:S(2)}) collective-permute-start(bf16[600,512]{1,0:T(8,128)(2,1)S(1)} %slice.37), channel_id=1, source_target_pairs={{0,2},{1,3},{2,0},{3,1},{4,6},{5,7},{6,4},{7,5},{8,10},{9,11},{10,... | collective-permute-start | bytes 1843208 | tf_op jit(solution)/shard_map/ppermute | solution.py:228
  36.0 15.6 %collective-permute-start.9 = (bf16[600,512]{1,0:T(8,128)(2,1)S(1)}, bf16[600,512]{1,0:T(8,128)(2,1)S(1)}, u32[]{:S(2)}, u32[]{:S(2)}) collective-permute-start(bf16[600,512]{1,0:T(8,128)(2,1)S(1)} %slice.36), channel_id=1, source_target_pairs={{0,4},{1,5},{2,6},{3,7},{4,0},{5,1},{6,2},{7,3},{8,12},{9,13},{10,... | collective-permute-start | bytes 1843208 | tf_op jit(solution)/shard_map/ppermute | solution.py:228
  54.1 4.7 %collective-permute-start.11 = (bf16[152,1024]{1,0:T(8,128)(2,1)S(1)}, bf16[152,1024]{1,0:T(8,128)(2,1)S(1)}, u32[]{:S(2)}, u32[]{:S(2)}) collective-permute-start(bf16[152,1024]{1,0:T(8,128)(2,1)S(1)} %get-tuple-element.98), channel_id=1, source_target_pairs={{0,1},{1,0},{2,3},{3,2},{4,5},{5,4},{6,7},{7,6},{8,9},{9,8},{10,11... | collective-permute-start | bytes 933896 | tf_op jit(solution)/shard_map/ppermute | solution.py:213
  54.2 21.9 %collective-permute-start.22 = (bf16[152,1024]{1,0:T(8,128)(2,1)S(1)}, bf16[152,1024]{1,0:T(8,128)(2,1)S(1)}, u32[]{:S(2)}, u32[]{:S(2)}) collective-permute-start(bf16[152,1024]{1,0:T(8,128)(2,1)S(1)} %shard_map.92), channel_id=1, source_target_pairs={{0,2},{1,3},{2,0},{3,1},{4,6},{5,7},{6,4},{7,5},{8,10},{9,11},{10,... | collective-permute-start | bytes 933896 | tf_op jit(solution)/shard_map/ppermute | solution.py:228
  55.8 21.8 %collective-permute-start.23 = (bf16[152,1024]{1,0:T(8,128)(2,1)S(1)}, bf16[152,1024]{1,0:T(8,128)(2,1)S(1)}, u32[]{:S(2)}, u32[]{:S(2)}) collective-permute-start(bf16[152,1024]{1,0:T(8,128)(2,1)S(1)} %shard_map.93), channel_id=1, source_target_pairs={{0,4},{1,5},{2,6},{3,7},{4,0},{5,1},{6,2},{7,3},{8,12},{9,13},{10,... | collective-permute-start | bytes 933896 | tf_op jit(solution)/shard_map/ppermute | solution.py:228
  59.0 9.4 %collective-permute-start.12 = (bf16[152,256]{1,0:T(8,128)(2,1)S(1)}, bf16[152,256]{1,0:T(8,128)(2,1)S(1)}, u32[]{:S(2)}, u32[]{:S(2)}) collective-permute-start(bf16[152,256]{1,0:T(8,128)(2,1)S(1)} %get-tuple-element.108), channel_id=1, source_target_pairs={{0,16},{8,24},{16,0},{24,8},{1,17},{9,25},{17,1},{25,9},{2,18},{10... | collective-permute-start | bytes 233480 | tf_op jit(solution)/shard_map/ppermute | solution.py:219
  63.8 6.7 %collective-permute-start.13 = (bf16[152,256]{1,0:T(8,128)(2,1)S(1)}, bf16[152,256]{1,0:T(8,128)(2,1)S(1)}, u32[]{:S(2)}, u32[]{:S(2)}) collective-permute-start(bf16[152,256]{1,0:T(8,128)(2,1)S(1)} %get-tuple-element.109), channel_id=1, source_target_pairs={{0,8},{8,0},{16,24},{24,16},{1,9},{9,1},{17,25},{25,17},{2,10},{10... | collective-permute-start | bytes 233480 | tf_op jit(solution)/shard_map/ppermute | solution.py:219
  63.8 6.7 %collective-permute-start.14 = (bf16[152,256]{1,0:T(8,128)(2,1)S(1)}, bf16[152,256]{1,0:T(8,128)(2,1)S(1)}, u32[]{:S(2)}, u32[]{:S(2)}) collective-permute-start(bf16[152,256]{1,0:T(8,128)(2,1)S(1)} %get-tuple-element.110), channel_id=1, source_target_pairs={{0,24},{8,16},{16,8},{24,0},{1,25},{9,17},{17,9},{25,1},{2,26},{10... | collective-permute-start | bytes 233480 | tf_op jit(solution)/shard_map/ppermute | solution.py:219
  70.6 8.0 %collective-permute-start.16 = (bf16[152,256]{1,0:T(8,128)(2,1)S(1)}, bf16[152,256]{1,0:T(8,128)(2,1)S(1)}, u32[]{:S(2)}, u32[]{:S(2)}) collective-permute-start(bf16[152,256]{1,0:T(8,128)(2,1)S(1)} %shard_map.98.refs_0_), channel_id=1, source_target_pairs={{0,16},{8,24},{16,0},{24,8},{1,17},{9,25},{17,1},{25,9},{2,18},{10... | collective-permute-start | bytes 233480 | tf_op jit(solution)/shard_map/ppermute | solution.py:219
  71.5 7.1 %collective-permute-start.18 = (bf16[152,256]{1,0:T(8,128)(2,1)S(1)}, bf16[152,256]{1,0:T(8,128)(2,1)S(1)}, u32[]{:S(2)}, u32[]{:S(2)}) collective-permute-start(bf16[152,256]{1,0:T(8,128)(2,1)S(1)} %shard_map.98.refs_0_), channel_id=1, source_target_pairs={{0,8},{8,0},{16,24},{24,16},{1,9},{9,1},{17,25},{25,17},{2,10},{10... | collective-permute-start | bytes 233480 | tf_op jit(solution)/shard_map/ppermute | solution.py:219
  73.8 6.3 %collective-permute-start.20 = (bf16[152,256]{1,0:T(8,128)(2,1)S(1)}, bf16[152,256]{1,0:T(8,128)(2,1)S(1)}, u32[]{:S(2)}, u32[]{:S(2)}) collective-permute-start(bf16[152,256]{1,0:T(8,128)(2,1)S(1)} %shard_map.98.refs_0_), channel_id=1, source_target_pairs={{0,24},{8,16},{16,8},{24,0},{1,25},{9,17},{17,9},{25,1},{2,26},{10... | collective-permute-start | bytes 233480 | tf_op jit(solution)/shard_map/ppermute | solution.py:219
  76.1 13.1 %collective-permute-start.27 = (bf16[152,1024]{1,0:T(8,128)(2,1)S(1)}, bf16[152,1024]{1,0:T(8,128)(2,1)S(1)}, u32[]{:S(2)}, u32[]{:S(2)}) collective-permute-start(bf16[152,1024]{1,0:T(8,128)(2,1)S(1)} %shard_map.107), channel_id=1, source_target_pairs={{0,6},{1,7},{2,4},{3,5},{4,2},{5,3},{6,0},{7,1},{8,14},{9,15},{10,... | collective-permute-start | bytes 933896 | tf_op jit(solution)/shard_map/ppermute | solution.py:228
  77.6 3.7 %collective-permute-start.15 = (bf16[152,256]{1,0:T(8,128)(2,1)S(1)}, bf16[152,256]{1,0:T(8,128)(2,1)S(1)}, u32[]{:S(2)}, u32[]{:S(2)}) collective-permute-start(bf16[152,256]{1,0:T(8,128)(2,1)S(1)} %shard_map.98.refs_0_), channel_id=1, source_target_pairs={{0,1},{1,0},{2,3},{3,2},{4,5},{5,4},{6,7},{7,6},{8,9},{9,8},{10,11... | collective-permute-start | bytes 233480 | tf_op jit(solution)/shard_map/ppermute | solution.py:213
  78.6 2.7 %collective-permute-start.17 = (bf16[152,256]{1,0:T(8,128)(2,1)S(1)}, bf16[152,256]{1,0:T(8,128)(2,1)S(1)}, u32[]{:S(2)}, u32[]{:S(2)}) collective-permute-start(bf16[152,256]{1,0:T(8,128)(2,1)S(1)} %collective-permute-done.16.refs_1_), channel_id=1, source_target_pairs={{0,1},{1,0},{2,3},{3,2},{4,5},{5,4},{6,7},{7,6},{8,9},{9,8},{10,11... | collective-permute-start | bytes 233480 | tf_op jit(solution)/shard_map/ppermute | solution.py:213
  78.6 2.7 %collective-permute-start.19 = (bf16[152,256]{1,0:T(8,128)(2,1)S(1)}, bf16[152,256]{1,0:T(8,128)(2,1)S(1)}, u32[]{:S(2)}, u32[]{:S(2)}) collective-permute-start(bf16[152,256]{1,0:T(8,128)(2,1)S(1)} %collective-permute-done.18.refs_2_), channel_id=1, source_target_pairs={{0,1},{1,0},{2,3},{3,2},{4,5},{5,4},{6,7},{7,6},{8,9},{9,8},{10,11... | collective-permute-start | bytes 233480 | tf_op jit(solution)/shard_map/ppermute | solution.py:213
  80.1 1.3 %collective-permute-start.21 = (bf16[152,256]{1,0:T(8,128)(2,1)S(1)}, bf16[152,256]{1,0:T(8,128)(2,1)S(1)}, u32[]{:S(2)}, u32[]{:S(2)}) collective-permute-start(bf16[152,256]{1,0:T(8,128)(2,1)S(1)} %collective-permute-done.20.refs_3_), channel_id=1, source_target_pairs={{0,1},{1,0},{2,3},{3,2},{4,5},{5,4},{6,7},{7,6},{8,9},{9,8},{10,11... | collective-permute-start | bytes 233480 | tf_op jit(solution)/shard_map/ppermute | solution.py:213
  81.9 7.4 %collective-permute-start.25 = (bf16[152,512]{1,0:T(8,128)(2,1)S(1)}, bf16[152,512]{1,0:T(8,128)(2,1)S(1)}, u32[]{:S(2)}, u32[]{:S(2)}) collective-permute-start(bf16[152,512]{1,0:T(8,128)(2,1)S(1)} %get-tuple-element.130), channel_id=1, source_target_pairs={{0,2},{1,3},{2,0},{3,1},{4,6},{5,7},{6,4},{7,5},{8,10},{9,11},{10,... | collective-permute-start | bytes 466952 | tf_op jit(solution)/shard_map/ppermute | solution.py:228
  82.5 6.8 %collective-permute-start.26 = (bf16[152,512]{1,0:T(8,128)(2,1)S(1)}, bf16[152,512]{1,0:T(8,128)(2,1)S(1)}, u32[]{:S(2)}, u32[]{:S(2)}) collective-permute-start(bf16[152,512]{1,0:T(8,128)(2,1)S(1)} %get-tuple-element.131), channel_id=1, source_target_pairs={{0,4},{1,5},{2,6},{3,7},{4,0},{5,1},{6,2},{7,3},{8,12},{9,13},{10,... | collective-permute-start | bytes 466952 | tf_op jit(solution)/shard_map/ppermute | solution.py:228
  86.0 6.7 %collective-permute-start.24 = (bf16[152,512]{1,0:T(8,128)(2,1)S(1)}, bf16[152,512]{1,0:T(8,128)(2,1)S(1)}, u32[]{:S(2)}, u32[]{:S(2)}) collective-permute-start(bf16[152,512]{1,0:T(8,128)(2,1)S(1)} %get-tuple-element.128), channel_id=1, source_target_pairs={{0,2},{1,3},{2,0},{3,1},{4,6},{5,7},{6,4},{7,5},{8,10},{9,11},{10,... | collective-permute-start | bytes 466952 | tf_op jit(solution)/shard_map/ppermute | solution.py:228
  88.0 7.0 %collective-permute-start.30 = (bf16[152,512]{1,0:T(8,128)(2,1)S(1)}, bf16[152,512]{1,0:T(8,128)(2,1)S(1)}, u32[]{:S(2)}, u32[]{:S(2)}) collective-permute-start(bf16[152,512]{1,0:T(8,128)(2,1)S(1)} %get-tuple-element.143), channel_id=1, source_target_pairs={{0,4},{1,5},{2,6},{3,7},{4,0},{5,1},{6,2},{7,3},{8,12},{9,13},{10,... | collective-permute-start | bytes 466952 | tf_op jit(solution)/shard_map/ppermute | solution.py:228
  89.3 7.9 %copy-start.1 = (bf16[147,1024]{1,0:T(8,128)(2,1)S(1)}, bf16[147,1024]{1,0:T(8,128)(2,1)}, u32[]{:S(2)}) copy-start(bf16[147,1024]{1,0:T(8,128)(2,1)} %param.12) | copy-start | bytes 903172
  89.3 5.9 %collective-permute-start.29 = (bf16[152,512]{1,0:T(8,128)(2,1)S(1)}, bf16[152,512]{1,0:T(8,128)(2,1)S(1)}, u32[]{:S(2)}, u32[]{:S(2)}) collective-permute-start(bf16[152,512]{1,0:T(8,128)(2,1)S(1)} %shard_map.109), channel_id=1, source_target_pairs={{0,2},{1,3},{2,0},{3,1},{4,6},{5,7},{6,4},{7,5},{8,10},{9,11},{10,... | collective-permute-start | bytes 466952 | tf_op jit(solution)/shard_map/ppermute | solution.py:228
  90.2 6.8 %collective-permute-start.28 = (bf16[152,512]{1,0:T(8,128)(2,1)S(1)}, bf16[152,512]{1,0:T(8,128)(2,1)S(1)}, u32[]{:S(2)}, u32[]{:S(2)}) collective-permute-start(bf16[152,512]{1,0:T(8,128)(2,1)S(1)} %shard_map.108), channel_id=1, source_target_pairs={{0,4},{1,5},{2,6},{3,7},{4,0},{5,1},{6,2},{7,3},{8,12},{9,13},{10,... | collective-permute-start | bytes 466952 | tf_op jit(solution)/shard_map/ppermute | solution.py:228

commit v9 on v8

--- a/solution.py
+++ b/solution.py
@@ -85,13 +85,14 @@
     x_refs, w_refs = refs[:count], refs[count : count + parts]
     xt_ref, t_ref, *f_refs = refs[count + parts :]
     n = x_refs[0].shape[1]
-    for j in range(count):
-        here = slice(j * n, (j + 1) * n)
-        xt = x_refs[j][:depth, :].T
-        xt_ref[here, :] = xt
+    group = 2 if count % 2 == 0 else 1
+    for j in range(0, count, group):
+        here = slice(j * n, (j + group) * n)
+        for i in range(j, j + group):
+            xt_ref[i * n : (i + 1) * n, :] = x_refs[i][:depth, :].T
         total = None
         for w_ref, f_ref in zip(w_refs, f_refs, strict=True):
-            f_ref[here, :], tangent = one_block(xt, w_ref, depth)
+            f_ref[here, :], tangent = one_block(xt_ref[here, :], w_ref, depth)
             total = tangent if total is None else total + tangent
         t_ref[here, :] = total
 
@@ -135,7 +136,7 @@
     else:
         shapes.append(jax.ShapeDtypeStruct((wide, n), last))
     kernel = functools.partial(next_kernel, depth, len(xts), len(totals), len(pieces), block, last is not None)
-    out = whole(kernel, shapes, *xts, *totals, *pieces, flops=2 * n * f * len(pieces) * (depth + wide), weight=0.5 if last is None else 1)
+    out = whole(kernel, shapes, *xts, *totals, *pieces, flops=2 * n * f * len(pieces) * (depth + wide), weight=0.5)
     return out[: len(pieces)], out[len(pieces) :]
 
 

time: 98.2 us -> 98.2 us (level)
  no operation moved by 1% of the time
where the time goes in v9:
time: 98.2 us; the launch traced here: 98.1 us
  starting transfers between devices  32.9 us (34%)
  waiting for transfers between devices  31 us (32%)
  Pallas kernels  27.8 us (28%)
  other arithmetic  4.41 us (4%)
  between operations  1.67 us (2%)
    pallas_call x24, Pallas kernels, whole(): pl.pallas_call(kernel, out_shape=shapes, compiler_params=params(), cost_e...  27.8 us
    ppermute x9, waiting for transfers between devices, along(): return lax.ppermute(a, 'samp', [(i, to(i)) for i in range(line)])  25.6 us
    ppermute x13, starting transfers between devices, across(): return lax.ppermute(a, 'feat', [(i, to(i)) for i in range(2 * xs * ys)])  15.8 us
    ppermute x9, starting transfers between devices, along(): return lax.ppermute(a, 'samp', [(i, to(i)) for i in range(line)])  15.3 us
    ppermute x13, waiting for transfers between devices, across(): return lax.ppermute(a, 'feat', [(i, to(i)) for i in range(2 * xs * ys)])  5.32 us
  transfers between devices with their start and end apart: 31, of which 11 were waited for; matrix products, arithmetic and copies ran while one was open for 2% of the time, Pallas kernels for 26%

profile of v9, /device:TPU:0, one launch (start us, length us, event | category | flops | bytes accessed | tf_op | source)
XLA Modules:
  0.0 98.1 jit_solution(2620150479196160695)
XLA Ops:
  0.7 1.5 %fusion.4.refs_1_.refs_4_ = bf16[600,1024]{1,0:T(8,128)(2,1)S(1)} fusion(bf16[147,1024]{1,0:T(8,128)(2,1)} %param.12, bf16[1,1024]{1,0:T(2,128)(2,1)} %param.11, bf16[440,1024]{1,0:T(8,128)(2,1)} %param.10), kind=kLoop, calls=%fused_computation.7 | loop fusion | flops 7372800 | bytes 2433024 | tf_op jit(solution)/shard_map/concatenate | solution.py:233
  2.1 3.0 %collective-permute-start.8 = (bf16[600,1024]{1,0:T(8,128)(2,1)S(1)}, bf16[600,1024]{1,0:T(8,128)(2,1)S(1)}, u32[]{:S(2)}, u32[]{:S(2)}) collective-permute-start(bf16[600,1024]{1,0:T(8,128)(2,1)S(1)} %fusion.4.refs_1_.refs_4_), channel_id=1, source_target_pairs={{0,4},{1,5},{2,6},{3,7},{4,0},{5,1},{6,2},{7,3},{8,12},{9,13},{10,... | collective-permute-start | bytes 3686408 | tf_op jit(solution)/shard_map/ppermute | solution.py:229
  5.1 1.5 %collective-permute-start.7 = (bf16[600,1024]{1,0:T(8,128)(2,1)S(1)}, bf16[600,1024]{1,0:T(8,128)(2,1)S(1)}, u32[]{:S(2)}, u32[]{:S(2)}) collective-permute-start(bf16[600,1024]{1,0:T(8,128)(2,1)S(1)} %fusion.4.refs_1_.refs_4_), channel_id=1, source_target_pairs={{0,2},{1,3},{2,0},{3,1},{4,6},{5,7},{6,4},{7,5},{8,10},{9,11},{10,... | collective-permute-start | bytes 3686408 | tf_op jit(solution)/shard_map/ppermute | solution.py:229
  6.8 0.7 subtract_convert_fusion
  7.7 2.7 %collective-permute-start = (bf16[600,256]{1,0:T(8,128)(2,1)S(1)}, bf16[600,256]{1,0:T(8,128)(2,1)S(1)}, u32[]{:S(2)}, u32[]{:S(2)}) collective-permute-start(bf16[600,256]{1,0:T(8,128)(2,1)S(1)} %fusion.10.refs_0_), channel_id=1, source_target_pairs={{0,16},{8,24},{16,0},{24,8},{1,17},{9,25},{17,1},{25,9},{2,18},{10... | collective-permute-start | bytes 921608 | tf_op jit(solution)/shard_map/ppermute | solution.py:220
  10.4 1.6 %collective-permute-start.1 = (bf16[600,256]{1,0:T(8,128)(2,1)S(1)}, bf16[600,256]{1,0:T(8,128)(2,1)S(1)}, u32[]{:S(2)}, u32[]{:S(2)}) collective-permute-start(bf16[600,256]{1,0:T(8,128)(2,1)S(1)} %fusion.10.refs_0_), channel_id=1, source_target_pairs={{0,8},{8,0},{16,24},{24,16},{1,9},{9,1},{17,25},{25,17},{2,10},{10... | collective-permute-start | bytes 921608 | tf_op jit(solution)/shard_map/ppermute | solution.py:220
  12.2 19.3 %collective-permute-done.refs_0_.refs_1_ = bf16[600,256]{1,0:T(8,128)(2,1)S(1)} collective-permute-done((bf16[600,256]{1,0:T(8,128)(2,1)S(1)}, bf16[600,256]{1,0:T(8,128)(2,1)S(1)}, u32[]{:S(2)}, u32[]{:S(2)}) %collective-permute-start) | collective-permute-done | bytes 307232 | tf_op jit(solution)/shard_map/ppermute | solution.py:220
  31.5 0.8 shard_map.86
  32.4 0.8 shard_map.87
  33.2 0.6 collective-permute-start.5
  33.8 0.8 shard_map.88
  35.3 0.6 collective-permute-start.10
  35.9 0.6 collective-permute-start.9
  36.5 0.8 shard_map.89
  37.4 2.5 %shard_map.90 = (bf16[1024,448]{1,0:T(8,128)(2,1)S(1)}, f32[1024,152]{1,0:T(8,128)S(1)}, bf16[1024,1024]{1,0:T(8,128)(2,1)S(1)}) custom-call(bf16[600,256]{1,0:T(8,128)(2,1)S(1)} %collective-permute-done.3.refs_0_.refs_4_, bf16[600,256]{1,0:T(8,128)(2,1)S(1)} %collective-permute-done.4.refs_1_.refs_5_, ...), custom_call_target="tpu_custom_call" | custom-call | flops 1258291200 | bytes 2457600 | tf_op jit(solution)/shard_map/pallas_call | solution.py:203
  39.9 9.0 %shard_map.91 = (bf16[2048,1024]{1,0:T(8,128)(2,1)S(1)}, bf16[2048,1024]{1,0:T(8,128)(2,1)S(1)}, f32[1024,152]{1,0:T(8,128)S(1)}, f32[1024,152]{1,0:T(8,128)S(1)}) custom-call(bf16[256,448]{1,0:T(8,128)(2,1)S(1)} %get-tuple-element.75.refs_0_, bf16[256,448]{1,0:T(8,128)(2,1)S(1)} %get-tuple-element.78.refs_1_, ...), custom_call_target="tpu_custom_call" | custom-call | flops 2516582400 | bytes 2768896 | tf_op jit(solution)/shard_map/pallas_call | solution.py:203
  48.8 0.9 shard_map.93
  49.7 0.9 shard_map.92
  50.5 0.7 collective-permute-done.10.refs_6_.refs_3_
  51.6 2.6 %shard_map.95 = (bf16[1024,512]{1,0:T(8,128)(2,1)S(1)}, bf16[1024,512]{1,0:T(8,128)(2,1)S(1)}, bf16[152,1024]{1,0:T(8,128)(2,1)S(1)}) custom-call(bf16[1024,448]{1,0:T(8,128)(2,1)S(1)} %get-tuple-element.85.refs_4_.refs_0_, f32[1024,152]{1,0:T(8,128)S(1)} %get-tuple-element.97.refs_1_, bf16[600,512]{1,0:T(8,128)(2,1)S(1)} %collective-permute-done.9.refs_5_.refs_2_, ...), custom_call_target="tpu_custom_call" | custom-call | flops 629145600 | bytes 1384448 | tf_op jit(solution)/shard_map/pallas_call | solution.py:203
  54.2 1.6 %collective-permute-start.22 = (bf16[152,1024]{1,0:T(8,128)(2,1)S(1)}, bf16[152,1024]{1,0:T(8,128)(2,1)S(1)}, u32[]{:S(2)}, u32[]{:S(2)}) collective-permute-start(bf16[152,1024]{1,0:T(8,128)(2,1)S(1)} %shard_map.92), channel_id=1, source_target_pairs={{0,2},{1,3},{2,0},{3,1},{4,6},{5,7},{6,4},{7,5},{8,10},{9,11},{10,... | collective-permute-start | bytes 933896 | tf_op jit(solution)/shard_map/ppermute | solution.py:229
  55.8 0.5 collective-permute-start.23
  56.3 2.6 %shard_map.94 = (bf16[1024,512]{1,0:T(8,128)(2,1)S(1)}, bf16[1024,512]{1,0:T(8,128)(2,1)S(1)}, f32[152,1024]{1,0:T(8,128)S(1)}) custom-call(bf16[256,448]{1,0:T(8,128)(2,1)S(1)} %get-tuple-element.75.refs_0_, bf16[256,448]{1,0:T(8,128)(2,1)S(1)} %get-tuple-element.78.refs_1_, bf16[256,448]{1,0:T(8,128)(2,1)S(1)} %get-tuple-element.81.refs_2_, ...), custom_call_target="tpu_custom_call" | custom-call | flops 629145600 | bytes 1384448 | tf_op jit(solution)/shard_map/pallas_call | solution.py:203
  59.0 4.9 %collective-permute-start.12 = (bf16[152,256]{1,0:T(8,128)(2,1)S(1)}, bf16[152,256]{1,0:T(8,128)(2,1)S(1)}, u32[]{:S(2)}, u32[]{:S(2)}) collective-permute-start(bf16[152,256]{1,0:T(8,128)(2,1)S(1)} %get-tuple-element.108), channel_id=1, source_target_pairs={{0,16},{8,24},{16,0},{24,8},{1,17},{9,25},{17,1},{25,9},{2,18},{10... | collective-permute-start | bytes 233480 | tf_op jit(solution)/shard_map/ppermute | solution.py:220
  63.8 1.5 %collective-permute-start.14 = (bf16[152,256]{1,0:T(8,128)(2,1)S(1)}, bf16[152,256]{1,0:T(8,128)(2,1)S(1)}, u32[]{:S(2)}, u32[]{:S(2)}) collective-permute-start(bf16[152,256]{1,0:T(8,128)(2,1)S(1)} %get-tuple-element.110), channel_id=1, source_target_pairs={{0,24},{8,16},{16,8},{24,0},{1,25},{9,17},{17,9},{25,1},{2,26},{10... | collective-permute-start | bytes 233480 | tf_op jit(solution)/shard_map/ppermute | solution.py:220
  65.4 0.8 shard_map.97
  66.2 2.2 %collective-permute-done.12.refs_0_ = bf16[152,256]{1,0:T(8,128)(2,1)S(1)} collective-permute-done((bf16[152,256]{1,0:T(8,128)(2,1)S(1)}, bf16[152,256]{1,0:T(8,128)(2,1)S(1)}, u32[]{:S(2)}, u32[]{:S(2)}) %collective-permute-start.12) | collective-permute-done | bytes 77856 | tf_op jit(solution)/shard_map/ppermute | solution.py:220
  68.4 2.1 %collective-permute-done.13.refs_1_ = bf16[152,256]{1,0:T(8,128)(2,1)S(1)} collective-permute-done((bf16[152,256]{1,0:T(8,128)(2,1)S(1)}, bf16[152,256]{1,0:T(8,128)(2,1)S(1)}, u32[]{:S(2)}, u32[]{:S(2)}) %collective-permute-start.13) | collective-permute-done | bytes 77856 | tf_op jit(solution)/shard_map/ppermute | solution.py:220
  70.6 0.9 collective-permute-start.16
  71.5 2.3 %collective-permute-start.18 = (bf16[152,256]{1,0:T(8,128)(2,1)S(1)}, bf16[152,256]{1,0:T(8,128)(2,1)S(1)}, u32[]{:S(2)}, u32[]{:S(2)}) collective-permute-start(bf16[152,256]{1,0:T(8,128)(2,1)S(1)} %shard_map.98.refs_0_), channel_id=1, source_target_pairs={{0,8},{8,0},{16,24},{24,16},{1,9},{9,1},{17,25},{25,17},{2,10},{10... | collective-permute-start | bytes 233480 | tf_op jit(solution)/shard_map/ppermute | solution.py:220
  73.8 1.2 %collective-permute-start.20 = (bf16[152,256]{1,0:T(8,128)(2,1)S(1)}, bf16[152,256]{1,0:T(8,128)(2,1)S(1)}, u32[]{:S(2)}, u32[]{:S(2)}) collective-permute-start(bf16[152,256]{1,0:T(8,128)(2,1)S(1)} %shard_map.98.refs_0_), channel_id=1, source_target_pairs={{0,24},{8,16},{16,8},{24,0},{1,25},{9,17},{17,9},{25,1},{2,26},{10... | collective-permute-start | bytes 233480 | tf_op jit(solution)/shard_map/ppermute | solution.py:220
  75.0 1.1 %shard_map.107 = bf16[152,1024]{1,0:T(8,128)(2,1)S(1)} custom-call(bf16[600,256]{1,0:T(8,128)(2,1)S(1)} %fusion.10.refs_0_, bf16[600,256]{1,0:T(8,128)(2,1)S(1)} %collective-permute-done.refs_0_.refs_1_, bf16[600,256]{1,0:T(8,128)(2,1)S(1)} %collective-permute-done.1.refs_0_.refs_2_, bf16[600,256]{1,0:T(8,128)(2,1)S(1)} %collective-permute-done.2.refs_0_.refs_3_, ...), custom_call_target="tpu_custom_call" | custom-call | flops 637534208 | bytes 6651904 | tf_op jit(solution)/shard_map/pallas_call | solution.py:203
  76.1 1.5 %collective-permute-start.27 = (bf16[152,1024]{1,0:T(8,128)(2,1)S(1)}, bf16[152,1024]{1,0:T(8,128)(2,1)S(1)}, u32[]{:S(2)}, u32[]{:S(2)}) collective-permute-start(bf16[152,1024]{1,0:T(8,128)(2,1)S(1)} %shard_map.107), channel_id=1, source_target_pairs={{0,6},{1,7},{2,4},{3,5},{4,2},{5,3},{6,0},{7,1},{8,14},{9,15},{10,... | collective-permute-start | bytes 933896 | tf_op jit(solution)/shard_map/ppermute | solution.py:229
  77.6 1.0 %collective-permute-done.16.refs_1_ = bf16[152,256]{1,0:T(8,128)(2,1)S(1)} collective-permute-done((bf16[152,256]{1,0:T(8,128)(2,1)S(1)}, bf16[152,256]{1,0:T(8,128)(2,1)S(1)}, u32[]{:S(2)}, u32[]{:S(2)}) %collective-permute-start.16) | collective-permute-done | bytes 77856 | tf_op jit(solution)/shard_map/ppermute | solution.py:220
  79.2 0.9 collective-permute-done.20.refs_3_
  81.9 0.6 collective-permute-start.25
  82.5 1.4 %collective-permute-start.26 = (bf16[152,512]{1,0:T(8,128)(2,1)S(1)}, bf16[152,512]{1,0:T(8,128)(2,1)S(1)}, u32[]{:S(2)}, u32[]{:S(2)}) collective-permute-start(bf16[152,512]{1,0:T(8,128)(2,1)S(1)} %get-tuple-element.131), channel_id=1, source_target_pairs={{0,4},{1,5},{2,6},{3,7},{4,0},{5,1},{6,2},{7,3},{8,12},{9,13},{10,... | collective-permute-start | bytes 466952 | tf_op jit(solution)/shard_map/ppermute | solution.py:229
  85.0 0.5 shard_map.101.refs_4_
  85.5 0.5 shard_map.104
  86.0 1.6 %collective-permute-start.24 = (bf16[152,512]{1,0:T(8,128)(2,1)S(1)}, bf16[152,512]{1,0:T(8,128)(2,1)S(1)}, u32[]{:S(2)}, u32[]{:S(2)}) collective-permute-start(bf16[152,512]{1,0:T(8,128)(2,1)S(1)} %get-tuple-element.128), channel_id=1, source_target_pairs={{0,2},{1,3},{2,0},{3,1},{4,6},{5,7},{6,4},{7,5},{8,10},{9,11},{10,... | collective-permute-start | bytes 466952 | tf_op jit(solution)/shard_map/ppermute | solution.py:229
  87.5 0.5 shard_map.106
  88.1 0.7 collective-permute-start.30
  89.3 0.9 collective-permute-start.29
  90.2 1.5 %collective-permute-start.28 = (bf16[152,512]{1,0:T(8,128)(2,1)S(1)}, bf16[152,512]{1,0:T(8,128)(2,1)S(1)}, u32[]{:S(2)}, u32[]{:S(2)}) collective-permute-start(bf16[152,512]{1,0:T(8,128)(2,1)S(1)} %shard_map.108), channel_id=1, source_target_pairs={{0,4},{1,5},{2,6},{3,7},{4,0},{5,1},{6,2},{7,3},{8,12},{9,13},{10,... | collective-permute-start | bytes 466952 | tf_op jit(solution)/shard_map/ppermute | solution.py:229
  91.7 1.0 %fusion.6 = f32[147,1024]{1,0:T(8,128)} fusion(f32[152,1024]{1,0:T(8,128)S(1)} %shard_map.97, bf16[152,1024]{1,0:T(8,128)(2,1)S(1)} %collective-permute-done.27, bf16[152,1024]{1,0:T(8,128)(2,1)S(1)} %collective-permute-done.23, bf16[152,1024]{1,0:T(8,128)(2,1)S(1)} %collective-permute-done.22), kind=kLoop, calls=%fused_computation.10 | loop fusion | flops 903168 | bytes 2107392 | tf_op jit(solution)/shard_map/add | solution.py:313
  92.7 2.3 %collective-permute-done.30 = bf16[152,512]{1,0:T(8,128)(2,1)S(1)} collective-permute-done((bf16[152,512]{1,0:T(8,128)(2,1)S(1)}, bf16[152,512]{1,0:T(8,128)(2,1)S(1)}, u32[]{:S(2)}, u32[]{:S(2)}) %collective-permute-start.30) | collective-permute-done | bytes 155680 | tf_op jit(solution)/shard_map/ppermute | solution.py:229
  95.2 1.8 %collective-permute-done.28 = bf16[152,512]{1,0:T(8,128)(2,1)S(1)} collective-permute-done((bf16[152,512]{1,0:T(8,128)(2,1)S(1)}, bf16[152,512]{1,0:T(8,128)(2,1)S(1)}, u32[]{:S(2)}, u32[]{:S(2)}) %collective-permute-start.28) | collective-permute-done | bytes 155680 | tf_op jit(solution)/shard_map/ppermute | solution.py:229
  97.1 0.9 maximum_add_fusion
  (55 shorter events, 5.4 us)
Async XLA Ops:
  0.6 6.2 %copy-start = (bf16[147,256]{1,0:T(8,128)(2,1)S(1)}, bf16[147,256]{1,0:T(8,128)(2,1)}, u32[]{:S(2)}) copy-start(bf16[147,256]{1,0:T(8,128)(2,1)} %refs_3_.1) | copy-start | bytes 225796
  0.6 6.9 %copy-start.2 = (bf16[440,256]{1,0:T(8,128)(2,1)S(1)}, bf16[440,256]{1,0:T(8,128)(2,1)}, u32[]{:S(2)}) copy-start(bf16[440,256]{1,0:T(8,128)(2,1)} %param.7) | copy-start | bytes 675844
  2.1 32.6 %collective-permute-start.8 = (bf16[600,1024]{1,0:T(8,128)(2,1)S(1)}, bf16[600,1024]{1,0:T(8,128)(2,1)S(1)}, u32[]{:S(2)}, u32[]{:S(2)}) collective-permute-start(bf16[600,1024]{1,0:T(8,128)(2,1)S(1)} %fusion.4.refs_1_.refs_4_), channel_id=1, source_target_pairs={{0,4},{1,5},{2,6},{3,7},{4,0},{5,1},{6,2},{7,3},{8,12},{9,13},{10,... | collective-permute-start | bytes 3686408 | tf_op jit(solution)/shard_map/ppermute | solution.py:229
  5.1 30.1 %collective-permute-start.7 = (bf16[600,1024]{1,0:T(8,128)(2,1)S(1)}, bf16[600,1024]{1,0:T(8,128)(2,1)S(1)}, u32[]{:S(2)}, u32[]{:S(2)}) collective-permute-start(bf16[600,1024]{1,0:T(8,128)(2,1)S(1)} %fusion.4.refs_1_.refs_4_), channel_id=1, source_target_pairs={{0,2},{1,3},{2,0},{3,1},{4,6},{5,7},{6,4},{7,5},{8,10},{9,11},{10,... | collective-permute-start | bytes 3686408 | tf_op jit(solution)/shard_map/ppermute | solution.py:229
  7.7 23.8 %collective-permute-start = (bf16[600,256]{1,0:T(8,128)(2,1)S(1)}, bf16[600,256]{1,0:T(8,128)(2,1)S(1)}, u32[]{:S(2)}, u32[]{:S(2)}) collective-permute-start(bf16[600,256]{1,0:T(8,128)(2,1)S(1)} %fusion.10.refs_0_), channel_id=1, source_target_pairs={{0,16},{8,24},{16,0},{24,8},{1,17},{9,25},{17,1},{25,9},{2,18},{10... | collective-permute-start | bytes 921608 | tf_op jit(solution)/shard_map/ppermute | solution.py:220
  10.4 22.8 %collective-permute-start.1 = (bf16[600,256]{1,0:T(8,128)(2,1)S(1)}, bf16[600,256]{1,0:T(8,128)(2,1)S(1)}, u32[]{:S(2)}, u32[]{:S(2)}) collective-permute-start(bf16[600,256]{1,0:T(8,128)(2,1)S(1)} %fusion.10.refs_0_), channel_id=1, source_target_pairs={{0,8},{8,0},{16,24},{24,16},{1,9},{9,1},{17,25},{25,17},{2,10},{10... | collective-permute-start | bytes 921608 | tf_op jit(solution)/shard_map/ppermute | solution.py:220
  12.0 22.7 %collective-permute-start.2 = (bf16[600,256]{1,0:T(8,128)(2,1)S(1)}, bf16[600,256]{1,0:T(8,128)(2,1)S(1)}, u32[]{:S(2)}, u32[]{:S(2)}) collective-permute-start(bf16[600,256]{1,0:T(8,128)(2,1)S(1)} %fusion.10.refs_0_), channel_id=1, source_target_pairs={{0,24},{8,16},{16,8},{24,0},{1,25},{9,17},{17,9},{25,1},{2,26},{10... | collective-permute-start | bytes 921608 | tf_op jit(solution)/shard_map/ppermute | solution.py:220
  31.5 4.4 %collective-permute-start.3 = (bf16[600,256]{1,0:T(8,128)(2,1)S(1)}, bf16[600,256]{1,0:T(8,128)(2,1)S(1)}, u32[]{:S(2)}, u32[]{:S(2)}) collective-permute-start(bf16[600,256]{1,0:T(8,128)(2,1)S(1)} %fusion.10.refs_0_), channel_id=1, source_target_pairs={{0,1},{1,0},{2,3},{3,2},{4,5},{5,4},{6,7},{7,6},{8,9},{9,8},{10,11... | collective-permute-start | bytes 921608 | tf_op jit(solution)/shard_map/ppermute | solution.py:214
  33.2 4.1 %collective-permute-start.5 = (bf16[600,256]{1,0:T(8,128)(2,1)S(1)}, bf16[600,256]{1,0:T(8,128)(2,1)S(1)}, u32[]{:S(2)}, u32[]{:S(2)}) collective-permute-start(bf16[600,256]{1,0:T(8,128)(2,1)S(1)} %collective-permute-done.1.refs_0_.refs_2_), channel_id=1, source_target_pairs={{0,1},{1,0},{2,3},{3,2},{4,5},{5,4},{6,7},{7,6},{8,9},{9,8},{10,11... | collective-permute-start | bytes 921608 | tf_op jit(solution)/shard_map/ppermute | solution.py:214
  34.6 2.7 %collective-permute-start.6 = (bf16[600,256]{1,0:T(8,128)(2,1)S(1)}, bf16[600,256]{1,0:T(8,128)(2,1)S(1)}, u32[]{:S(2)}, u32[]{:S(2)}) collective-permute-start(bf16[600,256]{1,0:T(8,128)(2,1)S(1)} %collective-permute-done.2.refs_0_.refs_3_), channel_id=1, source_target_pairs={{0,1},{1,0},{2,3},{3,2},{4,5},{5,4},{6,7},{7,6},{8,9},{9,8},{10,11... | collective-permute-start | bytes 921608 | tf_op jit(solution)/shard_map/ppermute | solution.py:214
  34.7 2.6 %collective-permute-start.4 = (bf16[600,256]{1,0:T(8,128)(2,1)S(1)}, bf16[600,256]{1,0:T(8,128)(2,1)S(1)}, u32[]{:S(2)}, u32[]{:S(2)}) collective-permute-start(bf16[600,256]{1,0:T(8,128)(2,1)S(1)} %collective-permute-done.refs_0_.refs_1_), channel_id=1, source_target_pairs={{0,1},{1,0},{2,3},{3,2},{4,5},{5,4},{6,7},{7,6},{8,9},{9,8},{10,11... | collective-permute-start | bytes 921608 | tf_op jit(solution)/shard_map/ppermute | solution.py:214
  35.3 15.9 %collective-permute-start.10 = (bf16[600,512]{1,0:T(8,128)(2,1)S(1)}, bf16[600,512]{1,0:T(8,128)(2,1)S(1)}, u32[]{:S(2)}, u32[]{:S(2)}) collective-permute-start(bf16[600,512]{1,0:T(8,128)(2,1)S(1)} %slice.37), channel_id=1, source_target_pairs={{0,2},{1,3},{2,0},{3,1},{4,6},{5,7},{6,4},{7,5},{8,10},{9,11},{10,... | collective-permute-start | bytes 1843208 | tf_op jit(solution)/shard_map/ppermute | solution.py:229
  35.9 15.6 %collective-permute-start.9 = (bf16[600,512]{1,0:T(8,128)(2,1)S(1)}, bf16[600,512]{1,0:T(8,128)(2,1)S(1)}, u32[]{:S(2)}, u32[]{:S(2)}) collective-permute-start(bf16[600,512]{1,0:T(8,128)(2,1)S(1)} %slice.36), channel_id=1, source_target_pairs={{0,4},{1,5},{2,6},{3,7},{4,0},{5,1},{6,2},{7,3},{8,12},{9,13},{10,... | collective-permute-start | bytes 1843208 | tf_op jit(solution)/shard_map/ppermute | solution.py:229
  54.1 4.7 %collective-permute-start.11 = (bf16[152,1024]{1,0:T(8,128)(2,1)S(1)}, bf16[152,1024]{1,0:T(8,128)(2,1)S(1)}, u32[]{:S(2)}, u32[]{:S(2)}) collective-permute-start(bf16[152,1024]{1,0:T(8,128)(2,1)S(1)} %get-tuple-element.98), channel_id=1, source_target_pairs={{0,1},{1,0},{2,3},{3,2},{4,5},{5,4},{6,7},{7,6},{8,9},{9,8},{10,11... | collective-permute-start | bytes 933896 | tf_op jit(solution)/shard_map/ppermute | solution.py:214
  54.2 21.9 %collective-permute-start.22 = (bf16[152,1024]{1,0:T(8,128)(2,1)S(1)}, bf16[152,1024]{1,0:T(8,128)(2,1)S(1)}, u32[]{:S(2)}, u32[]{:S(2)}) collective-permute-start(bf16[152,1024]{1,0:T(8,128)(2,1)S(1)} %shard_map.92), channel_id=1, source_target_pairs={{0,2},{1,3},{2,0},{3,1},{4,6},{5,7},{6,4},{7,5},{8,10},{9,11},{10,... | collective-permute-start | bytes 933896 | tf_op jit(solution)/shard_map/ppermute | solution.py:229
  55.8 21.8 %collective-permute-start.23 = (bf16[152,1024]{1,0:T(8,128)(2,1)S(1)}, bf16[152,1024]{1,0:T(8,128)(2,1)S(1)}, u32[]{:S(2)}, u32[]{:S(2)}) collective-permute-start(bf16[152,1024]{1,0:T(8,128)(2,1)S(1)} %shard_map.93), channel_id=1, source_target_pairs={{0,4},{1,5},{2,6},{3,7},{4,0},{5,1},{6,2},{7,3},{8,12},{9,13},{10,... | collective-permute-start | bytes 933896 | tf_op jit(solution)/shard_map/ppermute | solution.py:229
  59.0 9.5 %collective-permute-start.12 = (bf16[152,256]{1,0:T(8,128)(2,1)S(1)}, bf16[152,256]{1,0:T(8,128)(2,1)S(1)}, u32[]{:S(2)}, u32[]{:S(2)}) collective-permute-start(bf16[152,256]{1,0:T(8,128)(2,1)S(1)} %get-tuple-element.108), channel_id=1, source_target_pairs={{0,16},{8,24},{16,0},{24,8},{1,17},{9,25},{17,1},{25,9},{2,18},{10... | collective-permute-start | bytes 233480 | tf_op jit(solution)/shard_map/ppermute | solution.py:220
  63.8 6.7 %collective-permute-start.13 = (bf16[152,256]{1,0:T(8,128)(2,1)S(1)}, bf16[152,256]{1,0:T(8,128)(2,1)S(1)}, u32[]{:S(2)}, u32[]{:S(2)}) collective-permute-start(bf16[152,256]{1,0:T(8,128)(2,1)S(1)} %get-tuple-element.109), channel_id=1, source_target_pairs={{0,8},{8,0},{16,24},{24,16},{1,9},{9,1},{17,25},{25,17},{2,10},{10... | collective-permute-start | bytes 233480 | tf_op jit(solution)/shard_map/ppermute | solution.py:220
  63.8 6.7 %collective-permute-start.14 = (bf16[152,256]{1,0:T(8,128)(2,1)S(1)}, bf16[152,256]{1,0:T(8,128)(2,1)S(1)}, u32[]{:S(2)}, u32[]{:S(2)}) collective-permute-start(bf16[152,256]{1,0:T(8,128)(2,1)S(1)} %get-tuple-element.110), channel_id=1, source_target_pairs={{0,24},{8,16},{16,8},{24,0},{1,25},{9,17},{17,9},{25,1},{2,26},{10... | collective-permute-start | bytes 233480 | tf_op jit(solution)/shard_map/ppermute | solution.py:220
  70.6 8.1 %collective-permute-start.16 = (bf16[152,256]{1,0:T(8,128)(2,1)S(1)}, bf16[152,256]{1,0:T(8,128)(2,1)S(1)}, u32[]{:S(2)}, u32[]{:S(2)}) collective-permute-start(bf16[152,256]{1,0:T(8,128)(2,1)S(1)} %shard_map.98.refs_0_), channel_id=1, source_target_pairs={{0,16},{8,24},{16,0},{24,8},{1,17},{9,25},{17,1},{25,9},{2,18},{10... | collective-permute-start | bytes 233480 | tf_op jit(solution)/shard_map/ppermute | solution.py:220
  71.5 7.2 %collective-permute-start.18 = (bf16[152,256]{1,0:T(8,128)(2,1)S(1)}, bf16[152,256]{1,0:T(8,128)(2,1)S(1)}, u32[]{:S(2)}, u32[]{:S(2)}) collective-permute-start(bf16[152,256]{1,0:T(8,128)(2,1)S(1)} %shard_map.98.refs_0_), channel_id=1, source_target_pairs={{0,8},{8,0},{16,24},{24,16},{1,9},{9,1},{17,25},{25,17},{2,10},{10... | collective-permute-start | bytes 233480 | tf_op jit(solution)/shard_map/ppermute | solution.py:220
  73.8 6.3 %collective-permute-start.20 = (bf16[152,256]{1,0:T(8,128)(2,1)S(1)}, bf16[152,256]{1,0:T(8,128)(2,1)S(1)}, u32[]{:S(2)}, u32[]{:S(2)}) collective-permute-start(bf16[152,256]{1,0:T(8,128)(2,1)S(1)} %shard_map.98.refs_0_), channel_id=1, source_target_pairs={{0,24},{8,16},{16,8},{24,0},{1,25},{9,17},{17,9},{25,1},{2,26},{10... | collective-permute-start | bytes 233480 | tf_op jit(solution)/shard_map/ppermute | solution.py:220
  76.1 13.1 %collective-permute-start.27 = (bf16[152,1024]{1,0:T(8,128)(2,1)S(1)}, bf16[152,1024]{1,0:T(8,128)(2,1)S(1)}, u32[]{:S(2)}, u32[]{:S(2)}) collective-permute-start(bf16[152,1024]{1,0:T(8,128)(2,1)S(1)} %shard_map.107), channel_id=1, source_target_pairs={{0,6},{1,7},{2,4},{3,5},{4,2},{5,3},{6,0},{7,1},{8,14},{9,15},{10,... | collective-permute-start | bytes 933896 | tf_op jit(solution)/shard_map/ppermute | solution.py:229
  77.6 3.7 %collective-permute-start.15 = (bf16[152,256]{1,0:T(8,128)(2,1)S(1)}, bf16[152,256]{1,0:T(8,128)(2,1)S(1)}, u32[]{:S(2)}, u32[]{:S(2)}) collective-permute-start(bf16[152,256]{1,0:T(8,128)(2,1)S(1)} %shard_map.98.refs_0_), channel_id=1, source_target_pairs={{0,1},{1,0},{2,3},{3,2},{4,5},{5,4},{6,7},{7,6},{8,9},{9,8},{10,11... | collective-permute-start | bytes 233480 | tf_op jit(solution)/shard_map/ppermute | solution.py:214
  78.7 2.6 %collective-permute-start.17 = (bf16[152,256]{1,0:T(8,128)(2,1)S(1)}, bf16[152,256]{1,0:T(8,128)(2,1)S(1)}, u32[]{:S(2)}, u32[]{:S(2)}) collective-permute-start(bf16[152,256]{1,0:T(8,128)(2,1)S(1)} %collective-permute-done.16.refs_1_), channel_id=1, source_target_pairs={{0,1},{1,0},{2,3},{3,2},{4,5},{5,4},{6,7},{7,6},{8,9},{9,8},{10,11... | collective-permute-start | bytes 233480 | tf_op jit(solution)/shard_map/ppermute | solution.py:214
  78.7 2.6 %collective-permute-start.19 = (bf16[152,256]{1,0:T(8,128)(2,1)S(1)}, bf16[152,256]{1,0:T(8,128)(2,1)S(1)}, u32[]{:S(2)}, u32[]{:S(2)}) collective-permute-start(bf16[152,256]{1,0:T(8,128)(2,1)S(1)} %collective-permute-done.18.refs_2_), channel_id=1, source_target_pairs={{0,1},{1,0},{2,3},{3,2},{4,5},{5,4},{6,7},{7,6},{8,9},{9,8},{10,11... | collective-permute-start | bytes 233480 | tf_op jit(solution)/shard_map/ppermute | solution.py:214
  80.1 1.3 %collective-permute-start.21 = (bf16[152,256]{1,0:T(8,128)(2,1)S(1)}, bf16[152,256]{1,0:T(8,128)(2,1)S(1)}, u32[]{:S(2)}, u32[]{:S(2)}) collective-permute-start(bf16[152,256]{1,0:T(8,128)(2,1)S(1)} %collective-permute-done.20.refs_3_), channel_id=1, source_target_pairs={{0,1},{1,0},{2,3},{3,2},{4,5},{5,4},{6,7},{7,6},{8,9},{9,8},{10,11... | collective-permute-start | bytes 233480 | tf_op jit(solution)/shard_map/ppermute | solution.py:214
  81.9 7.4 %collective-permute-start.25 = (bf16[152,512]{1,0:T(8,128)(2,1)S(1)}, bf16[152,512]{1,0:T(8,128)(2,1)S(1)}, u32[]{:S(2)}, u32[]{:S(2)}) collective-permute-start(bf16[152,512]{1,0:T(8,128)(2,1)S(1)} %get-tuple-element.130), channel_id=1, source_target_pairs={{0,2},{1,3},{2,0},{3,1},{4,6},{5,7},{6,4},{7,5},{8,10},{9,11},{10,... | collective-permute-start | bytes 466952 | tf_op jit(solution)/shard_map/ppermute | solution.py:229
  82.5 6.8 %collective-permute-start.26 = (bf16[152,512]{1,0:T(8,128)(2,1)S(1)}, bf16[152,512]{1,0:T(8,128)(2,1)S(1)}, u32[]{:S(2)}, u32[]{:S(2)}) collective-permute-start(bf16[152,512]{1,0:T(8,128)(2,1)S(1)} %get-tuple-element.131), channel_id=1, source_target_pairs={{0,4},{1,5},{2,6},{3,7},{4,0},{5,1},{6,2},{7,3},{8,12},{9,13},{10,... | collective-permute-start | bytes 466952 | tf_op jit(solution)/shard_map/ppermute | solution.py:229
  86.0 6.7 %collective-permute-start.24 = (bf16[152,512]{1,0:T(8,128)(2,1)S(1)}, bf16[152,512]{1,0:T(8,128)(2,1)S(1)}, u32[]{:S(2)}, u32[]{:S(2)}) collective-permute-start(bf16[152,512]{1,0:T(8,128)(2,1)S(1)} %get-tuple-element.128), channel_id=1, source_target_pairs={{0,2},{1,3},{2,0},{3,1},{4,6},{5,7},{6,4},{7,5},{8,10},{9,11},{10,... | collective-permute-start | bytes 466952 | tf_op jit(solution)/shard_map/ppermute | solution.py:229
  88.1 7.0 %collective-permute-start.30 = (bf16[152,512]{1,0:T(8,128)(2,1)S(1)}, bf16[152,512]{1,0:T(8,128)(2,1)S(1)}, u32[]{:S(2)}, u32[]{:S(2)}) collective-permute-start(bf16[152,512]{1,0:T(8,128)(2,1)S(1)} %get-tuple-element.143), channel_id=1, source_target_pairs={{0,4},{1,5},{2,6},{3,7},{4,0},{5,1},{6,2},{7,3},{8,12},{9,13},{10,... | collective-permute-start | bytes 466952 | tf_op jit(solution)/shard_map/ppermute | solution.py:229
  89.3 7.9 %copy-start.1 = (bf16[147,1024]{1,0:T(8,128)(2,1)S(1)}, bf16[147,1024]{1,0:T(8,128)(2,1)}, u32[]{:S(2)}) copy-start(bf16[147,1024]{1,0:T(8,128)(2,1)} %param.12) | copy-start | bytes 903172
  89.3 5.9 %collective-permute-start.29 = (bf16[152,512]{1,0:T(8,128)(2,1)S(1)}, bf16[152,512]{1,0:T(8,128)(2,1)S(1)}, u32[]{:S(2)}, u32[]{:S(2)}) collective-permute-start(bf16[152,512]{1,0:T(8,128)(2,1)S(1)} %shard_map.109), channel_id=1, source_target_pairs={{0,2},{1,3},{2,0},{3,1},{4,6},{5,7},{6,4},{7,5},{8,10},{9,11},{10,... | collective-permute-start | bytes 466952 | tf_op jit(solution)/shard_map/ppermute | solution.py:229
  90.2 6.8 %collective-permute-start.28 = (bf16[152,512]{1,0:T(8,128)(2,1)S(1)}, bf16[152,512]{1,0:T(8,128)(2,1)S(1)}, u32[]{:S(2)}, u32[]{:S(2)}) collective-permute-start(bf16[152,512]{1,0:T(8,128)(2,1)S(1)} %shard_map.108), channel_id=1, source_target_pairs={{0,4},{1,5},{2,6},{3,7},{4,0},{5,1},{6,2},{7,3},{8,12},{9,13},{10,... | collective-permute-start | bytes 466952 | tf_op jit(solution)/shard_map/ppermute | solution.py:229
